TPU v7x, 32 devices: a whole 2x2x4 slice. The times are simulated.
32 devices in a mesh: st: 8 (over z, x), sb: 4 (over y, core).
Axes of the slice: x: 2, y: 2, z: 4, core: 2. Of those that a mesh axis runs over, the one named last changes fastest.
Arguments:
- volts: bfloat16 [2, 1024, 126976], P(None, 'st'), may hold values from -6 to 6
- prototype: float32 [16, 4096], replicated, may hold values from -1.5 to 1.5
- beam_channels: int32 [384], replicated, may hold values from 0 to 4095, as said below
- station_index: int32 [256], replicated, may hold values from 0 to 511, as said below
- delays: float32 [256, 256], replicated, may hold values from -64 to 64
- gains: float32 [256, 256], replicated, may hold values from 0.5 to 2
- assign: int32 [384, 1], replicated, may hold values from 0 to 3; in each aligned block of 384 rows (0 to 383, 384 to 767, ...) at most 160 rows name the same one
Outputs:
- visibility: float32 [2, 4, 8, 1024, 1024], P(None, 'sb', 'st')
- beam_out: float32 [4, 160, 2, 16, 512], P('sb', 'st')
Inputs may be any that keep to these rules, and one draw needn't show every extreme that they name: `beam_channels`: 384 different channels. `station_index`: 256 different stations. `assign`: no index of sb receives more than 160 list entries, and some index receives exactly 160; every index receives at least one.
All inputs are finite; a program needn't handle non-finite values.
Results may differ from a plain program's by a relative error of at most 0.0054.
Values may be sent and summed in bfloat16 or wider, within the bound.
No kernel may reach another device: no remote copies, remote signals or barrier semaphores. Data moves between devices by JAX's collectives and lax.ppermute only.
A program may use at most 320 MiB of HBM per device.

v0:
```python
import math

import jax
import jax.numpy as jnp
from jax import lax
from jax.sharding import PartitionSpec as P

NCH = 4096
FRAMES = 16
SLOTS = 160


TWO_PI = 2.0 * math.pi


def polyphase(volts, prototype, frame_count):
    tap_count = prototype.shape[0]
    length = prototype.shape[1]
    segments = volts.reshape(2, volts.shape[1], frame_count + tap_count - 1, length)
    summed = jnp.zeros((2, volts.shape[1], frame_count, length), jnp.float32)
    for tap_idx in range(tap_count):
        summed = summed + prototype[tap_idx] * segments[
            :, :, tap_idx : tap_idx + frame_count, :
        ].astype(jnp.float32)
    return summed.astype(jnp.bfloat16)


def dft_tables(channels, length):
    sample_ids = jnp.arange(length, dtype=jnp.int32)
    phase_ids = sample_ids[:, None] * channels[None, :] % length
    angles = phase_ids.astype(jnp.float32) * (TWO_PI / length)
    scale_dft = 1.0 / math.sqrt(length)
    return (
        (jnp.cos(angles) * scale_dft).astype(jnp.bfloat16),
        (jnp.sin(angles) * scale_dft).astype(jnp.bfloat16),
    )


def transform(flat_rows, cos_t, sin_t):
    real_part = jnp.dot(flat_rows[0], cos_t, preferred_element_type=jnp.float32) + jnp.dot(
        flat_rows[1], sin_t, preferred_element_type=jnp.float32
    )
    imag_part = jnp.dot(flat_rows[1], cos_t, preferred_element_type=jnp.float32) - jnp.dot(
        flat_rows[0], sin_t, preferred_element_type=jnp.float32
    )
    return jnp.stack([real_part, imag_part]).astype(jnp.bfloat16)


def correlate(grouped):
    stacked = jnp.concatenate([grouped[0], grouped[1]], axis=1)
    turned = jnp.concatenate([grouped[1], -grouped[0]], axis=1)
    inverse = 1.0 / grouped.shape[2]
    vis_re = jnp.dot(stacked, stacked.T, preferred_element_type=jnp.float32) * inverse
    vis_im = jnp.dot(turned, stacked.T, preferred_element_type=jnp.float32) * inverse
    return jnp.stack([vis_re, vis_im])


def beam_weights(delays, gains, channel, length, listed):
    angles = delays * (channel.astype(jnp.float32) * (TWO_PI / length))
    scaling = gains * (1.0 / math.sqrt(listed))
    return (
        (scaling * jnp.cos(angles)).astype(jnp.bfloat16),
        (-scaling * jnp.sin(angles)).astype(jnp.bfloat16),
    )


def combine(spectrum, w_re, w_im):
    real_in = spectrum[:, 0]
    imag_in = spectrum[:, 1]

    def product(operand, weight):
        return jnp.einsum("sfjp,sbj->sfpb", operand, weight, preferred_element_type=jnp.float32)

    out_re = product(real_in, w_re) - product(imag_in, w_im)
    out_im = product(imag_in, w_re) + product(real_in, w_im)
    stacked = jnp.stack([out_re, out_im], axis=1)
    return stacked.reshape(stacked.shape[0], 2, stacked.shape[2], -1)


def body(volts, prototype, beam_channels, station_index, delays, gains, assign):
    sig_dev = volts.shape[1]
    st_count = lax.axis_size("st")
    sb_count = lax.axis_size("sb")
    sb_here = lax.axis_index("sb")
    st_here = lax.axis_index("st")
    filtered = polyphase(volts, prototype, FRAMES)
    flat_rows = filtered.reshape(2, sig_dev * FRAMES, NCH)
    band_width = NCH // sb_count
    channels = sb_here * band_width + jnp.arange(band_width, dtype=jnp.int32)
    cos_t, sin_t = dft_tables(channels, NCH)
    spectra = transform(flat_rows, cos_t, sin_t).reshape(2, sig_dev, FRAMES, band_width)
    turned_over = lax.all_to_all(spectra, "st", split_axis=3, concat_axis=1, tiled=True)
    signals = turned_over.shape[1]
    visibility = correlate(turned_over.reshape(2, signals, -1)).reshape(2, 1, 1, signals, signals)
    owners = assign[:, 0]
    matches = (owners == sb_here).astype(jnp.int32)
    position = jnp.cumsum(matches) - 1
    slot_ids = jnp.arange(SLOTS, dtype=jnp.int32)
    picker = matches[None, :] * (position[None, :] == slot_ids[:, None]).astype(jnp.int32)
    filled = jnp.sum(picker, axis=1)
    slot_channel = jnp.sum(picker * beam_channels[None, :], axis=1)
    per_dev = SLOTS // st_count
    listed = station_index.shape[0]
    cos_b, sin_b = dft_tables(slot_channel, NCH)
    slot_spectra = transform(flat_rows, cos_b, sin_b) * filled.astype(jnp.bfloat16)[None, None, :]
    slot_spectra = slot_spectra.reshape(2, sig_dev, FRAMES, SLOTS).transpose(3, 0, 2, 1)
    stations_dev = sig_dev // 2
    local_ids = st_here * stations_dev + jnp.arange(stations_dev, dtype=jnp.int32)
    chooser = (station_index[:, None] == local_ids[None, :]).astype(jnp.float32)
    delay_local = jnp.sum(delays[:, :, None] * chooser[None, :, :], axis=1)
    gain_local = jnp.sum(gains[:, :, None] * chooser[None, :, :], axis=1)
    spectrum = slot_spectra.reshape(per_dev * lax.axis_size("st"), 2, FRAMES, stations_dev, 2)
    w_re, w_im = beam_weights(
        delay_local[None], gain_local[None], slot_channel[:, None, None], NCH, listed
    )
    beam_out = lax.psum_scatter(
        combine(spectrum, w_re, w_im), "st", scatter_dimension=0, tiled=True
    )
    beam_out = beam_out.reshape(1, per_dev, 2, FRAMES, -1)
    return (visibility, beam_out)


def solution(mesh):
    in_specs = (P(None, "st", None), P(), P(), P(), P(), P(), P())
    out_specs = (P(None, "sb", "st", None, None), P("sb", "st", None, None, None))
    return jax.shard_map(body, mesh=mesh, in_specs=in_specs, out_specs=out_specs, check_vma=False)
```

profile of v0, /device:TPU:0, one launch (start us, length us, event | category | flops | bytes accessed | tf_op | source)
XLA Modules:
  0.0 1400.5 jit_solution(17065347269239940945)
XLA Ops:
  7.2 64.2 %multiply_convert_fusion.23 = bf16[4096,1024]{1,0:T(8,128)(2,1)} fusion(s32[1024]{0:T(1024)S(1)} %iota_add_fusion), kind=kLoop, calls=%fused_computation.9.clone.1.clone.clone.clone.1 | loop fusion | flops 67108864 | bytes 8392704 | tf_op jit(solution)/shard_map/dot_general | solution.py:40
  71.4 64.1 %multiply_convert_fusion.22 = bf16[4096,1024]{1,0:T(8,128)(2,1)} fusion(s32[1024]{0:T(1024)S(1)} %iota_add_fusion), kind=kLoop, calls=%fused_computation.9.clone.clone.clone.clone.1 | loop fusion | flops 67108864 | bytes 8392704 | tf_op jit(solution)/shard_map/dot_general | solution.py:43
  135.7 84.1 %copy.88 = bf16[2,128,126976]{1,2,0:T(8,128)(2,1)} copy(bf16[2,128,126976]{2,1,0:T(8,128)(2,1)} %param.7) | data formatting | bytes 130023424 | tf_op args[0]
  219.9 189.2 %add_convert_fusion = bf16[2,128,16,4096]{1,3,2,0:T(8,128)(2,1)} fusion(bf16[2,128,31,4096]{1,3,2,0:T(8,128)(2,1)} %bitcast.103, f32[4096]{0:T(1024)S(1)} %bitcast.138, f32[4096]{0:T(1024)S(1)} %bitcast.139, f32[4096]{0:T(1024)S(1)} %bitcast.125, f32[4096]{0:T(1024)S(1)} %bitcast.126, f32[4096]{0:T(1024)S(1)} %bitcast.127, f32[4096]{0:T(1024)S(1)} %bitcast.128, ...), kind=kLoop, calls=%fused_computation | loop fusion | flops 805306368 | bytes 570687488 | tf_op jit(solution)/shard_map/convert_element_type | solution.py:25
  409.1 22.5 %fusion.106 = (bf16[1,128,16,4096]{1,3,2,0:T(8,128)(2,1)}, bf16[1,128,16,4096]{1,3,2,0:T(8,128)(2,1)}) fusion(bf16[2,128,16,4096]{1,3,2,0:T(8,128)(2,1)} %add_convert_fusion), kind=kLoop, calls=%fused_computation.137 | loop fusion | bytes 67108864 | tf_op jit(solution)/shard_map/slice | solution.py:40
  431.5 22.2 %copy.89 = bf16[1,128,16,4096]{3,2,1,0:T(8,128)(2,1)} copy(bf16[1,128,16,4096]{1,3,2,0:T(8,128)(2,1)} %get-tuple-element.20) | data formatting | bytes 33554432 | tf_op jit(solution)/shard_map/slice | solution.py:40
  453.8 22.3 %copy.90 = bf16[1,128,16,4096]{3,2,1,0:T(8,128)(2,1)} copy(bf16[1,128,16,4096]{1,3,2,0:T(8,128)(2,1)} %get-tuple-element.21) | data formatting | bytes 33554432 | tf_op jit(solution)/shard_map/slice | solution.py:41
  476.0 77.9 %fusion.15 = f32[2048,1024]{1,0:T(8,128)} fusion(bf16[2048,4096]{1,0:T(8,128)(2,1)} %bitcast.108, s32[1024]{0:T(1024)S(1)} %copy-done.7), kind=kOutput, calls=%fused_computation.30 | convolution fusion | flops 17246978048 | bytes 25169920 | tf_op jit(solution)/shard_map/dot_general | solution.py:40
  553.9 85.0 %fusion.14 = f32[2048,1024]{1,0:T(8,128)} fusion(bf16[2048,4096]{1,0:T(8,128)(2,1)S(1)} %bitcast.113, s32[1024]{0:T(1024)S(1)} %copy-done.7), kind=kOutput, calls=%fused_computation.29 | convolution fusion | flops 17246978048 | bytes 25169920 | tf_op jit(solution)/shard_map/dot_general | solution.py:43
  638.9 23.2 %add_convert_fusion.1 = bf16[2048,1024]{1,0:T(8,128)(2,1)} fusion(f32[2048,1024]{1,0:T(8,128)} %fusion.15, bf16[2048,4096]{1,0:T(8,128)(2,1)S(1)} %bitcast.114, bf16[4096,1024]{1,0:T(8,128)(2,1)} %multiply_convert_fusion.23), kind=kOutput, calls=%fused_computation.28 | convolution fusion | flops 17184063488 | bytes 37748736 | tf_op jit(solution)/shard_map/dot_general | solution.py:40
  669.4 24.3 %subtract_convert_fusion = bf16[2048,1024]{1,0:T(8,128)(2,1)} fusion(f32[2048,1024]{1,0:T(8,128)} %fusion.14, bf16[2048,4096]{1,0:T(8,128)(2,1)} %bitcast.109, bf16[4096,1024]{1,0:T(8,128)(2,1)} %multiply_convert_fusion.22), kind=kOutput, calls=%fused_computation.27 | convolution fusion | flops 17184063488 | bytes 37748736 | tf_op jit(solution)/shard_map/dot_general | solution.py:43
  701.0 7.6 pad_maximum_fusion.1
  708.6 7.4 all-to-all-start
  716.8 17.3 %fusion.61 = f32[2048,160]{0,1:T(8,128)S(1)} fusion(bf16[2048,4096]{1,0:T(8,128)(2,1)} %bitcast.110, s32[160]{0:T(256)S(1)} %get-tuple-element.19), kind=kOutput, calls=%fused_computation.80 | convolution fusion | flops 2694840320 | bytes 18088576 | tf_op jit(solution)/shard_map/dot_general | solution.py:40
  734.1 18.5 %fusion.60 = f32[2048,160]{0,1:T(8,128)} fusion(bf16[2048,4096]{1,0:T(8,128)(2,1)} %bitcast.112, s32[160]{0:T(256)S(1)} %get-tuple-element.19), kind=kOutput, calls=%fused_computation.79 | convolution fusion | flops 2694840320 | bytes 18088576 | tf_op jit(solution)/shard_map/dot_general | solution.py:43
  752.7 14.6 %fusion.47 = bf16[2048,160]{0,1:T(8,128)(2,1)S(1)} fusion(f32[2048,160]{0,1:T(8,128)S(1)} %fusion.61, bf16[2048,4096]{1,0:T(8,128)(2,1)S(1)} %bitcast.117, s32[160]{0:T(256)S(1)} %get-tuple-element.19), kind=kOutput, calls=%fused_computation.70 | convolution fusion | flops 2695495680 | bytes 18743936 | tf_op jit(solution)/shard_map/dot_general | solution.py:40
  767.8 17.7 %fusion.46 = bf16[2048,160]{0,1:T(8,128)(2,1)S(1)} fusion(f32[2048,160]{0,1:T(8,128)} %fusion.60, bf16[2048,4096]{1,0:T(8,128)(2,1)} %bitcast.111, s32[160]{0:T(256)S(1)} %get-tuple-element.19), kind=kOutput, calls=%fused_computation.68 | convolution fusion | flops 2695495680 | bytes 18743936 | tf_op jit(solution)/shard_map/dot_general | solution.py:43
  797.7 34.9 %fusion.21 = f32[160,16,2,256]{3,1,2,0:T(8,128)S(1)} fusion(f32[256,64]{0,1:T(8,128)S(1)} %get-tuple-element.45, f32[160]{0:T(256)S(1)} %convert_multiply_fusion, f32[256,64]{0,1:T(8,128)S(1)} %copy.100, bf16[160,1,16,64,2]{3,2,4,0,1:T(8,128)(2,1)S(1)} %copy.111), kind=kOutput, calls=%fused_computation.35 | convolution fusion | flops 175636480 | bytes 6029952 | tf_op jit(solution)/shard_map/sfjp,sbj->sfpb/dot_general | solution.py:72
  832.5 34.3 %fusion.48 = f32[160,16,2,256]{3,1,2,0:T(8,128)S(1)} fusion(f32[160,16,2,256]{3,1,2,0:T(8,128)S(1)} %fusion.21, f32[160]{0:T(256)S(1)} %convert_multiply_fusion, f32[256,64]{0,1:T(8,128)S(1)} %copy.100, f32[256,64]{0,1:T(8,128)S(1)} %get-tuple-element.44, bf16[160,1,16,64,2]{3,2,4,0,1:T(8,128)(2,1)S(1)} %copy.110), kind=kOutput, calls=%fused_computation.71 | convolution fusion | flops 176947200 | bytes 11272832 | tf_op jit(solution)/shard_map/sfjp,sbj->sfpb/dot_general | solution.py:72
  866.9 7.4 copy.102
  874.3 8.0 stack.45
  882.3 34.8 %fusion.19 = f32[160,16,2,256]{3,1,2,0:T(8,128)S(1)} fusion(f32[256,64]{0,1:T(8,128)S(1)} %get-tuple-element.45, f32[160]{0:T(256)S(1)} %convert_multiply_fusion, f32[256,64]{0,1:T(8,128)S(1)} %copy.100, bf16[160,1,16,64,2]{3,2,4,0,1:T(8,128)(2,1)S(1)} %copy.110), kind=kOutput, calls=%fused_computation.34 | convolution fusion | flops 175636480 | bytes 6029952 | tf_op jit(solution)/shard_map/sfjp,sbj->sfpb/dot_general | solution.py:72
  917.1 34.6 %fusion.51 = f32[160,16,2,256]{3,1,2,0:T(8,128)S(1)} fusion(f32[160,16,2,256]{3,1,2,0:T(8,128)S(1)} %fusion.19, f32[160]{0:T(256)S(1)} %convert_multiply_fusion, f32[256,64]{0,1:T(8,128)S(1)} %copy.100, f32[256,64]{0,1:T(8,128)S(1)} %get-tuple-element.44, bf16[160,1,16,64,2]{3,2,4,0,1:T(8,128)(2,1)S(1)} %copy.111), kind=kOutput, calls=%fused_computation.72 | convolution fusion | flops 176947200 | bytes 11272832 | tf_op jit(solution)/shard_map/sfjp,sbj->sfpb/dot_general | solution.py:72
  951.7 7.4 copy.103
  959.2 8.0 stack.46
  967.1 10.5 pad_maximum_fusion
  979.5 327.1 %all-reduce.3.cloned.1.call-done = f32[160,2,16,512]{3,2,0,1:T(8,128)} async-done(((f32[160,2,16,512]{3,2,0,1:T(8,128)}), f32[160,2,16,512]{3,2,0,1:T(8,128)}) %all-reduce.3.cloned.1.call-update) | async-done | bytes 10485776
  1309.2 10.0 copy.93
  1332.2 8.0 bitcast_negate_fusion
  1355.8 16.3 %multiply_bitcast_fusion.1 = f32[1,1024,1024]{2,1,0:T(8,128)} fusion(bf16[1024,4096]{1,0:T(8,128)(2,1)} %constant_dynamic-update-slice_fusion), kind=kOutput, calls=%fused_computation.55 | convolution fusion | flops 8590983168 | bytes 12582912 | tf_op jit(solution)/shard_map/dot_general | solution.py:53
  1372.1 12.8 multiply_bitcast_fusion
  1384.9 8.5 maximum_bitcast_fusion
  (69 shorter events, 60.4 us)
Async XLA Ops:
  7.2 64.2 %copy-start.6 = (s32[1024]{0:T(1024)}, s32[1024]{0:T(1024)S(1)}, u32[]{:S(2)}) copy-start(s32[1024]{0:T(1024)S(1)} %iota_add_fusion) | copy-start | bytes 12292
  7.2 128.3 %copy-start.3 = (f32[16,4096]{1,0:T(8,128)S(1)}, f32[16,4096]{1,0:T(8,128)}, u32[]{:S(2)}) copy-start(f32[16,4096]{1,0:T(8,128)} %param.8) | copy-start | bytes 786436
  453.8 22.3 %copy-start.7 = (s32[1024]{0:T(1024)S(1)}, s32[1024]{0:T(1024)}, u32[]{:S(2)}) copy-start(s32[1024]{0:T(1024)} %copy-done.6) | copy-start | bytes 12292
  476.0 77.9 %copy-start.1 = (bf16[1,128,16,4096]{3,2,1,0:T(8,128)(2,1)S(1)}, bf16[1,128,16,4096]{3,2,1,0:T(8,128)(2,1)}, u32[]{:S(2)}) copy-start(bf16[1,128,16,4096]{3,2,1,0:T(8,128)(2,1)} %copy.90) | copy-start | bytes 50331652
  708.6 7.4 copy-start.9
  708.6 8.1 copy-start.8
  708.6 600.6 %all-to-all-start = ((bf16[2,128,16,1024]{1,2,0,3:T(8,128)(2,1)}), bf16[2,128,16,1024]{1,2,0,3:T(8,128)(2,1)}, u32[]{:S(2)}, u32[]{:S(2)}) async-start(bf16[2,128,16,1024]{1,2,0,3:T(8,128)(2,1)} %pad_maximum_fusion.1), calls=%async_computation | async-start | bytes 16777216 | tf_op jit(solution)/shard_map/all_to_all | solution.py:92
  716.0 590.6 %all-reduce.3.cloned.1.call-start = ((), (), s32[]{:S(2)}) async-start(), calls=%async_computation.1 | async-start | bytes 20971520
  716.8 35.8 %slice-start = ((s8[16777216]{0:T(1024)(128)(4,1)}), s8[4194304]{0:T(1024)(128)(4,1)S(1)}, s32[]{:S(2)}) async-start(s8[16777216]{0:T(1024)(128)(4,1)} %bitcast.115), calls=%async_computation.2 | async-start | bytes 8388608
  716.8 35.8 %slice-start.1 = ((s8[16777216]{0:T(1024)(128)(4,1)}), s8[4194304]{0:T(1024)(128)(4,1)S(1)}, s32[]{:S(2)}) async-start(s8[16777216]{0:T(1024)(128)(4,1)} %bitcast.115), calls=%async_computation.3 | async-start | bytes 8388608
  734.1 18.5 %slice-start.2 = ((s8[16777216]{0:T(1024)(128)(4,1)}), s8[4194304]{0:T(1024)(128)(4,1)S(1)}, s32[]{:S(2)}) async-start(s8[16777216]{0:T(1024)(128)(4,1)} %bitcast.115), calls=%async_computation.4 | async-start | bytes 8388608
  734.1 18.5 %slice-start.3 = ((s8[16777216]{0:T(1024)(128)(4,1)}), s8[4194304]{0:T(1024)(128)(4,1)S(1)}, s32[]{:S(2)}) async-start(s8[16777216]{0:T(1024)(128)(4,1)} %bitcast.115), calls=%async_computation.5 | async-start | bytes 8388608
  785.6 4.2 copy-start.10
  785.6 4.3 copy-start.4
  785.6 4.3 copy-start.5
  977.6 0.7 copy-start.11
  1347.1 4.5 copy-start
  1355.8 16.3 %copy-start.2 = (bf16[1024,2048]{1,0:T(8,128)(2,1)S(1)}, bf16[1024,2048]{1,0:T(8,128)(2,1)}, u32[]{:S(2)}) copy-start(bf16[1024,2048]{1,0:T(8,128)(2,1)} %get-tuple-element.24) | copy-start | bytes 12582916
Sparse Core Ops, SparseCore 0:
  977.8 328.7 all-reduce.2
where the time goes:
time: 1410 us; the launch traced here: 1400 us
  matrix products  446 us (32%)
  other arithmetic  358 us (25%)
  waiting for transfers between devices  327 us (23%)
  local copies, waits for them, and re-layouts  247 us (18%)
  between operations  15.3 us (1%)
    unnamed x2, waiting for transfers between devices  327 us
    convert_element_type x1, other arithmetic, polyphase(): return summed.astype(jnp.bfloat16)  189 us
    dot_general x4, matrix products, product(): jnp.einsum('sfjp,sbj->sfpb', operand, weight, preferred_element_type=jnp....  139 us
    dot_general x2, matrix products, transform(): jnp.dot(flat_rows[1], cos_t, preferred_element_type=jnp.float32)  103 us
    unnamed x38, local copies, waits for them, and re-layouts  96.2 us
    dot_general x2, matrix products, transform(): jnp.dot(flat_rows[0], cos_t, preferred_element_type=jnp.float32)  95.2 us
    dot_general x1, other arithmetic, transform(): jnp.dot(flat_rows[1], sin_t, preferred_element_type=jnp.float32)  64.2 us
    dot_general x1, other arithmetic, transform(): jnp.dot(flat_rows[0], sin_t, preferred_element_type=jnp.float32)  64.1 us
  transfers between devices with their start and end apart: 2, of which 1 were waited for; matrix products, arithmetic and copies ran while one was open for 19% of the time, Pallas kernels for 0%

commit v1 on v0

v1 whole, which is shorter than its diff:
```python
import functools
import math

import jax
import jax.numpy as jnp
from jax import lax
from jax.experimental import pallas as pl
from jax.experimental.pallas import tpu as pltpu
from jax.sharding import PartitionSpec as P

NCH = 4096
FRAMES = 16
SLOTS = 160
RADIX = 8
LANES = 128
ROWS = 16
CHUNK = 32
VMEM = 56 * 1024 * 1024

TWO_PI = 2.0 * math.pi
NT = (((1,), (1,)), ((), ()))


def phase(turns, length):
    angles = (turns % length).astype(jnp.float32) * (TWO_PI / length)
    return jnp.cos(angles), jnp.sin(angles)


def table_kernel(hi_c, hi_s, lo_c, lo_s, out):
    coarse = hi_c.shape[1]
    fine = lo_c.shape[1]
    width = lo_c.shape[2]
    depth = coarse * fine

    def branch(b, carry):
        low_c, low_s = lo_c[b], lo_s[b]

        def block(a, inner):
            high_c, high_s = hi_c[b, pl.ds(a, 1), :], hi_s[b, pl.ds(a, 1), :]
            cos_t = high_c * low_c - high_s * low_s
            sin_t = high_s * low_c + high_c * low_s
            top = pl.multiple_of(a * fine, fine)
            out[b, pl.ds(top, fine), :width] = cos_t.astype(out.dtype)
            out[b, pl.ds(top, fine), width:] = (-sin_t).astype(out.dtype)
            out[b, pl.ds(depth + top, fine), :width] = sin_t.astype(out.dtype)
            out[b, pl.ds(depth + top, fine), width:] = cos_t.astype(out.dtype)
            return inner

        return lax.fori_loop(0, coarse, block, carry)

    lax.fori_loop(0, hi_c.shape[0], branch, 0)


def radix8(re, im):
    half = math.sqrt(0.5)

    def four(xr, xi):
        ar, ai, br, bi = xr[0] + xr[2], xi[0] + xi[2], xr[0] - xr[2], xi[0] - xi[2]
        cr, ci, dr, di = xr[1] + xr[3], xi[1] + xi[3], xr[1] - xr[3], xi[1] - xi[3]
        return [ar + cr, br + di, ar - cr, br - di], [ai + ci, bi - dr, ai - ci, bi + dr]

    er, ei = four(re[0::2], im[0::2])
    odd_r, odd_i = four(re[1::2], im[1::2])
    tr = [odd_r[0], (odd_r[1] + odd_i[1]) * half, odd_i[2], (odd_i[3] - odd_r[3]) * half]
    ti = [odd_i[0], (odd_i[1] - odd_r[1]) * half, -odd_r[2], (odd_r[3] + odd_i[3]) * -half]
    return (
        [e + t for e, t in zip(er, tr)] + [e - t for e, t in zip(er, tr)],
        [e + t for e, t in zip(ei, ti)] + [e - t for e, t in zip(ei, ti)],
    )


def swap_blocks(parts, lane_ids):
    count = len(parts)
    width = LANES // count
    parts = list(parts)
    step = 1
    while step < count:
        keep = (lane_ids // width) % (2 * step) < step
        for b in range(count):
            if b & step == 0:
                low, high = parts[b], parts[b + step]
                parts[b] = jnp.where(keep, low, pltpu.roll(high, step * width, 1))
                parts[b + step] = jnp.where(keep, pltpu.roll(low, LANES - step * width, 1), high)
        step *= 2
    return parts


def channel_kernel(volts, prototype, table, *rest):
    outs = rest[:RADIX]
    branches, filtered, product = rest[RADIX:]
    taps = prototype.shape[0]
    length = prototype.shape[1]
    frames = filtered.shape[2]
    depth = length // RADIX

    def column(j, carry):
        def strip(n1, inner):
            base = pl.multiple_of(n1 * depth + j * LANES, LANES)
            coefs = [prototype[t : t + 1, pl.ds(base, LANES)] for t in range(taps)]
            for part in range(2):
                sums = [None] * frames
                for seg in range(frames + taps - 1):
                    start = pl.multiple_of(seg * length + base, LANES)
                    value = volts[part, :, pl.ds(start, LANES)].astype(jnp.float32)
                    for f in range(max(0, seg - taps + 1), min(frames, seg + 1)):
                        term = coefs[seg - f] * value
                        sums[f] = term if sums[f] is None else sums[f] + term
                    if seg >= taps - 1:
                        filtered[part, n1, seg - taps + 1] = sums[seg - taps + 1]
            return inner

        lax.fori_loop(0, RADIX, strip, 0)

        def butterfly(f, inner):
            re, im = radix8(
                [filtered[0, n1, f] for n1 in range(RADIX)],
                [filtered[1, n1, f] for n1 in range(RADIX)],
            )
            for b in range(RADIX):
                branches[b, f, :, pl.ds(pl.multiple_of(j * LANES, LANES), LANES)] = re[b].astype(branches.dtype)
                branches[b, f, :, pl.ds(pl.multiple_of(depth + j * LANES, LANES), LANES)] = im[b].astype(branches.dtype)
            return inner

        lax.fori_loop(0, frames, butterfly, 0)
        return carry

    lax.fori_loop(0, depth // LANES, column, 0)

    def multiply(b, carry):
        rows = branches[b].reshape(frames * ROWS, 2 * depth)
        product[b] = jnp.dot(rows, table[b], preferred_element_type=jnp.float32)
        return carry

    lax.fori_loop(0, RADIX, multiply, 0)
    lane_ids = lax.broadcasted_iota(jnp.int32, (ROWS, LANES), 1)

    def regroup(f, carry):
        top = pl.multiple_of(f * ROWS, ROWS)
        for part in range(2):
            pieces = [product[b, pl.ds(top, ROWS), part * LANES : (part + 1) * LANES] for b in range(RADIX)]
            for g, piece in enumerate(swap_blocks(pieces, lane_ids)):
                lane = pl.multiple_of(part * frames * LANES + f * LANES, LANES)
                outs[g][:, pl.ds(lane, LANES)] = piece.astype(outs[g].dtype)
        return carry

    lax.fori_loop(0, frames, regroup, 0)


def channelise(volts, prototype, table, first, count):
    length = volts.shape[2]
    steps = count // ROWS
    depth = NCH // RADIX
    wide = 2 * FRAMES * LANES
    work = 2 * count * FRAMES * NCH
    return pl.pallas_call(
        channel_kernel,
        grid=(steps,),
        in_specs=[
            pl.BlockSpec((2, ROWS, length), lambda i: (0, first // ROWS + i, 0)),
            pl.BlockSpec(prototype.shape, lambda i: (0, 0)),
            pl.BlockSpec(table.shape, lambda i: (0, 0, 0)),
        ],
        out_specs=[pl.BlockSpec((ROWS, wide), lambda i: (i, 0))] * RADIX
        + [pl.BlockSpec((RADIX, FRAMES, ROWS, 2 * depth), lambda i: (0, 0, i, 0))],
        out_shape=[jax.ShapeDtypeStruct((count, wide), jnp.bfloat16)] * RADIX
        + [jax.ShapeDtypeStruct((RADIX, FRAMES, count, 2 * depth), jnp.bfloat16)],
        scratch_shapes=[
            pltpu.VMEM((2, RADIX, FRAMES, ROWS, LANES), jnp.float32),
            pltpu.VMEM((RADIX, FRAMES * ROWS, 2 * LANES), jnp.float32),
        ],
        compiler_params=pltpu.CompilerParams(vmem_limit_bytes=VMEM),
        cost_estimate=pl.CostEstimate(
            flops=work * 2 * depth, bytes_accessed=2 * count * length * 2 + 4 * work, transcendentals=0
        ),
    )(volts, prototype, table)


def slot_kernel(row_branch, hi_c, hi_s, lo_c, lo_s, *rest):
    chunks = rest[: len(rest) - 2]
    table, total = rest[len(rest) - 2 :]
    chunks, outs = [c for c in chunks if len(c.shape) == 4], [c for c in chunks if len(c.shape) == 2]
    depth = chunks[0].shape[3] // 2
    f_step = chunks[0].shape[1]

    @pl.when(pl.program_id(0) == 0)
    def _():
        for a in range(hi_c.shape[1]):
            high_c, high_s = hi_c[:, a : a + 1], hi_s[:, a : a + 1]
            table[:, a * LANES : (a + 1) * LANES] = (high_c * lo_c[...] - high_s * lo_s[...]).astype(table.dtype)
            table[:, depth + a * LANES : depth + (a + 1) * LANES] = (
                high_s * lo_c[...] + high_c * lo_s[...]
            ).astype(table.dtype)

    total[...] = jnp.zeros_like(total)

    def branch(b, carry):
        rows = jnp.concatenate([c[b, f] for f in range(f_step) for c in chunks], axis=0)
        got = lax.dot_general(table[...], rows, NT, preferred_element_type=jnp.float32)
        total[...] = jnp.where(row_branch[...] == b, got, total[...])
        return carry

    lax.fori_loop(0, RADIX, branch, 0)
    sig = total.shape[1] // f_step
    per = total.shape[0] // len(outs)
    for s, out in enumerate(outs):
        out[...] = jnp.concatenate(
            [total[s * per : (s + 1) * per, f * sig : (f + 1) * sig] for f in range(f_step)], axis=0
        ).astype(out.dtype)


def slot_spectra(row_channel, row_filled, row_turned, chunks, st_count):
    depth = NCH // RADIX
    rows = row_channel.shape[0]
    sig_dev = sum(c.shape[2] for c in chunks)
    f_step = 2 * LANES // sig_dev
    per = rows // st_count
    coarse = jnp.arange(depth // LANES, dtype=jnp.int32) * LANES
    fine = jnp.arange(LANES, dtype=jnp.int32)
    hi_c, hi_s = phase(row_channel[:, None] * coarse[None, :] + row_turned[:, None] * (NCH // 4), NCH)
    lo_c, lo_s = phase(row_channel[:, None] * fine[None, :], NCH)
    scaling = row_filled.astype(jnp.float32)[:, None] * (1.0 / math.sqrt(NCH))
    row_branch = (row_channel % RADIX)[:, None]
    small = [row_branch, hi_c * scaling, hi_s * scaling, lo_c, lo_s]
    return pl.pallas_call(
        slot_kernel,
        grid=(FRAMES // f_step,),
        in_specs=[pl.BlockSpec(x.shape, lambda i: (0, 0)) for x in small]
        + [pl.BlockSpec((RADIX, f_step, c.shape[2], 2 * depth), lambda i: (0, i, 0, 0)) for c in chunks],
        out_specs=[pl.BlockSpec((f_step * per, sig_dev), lambda i: (i, 0))] * st_count,
        out_shape=[jax.ShapeDtypeStruct((FRAMES * per, sig_dev), jnp.bfloat16)] * st_count,
        scratch_shapes=[
            pltpu.VMEM((rows, 2 * depth), jnp.bfloat16),
            pltpu.VMEM((rows, f_step * sig_dev), jnp.float32),
        ],
        compiler_params=pltpu.CompilerParams(vmem_limit_bytes=VMEM),
        cost_estimate=pl.CostEstimate(
            flops=2 * rows * 2 * NCH * FRAMES * sig_dev,
            bytes_accessed=4 * NCH * FRAMES * sig_dev,
            transcendentals=0,
        ),
    )(*small, *chunks)


def correlate(here, received, st_count):
    flat = [(c, s, piece) for c, row in enumerate(received) for s, piece in enumerate(row)]
    rows = [row[0].shape[0] for row in received]
    sig_dev = sum(rows)
    signals = sig_dev * st_count
    wide = flat[0][2].shape[1]
    block = min(256, signals)
    blocks = signals // block
    half = wide // 2

    def kernel(here_ref, *refs):
        pieces, (out, held, sems) = refs[:-3], refs[-3:]
        copies = []
        for index, (c, s, _) in enumerate(flat):
            top = (here_ref[0] ^ s) * sig_dev + sum(rows[:c])
            dst = held.at[pl.ds(pl.multiple_of(top, ROWS), rows[c])]
            copies.append(pltpu.make_async_copy(pieces[index], dst, sems.at[index]))
        for copy in copies:
            copy.start()
        for copy in copies:
            copy.wait()
        inverse = 1.0 / half

        def product(left, right):
            return lax.dot_general(left, right, NT, preferred_element_type=jnp.float32)

        for i in range(blocks):
            for j in range(i + 1):
                at_i, at_j = slice(i * block, (i + 1) * block), slice(j * block, (j + 1) * block)
                re = (
                    product(held[at_i, :half], held[at_j, :half]) + product(held[at_i, half:], held[at_j, half:])
                ) * inverse
                im = (
                    product(held[at_i, half:], held[at_j, :half]) - product(held[at_i, :half], held[at_j, half:])
                ) * inverse
                out[0, at_i, at_j] = re
                out[1, at_i, at_j] = im
                if i != j:
                    out[0, at_j, at_i] = re.T
                    out[1, at_j, at_i] = -im.T

    return pl.pallas_call(
        kernel,
        in_specs=[pl.BlockSpec(memory_space=pltpu.SMEM)] + [pl.BlockSpec(memory_space=pl.ANY)] * len(flat),
        out_specs=pl.BlockSpec(memory_space=pltpu.VMEM),
        out_shape=jax.ShapeDtypeStruct((2, signals, signals), jnp.float32),
        scratch_shapes=[
            pltpu.VMEM((signals, wide), jnp.bfloat16),
            pltpu.SemaphoreType.DMA((len(flat),)),
        ],
        compiler_params=pltpu.CompilerParams(vmem_limit_bytes=VMEM),
        cost_estimate=pl.CostEstimate(
            flops=2 * signals * signals * wide,
            bytes_accessed=2 * signals * wide + 8 * signals * signals,
            transcendentals=0,
        ),
    )(here, *[piece for _, _, piece in flat])


def weight_kernel(channel, delays, gains, out):
    beams = delays.shape[0]
    turns = delays[...] * (channel[pl.program_id(0)].astype(jnp.float32) * (1.0 / NCH))
    part = turns - jnp.floor(turns + 0.5)
    square = part * part
    cos_t = jnp.full_like(part, TWO_PI**16 / math.factorial(16))
    sin_t = jnp.full_like(part, -(TWO_PI**15) / math.factorial(15))
    for power in range(14, -1, -2):
        sign = -1.0 if power % 4 == 2 else 1.0
        cos_t = cos_t * square + sign * TWO_PI**power / math.factorial(power)
        if power > 0:
            sign = -1.0 if (power - 1) % 4 == 3 else 1.0
            sin_t = sin_t * square + sign * TWO_PI ** (power - 1) / math.factorial(power - 1)
    scaled = gains[...] * (1.0 / math.sqrt(gains.shape[1]))
    out[0, :beams] = (scaled * cos_t).astype(out.dtype)
    out[0, beams:] = (-scaled * sin_t * part).astype(out.dtype)


def beam_weights(channel, delays, gains):
    beams, listed = delays.shape
    slots = channel.shape[0]
    return pl.pallas_call(
        weight_kernel,
        grid=(slots,),
        in_specs=[
            pl.BlockSpec(memory_space=pltpu.SMEM),
            pl.BlockSpec(delays.shape, lambda i: (0, 0)),
            pl.BlockSpec(gains.shape, lambda i: (0, 0)),
        ],
        out_specs=pl.BlockSpec((1, 2 * beams, listed), lambda i: (i, 0, 0)),
        out_shape=jax.ShapeDtypeStruct((slots, 2 * beams, listed), jnp.bfloat16),
        cost_estimate=pl.CostEstimate(
            flops=40 * slots * beams * listed, bytes_accessed=4 * slots * beams * listed, transcendentals=0
        ),
    )(channel, delays, gains)


def combine(pieces, chooser, weights):
    slots, beams2, listed = weights.shape
    beams = beams2 // 2
    sig_dev = pieces[0].shape[1]
    total_rows = pieces[0].shape[0]
    tiles = 2 * listed // LANES

    def kernel(*refs):
        got, (choose, weight, out, picked) = refs[: len(pieces)], refs[len(pieces) :]
        acc = None
        for s, piece in enumerate(got):
            term = jnp.dot(
                piece[...], choose[s * sig_dev : (s + 1) * sig_dev, :], preferred_element_type=jnp.float32
            )
            acc = term if acc is None else acc + term
        for lane in range(tiles):
            picked[lane] = acc[:, lane * LANES : (lane + 1) * LANES]
        for i in range(slots):
            rows = jnp.concatenate(
                [
                    jnp.concatenate(
                        [
                            picked[p * tiles // 2 + lane, pl.ds(part * slots + i, FRAMES, 2 * slots), :]
                            for lane in range(tiles // 2)
                        ],
                        axis=1,
                    )
                    for p in range(2)
                    for part in range(2)
                ],
                axis=0,
            )
            mixed = lax.dot_general(rows.astype(jnp.bfloat16), weight[i], NT, preferred_element_type=jnp.float32)
            for p in range(2):
                at = 2 * FRAMES * p
                of_re, of_im = mixed[at : at + FRAMES], mixed[at + FRAMES : at + 2 * FRAMES]
                out[0, i, 0, :, p * beams : (p + 1) * beams] = of_re[:, :beams] - of_im[:, beams:]
                out[0, i, 1, :, p * beams : (p + 1) * beams] = of_im[:, :beams] + of_re[:, beams:]

    return pl.pallas_call(
        kernel,
        out_shape=jax.ShapeDtypeStruct((1, slots, 2, FRAMES, 2 * beams), jnp.float32),
        scratch_shapes=[pltpu.VMEM((tiles, total_rows, LANES), jnp.float32)],
        compiler_params=pltpu.CompilerParams(vmem_limit_bytes=VMEM),
        cost_estimate=pl.CostEstimate(
            flops=2 * total_rows * 2 * listed * (sig_dev * len(pieces) + 2 * beams),
            bytes_accessed=8 * total_rows * listed,
            transcendentals=0,
        ),
    )(*pieces, chooser, weights)


def exchange(pieces, st_count):
    return [pieces[0]] + [
        lax.ppermute(pieces[s], "st", [(i, i ^ s) for i in range(st_count)]) for s in range(1, st_count)
    ]


def after(value, other):
    return lax.optimization_barrier((value, other))[0]


def body(volts, prototype, beam_channels, station_index, delays, gains, assign):
    sig_dev = volts.shape[1]
    st_count = lax.axis_size("st")
    sb_count = lax.axis_size("sb")
    sb_here = lax.axis_index("sb").astype(jnp.int32)
    st_here = lax.axis_index("st").astype(jnp.int32)
    partner = st_here ^ jnp.arange(st_count, dtype=jnp.int32)

    band = NCH // sb_count
    fine = band // RADIX // st_count
    depth = NCH // RADIX
    low = (partner[:, None] * fine + jnp.arange(fine, dtype=jnp.int32)[None, :]).reshape(-1)
    channels = sb_here * band + jnp.arange(RADIX, dtype=jnp.int32)[:, None] + RADIX * low[None, :]
    lo_ids = jnp.arange(ROWS, dtype=jnp.int32)
    hi_ids = jnp.arange(depth // ROWS, dtype=jnp.int32) * ROWS
    lo_c, lo_s = phase(channels[:, None, :] * lo_ids[None, :, None], NCH)
    hi_c, hi_s = phase(channels[:, None, :] * hi_ids[None, :, None], NCH)
    scale = 1.0 / math.sqrt(NCH)
    table = pl.pallas_call(
        table_kernel,
        out_shape=jax.ShapeDtypeStruct((RADIX, 2 * depth, 2 * LANES), jnp.bfloat16),
        compiler_params=pltpu.CompilerParams(vmem_limit_bytes=VMEM),
    )(hi_c * scale, hi_s * scale, lo_c, lo_s)

    chunk = min(CHUNK, sig_dev)
    received, branches = [], []
    for first in range(0, sig_dev, chunk):
        if len(received) > 1:
            table = after(table, received[-2])
        *groups, kept = channelise(volts, prototype, table, first, chunk)
        table = after(table, groups[0])
        branches.append(kept)
        if st_count > RADIX:
            inner = st_count // RADIX
            split = [
                jnp.moveaxis(g.reshape(chunk, 2 * FRAMES, RADIX, inner, fine), 3, 0).reshape(inner, chunk, -1)
                for g in groups
            ]
            groups = [piece[d] for piece in split for d in range(inner)]
        received.append(exchange(groups, st_count))

    owners = assign[:, 0]
    matches = (owners == sb_here).astype(jnp.int32)
    position = jnp.cumsum(matches) - 1
    per_dev = SLOTS // st_count
    slot_ids = (partner[:, None] * per_dev + jnp.arange(per_dev, dtype=jnp.int32)[None, :]).reshape(-1)
    picker = matches[None, :] * (position[None, :] == slot_ids[:, None]).astype(jnp.int32)
    filled = jnp.sum(picker, axis=1)
    slot_channel = jnp.sum(picker * beam_channels[None, :], axis=1)

    def by_row(values):
        spread = jnp.broadcast_to(values.reshape(st_count, 1, per_dev), (st_count, 2, per_dev))
        return spread.reshape(-1)

    turned = jnp.broadcast_to(jnp.arange(2, dtype=jnp.int32)[None, :, None], (st_count, 2, per_dev)).reshape(-1)
    if len(received) > 1:
        slot_channel = after(slot_channel, received[-2])
    spectra = slot_spectra(by_row(slot_channel), by_row(filled), turned, branches, st_count)
    slot_pieces = exchange(spectra, st_count)

    weights = beam_weights(after(slot_channel[:per_dev], (spectra[0], received[-1])), delays, gains)
    signal_ids = (partner[:, None] * sig_dev + jnp.arange(sig_dev, dtype=jnp.int32)[None, :]).reshape(-1)
    wanted = (station_index[None, :] * 2 + jnp.arange(2, dtype=jnp.int32)[:, None]).reshape(-1)
    chooser = (signal_ids[:, None] == wanted[None, :]).astype(jnp.bfloat16)

    visibility = correlate(after(st_here[None], weights), received, st_count)
    signals = visibility.shape[1]
    beam_out = combine(slot_pieces, chooser, after(weights, visibility))
    return (visibility.reshape(2, 1, 1, signals, signals), beam_out)


def solution(mesh):
    in_specs = (P(None, "st", None), P(), P(), P(), P(), P(), P())
    out_specs = (P(None, "sb", "st", None, None), P("sb", "st", None, None, None))
    return jax.shard_map(body, mesh=mesh, in_specs=in_specs, out_specs=out_specs, check_vma=False)
```

time: 1410 us -> 376 us (0.27)
  matrix products: 446 us -> 0 us
  other arithmetic: 358 us -> 8.05 us
  waiting for transfers between devices: 327 us -> 47.2 us
  local copies, waits for them, and re-layouts: 247 us -> 3.61 us
  Pallas kernels: 0 us -> 242 us
  starting transfers between devices: 7.42 us -> 73.7 us
    dot_general x14 -> x0, matrix products: 446 us -> none  [the longest x4 139 us: product(): jnp.einsum('sfjp,sbj->sfpb', operand, weight, preferred_element_type=jnp....]
    unnamed x2 -> x0, waiting for transfers between devices: 327 us -> none
    pallas_call x0 -> x9, Pallas kernels: none -> 242 us  [the longest x4 170 us: channelise(): pl.pallas_call(channel_kernel, grid=(steps,), in_specs=[pl.BlockSpec((2,...]
    convert_element_type x3 -> x2, other arithmetic: 189 us -> 1.31 us  [the longest x1 1.23 us: body(): chooser = (signal_ids[:, None] == wanted[None, :]).astype(jnp.bfloat16)]
    dot_general x2 -> x0, other arithmetic: 128 us -> none  [the longest x1 64.2 us: transform(): jnp.dot(flat_rows[1], sin_t, preferred_element_type=jnp.float32)]
    unnamed x38 -> x81, local copies, waits for them, and re-layouts: 96.2 us -> 2.04 us
    slice x9 -> x2, local copies, waits for them, and re-layouts: 88.3 us -> 0.59 us  [the longest x1 0.51 us: body(): slot_channel[:per_dev]]
    ppermute x0 -> x35, starting transfers between devices: none -> 73.7 us  [exchange(): lax.ppermute(pieces[s], 'st', [(i, i ^ s) for i in range(st_count)])]
  transfers between devices with their start and end apart: 2 -> 35, of which waited for: 1 -> 6; matrix products, arithmetic and copies ran while one was open for 19% -> 2% of each run, Pallas kernels for 0% -> 50%
where the time goes in v1:
time: 376 us
  Pallas kernels  242 us (64%)
  starting transfers between devices  73.7 us (20%)
  waiting for transfers between devices  47.2 us (13%)
  other arithmetic  8.05 us (2%)
    pallas_call x4, Pallas kernels, channelise(): pl.pallas_call(channel_kernel, grid=(steps,), in_specs=[pl.BlockSpec((2,...  170 us
    ppermute x35, starting transfers between devices, exchange(): lax.ppermute(pieces[s], 'st', [(i, i ^ s) for i in range(st_count)])  73.7 us
    ppermute x35, waiting for transfers between devices, exchange(): lax.ppermute(pieces[s], 'st', [(i, i ^ s) for i in range(st_count)])  47.2 us
    pallas_call x1, Pallas kernels, slot_spectra(): pl.pallas_call(slot_kernel, grid=(FRAMES // f_step,), in_specs=[pl.BlockS...  28.3 us
    pallas_call x1, Pallas kernels, correlate(): pl.pallas_call(kernel, in_specs=[pl.BlockSpec(memory_space=pltpu.SMEM)] +...  18.1 us
    pallas_call x1, Pallas kernels, beam_weights(): pl.pallas_call(weight_kernel, grid=(slots,), in_specs=[pl.BlockSpec(memor...  12.6 us
    pallas_call x1, Pallas kernels, combine(): pl.pallas_call(kernel, out_shape=jax.ShapeDtypeStruct((1, slots, 2, FRAME...  7.54 us
  transfers between devices with their start and end apart: 35, of which 6 were waited for; matrix products, arithmetic and copies ran while one was open for 2% of the time, Pallas kernels for 50%

profile of v1, /device:TPU:0, one launch (start us, length us, event | category | flops | bytes accessed | tf_op | source)
XLA Modules:
  0.0 376.1 jit_solution(2066535308241293755)
XLA Ops:
  3.1 5.6 %shard_map.86.table = bf16[8,1024,256]{2,1,0:T(8,128)(2,1)} custom-call(f32[8,32,128]{2,1,0:T(8,128)} %get-tuple-element.121.hi_c, f32[8,32,128]{2,1,0:T(8,128)} %get-tuple-element.120.hi_s, f32[8,16,128]{2,1,0:T(8,128)} %get-tuple-element.123.lo_c, f32[8,16,128]{2,1,0:T(8,128)} %get-tuple-element.122.lo_s), custom_call_target="tpu_custom_call" | custom-call | tf_op jit(solution)/shard_map/pallas_call | solution.py:420
  8.8 42.4 %shard_map.87 = (bf16[32,4096]{1,0:T(8,128)(2,1)}, bf16[32,4096]{1,0:T(8,128)(2,1)}, bf16[32,4096]{1,0:T(8,128)(2,1)}, bf16[32,4096]{1,0:T(8,128)(2,1)}, bf16[32...) custom-call(bf16[2,128,126976]{2,1,0:T(8,128)(2,1)} %volts.7, ...), custom_call_target="tpu_custom_call" | custom-call | flops 4294967296 | bytes 33030144 | tf_op jit(solution)/shard_map/pallas_call | solution.py:155
  51.2 2.9 collective-permute-start
  55.7 3.0 collective-permute-start.3
  60.0 42.6 %shard_map.88 = (bf16[32,4096]{1,0:T(8,128)(2,1)}, bf16[32,4096]{1,0:T(8,128)(2,1)}, bf16[32,4096]{1,0:T(8,128)(2,1)}, bf16[32,4096]{1,0:T(8,128)(2,1)}, bf16[32...) custom-call(bf16[2,128,126976]{2,1,0:T(8,128)(2,1)} %volts.7, ...), custom_call_target="tpu_custom_call" | custom-call | flops 4294967296 | bytes 33030144 | tf_op jit(solution)/shard_map/pallas_call | solution.py:155
  103.7 3.7 collective-permute-start.5
  107.5 1.7 collective-permute-start.14
  109.3 1.8 collective-permute-start.16
  111.1 3.8 %collective-permute-done.5.refs_6_ = bf16[32,4096]{1,0:T(8,128)(2,1)S(1)} collective-permute-done((bf16[32,4096]{1,0:T(8,128)(2,1)S(1)}, bf16[32,4096]{1,0:T(8,128)(2,1)S(1)}, u32[]{:S(2)}, u32[]{:S(2)}) %collective-permute-start.5) | collective-permute-done | bytes 262176 | tf_op jit(solution)/shard_map/ppermute | solution.py:394
  114.9 11.4 %collective-permute-start.17 = (bf16[32,4096]{1,0:T(8,128)(2,1)}, bf16[32,4096]{1,0:T(8,128)(2,1)S(1)}, u32[]{:S(2)}, u32[]{:S(2)}) collective-permute-start(bf16[32,4096]{1,0:T(8,128)(2,1)} %get-tuple-element.83), channel_id=1, source_target_pairs={{0,16},{4,20},{8,24},{12,28},{16,0},{20,4},{24,8},{28,12},{1,17},{... | collective-permute-start | bytes 786440 | tf_op jit(solution)/shard_map/ppermute | solution.py:394
  126.4 9.4 %collective-permute-start.18 = (bf16[32,4096]{1,0:T(8,128)(2,1)}, bf16[32,4096]{1,0:T(8,128)(2,1)S(1)}, u32[]{:S(2)}, u32[]{:S(2)}) collective-permute-start(bf16[32,4096]{1,0:T(8,128)(2,1)} %get-tuple-element.84), channel_id=1, source_target_pairs={{0,20},{4,16},{8,28},{12,24},{16,4},{20,0},{24,12},{28,8},{1,21},{... | collective-permute-start | bytes 786440 | tf_op jit(solution)/shard_map/ppermute | solution.py:394
  135.8 42.5 %shard_map.89 = (bf16[32,4096]{1,0:T(8,128)(2,1)}, bf16[32,4096]{1,0:T(8,128)(2,1)}, bf16[32,4096]{1,0:T(8,128)(2,1)}, bf16[32,4096]{1,0:T(8,128)(2,1)}, bf16[32...) custom-call(bf16[2,128,126976]{2,1,0:T(8,128)(2,1)} %volts.7, ...), custom_call_target="tpu_custom_call" | custom-call | flops 4294967296 | bytes 33030144 | tf_op jit(solution)/shard_map/pallas_call | solution.py:155
  178.4 6.6 %collective-permute-start.19 = (bf16[32,4096]{1,0:T(8,128)(2,1)}, bf16[32,4096]{1,0:T(8,128)(2,1)S(1)}, u32[]{:S(2)}, u32[]{:S(2)}) collective-permute-start(bf16[32,4096]{1,0:T(8,128)(2,1)} %get-tuple-element.85), channel_id=1, source_target_pairs={{0,24},{4,28},{8,16},{12,20},{16,8},{20,12},{24,0},{28,4},{1,25},{... | collective-permute-start | bytes 786440 | tf_op jit(solution)/shard_map/ppermute | solution.py:394
  185.0 3.6 collective-permute-start.20
  189.4 3.1 collective-permute-done.19.refs_14_
  192.5 8.7 %collective-permute-done.20.refs_15_ = bf16[32,4096]{1,0:T(8,128)(2,1)S(1)} collective-permute-done((bf16[32,4096]{1,0:T(8,128)(2,1)}, bf16[32,4096]{1,0:T(8,128)(2,1)S(1)}, u32[]{:S(2)}, u32[]{:S(2)}) %collective-permute-start.20) | collective-permute-done | bytes 262176 | tf_op jit(solution)/shard_map/ppermute | solution.py:394
  201.2 1.7 collective-permute-start.12
  202.9 3.6 collective-permute-start.7
  206.5 21.8 %collective-permute-done.10.refs_20_ = bf16[32,4096]{1,0:T(8,128)(2,1)S(1)} collective-permute-done((bf16[32,4096]{1,0:T(8,128)(2,1)}, bf16[32,4096]{1,0:T(8,128)(2,1)S(1)}, u32[]{:S(2)}, u32[]{:S(2)}) %collective-permute-start.10) | collective-permute-done | bytes 262176 | tf_op jit(solution)/shard_map/ppermute | solution.py:394
  228.9 6.1 %collective-permute-done.11.refs_21_ = bf16[32,4096]{1,0:T(8,128)(2,1)S(1)} collective-permute-done((bf16[32,4096]{1,0:T(8,128)(2,1)}, bf16[32,4096]{1,0:T(8,128)(2,1)S(1)}, u32[]{:S(2)}, u32[]{:S(2)}) %collective-permute-start.11) | collective-permute-done | bytes 262176 | tf_op jit(solution)/shard_map/ppermute | solution.py:394
  235.0 42.5 %shard_map.90 = (bf16[32,4096]{1,0:T(8,128)(2,1)}, bf16[32,4096]{1,0:T(8,128)(2,1)}, bf16[32,4096]{1,0:T(8,128)(2,1)}, bf16[32,4096]{1,0:T(8,128)(2,1)}, bf16[32...) custom-call(bf16[2,128,126976]{2,1,0:T(8,128)(2,1)} %volts.7, ...), custom_call_target="tpu_custom_call" | custom-call | flops 4294967296 | bytes 33030144 | tf_op jit(solution)/shard_map/pallas_call | solution.py:155
  278.6 2.6 collective-permute-start.22
  281.2 3.5 collective-permute-start.24
  289.5 1.8 collective-permute-start.26
  291.3 3.5 collective-permute-done.22.refs_26_
  294.8 28.3 %shard_map.91 = (bf16[640,128]{1,0:T(8,128)(2,1)}, bf16[640,128]{1,0:T(8,128)(2,1)}, bf16[640,128]{1,0:T(8,128)(2,1)}, bf16[640,128]{1,0:T(8,128)(2,1)}, bf16[64...) custom-call(s32[320,1]{1,0:T(8,128)} %add_select_fusion.1.row_branch, ...), custom_call_target="tpu_custom_call" | custom-call | flops 10737418240 | bytes 33554432 | tf_op jit(solution)/shard_map/pallas_call | solution.py:224
  325.3 12.6 %shard_map.92.refs_9_ = bf16[20,512,256]{2,1,0:T(8,128)(2,1)} custom-call(s32[20]{0:T(128)} %slice.12.channel, f32[256,256]{1,0:T(8,128)} %delays.1, f32[256,256]{1,0:T(8,128)} %gains.1), custom_call_target="tpu_custom_call" | custom-call | flops 52428800 | bytes 5242880 | tf_op jit(solution)/shard_map/pallas_call | solution.py:324
  337.9 3.3 collective-permute-start.30
  341.2 2.3 collective-permute-start.31
  344.4 4.4 %collective-permute-start.33 = (bf16[640,128]{1,0:T(8,128)(2,1)}, bf16[640,128]{1,0:T(8,128)(2,1)S(1)}, u32[]{:S(2)}, u32[]{:S(2)}) collective-permute-start(bf16[640,128]{1,0:T(8,128)(2,1)} %get-tuple-element.105), channel_id=1, source_target_pairs={{0,24},{4,28},{8,16},{12,20},{16,8},{20,12},{24,0},{28,4},{1,25},{... | collective-permute-start | bytes 491528 | tf_op jit(solution)/shard_map/ppermute | solution.py:394
  348.9 18.1 %shard_map.93 = f32[2,1024,1024]{2,1,0:T(8,128)} custom-call(s32[1]{0:T(128)} %bitcast.here_ref, bf16[32,4096]{1,0:T(8,128)(2,1)} %get-tuple-element.55.refs_0_, bf16[32,4096]{1,0:T(8,128)(2,1)} %copy-done.10, bf16[32,4096]{1,0:T(8,128)(2,1)} %copy-done.11, bf16[32,4096]{1,0:T(8,128)(2,1)} %copy-done.12, bf16[32,4096]{1,0:T(8,128)(2,1)} %copy-done.13, ...), custom_call_target="tpu_custom_call" | custom-call | flops 8589934592 | bytes 16777216 | tf_op jit(solution)/shard_map/pallas_call | solution.py:285
  368.6 7.5 %shard_map.94 = f32[1,20,2,16,512]{4,3,2,1,0:T(8,128)} custom-call(bf16[640,128]{1,0:T(8,128)(2,1)} %get-tuple-element.89.refs_0_, bf16[640,128]{1,0:T(8,128)(2,1)} %copy-done, bf16[640,128]{1,0:T(8,128)(2,1)} %copy-done.1, bf16[640,128]{1,0:T(8,128)(2,1)} %copy-done.2, bf16[640,128]{1,0:T(8,128)(2,1)} %copy-done.3, bf16[640,128]{1,0:T(8,128)(2,1)} %copy-done.4, ...), custom_call_target="tpu_custom_call" | custom-call | flops 1006632960 | bytes 1310720 | tf_op jit(solution)/shard_map/pallas_call | solution.py:379
  (167 shorter events, 18.1 us)
Async XLA Ops:
  51.2 52.5 %collective-permute-start = (bf16[32,4096]{1,0:T(8,128)(2,1)}, bf16[32,4096]{1,0:T(8,128)(2,1)S(1)}, u32[]{:S(2)}, u32[]{:S(2)}) collective-permute-start(bf16[32,4096]{1,0:T(8,128)(2,1)} %get-tuple-element.59), channel_id=1, source_target_pairs={{0,4},{4,0},{8,12},{12,8},{16,20},{20,16},{24,28},{28,24},{1,5},{5... | collective-permute-start | bytes 786440 | tf_op jit(solution)/shard_map/ppermute | solution.py:394
  54.2 53.3 %collective-permute-start.1 = (bf16[32,4096]{1,0:T(8,128)(2,1)}, bf16[32,4096]{1,0:T(8,128)(2,1)S(1)}, u32[]{:S(2)}, u32[]{:S(2)}) collective-permute-start(bf16[32,4096]{1,0:T(8,128)(2,1)} %get-tuple-element.60), channel_id=1, source_target_pairs={{0,8},{4,12},{8,0},{12,4},{16,24},{20,28},{24,16},{28,20},{1,9},{5... | collective-permute-start | bytes 786440 | tf_op jit(solution)/shard_map/ppermute | solution.py:394
  55.7 51.8 %collective-permute-start.2 = (bf16[32,4096]{1,0:T(8,128)(2,1)}, bf16[32,4096]{1,0:T(8,128)(2,1)S(1)}, u32[]{:S(2)}, u32[]{:S(2)}) collective-permute-start(bf16[32,4096]{1,0:T(8,128)(2,1)} %get-tuple-element.61), channel_id=1, source_target_pairs={{0,12},{4,8},{8,4},{12,0},{16,28},{20,24},{24,20},{28,16},{1,13},{... | collective-permute-start | bytes 786440 | tf_op jit(solution)/shard_map/ppermute | solution.py:394
  55.7 53.5 %collective-permute-start.3 = (bf16[32,4096]{1,0:T(8,128)(2,1)}, bf16[32,4096]{1,0:T(8,128)(2,1)S(1)}, u32[]{:S(2)}, u32[]{:S(2)}) collective-permute-start(bf16[32,4096]{1,0:T(8,128)(2,1)} %get-tuple-element.62), channel_id=1, source_target_pairs={{0,16},{4,20},{8,24},{12,28},{16,0},{20,4},{24,8},{28,12},{1,17},{... | collective-permute-start | bytes 786440 | tf_op jit(solution)/shard_map/ppermute | solution.py:394
  58.7 50.5 %collective-permute-start.4 = (bf16[32,4096]{1,0:T(8,128)(2,1)}, bf16[32,4096]{1,0:T(8,128)(2,1)S(1)}, u32[]{:S(2)}, u32[]{:S(2)}) collective-permute-start(bf16[32,4096]{1,0:T(8,128)(2,1)} %get-tuple-element.63), channel_id=1, source_target_pairs={{0,20},{4,16},{8,28},{12,24},{16,4},{20,0},{24,12},{28,8},{1,21},{... | collective-permute-start | bytes 786440 | tf_op jit(solution)/shard_map/ppermute | solution.py:394
  107.4 18.9 %collective-permute-start.6 = (bf16[32,4096]{1,0:T(8,128)(2,1)S(1)}, bf16[32,4096]{1,0:T(8,128)(2,1)S(1)}, u32[]{:S(2)}, u32[]{:S(2)}) collective-permute-start(bf16[32,4096]{1,0:T(8,128)(2,1)S(1)} %copy-done.38), channel_id=1, source_target_pairs={{0,28},{4,24},{8,20},{12,16},{16,12},{20,8},{24,4},{28,0},{1,29},{... | collective-permute-start | bytes 786440 | tf_op jit(solution)/shard_map/ppermute | solution.py:394
  107.5 70.8 %collective-permute-start.14 = (bf16[32,4096]{1,0:T(8,128)(2,1)}, bf16[32,4096]{1,0:T(8,128)(2,1)S(1)}, u32[]{:S(2)}, u32[]{:S(2)}) collective-permute-start(bf16[32,4096]{1,0:T(8,128)(2,1)} %get-tuple-element.80), channel_id=1, source_target_pairs={{0,4},{4,0},{8,12},{12,8},{16,20},{20,16},{24,28},{28,24},{1,5},{5... | collective-permute-start | bytes 786440 | tf_op jit(solution)/shard_map/ppermute | solution.py:394
  109.3 75.7 %collective-permute-start.15 = (bf16[32,4096]{1,0:T(8,128)(2,1)}, bf16[32,4096]{1,0:T(8,128)(2,1)S(1)}, u32[]{:S(2)}, u32[]{:S(2)}) collective-permute-start(bf16[32,4096]{1,0:T(8,128)(2,1)} %get-tuple-element.81), channel_id=1, source_target_pairs={{0,8},{4,12},{8,0},{12,4},{16,24},{20,28},{24,16},{28,20},{1,9},{5... | collective-permute-start | bytes 786440 | tf_op jit(solution)/shard_map/ppermute | solution.py:394
  109.3 79.3 %collective-permute-start.16 = (bf16[32,4096]{1,0:T(8,128)(2,1)}, bf16[32,4096]{1,0:T(8,128)(2,1)S(1)}, u32[]{:S(2)}, u32[]{:S(2)}) collective-permute-start(bf16[32,4096]{1,0:T(8,128)(2,1)} %get-tuple-element.82), channel_id=1, source_target_pairs={{0,12},{4,8},{8,4},{12,0},{16,28},{20,24},{24,20},{28,16},{1,13},{... | collective-permute-start | bytes 786440 | tf_op jit(solution)/shard_map/ppermute | solution.py:394
  114.9 73.7 %collective-permute-start.17 = (bf16[32,4096]{1,0:T(8,128)(2,1)}, bf16[32,4096]{1,0:T(8,128)(2,1)S(1)}, u32[]{:S(2)}, u32[]{:S(2)}) collective-permute-start(bf16[32,4096]{1,0:T(8,128)(2,1)} %get-tuple-element.83), channel_id=1, source_target_pairs={{0,16},{4,20},{8,24},{12,28},{16,0},{20,4},{24,8},{28,12},{1,17},{... | collective-permute-start | bytes 786440 | tf_op jit(solution)/shard_map/ppermute | solution.py:394
  126.4 63.0 %collective-permute-start.18 = (bf16[32,4096]{1,0:T(8,128)(2,1)}, bf16[32,4096]{1,0:T(8,128)(2,1)S(1)}, u32[]{:S(2)}, u32[]{:S(2)}) collective-permute-start(bf16[32,4096]{1,0:T(8,128)(2,1)} %get-tuple-element.84), channel_id=1, source_target_pairs={{0,20},{4,16},{8,28},{12,24},{16,4},{20,0},{24,12},{28,8},{1,21},{... | collective-permute-start | bytes 786440 | tf_op jit(solution)/shard_map/ppermute | solution.py:394
  185.0 16.2 %collective-permute-start.20 = (bf16[32,4096]{1,0:T(8,128)(2,1)}, bf16[32,4096]{1,0:T(8,128)(2,1)S(1)}, u32[]{:S(2)}, u32[]{:S(2)}) collective-permute-start(bf16[32,4096]{1,0:T(8,128)(2,1)} %get-tuple-element.86), channel_id=1, source_target_pairs={{0,28},{4,24},{8,20},{12,16},{16,12},{20,8},{24,4},{28,0},{1,29},{... | collective-permute-start | bytes 786440 | tf_op jit(solution)/shard_map/ppermute | solution.py:394
  188.6 39.7 %collective-permute-start.10 = (bf16[32,4096]{1,0:T(8,128)(2,1)}, bf16[32,4096]{1,0:T(8,128)(2,1)S(1)}, u32[]{:S(2)}, u32[]{:S(2)}) collective-permute-start(bf16[32,4096]{1,0:T(8,128)(2,1)} %get-tuple-element.71), channel_id=1, source_target_pairs={{0,16},{4,20},{8,24},{12,28},{16,0},{20,4},{24,8},{28,12},{1,17},{... | collective-permute-start | bytes 786440 | tf_op jit(solution)/shard_map/ppermute | solution.py:394
  188.6 46.4 %collective-permute-start.11 = (bf16[32,4096]{1,0:T(8,128)(2,1)}, bf16[32,4096]{1,0:T(8,128)(2,1)S(1)}, u32[]{:S(2)}, u32[]{:S(2)}) collective-permute-start(bf16[32,4096]{1,0:T(8,128)(2,1)} %get-tuple-element.72), channel_id=1, source_target_pairs={{0,20},{4,16},{8,28},{12,24},{16,4},{20,0},{24,12},{28,8},{1,21},{... | collective-permute-start | bytes 786440 | tf_op jit(solution)/shard_map/ppermute | solution.py:394
  201.2 76.5 %collective-permute-start.12 = (bf16[32,4096]{1,0:T(8,128)(2,1)}, bf16[32,4096]{1,0:T(8,128)(2,1)S(1)}, u32[]{:S(2)}, u32[]{:S(2)}) collective-permute-start(bf16[32,4096]{1,0:T(8,128)(2,1)} %get-tuple-element.73), channel_id=1, source_target_pairs={{0,24},{4,28},{8,16},{12,20},{16,8},{20,12},{24,0},{28,4},{1,25},{... | collective-permute-start | bytes 786440 | tf_op jit(solution)/shard_map/ppermute | solution.py:394
  202.9 75.7 %collective-permute-start.13 = (bf16[32,4096]{1,0:T(8,128)(2,1)}, bf16[32,4096]{1,0:T(8,128)(2,1)S(1)}, u32[]{:S(2)}, u32[]{:S(2)}) collective-permute-start(bf16[32,4096]{1,0:T(8,128)(2,1)} %get-tuple-element.74), channel_id=1, source_target_pairs={{0,28},{4,24},{8,20},{12,16},{16,12},{20,8},{24,4},{28,0},{1,29},{... | collective-permute-start | bytes 786440 | tf_op jit(solution)/shard_map/ppermute | solution.py:394
  202.9 78.2 %collective-permute-start.7 = (bf16[32,4096]{1,0:T(8,128)(2,1)}, bf16[32,4096]{1,0:T(8,128)(2,1)S(1)}, u32[]{:S(2)}, u32[]{:S(2)}) collective-permute-start(bf16[32,4096]{1,0:T(8,128)(2,1)} %get-tuple-element.68), channel_id=1, source_target_pairs={{0,4},{4,0},{8,12},{12,8},{16,20},{20,16},{24,28},{28,24},{1,5},{5... | collective-permute-start | bytes 786440 | tf_op jit(solution)/shard_map/ppermute | solution.py:394
  228.3 52.9 %collective-permute-start.8 = (bf16[32,4096]{1,0:T(8,128)(2,1)}, bf16[32,4096]{1,0:T(8,128)(2,1)S(1)}, u32[]{:S(2)}, u32[]{:S(2)}) collective-permute-start(bf16[32,4096]{1,0:T(8,128)(2,1)} %get-tuple-element.69), channel_id=1, source_target_pairs={{0,8},{4,12},{8,0},{12,4},{16,24},{20,28},{24,16},{28,20},{1,9},{5... | collective-permute-start | bytes 786440 | tf_op jit(solution)/shard_map/ppermute | solution.py:394
  235.0 49.8 %collective-permute-start.9 = (bf16[32,4096]{1,0:T(8,128)(2,1)}, bf16[32,4096]{1,0:T(8,128)(2,1)S(1)}, u32[]{:S(2)}, u32[]{:S(2)}) collective-permute-start(bf16[32,4096]{1,0:T(8,128)(2,1)} %get-tuple-element.70), channel_id=1, source_target_pairs={{0,12},{4,8},{8,4},{12,0},{16,28},{20,24},{24,20},{28,16},{1,13},{... | collective-permute-start | bytes 786440 | tf_op jit(solution)/shard_map/ppermute | solution.py:394
  278.6 16.3 %collective-permute-start.22 = (bf16[32,4096]{1,0:T(8,128)(2,1)}, bf16[32,4096]{1,0:T(8,128)(2,1)S(1)}, u32[]{:S(2)}, u32[]{:S(2)}) collective-permute-start(bf16[32,4096]{1,0:T(8,128)(2,1)} %get-tuple-element.92), channel_id=1, source_target_pairs={{0,8},{4,12},{8,0},{12,4},{16,24},{20,28},{24,16},{28,20},{1,9},{5... | collective-permute-start | bytes 786440 | tf_op jit(solution)/shard_map/ppermute | solution.py:394
  281.1 42.1 %collective-permute-start.23 = (bf16[32,4096]{1,0:T(8,128)(2,1)}, bf16[32,4096]{1,0:T(8,128)(2,1)S(1)}, u32[]{:S(2)}, u32[]{:S(2)}) collective-permute-start(bf16[32,4096]{1,0:T(8,128)(2,1)} %get-tuple-element.93), channel_id=1, source_target_pairs={{0,12},{4,8},{8,4},{12,0},{16,28},{20,24},{24,20},{28,16},{1,13},{... | collective-permute-start | bytes 786440 | tf_op jit(solution)/shard_map/ppermute | solution.py:394
  281.2 42.3 %collective-permute-start.24 = (bf16[32,4096]{1,0:T(8,128)(2,1)}, bf16[32,4096]{1,0:T(8,128)(2,1)S(1)}, u32[]{:S(2)}, u32[]{:S(2)}) collective-permute-start(bf16[32,4096]{1,0:T(8,128)(2,1)} %get-tuple-element.94), channel_id=1, source_target_pairs={{0,16},{4,20},{8,24},{12,28},{16,0},{20,4},{24,8},{28,12},{1,17},{... | collective-permute-start | bytes 786440 | tf_op jit(solution)/shard_map/ppermute | solution.py:394
  284.8 40.5 %collective-permute-start.25 = (bf16[32,4096]{1,0:T(8,128)(2,1)}, bf16[32,4096]{1,0:T(8,128)(2,1)S(1)}, u32[]{:S(2)}, u32[]{:S(2)}) collective-permute-start(bf16[32,4096]{1,0:T(8,128)(2,1)} %get-tuple-element.95), channel_id=1, source_target_pairs={{0,20},{4,16},{8,28},{12,24},{16,4},{20,0},{24,12},{28,8},{1,21},{... | collective-permute-start | bytes 786440 | tf_op jit(solution)/shard_map/ppermute | solution.py:394
  289.5 35.7 %collective-permute-start.26 = (bf16[32,4096]{1,0:T(8,128)(2,1)}, bf16[32,4096]{1,0:T(8,128)(2,1)S(1)}, u32[]{:S(2)}, u32[]{:S(2)}) collective-permute-start(bf16[32,4096]{1,0:T(8,128)(2,1)} %get-tuple-element.96), channel_id=1, source_target_pairs={{0,24},{4,28},{8,16},{12,20},{16,8},{20,12},{24,0},{28,4},{1,25},{... | collective-permute-start | bytes 786440 | tf_op jit(solution)/shard_map/ppermute | solution.py:394
  294.8 30.4 %collective-permute-start.27 = (bf16[32,4096]{1,0:T(8,128)(2,1)}, bf16[32,4096]{1,0:T(8,128)(2,1)S(1)}, u32[]{:S(2)}, u32[]{:S(2)}) collective-permute-start(bf16[32,4096]{1,0:T(8,128)(2,1)} %get-tuple-element.97), channel_id=1, source_target_pairs={{0,28},{4,24},{8,20},{12,16},{16,12},{20,8},{24,4},{28,0},{1,29},{... | collective-permute-start | bytes 786440 | tf_op jit(solution)/shard_map/ppermute | solution.py:394
  323.2 21.1 %collective-permute-start.28 = (bf16[640,128]{1,0:T(8,128)(2,1)}, bf16[640,128]{1,0:T(8,128)(2,1)S(1)}, u32[]{:S(2)}, u32[]{:S(2)}) collective-permute-start(bf16[640,128]{1,0:T(8,128)(2,1)} %get-tuple-element.100), channel_id=1, source_target_pairs={{0,4},{4,0},{8,12},{12,8},{16,20},{20,16},{24,28},{28,24},{1,5},{5... | collective-permute-start | bytes 491528 | tf_op jit(solution)/shard_map/ppermute | solution.py:394
  323.5 25.3 %collective-permute-start.29 = (bf16[640,128]{1,0:T(8,128)(2,1)}, bf16[640,128]{1,0:T(8,128)(2,1)S(1)}, u32[]{:S(2)}, u32[]{:S(2)}) collective-permute-start(bf16[640,128]{1,0:T(8,128)(2,1)} %get-tuple-element.101), channel_id=1, source_target_pairs={{0,8},{4,12},{8,0},{12,4},{16,24},{20,28},{24,16},{28,20},{1,9},{5... | collective-permute-start | bytes 491528 | tf_op jit(solution)/shard_map/ppermute | solution.py:394
  337.9 29.1 %collective-permute-start.30 = (bf16[640,128]{1,0:T(8,128)(2,1)}, bf16[640,128]{1,0:T(8,128)(2,1)S(1)}, u32[]{:S(2)}, u32[]{:S(2)}) collective-permute-start(bf16[640,128]{1,0:T(8,128)(2,1)} %get-tuple-element.102), channel_id=1, source_target_pairs={{0,12},{4,8},{8,4},{12,0},{16,28},{20,24},{24,20},{28,16},{1,13},{... | collective-permute-start | bytes 491528 | tf_op jit(solution)/shard_map/ppermute | solution.py:394
  341.2 25.9 %collective-permute-start.31 = (bf16[640,128]{1,0:T(8,128)(2,1)}, bf16[640,128]{1,0:T(8,128)(2,1)S(1)}, u32[]{:S(2)}, u32[]{:S(2)}) collective-permute-start(bf16[640,128]{1,0:T(8,128)(2,1)} %get-tuple-element.103), channel_id=1, source_target_pairs={{0,16},{4,20},{8,24},{12,28},{16,0},{20,4},{24,8},{28,12},{1,17},{... | collective-permute-start | bytes 491528 | tf_op jit(solution)/shard_map/ppermute | solution.py:394
  343.5 23.6 %collective-permute-start.32 = (bf16[640,128]{1,0:T(8,128)(2,1)}, bf16[640,128]{1,0:T(8,128)(2,1)S(1)}, u32[]{:S(2)}, u32[]{:S(2)}) collective-permute-start(bf16[640,128]{1,0:T(8,128)(2,1)} %get-tuple-element.104), channel_id=1, source_target_pairs={{0,20},{4,16},{8,28},{12,24},{16,4},{20,0},{24,12},{28,8},{1,21},{... | collective-permute-start | bytes 491528 | tf_op jit(solution)/shard_map/ppermute | solution.py:394
  344.4 22.7 %collective-permute-start.33 = (bf16[640,128]{1,0:T(8,128)(2,1)}, bf16[640,128]{1,0:T(8,128)(2,1)S(1)}, u32[]{:S(2)}, u32[]{:S(2)}) collective-permute-start(bf16[640,128]{1,0:T(8,128)(2,1)} %get-tuple-element.105), channel_id=1, source_target_pairs={{0,24},{4,28},{8,16},{12,20},{16,8},{20,12},{24,0},{28,4},{1,25},{... | collective-permute-start | bytes 491528 | tf_op jit(solution)/shard_map/ppermute | solution.py:394
  348.8 18.4 %collective-permute-start.34 = (bf16[640,128]{1,0:T(8,128)(2,1)}, bf16[640,128]{1,0:T(8,128)(2,1)S(1)}, u32[]{:S(2)}, u32[]{:S(2)}) collective-permute-start(bf16[640,128]{1,0:T(8,128)(2,1)} %get-tuple-element.106), channel_id=1, source_target_pairs={{0,28},{4,24},{8,20},{12,16},{16,12},{20,8},{24,4},{28,0},{1,29},{... | collective-permute-start | bytes 491528 | tf_op jit(solution)/shard_map/ppermute | solution.py:394
  (43 other events, 1804.2 us)

commit v2 on v1

v2 whole, which is shorter than its diff:
```python
import functools
import math

import jax
import jax.numpy as jnp
from jax import lax
from jax.experimental import pallas as pl
from jax.experimental.pallas import tpu as pltpu
from jax.sharding import PartitionSpec as P

NCH = 4096
FRAMES = 16
SLOTS = 160
RADIX = 8
LANES = 128
ROWS = 16
VMEM = 56 * 1024 * 1024

TWO_PI = 2.0 * math.pi
NT = (((1,), (1,)), ((), ()))


def phase(turns, length):
    angles = (turns % length).astype(jnp.float32) * (TWO_PI / length)
    return jnp.cos(angles), jnp.sin(angles)


def table_kernel(hi_c, hi_s, lo_c, lo_s, out):
    fine, width = lo_c.shape
    depth = hi_c.shape[0] * fine

    def block(a, carry):
        top = pl.multiple_of(a * fine, fine)
        high_c, high_s = hi_c[pl.ds(a, 1), :], hi_s[pl.ds(a, 1), :]
        cos_t = (high_c * lo_c[...] - high_s * lo_s[...]).astype(out.dtype)
        sin_t = (high_s * lo_c[...] + high_c * lo_s[...]).astype(out.dtype)
        out[pl.ds(top, fine), :width] = cos_t
        out[pl.ds(top, fine), width:] = -sin_t
        out[pl.ds(depth + top, fine), :width] = sin_t
        out[pl.ds(depth + top, fine), width:] = cos_t
        return carry

    lax.fori_loop(0, hi_c.shape[0], block, 0)


def transform_table():
    depth = NCH // RADIX
    out_ids = jnp.arange(depth, dtype=jnp.int32)[None, :]
    lo_c, lo_s = phase(jnp.arange(ROWS, dtype=jnp.int32)[:, None] * out_ids, depth)
    hi_c, hi_s = phase(jnp.arange(0, depth, ROWS, dtype=jnp.int32)[:, None] * out_ids, depth)
    scale = 1.0 / math.sqrt(NCH)
    return pl.pallas_call(
        table_kernel, out_shape=jax.ShapeDtypeStruct((2 * depth, 2 * depth), jnp.bfloat16)
    )(hi_c * scale, hi_s * scale, lo_c, lo_s)


def radix8(re, im):
    half = math.sqrt(0.5)

    def four(xr, xi):
        ar, ai, br, bi = xr[0] + xr[2], xi[0] + xi[2], xr[0] - xr[2], xi[0] - xi[2]
        cr, ci, dr, di = xr[1] + xr[3], xi[1] + xi[3], xr[1] - xr[3], xi[1] - xi[3]
        return [ar + cr, br + di, ar - cr, br - di], [ai + ci, bi - dr, ai - ci, bi + dr]

    er, ei = four(re[0::2], im[0::2])
    odd_r, odd_i = four(re[1::2], im[1::2])
    tr = [odd_r[0], (odd_r[1] + odd_i[1]) * half, odd_i[2], (odd_i[3] - odd_r[3]) * half]
    ti = [odd_i[0], (odd_i[1] - odd_r[1]) * half, -odd_r[2], (odd_r[3] + odd_i[3]) * -half]
    return (
        [e + t for e, t in zip(er, tr)] + [e - t for e, t in zip(er, tr)],
        [e + t for e, t in zip(ei, ti)] + [e - t for e, t in zip(ei, ti)],
    )


def swap_blocks(parts, lane_ids):
    count = len(parts)
    width = LANES // count
    parts = list(parts)
    step = 1
    while step < count:
        keep = (lane_ids // width) % (2 * step) < step
        for b in range(count):
            if b & step == 0:
                low, high = parts[b], parts[b + step]
                parts[b] = jnp.where(keep, low, pltpu.roll(high, step * width, 1))
                parts[b + step] = jnp.where(keep, pltpu.roll(low, LANES - step * width, 1), high)
        step *= 2
    return parts


def channel_kernel(row_block, volts, taps_wide, turn_c, turn_s, table, outs, branches, filtered, product):
    taps = taps_wide.shape[0]
    length = taps_wide.shape[2]
    frames = filtered.shape[2]
    depth = length // RADIX
    bands = depth // LANES

    def column(j, carry):
        lane = pl.multiple_of(j * LANES, LANES)

        def strip(n1, inner):
            base = pl.multiple_of(n1 * depth + j * LANES, LANES)
            for part in range(2):
                sums = [None] * frames
                for seg in range(frames + taps - 1):
                    start = pl.multiple_of(seg * length + base, LANES)
                    value = volts[part, :, pl.ds(start, LANES)].astype(jnp.float32)
                    for f in range(max(0, seg - taps + 1), min(frames, seg + 1)):
                        coef = taps_wide[seg - f, :, pl.ds(base, LANES)]
                        term = value * jnp.concatenate([coef, coef], axis=0)
                        sums[f] = term if sums[f] is None else sums[f] + term
                    if seg >= taps - 1:
                        filtered[part, n1, seg - taps + 1] = sums[seg - taps + 1]
            return inner

        lax.fori_loop(0, RADIX, strip, 0)

        def butterfly(f, inner):
            re, im = radix8(
                [filtered[0, n1, f] for n1 in range(RADIX)],
                [filtered[1, n1, f] for n1 in range(RADIX)],
            )
            for b in range(RADIX):
                turned_r, turned_i = re[b], im[b]
                if b > 0:
                    cos_t, sin_t = turn_c[b : b + 1, pl.ds(lane, LANES)], turn_s[b : b + 1, pl.ds(lane, LANES)]
                    turned_r, turned_i = re[b] * cos_t + im[b] * sin_t, im[b] * cos_t - re[b] * sin_t
                branches[b, f, :, pl.ds(lane, LANES)] = turned_r.astype(branches.dtype)
                branches[b, f, :, pl.ds(pl.multiple_of(depth + lane, LANES), LANES)] = turned_i.astype(branches.dtype)
            return inner

        lax.fori_loop(0, frames, butterfly, 0)
        return carry

    lax.fori_loop(0, bands, column, 0)

    def multiply(b, carry):
        rows = branches[b].reshape(frames * ROWS, 2 * depth)
        product[b] = jnp.dot(rows, table[...], preferred_element_type=jnp.float32)
        return carry

    lax.fori_loop(0, RADIX, multiply, 0)
    lane_ids = lax.broadcasted_iota(jnp.int32, (ROWS, LANES), 1)

    def regroup(f, carry):
        top = pl.multiple_of(f * ROWS, ROWS)
        for part in range(2):
            for band in range(bands):
                lane = part * depth + band * LANES
                pieces = [product[b, pl.ds(top, ROWS), lane : lane + LANES] for b in range(RADIX)]
                for g, piece in enumerate(swap_blocks(pieces, lane_ids)):
                    at = pl.multiple_of((part * frames + f) * LANES, LANES)
                    outs[g, band, :, pl.ds(at, LANES)] = piece.astype(outs.dtype)
        return carry

    lax.fori_loop(0, frames, regroup, 0)


def channelise(row_block, volts, taps_wide, turn_c, turn_s, table):
    length = volts.shape[2]
    depth = NCH // RADIX
    bands = depth // LANES
    wide = 2 * FRAMES * LANES
    work = 2 * ROWS * FRAMES * NCH
    return pl.pallas_call(
        channel_kernel,
        grid_spec=pltpu.PrefetchScalarGridSpec(
            num_scalar_prefetch=1,
            grid=(1,),
            in_specs=[
                pl.BlockSpec((2, ROWS, length), lambda i, row: (0, row[0], 0)),
                pl.BlockSpec(taps_wide.shape, lambda i, row: (0, 0, 0)),
                pl.BlockSpec(turn_c.shape, lambda i, row: (0, 0)),
                pl.BlockSpec(turn_s.shape, lambda i, row: (0, 0)),
                pl.BlockSpec(table.shape, lambda i, row: (0, 0)),
            ],
            out_specs=[
                pl.BlockSpec((RADIX, bands, ROWS, wide), lambda i, row: (0, 0, 0, 0)),
                pl.BlockSpec((RADIX, FRAMES, ROWS, 2 * depth), lambda i, row: (0, 0, 0, 0)),
            ],
            scratch_shapes=[
                pltpu.VMEM((2, RADIX, FRAMES, ROWS, LANES), jnp.float32),
                pltpu.VMEM((RADIX, FRAMES * ROWS, 2 * depth), jnp.float32),
            ],
        ),
        out_shape=[
            jax.ShapeDtypeStruct((RADIX, bands, ROWS, wide), jnp.bfloat16),
            jax.ShapeDtypeStruct((RADIX, FRAMES, ROWS, 2 * depth), jnp.bfloat16),
        ],
        compiler_params=pltpu.CompilerParams(vmem_limit_bytes=VMEM),
        cost_estimate=pl.CostEstimate(
            flops=work * 4 * depth, bytes_accessed=4 * ROWS * length + 4 * work, transcendentals=0
        ),
    )(row_block, volts, taps_wide, turn_c, turn_s, table)


def slot_kernel(row_branch, hi_c, hi_s, lo_c, lo_s, *rest):
    chunks, (out, table, total) = rest[:-3], rest[-3:]
    depth = chunks[0].shape[3] // 2
    f_step = chunks[0].shape[1]

    @pl.when(pl.program_id(0) == 0)
    def _():
        for a in range(hi_c.shape[1]):
            high_c, high_s = hi_c[:, a : a + 1], hi_s[:, a : a + 1]
            table[:, a * LANES : (a + 1) * LANES] = (high_c * lo_c[...] - high_s * lo_s[...]).astype(table.dtype)
            table[:, depth + a * LANES : depth + (a + 1) * LANES] = (
                high_s * lo_c[...] + high_c * lo_s[...]
            ).astype(table.dtype)

    total[...] = jnp.zeros_like(total)

    def branch(b, carry):
        rows = jnp.concatenate([c[b, f] for f in range(f_step) for c in chunks], axis=0)
        got = lax.dot_general(table[...], rows, NT, preferred_element_type=jnp.float32)
        total[...] = jnp.where(row_branch[...] == b, got, total[...])
        return carry

    lax.fori_loop(0, RADIX, branch, 0)
    per = out.shape[1]
    for d in range(out.shape[0]):
        out[d] = total[d * per : (d + 1) * per].astype(out.dtype)


def slot_spectra(row_channel, row_filled, row_turned, chunks, per):
    depth = NCH // RADIX
    rows = row_channel.shape[0]
    signals = sum(c.shape[2] for c in chunks)
    f_step = min(FRAMES, 2 * LANES // signals)
    coarse = jnp.arange(depth // LANES, dtype=jnp.int32) * LANES
    fine = jnp.arange(LANES, dtype=jnp.int32)
    whole = row_channel - row_channel % RADIX
    hi_c, hi_s = phase(whole[:, None] * coarse[None, :] + row_turned[:, None] * (NCH // 4), NCH)
    lo_c, lo_s = phase(whole[:, None] * fine[None, :], NCH)
    scaling = row_filled.astype(jnp.float32)[:, None] * (1.0 / math.sqrt(NCH))
    row_branch = (row_channel % RADIX)[:, None]
    small = [row_branch, hi_c * scaling, hi_s * scaling, lo_c, lo_s]
    return pl.pallas_call(
        slot_kernel,
        grid=(FRAMES // f_step,),
        in_specs=[pl.BlockSpec(x.shape, lambda i: (0, 0)) for x in small]
        + [pl.BlockSpec((RADIX, f_step, c.shape[2], 2 * depth), lambda i: (0, i, 0, 0)) for c in chunks],
        out_specs=pl.BlockSpec((rows // per, per, f_step * signals), lambda i: (0, 0, i)),
        out_shape=jax.ShapeDtypeStruct((rows // per, per, FRAMES * signals), jnp.bfloat16),
        scratch_shapes=[
            pltpu.VMEM((rows, 2 * depth), jnp.bfloat16),
            pltpu.VMEM((rows, f_step * signals), jnp.float32),
        ],
        compiler_params=pltpu.CompilerParams(vmem_limit_bytes=VMEM),
        cost_estimate=pl.CostEstimate(
            flops=2 * rows * 2 * NCH * FRAMES * signals,
            bytes_accessed=4 * NCH * FRAMES * signals,
            transcendentals=0,
        ),
    )(*small, *chunks)


def correlate(received):
    senders, sub, wide = received[0].shape
    chunks = len(received)
    signals = senders * sub * chunks
    if chunks == 1:
        received = [received[0].reshape(1, signals, wide)]
        senders, sub = 1, signals
    block = min(256, signals)
    blocks = signals // block
    half = wide // 2

    def kernel(*refs):
        parts, (out, held, sems) = refs[:chunks], refs[chunks:]
        copies = []
        for c, part in enumerate(parts):
            for d in range(senders):
                dst = held.at[pl.ds((d * chunks + c) * sub, sub)]
                copies.append(pltpu.make_async_copy(part.at[d], dst, sems.at[c * senders + d]))
        for copy in copies:
            copy.start()
        for copy in copies:
            copy.wait()
        inverse = 1.0 / half

        def product(left, right):
            return lax.dot_general(left, right, NT, preferred_element_type=jnp.float32)

        for i in range(blocks):
            for j in range(i + 1):
                at_i, at_j = slice(i * block, (i + 1) * block), slice(j * block, (j + 1) * block)
                re = (
                    product(held[at_i, :half], held[at_j, :half]) + product(held[at_i, half:], held[at_j, half:])
                ) * inverse
                im = (
                    product(held[at_i, half:], held[at_j, :half]) - product(held[at_i, :half], held[at_j, half:])
                ) * inverse
                out[0, at_i, at_j] = re
                out[1, at_i, at_j] = im
                if i != j:
                    out[0, at_j, at_i] = re.T
                    out[1, at_j, at_i] = -im.T

    return pl.pallas_call(
        kernel,
        in_specs=[pl.BlockSpec(memory_space=pl.ANY)] * chunks,
        out_specs=pl.BlockSpec(memory_space=pltpu.VMEM),
        out_shape=jax.ShapeDtypeStruct((2, signals, signals), jnp.float32),
        scratch_shapes=[
            pltpu.VMEM((signals, wide), jnp.bfloat16),
            pltpu.SemaphoreType.DMA((chunks * senders,)),
        ],
        compiler_params=pltpu.CompilerParams(vmem_limit_bytes=VMEM),
        cost_estimate=pl.CostEstimate(
            flops=2 * signals * signals * wide,
            bytes_accessed=2 * signals * wide + 8 * signals * signals,
            transcendentals=0,
        ),
    )(*received)


def weight_kernel(channel, delays, gains, out):
    beams = delays.shape[0]
    turns = delays[...] * (channel[pl.program_id(0)].astype(jnp.float32) * (1.0 / NCH))
    part = turns - jnp.floor(turns + 0.5)
    square = part * part
    cos_t = jnp.full_like(part, TWO_PI**16 / math.factorial(16))
    sin_t = jnp.full_like(part, -(TWO_PI**15) / math.factorial(15))
    for power in range(14, -1, -2):
        sign = -1.0 if power % 4 == 2 else 1.0
        cos_t = cos_t * square + sign * TWO_PI**power / math.factorial(power)
        if power > 0:
            sign = -1.0 if (power - 1) % 4 == 3 else 1.0
            sin_t = sin_t * square + sign * TWO_PI ** (power - 1) / math.factorial(power - 1)
    scaled = gains[...] * (1.0 / math.sqrt(gains.shape[1]))
    out[0, :beams] = (scaled * cos_t).astype(out.dtype)
    out[0, beams:] = (-scaled * sin_t * part).astype(out.dtype)


def beam_weights(channel, delays, gains):
    beams, listed = delays.shape
    slots = channel.shape[0]
    return pl.pallas_call(
        weight_kernel,
        grid=(slots,),
        in_specs=[
            pl.BlockSpec(memory_space=pltpu.SMEM),
            pl.BlockSpec(delays.shape, lambda i: (0, 0)),
            pl.BlockSpec(gains.shape, lambda i: (0, 0)),
        ],
        out_specs=pl.BlockSpec((1, 2 * beams, listed), lambda i: (i, 0, 0)),
        out_shape=jax.ShapeDtypeStruct((slots, 2 * beams, listed), jnp.bfloat16),
        cost_estimate=pl.CostEstimate(
            flops=40 * slots * beams * listed, bytes_accessed=4 * slots * beams * listed, transcendentals=0
        ),
    )(channel, delays, gains)


def combine(spectra, chooser, weights):
    slots, beams2, listed = weights.shape
    beams = beams2 // 2
    senders, rows, lanes = spectra.shape
    count = LANES * FRAMES // lanes
    groups = senders // count
    tiles = 2 * listed // LANES

    def kernel(spectrum, choose, weight, out, ordered, picked):
        lane_ids = lax.broadcasted_iota(jnp.int32, (rows, LANES), 1)
        for q in range(groups):
            for t in range(lanes // LANES):
                pieces = [
                    spectrum[q * count + i, :, t * LANES : (t + 1) * LANES].astype(jnp.float32) for i in range(count)
                ]
                for f, piece in enumerate(swap_blocks(pieces, lane_ids)):
                    top = (t * count + f) * rows
                    ordered[q, top : top + rows, :] = piece
        acc = None
        for q in range(groups):
            term = jnp.dot(
                ordered[q].astype(jnp.bfloat16),
                choose[q * LANES : (q + 1) * LANES, :],
                preferred_element_type=jnp.float32,
            )
            acc = term if acc is None else acc + term
        for lane in range(tiles):
            picked[lane] = acc[:, lane * LANES : (lane + 1) * LANES]
        for i in range(slots):
            chosen = [
                jnp.concatenate(
                    [
                        picked[p * tiles // 2 + lane, pl.ds(part * slots + i, FRAMES, rows), :]
                        for lane in range(tiles // 2)
                    ],
                    axis=1,
                )
                for p in range(2)
                for part in range(2)
            ]
            stacked = jnp.concatenate(chosen, axis=0).astype(jnp.bfloat16)
            mixed = lax.dot_general(stacked, weight[i], NT, preferred_element_type=jnp.float32)
            for p in range(2):
                at = 2 * FRAMES * p
                of_re, of_im = mixed[at : at + FRAMES], mixed[at + FRAMES : at + 2 * FRAMES]
                out[0, i, 0, :, p * beams : (p + 1) * beams] = of_re[:, :beams] - of_im[:, beams:]
                out[0, i, 1, :, p * beams : (p + 1) * beams] = of_im[:, :beams] + of_re[:, beams:]

    return pl.pallas_call(
        kernel,
        out_shape=jax.ShapeDtypeStruct((1, slots, 2, FRAMES, 2 * beams), jnp.float32),
        scratch_shapes=[
            pltpu.VMEM((groups, FRAMES * rows, LANES), jnp.float32),
            pltpu.VMEM((tiles, FRAMES * rows, LANES), jnp.float32),
        ],
        compiler_params=pltpu.CompilerParams(vmem_limit_bytes=VMEM),
        cost_estimate=pl.CostEstimate(
            flops=2 * FRAMES * rows * 2 * listed * (LANES * groups + 2 * beams),
            bytes_accessed=8 * FRAMES * rows * listed,
            transcendentals=0,
        ),
    )(spectra, chooser, weights)


def after(value, other):
    return lax.optimization_barrier((value, other))[0]


def body(volts, prototype, beam_channels, station_index, delays, gains, assign):
    sig_dev = volts.shape[1]
    st_count = lax.axis_size("st")
    sb_count = lax.axis_size("sb")
    devices = st_count * sb_count
    sb_here = lax.axis_index("sb").astype(jnp.int32)
    st_here = lax.axis_index("st").astype(jnp.int32)
    depth = NCH // RADIX
    band = NCH // sb_count
    fine = band // RADIX // st_count

    table = transform_table()
    turn_c, turn_s = phase(
        jnp.arange(RADIX, dtype=jnp.int32)[:, None] * jnp.arange(depth, dtype=jnp.int32)[None, :], NCH
    )
    taps_wide = jnp.broadcast_to(prototype[:, None, :], (prototype.shape[0], 8, NCH))

    def exchange(x):
        return lax.all_to_all(x, ("st", "sb"), split_axis=0, concat_axis=0, tiled=True)

    share = sig_dev // sb_count
    inside = (sb_here * share) % ROWS
    received, branches = [], []
    for c in range(max(1, share // ROWS)):
        row_block = (sb_here * share // ROWS + c)[None]
        groups, kept = channelise(row_block, volts, taps_wide, turn_c, turn_s, table)
        if c == 0:
            assign, beam_channels, station_index = after((assign, beam_channels, station_index), groups)
        table = after(table, groups)
        branches.append(kept)
        inner = st_count // RADIX
        if share < ROWS:
            groups = lax.dynamic_slice_in_dim(groups, inside, share, axis=2)
        if inner > 1:
            split = groups.reshape(RADIX, sb_count, -1, 2 * FRAMES, RADIX, inner, fine)
            groups = split.transpose(0, 5, 1, 2, 3, 4, 6)
        received.append(exchange(groups.reshape(devices, min(share, ROWS), -1)))

    per_dev = SLOTS // st_count
    owners = assign[:, 0]
    taken = (owners[:, None] == jnp.arange(sb_count, dtype=jnp.int32)[None, :]).astype(jnp.int32)
    position = jnp.sum(taken * jnp.cumsum(taken, axis=0), axis=1) - 1
    place = owners * SLOTS + position
    slot_ids = (
        jnp.arange(st_count, dtype=jnp.int32)[:, None, None] * per_dev
        + jnp.arange(sb_count, dtype=jnp.int32)[None, :, None] * SLOTS
        + jnp.arange(per_dev, dtype=jnp.int32)[None, None, :]
    ).reshape(-1)
    picker = (place[None, :] == slot_ids[:, None]).astype(jnp.int32)
    filled = jnp.sum(picker, axis=1)
    slot_channel = jnp.sum(picker * beam_channels[None, :], axis=1)

    def by_row(values):
        return jnp.broadcast_to(values.reshape(devices, 1, per_dev), (devices, 2, per_dev)).reshape(-1)

    turned = jnp.broadcast_to(jnp.arange(2, dtype=jnp.int32)[None, :, None], (devices, 2, per_dev)).reshape(-1)
    mine = lax.dynamic_slice_in_dim(slot_channel, (st_here * sb_count + sb_here) * per_dev, per_dev)
    weights = beam_weights(after(mine, branches), delays, gains)
    if len(received) > 1:
        slot_channel = after(slot_channel, (received[0], weights))
    spectra = slot_spectra(by_row(slot_channel), by_row(filled), turned, branches, 2 * per_dev)
    if share < ROWS:
        spectra = spectra.reshape(devices, 2 * per_dev, FRAMES, ROWS)
        spectra = lax.dynamic_slice_in_dim(spectra, inside, share, axis=3).reshape(devices, 2 * per_dev, -1)
    slot_received = exchange(spectra)

    signal_ids = jnp.arange(sig_dev * st_count, dtype=jnp.int32)
    wanted = (station_index[None, :] * 2 + jnp.arange(2, dtype=jnp.int32)[:, None]).reshape(-1)
    chooser = (signal_ids[:, None] == wanted[None, :]).astype(jnp.bfloat16)

    visibility = correlate(after(received, spectra))
    signals = visibility.shape[1]
    beam_out = combine(slot_received, chooser, after(weights, visibility))
    return (visibility.reshape(2, 1, 1, signals, signals), beam_out)


def solution(mesh):
    in_specs = (P(None, "st", None), P(), P(), P(), P(), P(), P())
    out_specs = (P(None, "sb", "st", None, None), P("sb", "st", None, None, None))
    return jax.shard_map(body, mesh=mesh, in_specs=in_specs, out_specs=out_specs, check_vma=False)
```

time: 376 us -> 293 us (0.78)
  Pallas kernels: 242 us -> 133 us
  waiting for transfers between devices: 47.2 us -> 120 us
  starting transfers between devices: 73.7 us -> 18.3 us
  other arithmetic: 8.05 us -> 14.9 us
    all_to_all x0 -> x3, waiting for transfers between devices: none -> 120 us  [exchange(): lax.all_to_all(x, ('st', 'sb'), split_axis=0, concat_axis=0, tiled=True)]
    pallas_call x6 -> x4, Pallas kernels: 194 us -> 91.8 us  [the longest x2 70.7 us: channelise(): pl.pallas_call(channel_kernel, grid_spec=pltpu.PrefetchScalarGridSpec(num...]
    ppermute x35 -> x0, starting transfers between devices: 73.7 us -> none  [exchange(): lax.ppermute(pieces[s], 'st', [(i, i ^ s) for i in range(st_count)])]
    ppermute x35 -> x0, waiting for transfers between devices: 47.2 us -> none  [exchange(): lax.ppermute(pieces[s], 'st', [(i, i ^ s) for i in range(st_count)])]
    all_to_all x0 -> x3, starting transfers between devices: none -> 18.3 us  [exchange(): lax.all_to_all(x, ('st', 'sb'), split_axis=0, concat_axis=0, tiled=True)]
    pallas_call x1, Pallas kernels: 28.3 us -> 19.9 us  [slot_spectra(): pl.pallas_call(slot_kernel, grid=(FRAMES // f_step,), in_specs=[pl.BlockS...]
  transfers between devices with their start and end apart: 35 -> 3, of which waited for: 6 -> 3; matrix products, arithmetic and copies ran while one was open for 2% -> 5% of each run, Pallas kernels for 50% -> 29%
where the time goes in v2:
time: 293 us; the launch traced here: 292 us
  Pallas kernels  133 us (45%)
  waiting for transfers between devices  120 us (41%)
  starting transfers between devices  18.3 us (6%)
  other arithmetic  14.9 us (5%)
  local copies, waits for them, and re-layouts  5.61 us (2%)
    all_to_all x3, waiting for transfers between devices, exchange(): lax.all_to_all(x, ('st', 'sb'), split_axis=0, concat_axis=0, tiled=True)  120 us
    pallas_call x2, Pallas kernels, channelise(): pl.pallas_call(channel_kernel, grid_spec=pltpu.PrefetchScalarGridSpec(num...  70.7 us
    pallas_call x1, Pallas kernels, slot_spectra(): pl.pallas_call(slot_kernel, grid=(FRAMES // f_step,), in_specs=[pl.BlockS...  19.9 us
    pallas_call x1, Pallas kernels, correlate(): pl.pallas_call(kernel, in_specs=[pl.BlockSpec(memory_space=pl.ANY)] * chu...  18.4 us
    all_to_all x3, starting transfers between devices, exchange(): lax.all_to_all(x, ('st', 'sb'), split_axis=0, concat_axis=0, tiled=True)  18.3 us
    pallas_call x1, Pallas kernels, beam_weights(): pl.pallas_call(weight_kernel, grid=(slots,), in_specs=[pl.BlockSpec(memor...  12.4 us
    pallas_call x1, Pallas kernels, combine(): pl.pallas_call(kernel, out_shape=jax.ShapeDtypeStruct((1, slots, 2, FRAME...  8.71 us
  transfers between devices with their start and end apart: 3, of which 3 were waited for; matrix products, arithmetic and copies ran while one was open for 5% of the time, Pallas kernels for 29%

profile of v2, /device:TPU:0, one launch (start us, length us, event | category | flops | bytes accessed | tf_op | source)
XLA Modules:
  0.0 292.2 jit_solution(7489738845787484051)
XLA Ops:
  0.6 0.7 fusion.36
  1.3 0.8 fusion.29
  2.1 1.0 sine_multiply_fusion.1
  3.1 2.7 shard_map.86.table
  5.8 2.5 broadcast_in_dim.15.taps_wide
  8.3 35.3 %shard_map.87 = (bf16[8,4,16,4096]{3,2,1,0:T(8,128)(2,1)}, bf16[8,16,16,1024]{3,2,1,0:T(8,128)(2,1)}) custom-call(s32[1]{0:T(128)} %bitcast.row_block, bf16[2,128,126976]{2,1,0:T(8,128)(2,1)} %volts.3, f32[16,8,4096]{2,1,0:T(8,128)} %broadcast_in_dim.15.taps_wide, f32[8,512]{1,0:T(8,128)} %get-tuple-element.47.turn_c, f32[8,512]{1,0:T(8,128)} %get-tuple-element.46.turn_s, ...), custom_call_target="tpu_custom_call" | custom-call | flops 4294967296 | bytes 16515072 | tf_op jit(solution)/shard_map/pallas_call | solution.py:165
  43.6 7.4 %all-to-all-start = ((bf16[32,16,4096]{2,1,0:T(8,128)(2,1)}), bf16[32,16,4096]{2,1,0:T(8,128)(2,1)}, u32[]{:S(2)}, u32[]{:S(2)}) async-start(bf16[32,16,4096]{2,1,0:T(8,128)(2,1)} %bitcast.27), calls=%async_computation | async-start | bytes 8388608 | tf_op jit(solution)/shard_map/all_to_all | solution.py:441
  51.0 35.4 %shard_map.88 = (bf16[8,4,16,4096]{3,2,1,0:T(8,128)(2,1)}, bf16[8,16,16,1024]{3,2,1,0:T(8,128)(2,1)}) custom-call(s32[1]{0:T(128)} %bitcast.2.row_block, bf16[2,128,126976]{2,1,0:T(8,128)(2,1)} %volts.3, f32[16,8,4096]{2,1,0:T(8,128)} %broadcast_in_dim.15.taps_wide, f32[8,512]{1,0:T(8,128)} %get-tuple-element.47.turn_c, f32[8,512]{1,0:T(8,128)} %get-tuple-element.46.turn_s, ...), custom_call_target="tpu_custom_call" | custom-call | flops 4294967296 | bytes 16515072 | tf_op jit(solution)/shard_map/pallas_call | solution.py:165
  86.4 59.0 %all-to-all-done.refs_0_ = bf16[32,16,4096]{2,1,0:T(8,128)(2,1)} async-done(((bf16[32,16,4096]{2,1,0:T(8,128)(2,1)}), bf16[32,16,4096]{2,1,0:T(8,128)(2,1)}, u32[]{:S(2)}, u32[]{:S(2)}) %all-to-all-start) | async-done | bytes 4194336 | tf_op jit(solution)/shard_map/all_to_all | solution.py:441
  145.4 5.4 %all-to-all-start.1 = ((bf16[32,16,4096]{2,1,0:T(8,128)(2,1)}), bf16[32,16,4096]{2,1,0:T(8,128)(2,1)}, u32[]{:S(2)}, u32[]{:S(2)}) async-start(bf16[32,16,4096]{2,1,0:T(8,128)(2,1)} %bitcast.26), calls=%async_computation.1 | async-start | bytes 8388608 | tf_op jit(solution)/shard_map/all_to_all | solution.py:441
  150.9 1.2 reduce-window.6
  152.1 0.2 slice_reduce_fusion
  152.3 0.2 reduce-window.9
  152.6 0.1 add.159
  152.9 0.4 fusion.2
  153.3 0.6 dynamic_slice.3.channel
  153.9 0.1 mul.295
  154.1 0.1 mul.301
  154.3 12.4 %shard_map.89.weight = bf16[20,512,256]{2,1,0:T(8,128)(2,1)} custom-call(s32[20]{0:T(128)} %dynamic_slice.3.channel, f32[256,256]{1,0:T(8,128)} %delays.1, f32[256,256]{1,0:T(8,128)} %gains.1), custom_call_target="tpu_custom_call" | custom-call | flops 52428800 | bytes 5242880 | tf_op jit(solution)/shard_map/pallas_call | solution.py:339
  166.7 0.3 reshape.221
  167.3 0.3 copy.21
  167.5 1.1 add_select_fusion.1.row_branch
  168.6 3.9 %fusion.10 = (f32[1280,128]{1,0:T(8,128)}, f32[1280,128]{1,0:T(8,128)}) fusion(s32[1280]{0:T(1024)S(1)} %fusion.35), kind=kLoop, calls=%fused_computation.21 | loop fusion | flops 2293760 | bytes 1315840 | tf_op jit(solution)/shard_map/sin | solution.py:25
  172.5 3.8 %sine_multiply_fusion = (f32[1280,4]{1,0:T(8,128)}, f32[1280,4]{1,0:T(8,128)}) fusion(f32[1280,4]{1,0:T(8,128)S(1)} %copy.21, f32[1280]{0:T(1024)S(1)} %mul.301), kind=kLoop, calls=%fused_computation.18 | loop fusion | flops 15360 | bytes 66560 | tf_op jit(solution)/shard_map/mul | solution.py:237
  176.3 19.9 %shard_map.90 = bf16[32,40,512]{2,1,0:T(8,128)(2,1)} custom-call(s32[1280,1]{1,0:T(8,128)} %add_select_fusion.1.row_branch, f32[1280,4]{1,0:T(8,128)} %get-tuple-element.39.hi_c, f32[1280,4]{1,0:T(8,128)} %get-tuple-element.38.hi_s, f32[1280,128]{1,0:T(8,128)} %get-tuple-element.41.lo_c, f32[1280,128]{1,0:T(8,128)} %get-tuple-element.40.lo_s, ...), custom_call_target="tpu_custom_call" | custom-call | flops 10737418240 | bytes 8388608 | tf_op jit(solution)/shard_map/pallas_call | solution.py:238
  196.2 48.9 %all-to-all-done.1.refs_1_ = bf16[32,16,4096]{2,1,0:T(8,128)(2,1)} async-done(((bf16[32,16,4096]{2,1,0:T(8,128)(2,1)}), bf16[32,16,4096]{2,1,0:T(8,128)(2,1)}, u32[]{:S(2)}, u32[]{:S(2)}) %all-to-all-start.1) | async-done | bytes 4194336 | tf_op jit(solution)/shard_map/all_to_all | solution.py:441
  245.2 5.5 %all-to-all-start.2 = ((bf16[32,40,512]{2,1,0:T(8,128)(2,1)}), bf16[32,40,512]{2,1,0:T(8,128)(2,1)S(1)}, u32[]{:S(2)}, u32[]{:S(2)}) async-start(bf16[32,40,512]{2,1,0:T(8,128)(2,1)} %shard_map.90), calls=%async_computation.2 | async-start | bytes 2621440 | tf_op jit(solution)/shard_map/all_to_all | solution.py:441
  250.7 1.4 fusion.choose
  252.1 18.4 %shard_map.91 = f32[2,1024,1024]{2,1,0:T(8,128)} custom-call(bf16[32,16,4096]{2,1,0:T(8,128)(2,1)} %all-to-all-done.refs_0_, bf16[32,16,4096]{2,1,0:T(8,128)(2,1)} %all-to-all-done.1.refs_1_), custom_call_target="tpu_custom_call" | custom-call | flops 8589934592 | bytes 16777216 | tf_op jit(solution)/shard_map/pallas_call | solution.py:300
  270.5 11.8 %all-to-all-done.2.spectrum = bf16[32,40,512]{2,1,0:T(8,128)(2,1)S(1)} async-done(((bf16[32,40,512]{2,1,0:T(8,128)(2,1)}), bf16[32,40,512]{2,1,0:T(8,128)(2,1)S(1)}, u32[]{:S(2)}, u32[]{:S(2)}) %all-to-all-start.2) | async-done | bytes 1310752 | tf_op jit(solution)/shard_map/all_to_all | solution.py:441
  282.4 1.1 copy-done
  283.5 8.7 %shard_map.92 = f32[1,20,2,16,512]{4,3,2,1,0:T(8,128)} custom-call(bf16[32,40,512]{2,1,0:T(8,128)(2,1)} %copy-done, bf16[1024,512]{1,0:T(8,128)(2,1)} %fusion.choose, bf16[20,512,256]{2,1,0:T(8,128)(2,1)} %shard_map.89.weight), custom_call_target="tpu_custom_call" | custom-call | flops 1006632960 | bytes 1310720 | tf_op jit(solution)/shard_map/pallas_call | solution.py:403
  (30 shorter events, 0.8 us)
Async XLA Ops:
  43.6 101.8 %all-to-all-start = ((bf16[32,16,4096]{2,1,0:T(8,128)(2,1)}), bf16[32,16,4096]{2,1,0:T(8,128)(2,1)}, u32[]{:S(2)}, u32[]{:S(2)}) async-start(bf16[32,16,4096]{2,1,0:T(8,128)(2,1)} %bitcast.27), calls=%async_computation | async-start | bytes 8388608 | tf_op jit(solution)/shard_map/all_to_all | solution.py:441
  145.4 5.4 %copy-start.2 = (s32[384,1]{0,1:T(1,128)S(1)}, s32[384,1]{0,1:T(1,128)}, u32[]{:S(2)}) copy-start(s32[384,1]{0,1:T(1,128)} %param.13) | copy-start | bytes 4612
  145.4 7.5 %copy-start.1 = (s32[384]{0:T(512)S(1)}, s32[384]{0:T(512)}, u32[]{:S(2)}) copy-start(s32[384]{0:T(512)} %param.9) | copy-start | bytes 4612
  145.4 99.8 %all-to-all-start.1 = ((bf16[32,16,4096]{2,1,0:T(8,128)(2,1)}), bf16[32,16,4096]{2,1,0:T(8,128)(2,1)}, u32[]{:S(2)}, u32[]{:S(2)}) async-start(bf16[32,16,4096]{2,1,0:T(8,128)(2,1)} %bitcast.26), calls=%async_computation.1 | async-start | bytes 8388608 | tf_op jit(solution)/shard_map/all_to_all | solution.py:441
  176.3 74.3 %copy-start.3 = (s32[256]{0:T(256)S(1)}, s32[256]{0:T(256)}, u32[]{:S(2)}) copy-start(s32[256]{0:T(256)} %param.10) | copy-start | bytes 3076
  245.2 37.2 %all-to-all-start.2 = ((bf16[32,40,512]{2,1,0:T(8,128)(2,1)}), bf16[32,40,512]{2,1,0:T(8,128)(2,1)S(1)}, u32[]{:S(2)}, u32[]{:S(2)}) async-start(bf16[32,40,512]{2,1,0:T(8,128)(2,1)} %shard_map.90), calls=%async_computation.2 | async-start | bytes 2621440 | tf_op jit(solution)/shard_map/all_to_all | solution.py:441
  282.4 1.1 copy-start

commit v3 on v2

v3 whole, which is shorter than its diff:
```python
import functools
import math

import jax
import jax.numpy as jnp
from jax import lax
from jax.experimental import pallas as pl
from jax.experimental.pallas import tpu as pltpu
from jax.sharding import Mesh
from jax.sharding import PartitionSpec as P

NCH = 4096
FRAMES = 16
SLOTS = 160
RADIX = 8
LANES = 128
ROWS = 16
VMEM = 56 * 1024 * 1024

TWO_PI = 2.0 * math.pi
NT = (((1,), (1,)), ((), ()))


def phase(turns, length):
    angles = (turns % length).astype(jnp.float32) * (TWO_PI / length)
    return jnp.cos(angles), jnp.sin(angles)


def table_kernel(hi_c, hi_s, lo_c, lo_s, out):
    fine, width = lo_c.shape
    depth = hi_c.shape[0] * fine

    def block(a, carry):
        top = pl.multiple_of(a * fine, fine)
        high_c, high_s = hi_c[pl.ds(a, 1), :], hi_s[pl.ds(a, 1), :]
        cos_t = (high_c * lo_c[...] - high_s * lo_s[...]).astype(out.dtype)
        sin_t = (high_s * lo_c[...] + high_c * lo_s[...]).astype(out.dtype)
        out[pl.ds(top, fine), :width] = cos_t
        out[pl.ds(top, fine), width:] = -sin_t
        out[pl.ds(depth + top, fine), :width] = sin_t
        out[pl.ds(depth + top, fine), width:] = cos_t
        return carry

    lax.fori_loop(0, hi_c.shape[0], block, 0)


def transform_table(out_ids):
    depth = NCH // RADIX
    out_ids = out_ids[None, :]
    lo_c, lo_s = phase(jnp.arange(ROWS, dtype=jnp.int32)[:, None] * out_ids, depth)
    hi_c, hi_s = phase(jnp.arange(0, depth, ROWS, dtype=jnp.int32)[:, None] * out_ids, depth)
    scale = 1.0 / math.sqrt(NCH)
    return pl.pallas_call(
        table_kernel, out_shape=jax.ShapeDtypeStruct((2 * depth, 2 * depth), jnp.bfloat16)
    )(hi_c * scale, hi_s * scale, lo_c, lo_s)


def radix8(re, im):
    half = math.sqrt(0.5)

    def four(xr, xi):
        ar, ai, br, bi = xr[0] + xr[2], xi[0] + xi[2], xr[0] - xr[2], xi[0] - xi[2]
        cr, ci, dr, di = xr[1] + xr[3], xi[1] + xi[3], xr[1] - xr[3], xi[1] - xi[3]
        return [ar + cr, br + di, ar - cr, br - di], [ai + ci, bi - dr, ai - ci, bi + dr]

    er, ei = four(re[0::2], im[0::2])
    odd_r, odd_i = four(re[1::2], im[1::2])
    tr = [odd_r[0], (odd_r[1] + odd_i[1]) * half, odd_i[2], (odd_i[3] - odd_r[3]) * half]
    ti = [odd_i[0], (odd_i[1] - odd_r[1]) * half, -odd_r[2], (odd_r[3] + odd_i[3]) * -half]
    return (
        [e + t for e, t in zip(er, tr)] + [e - t for e, t in zip(er, tr)],
        [e + t for e, t in zip(ei, ti)] + [e - t for e, t in zip(ei, ti)],
    )


def swap_blocks(parts, lane_ids):
    count = len(parts)
    width = LANES // count
    parts = list(parts)
    step = 1
    while step < count:
        keep = (lane_ids // width) % (2 * step) < step
        for b in range(count):
            if b & step == 0:
                low, high = parts[b], parts[b + step]
                parts[b] = jnp.where(keep, low, pltpu.roll(high, step * width, 1))
                parts[b + step] = jnp.where(keep, pltpu.roll(low, LANES - step * width, 1), high)
        step *= 2
    return parts


def gather_blocks(parts, lane_ids):
    count = len(parts)
    width = LANES // count
    turned = [parts[0]] + [pltpu.roll(parts[b], b * width, 1) for b in range(1, count)]
    turned = [turned[-b % count] for b in range(count)]
    step = 1
    while step < count:
        moved = (lane_ids // width) & step != 0
        turned = [jnp.where(moved, turned[(g - step) % count], turned[g]) for g in range(count)]
        step *= 2
    return [turned[0]] + [pltpu.roll(turned[g], LANES - g * width, 1) for g in range(1, count)]


def channel_kernel(first, row_block, volts, taps_wide, turn_c, turn_s, table, *rest):
    outs, (branches, filtered, product) = rest[:-3], rest[-3:]
    near = RADIX // len(outs)
    taps = taps_wide.shape[0]
    length = taps_wide.shape[2]
    frames = filtered.shape[2]
    depth = length // RADIX
    bands = depth // LANES

    def column(j, carry):
        lane = pl.multiple_of(j * LANES, LANES)

        def strip(n1, inner):
            base = pl.multiple_of(n1 * depth + j * LANES, LANES)
            for part in range(2):
                sums = [None] * frames
                for seg in range(frames + taps - 1):
                    start = pl.multiple_of((first + seg) * length + base, LANES)
                    value = volts[part, :, pl.ds(start, LANES)].astype(jnp.float32)
                    for f in range(max(0, seg - taps + 1), min(frames, seg + 1)):
                        coef = taps_wide[seg - f, :, pl.ds(base, LANES)]
                        term = value * jnp.concatenate([coef, coef], axis=0)
                        sums[f] = term if sums[f] is None else sums[f] + term
                    if seg >= taps - 1:
                        filtered[part, n1, seg - taps + 1] = sums[seg - taps + 1]
            return inner

        lax.fori_loop(0, RADIX, strip, 0)

        def butterfly(f, inner):
            re, im = radix8(
                [filtered[0, n1, f] for n1 in range(RADIX)],
                [filtered[1, n1, f] for n1 in range(RADIX)],
            )
            for b in range(RADIX):
                turned_r, turned_i = re[b], im[b]
                if b > 0:
                    cos_t, sin_t = turn_c[b : b + 1, pl.ds(lane, LANES)], turn_s[b : b + 1, pl.ds(lane, LANES)]
                    turned_r, turned_i = re[b] * cos_t + im[b] * sin_t, im[b] * cos_t - re[b] * sin_t
                branches[b, f, :, pl.ds(lane, LANES)] = turned_r.astype(branches.dtype)
                branches[b, f, :, pl.ds(pl.multiple_of(depth + lane, LANES), LANES)] = turned_i.astype(branches.dtype)
            return inner

        lax.fori_loop(0, frames, butterfly, 0)
        return carry

    lax.fori_loop(0, bands, column, 0)

    def multiply(b, carry):
        rows = branches[b].reshape(frames * ROWS, 2 * depth)
        product[b] = jnp.dot(rows, table[...], preferred_element_type=jnp.float32)
        return carry

    lax.fori_loop(0, RADIX, multiply, 0)
    lane_ids = lax.broadcasted_iota(jnp.int32, (ROWS, LANES), 1)

    def regroup(f, carry):
        top = pl.multiple_of(f * ROWS, ROWS)
        for part in range(2):
            for band in range(bands):
                lane = part * depth + band * LANES
                pieces = [product[b, pl.ds(top, ROWS), lane : lane + LANES] for b in range(RADIX)]
                for g, piece in enumerate(gather_blocks(pieces, lane_ids)):
                    at = pl.multiple_of((part * frames + f) * LANES, LANES)
                    out = outs[g // near]
                    out[g % near, band, :, pl.ds(at, LANES)] = piece.astype(out.dtype)
        return carry

    lax.fori_loop(0, frames, regroup, 0)


def channelise(row_block, volts, taps_wide, turn_c, turn_s, table, first, frames, far):
    taps = taps_wide.shape[0]
    length = volts.shape[2] if first > 0 else (frames + taps - 1) * NCH
    depth = NCH // RADIX
    bands = depth // LANES
    wide = 2 * frames * LANES
    near = RADIX // far
    work = 2 * ROWS * frames * NCH
    return pl.pallas_call(
        functools.partial(channel_kernel, first),
        grid_spec=pltpu.PrefetchScalarGridSpec(
            num_scalar_prefetch=1,
            grid=(1,),
            in_specs=[
                pl.BlockSpec((2, ROWS, length), lambda i, row: (0, row[0], 0)),
                pl.BlockSpec(taps_wide.shape, lambda i, row: (0, 0, 0)),
                pl.BlockSpec(turn_c.shape, lambda i, row: (0, 0)),
                pl.BlockSpec(turn_s.shape, lambda i, row: (0, 0)),
                pl.BlockSpec(table.shape, lambda i, row: (0, 0)),
            ],
            out_specs=[pl.BlockSpec((near, bands, ROWS, wide), lambda i, row: (0, 0, 0, 0))] * far
            + [pl.BlockSpec((RADIX, frames, ROWS, 2 * depth), lambda i, row: (0, 0, 0, 0))],
            scratch_shapes=[
                pltpu.VMEM((2, RADIX, frames, ROWS, LANES), jnp.float32),
                pltpu.VMEM((RADIX, frames * ROWS, 2 * depth), jnp.float32),
            ],
        ),
        out_shape=[jax.ShapeDtypeStruct((near, bands, ROWS, wide), jnp.bfloat16)] * far
        + [jax.ShapeDtypeStruct((RADIX, frames, ROWS, 2 * depth), jnp.bfloat16)],
        compiler_params=pltpu.CompilerParams(vmem_limit_bytes=VMEM),
        cost_estimate=pl.CostEstimate(
            flops=work * 8 * depth, bytes_accessed=4 * ROWS * length + 4 * work, transcendentals=0
        ),
    )(row_block, volts, taps_wide, turn_c, turn_s, table)


def slot_kernel(far, row_branch, hi_c, hi_s, lo_c, lo_s, *rest):
    chunks, outs, (table, total) = rest[: -2 - far], rest[-2 - far : -2], rest[-2:]
    depth = chunks[0].shape[3] // 2
    for a in range(hi_c.shape[1]):
        high_c, high_s = hi_c[:, a : a + 1], hi_s[:, a : a + 1]
        table[:, a * LANES : (a + 1) * LANES] = (high_c * lo_c[...] - high_s * lo_s[...]).astype(table.dtype)
        table[:, depth + a * LANES : depth + (a + 1) * LANES] = (
            high_s * lo_c[...] + high_c * lo_s[...]
        ).astype(table.dtype)
    total[...] = jnp.zeros_like(total)

    def branch(b, carry):
        rows = jnp.concatenate([c[b].reshape(c.shape[1] * c.shape[2], c.shape[3]) for c in chunks], axis=0)
        got = lax.dot_general(table[...], rows, NT, preferred_element_type=jnp.float32)
        total[...] = jnp.where(row_branch[...] == b, got, total[...])
        return carry

    lax.fori_loop(0, RADIX, branch, 0)
    plane, per = outs[0].shape[:2]
    for s, out in enumerate(outs):
        for d in range(plane):
            top = (s * plane + d) * per
            out[d] = total[top : top + per].astype(out.dtype)


def slot_spectra(row_channel, row_filled, row_turned, chunks, per, far):
    depth = NCH // RADIX
    rows = row_channel.shape[0]
    samples = sum(c.shape[1] * c.shape[2] for c in chunks)
    plane = rows // per // far
    coarse = jnp.arange(depth // LANES, dtype=jnp.int32) * LANES
    fine = jnp.arange(LANES, dtype=jnp.int32)
    whole = row_channel - row_channel % RADIX
    hi_c, hi_s = phase(whole[:, None] * coarse[None, :] + row_turned[:, None] * (NCH // 4), NCH)
    lo_c, lo_s = phase(whole[:, None] * fine[None, :], NCH)
    scaling = row_filled.astype(jnp.float32)[:, None] * (1.0 / math.sqrt(NCH))
    row_branch = (row_channel % RADIX)[:, None]
    return pl.pallas_call(
        functools.partial(slot_kernel, far),
        out_shape=[jax.ShapeDtypeStruct((plane, per, samples), jnp.bfloat16)] * far,
        scratch_shapes=[pltpu.VMEM((rows, 2 * depth), jnp.bfloat16), pltpu.VMEM((rows, samples), jnp.float32)],
        compiler_params=pltpu.CompilerParams(vmem_limit_bytes=VMEM),
        cost_estimate=pl.CostEstimate(
            flops=2 * rows * 2 * NCH * samples, bytes_accessed=4 * NCH * samples, transcendentals=0
        ),
    )(row_branch, hi_c * scaling, hi_s * scaling, lo_c, lo_s, *chunks)


def correlate(here, pieces, far, halves):
    senders = pieces[0][0].shape[0]
    sub = pieces[0][0].shape[1] if halves == 1 else ROWS
    lanes = pieces[0][0].shape[2] // (2 * pieces[0][5])
    half = FRAMES * lanes
    block = senders * halves * sub
    signals = far * block

    def kernel(here_ref, *refs):
        parts, (out, held, sems) = refs[: len(pieces)], refs[len(pieces) :]
        copies = []
        for index, (_, partner, row, which, first, frames) in enumerate(pieces):
            for part in range(2):
                src = parts[index].at[:, pl.ds(row, sub), pl.ds(part * frames * lanes, frames * lanes)]
                dst = held.at[here_ref[0] ^ partner, :, which, :, pl.ds(part * half + first * lanes, frames * lanes)]
                copies.append(pltpu.make_async_copy(src, dst, sems.at[2 * index + part]))
        for copy in copies:
            copy.start()
        for copy in copies:
            copy.wait()
        inverse = 1.0 / half

        def product(left, right):
            return lax.dot_general(left, right, NT, preferred_element_type=jnp.float32)

        for i in range(far):
            left = held[i].reshape(block, 2 * half)
            for j in range(i + 1):
                right = held[j].reshape(block, 2 * half)
                at_i, at_j = slice(i * block, (i + 1) * block), slice(j * block, (j + 1) * block)
                re = (
                    product(left[:, :half], right[:, :half]) + product(left[:, half:], right[:, half:])
                ) * inverse
                im = (
                    product(left[:, half:], right[:, :half]) - product(left[:, :half], right[:, half:])
                ) * inverse
                out[0, at_i, at_j] = re
                out[1, at_i, at_j] = im
                if i != j:
                    out[0, at_j, at_i] = re.T
                    out[1, at_j, at_i] = -im.T

    return pl.pallas_call(
        kernel,
        in_specs=[pl.BlockSpec(memory_space=pltpu.SMEM)] + [pl.BlockSpec(memory_space=pl.ANY)] * len(pieces),
        out_specs=pl.BlockSpec(memory_space=pltpu.VMEM),
        out_shape=jax.ShapeDtypeStruct((2, signals, signals), jnp.float32),
        scratch_shapes=[
            pltpu.VMEM((far, senders, halves, sub, 2 * half), jnp.bfloat16),
            pltpu.SemaphoreType.DMA((2 * len(pieces),)),
        ],
        compiler_params=pltpu.CompilerParams(vmem_limit_bytes=VMEM),
        cost_estimate=pl.CostEstimate(
            flops=4 * signals * signals * half,
            bytes_accessed=4 * signals * half + 8 * signals * signals,
            transcendentals=0,
        ),
    )(here, *[piece[0] for piece in pieces])


def weight_kernel(channel, delays, gains, out):
    beams = delays.shape[0]
    turns = delays[...] * (channel[pl.program_id(0)].astype(jnp.float32) * (1.0 / NCH))
    part = turns - jnp.floor(turns + 0.5)
    square = part * part
    cos_t = jnp.full_like(part, TWO_PI**16 / math.factorial(16))
    sin_t = jnp.full_like(part, -(TWO_PI**15) / math.factorial(15))
    for power in range(14, -1, -2):
        sign = -1.0 if power % 4 == 2 else 1.0
        cos_t = cos_t * square + sign * TWO_PI**power / math.factorial(power)
        if power > 0:
            sign = -1.0 if (power - 1) % 4 == 3 else 1.0
            sin_t = sin_t * square + sign * TWO_PI ** (power - 1) / math.factorial(power - 1)
    scaled = gains[...] * (1.0 / math.sqrt(gains.shape[1]))
    out[0, :beams] = (scaled * cos_t).astype(out.dtype)
    out[0, beams:] = (-scaled * sin_t * part).astype(out.dtype)


def beam_weights(channel, delays, gains):
    beams, listed = delays.shape
    slots = channel.shape[0]
    return pl.pallas_call(
        weight_kernel,
        grid=(slots,),
        in_specs=[
            pl.BlockSpec(memory_space=pltpu.SMEM),
            pl.BlockSpec(delays.shape, lambda i: (0, 0)),
            pl.BlockSpec(gains.shape, lambda i: (0, 0)),
        ],
        out_specs=pl.BlockSpec((1, 2 * beams, listed), lambda i: (i, 0, 0)),
        out_shape=jax.ShapeDtypeStruct((slots, 2 * beams, listed), jnp.bfloat16),
        cost_estimate=pl.CostEstimate(
            flops=40 * slots * beams * listed, bytes_accessed=4 * slots * beams * listed, transcendentals=0
        ),
    )(channel, delays, gains)


def combine(spectra, chooser, weights, halves, sub):
    slots, beams2, listed = weights.shape
    beams = beams2 // 2
    rows = 2 * slots
    senders = spectra[0].shape[0]
    partners = sum(x.shape[1] for x in spectra) // rows
    count = LANES // sub
    inner = senders // count
    groups = partners * halves * inner
    tiles = 2 * listed // LANES

    def kernel(*refs):
        got, (choose, weight, out, ordered, picked) = refs[: len(spectra)], refs[len(spectra) :]
        lane_ids = lax.broadcasted_iota(jnp.int32, (rows, LANES), 1)
        where = [(x, k * rows) for x in got for k in range(x.shape[1] // rows)]
        for s, (spectrum, row) in enumerate(where):
            for h in range(halves):
                for q in range(inner):
                    for t in range(FRAMES // count):
                        lane = h * FRAMES * sub + t * LANES
                        pieces = [
                            spectrum[q * count + i, row : row + rows, lane : lane + LANES].astype(jnp.float32)
                            for i in range(count)
                        ]
                        for f, piece in enumerate(swap_blocks(pieces, lane_ids)):
                            top = (t * count + f) * rows
                            ordered[(s * halves + h) * inner + q, top : top + rows, :] = piece
        acc = None
        for q in range(groups):
            term = jnp.dot(
                ordered[q].astype(jnp.bfloat16),
                choose[q * LANES : (q + 1) * LANES, :],
                preferred_element_type=jnp.float32,
            )
            acc = term if acc is None else acc + term
        for lane in range(tiles):
            picked[lane] = acc[:, lane * LANES : (lane + 1) * LANES]
        for i in range(slots):
            chosen = [
                jnp.concatenate(
                    [
                        picked[p * tiles // 2 + lane, pl.ds(part * slots + i, FRAMES, rows), :]
                        for lane in range(tiles // 2)
                    ],
                    axis=1,
                )
                for p in range(2)
                for part in range(2)
            ]
            stacked = jnp.concatenate(chosen, axis=0).astype(jnp.bfloat16)
            mixed = lax.dot_general(stacked, weight[i], NT, preferred_element_type=jnp.float32)
            for p in range(2):
                at = 2 * FRAMES * p
                of_re, of_im = mixed[at : at + FRAMES], mixed[at + FRAMES : at + 2 * FRAMES]
                out[0, i, 0, :, p * beams : (p + 1) * beams] = of_re[:, :beams] - of_im[:, beams:]
                out[0, i, 1, :, p * beams : (p + 1) * beams] = of_im[:, :beams] + of_re[:, beams:]

    return pl.pallas_call(
        kernel,
        out_shape=jax.ShapeDtypeStruct((1, slots, 2, FRAMES, 2 * beams), jnp.float32),
        scratch_shapes=[
            pltpu.VMEM((groups, FRAMES * rows, LANES), jnp.float32),
            pltpu.VMEM((tiles, FRAMES * rows, LANES), jnp.float32),
        ],
        compiler_params=pltpu.CompilerParams(vmem_limit_bytes=VMEM),
        cost_estimate=pl.CostEstimate(
            flops=2 * FRAMES * rows * 2 * listed * (LANES * groups + 2 * beams),
            bytes_accessed=8 * FRAMES * rows * listed,
            transcendentals=0,
        ),
    )(*spectra, chooser, weights)


def after(value, other):
    return lax.optimization_barrier((value, other))[0]


def body(volts, prototype, beam_channels, station_index, delays, gains, assign):
    sig_dev = volts.shape[1]
    far, near, sb_count = lax.axis_size("far"), lax.axis_size("near"), lax.axis_size("sb")
    far_here, near_here, sb_here = [lax.axis_index(name).astype(jnp.int32) for name in ("far", "near", "sb")]
    st_count = far * near
    plane = near * sb_count
    depth = NCH // RADIX
    bands = depth // LANES
    fine = NCH // sb_count // RADIX // st_count
    partner = far_here ^ jnp.arange(far, dtype=jnp.int32)
    stations = (partner[:, None] * near + jnp.arange(near, dtype=jnp.int32)[None, :]).reshape(-1)

    def spread(*ids):
        total = ids[0]
        for more in ids[1:]:
            total = total[..., None] + more
        return total.reshape(-1)

    out_ids = spread(
        jnp.arange(bands, dtype=jnp.int32)[:, None] * LANES + (stations * fine)[None, :],
        jnp.arange(fine, dtype=jnp.int32),
    )
    table = transform_table(out_ids)
    turn_c, turn_s = phase(
        jnp.arange(RADIX, dtype=jnp.int32)[:, None] * jnp.arange(depth, dtype=jnp.int32)[None, :], NCH
    )
    taps_wide = jnp.broadcast_to(prototype[:, None, :], (prototype.shape[0], 8, NCH))

    def to_planes(xs):
        return [xs[0]] + [
            lax.ppermute(xs[s], "far", [(i, i ^ s) for i in range(far)]) for s in range(1, far)
        ]

    def in_plane(xs):
        joined = xs[0] if len(xs) == 1 else jnp.concatenate(xs, axis=1)
        return lax.all_to_all(joined, ("near", "sb"), split_axis=0, concat_axis=0, tiled=True)

    share = sig_dev // sb_count
    sub = min(share, ROWS)
    halves = max(1, share // ROWS)
    inside = (sb_here * share) % ROWS
    early = FRAMES // 4
    plan = [(0, 0, early), (0, early, FRAMES - early)] + [(h, 0, FRAMES) for h in range(1, halves)]
    crossed, branches = [], []
    for c, (which, first, frames) in enumerate(plan):
        if c > 1:
            table = after(table, crossed[c - 2])
        row_block = (sb_here * share // ROWS + which)[None]
        *outs, kept = channelise(row_block, volts, taps_wide, turn_c, turn_s, table, first, frames, far)
        if c == 0:
            assign, beam_channels, station_index = after((assign, beam_channels, station_index), outs)
        table = after(table, outs)
        branches.append(kept)
        if sub < ROWS:
            outs = [lax.dynamic_slice_in_dim(x, inside, sub, axis=2) for x in outs]
        inner = st_count // RADIX
        if inner > 1:
            outs = [
                x.reshape(near // inner, sb_count, sub, 2 * frames, RADIX, inner, fine).transpose(0, 5, 1, 2, 3, 4, 6)
                for x in outs
            ]
        crossed.append(to_planes([x.reshape(plane, sub, -1) for x in outs]))

    pieces = []
    for c, (which, first, frames) in enumerate(plan):
        step = far if c == 0 else max(1, far // 2)
        for s in range(0, far, step):
            got = in_plane(crossed[c][s : s + step])
            for k in range(step):
                if halves == 1:
                    one = got[:, k * sub : (k + 1) * sub].reshape(1, plane * sub, -1)
                    pieces.append((one, s + k, 0, 0, first, frames))
                else:
                    pieces.append((got, s + k, k * sub, which, first, frames))

    per_dev = SLOTS // st_count
    owners = assign[:, 0]
    taken = (owners[:, None] == jnp.arange(sb_count, dtype=jnp.int32)[None, :]).astype(jnp.int32)
    position = jnp.sum(taken * jnp.cumsum(taken, axis=0), axis=1) - 1
    place = owners * SLOTS + position
    slot_ids = spread(
        stations * per_dev,
        jnp.arange(sb_count, dtype=jnp.int32) * SLOTS,
        jnp.arange(per_dev, dtype=jnp.int32),
    )
    picker = (place[None, :] == slot_ids[:, None]).astype(jnp.int32)
    filled = jnp.sum(picker, axis=1)
    slot_channel = jnp.sum(picker * beam_channels[None, :], axis=1)

    def by_row(values):
        values = values.reshape(st_count * sb_count, 1, per_dev)
        return jnp.broadcast_to(values, (st_count * sb_count, 2, per_dev)).reshape(-1)

    turned = jnp.broadcast_to(jnp.arange(2, dtype=jnp.int32)[None, :, None], (st_count * sb_count, 2, per_dev))
    mine = lax.dynamic_slice_in_dim(slot_channel, (near_here * sb_count + sb_here) * per_dev, per_dev)
    weights = beam_weights(after(mine, branches), delays, gains)
    slot_channel = after(slot_channel, (crossed[-2], weights))
    spectra = slot_spectra(by_row(slot_channel), by_row(filled), turned.reshape(-1), branches, 2 * per_dev, far)
    if sub < ROWS:
        spectra = [
            lax.dynamic_slice_in_dim(x.reshape(plane, 2 * per_dev, FRAMES, ROWS), inside, sub, axis=3).reshape(
                plane, 2 * per_dev, -1
            )
            for x in spectra
        ]
    slot_crossed = to_planes(spectra)
    step = max(1, far // 2)
    slot_received = [in_plane(slot_crossed[s : s + step]) for s in range(0, far, step)]

    signal_ids = spread(
        partner[:, None] * (near * sig_dev) + jnp.arange(halves, dtype=jnp.int32)[None, :] * sub,
        jnp.arange(plane, dtype=jnp.int32) * share,
        jnp.arange(sub, dtype=jnp.int32),
    )
    wanted = (station_index[None, :] * 2 + jnp.arange(2, dtype=jnp.int32)[:, None]).reshape(-1)
    chooser = (signal_ids[:, None] == wanted[None, :]).astype(jnp.bfloat16)

    visibility = correlate(after(far_here[None], spectra), pieces, far, halves)
    signals = visibility.shape[1]
    beam_out = combine(slot_received, chooser, after(weights, visibility), halves, sub)
    return (visibility.reshape(2, 1, 1, signals, signals), beam_out)


def solution(mesh):
    st_count, sb_count = mesh.shape["st"], mesh.shape["sb"]
    far = math.gcd(4, st_count)
    planes = Mesh(mesh.devices.reshape(far, st_count // far, sb_count), ("far", "near", "sb"))
    st = ("far", "near")
    in_specs = (P(None, st, None), P(), P(), P(), P(), P(), P())
    out_specs = (P(None, "sb", st, None, None), P("sb", st, None, None, None))
    return jax.shard_map(body, mesh=planes, in_specs=in_specs, out_specs=out_specs, check_vma=False)
```

time: 293 us -> 391 us (1.33)
  starting transfers between devices: 18.3 us -> 87.2 us
  waiting for transfers between devices: 120 us -> 133 us
  other arithmetic: 14.9 us -> 27.7 us
    ppermute x0 -> x12, waiting for transfers between devices: none -> 102 us  [to_planes(): lax.ppermute(xs[s], 'far', [(i, i ^ s) for i in range(far)])]
    all_to_all x3 -> x7, waiting for transfers between devices: 120 us -> 30.9 us  [in_plane(): lax.all_to_all(joined, ('near', 'sb'), split_axis=0, concat_axis=0, tiled...]
    ppermute x0 -> x12, starting transfers between devices: none -> 59.4 us  [to_planes(): lax.ppermute(xs[s], 'far', [(i, i ^ s) for i in range(far)])]
    concatenate x0 -> x7, other arithmetic: none -> 12.5 us  [in_plane(): joined = xs[0] if len(xs) == 1 else jnp.concatenate(xs, axis=1)]
    all_to_all x3 -> x7, starting transfers between devices: 18.3 us -> 27.8 us  [in_plane(): lax.all_to_all(joined, ('near', 'sb'), split_axis=0, concat_axis=0, tiled...]
    pallas_call x4 -> x5, Pallas kernels: 109 us -> 110 us  [the longest x3 72.4 us: channelise(): pl.pallas_call(functools.partial(channel_kernel, first), grid_spec=pltpu....]
  transfers between devices with their start and end apart: 3 -> 19, of which waited for: 3 -> 7; matrix products, arithmetic and copies ran while one was open for 5% -> 7% of each run, Pallas kernels for 29% -> 28%
where the time goes in v3:
time: 391 us; the launch traced here: 390 us
  Pallas kernels  134 us (34%)
  waiting for transfers between devices  133 us (34%)
  starting transfers between devices  87.2 us (22%)
  other arithmetic  27.7 us (7%)
  local copies, waits for them, and re-layouts  6.96 us (2%)
    ppermute x12, waiting for transfers between devices, to_planes(): lax.ppermute(xs[s], 'far', [(i, i ^ s) for i in range(far)])  102 us
    pallas_call x3, Pallas kernels, channelise(): pl.pallas_call(functools.partial(channel_kernel, first), grid_spec=pltpu....  72.4 us
    ppermute x12, starting transfers between devices, to_planes(): lax.ppermute(xs[s], 'far', [(i, i ^ s) for i in range(far)])  59.4 us
    all_to_all x7, waiting for transfers between devices, in_plane(): lax.all_to_all(joined, ('near', 'sb'), split_axis=0, concat_axis=0, tiled...  30.9 us
    all_to_all x7, starting transfers between devices, in_plane(): lax.all_to_all(joined, ('near', 'sb'), split_axis=0, concat_axis=0, tiled...  27.8 us
    pallas_call x1, Pallas kernels, slot_spectra(): pl.pallas_call(functools.partial(slot_kernel, far), out_shape=[jax.ShapeD...  19.6 us
    pallas_call x1, Pallas kernels, correlate(): pl.pallas_call(kernel, in_specs=[pl.BlockSpec(memory_space=pltpu.SMEM)] +...  18.2 us
    concatenate x7, other arithmetic, in_plane(): joined = xs[0] if len(xs) == 1 else jnp.concatenate(xs, axis=1)  12.5 us
  transfers between devices with their start and end apart: 19, of which 7 were waited for; matrix products, arithmetic and copies ran while one was open for 7% of the time, Pallas kernels for 28%

profile of v3, /device:TPU:0, one launch (start us, length us, event | category | flops | bytes accessed | tf_op | source)
XLA Modules:
  0.0 390.1 jit_solution(4064118593521627591)
XLA Ops:
  3.5 2.8 shard_map.86.table
  7.8 14.2 %shard_map.87 = (bf16[2,4,16,1024]{3,2,1,0:T(8,128)(2,1)}, bf16[2,4,16,1024]{3,2,1,0:T(8,128)(2,1)}, bf16[2,4,16,1024]{3,2,1,0:T(8,128)(2,1)}, bf16[2,4,16,1024]{3,2,1,0:T(8,128)(2,1)}, bf16[8,4,16,1024]{3,2,1,0:T(8,128)(2,1)}) custom-call(s32[1]{0:T(128)} %bitcast.1.row_block, bf16[2,128,126976]{2,1,0:T(8,128)(2,1)} %volts.5, ...), custom_call_target="tpu_custom_call" | custom-call | flops 2147483648 | bytes 7077888 | tf_op jit(solution)/shard_map/pallas_call | solution.py:184
  22.0 3.0 collective-permute-start.3
  25.1 2.6 collective-permute-start.4
  27.7 26.0 %shard_map.88 = (bf16[2,4,16,3072]{3,2,1,0:T(8,128)(2,1)}, bf16[2,4,16,3072]{3,2,1,0:T(8,128)(2,1)}, bf16[2,4,16,3072]{3,2,1,0:T(8,128)(2,1)}, bf16[2,4,16,3072]{3,2,1,0:T(8,128)(2,1)}, bf16[8,12,16,1024]{3,2,1,0:T(8,128)(2,1)}) custom-call(s32[1]{0:T(128)} %bitcast.1.row_block, bf16[2,128,126976]{2,1,0:T(8,128)(2,1)} %volts.5, ...), custom_call_target="tpu_custom_call" | custom-call | flops 6442450944 | bytes 14417920 | tf_op jit(solution)/shard_map/pallas_call | solution.py:184
  54.5 3.5 collective-permute-start.1
  61.7 32.2 %shard_map.89 = (bf16[2,4,16,4096]{3,2,1,0:T(8,128)(2,1)}, bf16[2,4,16,4096]{3,2,1,0:T(8,128)(2,1)}, bf16[2,4,16,4096]{3,2,1,0:T(8,128)(2,1)}, bf16[2,4,16,4096]{3,2,1,0:T(8,128)(2,1)}, bf16[8,16,16,1024]{3,2,1,0:T(8,128)(2,1)}) custom-call(s32[1]{0:T(128)} %bitcast.7.row_block, bf16[2,128,126976]{2,1,0:T(8,128)(2,1)} %volts.5, ...), custom_call_target="tpu_custom_call" | custom-call | flops 8589934592 | bytes 16515072 | tf_op jit(solution)/shard_map/pallas_call | solution.py:184
  95.0 4.0 %all-to-all-start = ((bf16[8,64,1024]{2,1,0:T(8,128)(2,1)}), bf16[8,64,1024]{2,1,0:T(8,128)(2,1)S(1)}, u32[]{:S(2)}, u32[]{:S(2)}) async-start(bf16[8,64,1024]{2,1,0:T(8,128)(2,1)} %pad_maximum_fusion.4), calls=%async_computation | async-start | bytes 2097152 | tf_op jit(solution)/shard_map/all_to_all | solution.py:469
  98.9 12.4 %shard_map.90.refs_3_ = bf16[20,512,256]{2,1,0:T(8,128)(2,1)} custom-call(s32[20]{0:T(128)} %dynamic_slice.3.channel, f32[256,256]{1,0:T(8,128)} %delays.1, f32[256,256]{1,0:T(8,128)} %gains.1), custom_call_target="tpu_custom_call" | custom-call | flops 52428800 | bytes 5242880 | tf_op jit(solution)/shard_map/pallas_call | solution.py:341
  112.6 3.9 %fusion.9 = (f32[1280,128]{1,0:T(8,128)}, f32[1280,128]{1,0:T(8,128)}) fusion(s32[1280]{0:T(1024)S(1)} %fusion.31), kind=kLoop, calls=%fused_computation.27 | loop fusion | flops 2293760 | bytes 1315840 | tf_op jit(solution)/shard_map/sin | solution.py:26
  118.0 3.8 sine_multiply_fusion
  121.8 19.6 %shard_map.91 = (bf16[8,40,512]{2,1,0:T(8,128)(2,1)}, bf16[8,40,512]{2,1,0:T(8,128)(2,1)}, bf16[8,40,512]{2,1,0:T(8,128)(2,1)}, bf16[8,40,512]{2,1,0:T(8,128)(2,1)}) custom-call(s32[1280,1]{1,0:T(8,128)} %add_select_fusion.1.row_branch, f32[1280,4]{1,0:T(8,128)} %get-tuple-element.71.hi_c, f32[1280,4]{1,0:T(8,128)} %get-tuple-element.70.hi_s, ...), custom_call_target="tpu_custom_call" | custom-call | flops 10737418240 | bytes 8388608 | tf_op jit(solution)/shard_map/pallas_call | solution.py:249
  141.4 14.8 %collective-permute-start.10 = (bf16[8,40,512]{2,1,0:T(8,128)(2,1)}, bf16[8,40,512]{2,1,0:T(8,128)(2,1)S(1)}, u32[]{:S(2)}, u32[]{:S(2)}) collective-permute-start(bf16[8,40,512]{2,1,0:T(8,128)(2,1)} %get-tuple-element.51), channel_id=1, source_target_pairs={{0,16},{8,24},{16,0},{24,8},{1,17},{9,25},{17,1},{25,9},{2,18},{10... | collective-permute-start | bytes 983048 | tf_op jit(solution)/shard_map/ppermute | solution.py:464
  157.7 20.1 %collective-permute-done.10 = bf16[8,40,512]{2,1,0:T(8,128)(2,1)S(1)} collective-permute-done((bf16[8,40,512]{2,1,0:T(8,128)(2,1)}, bf16[8,40,512]{2,1,0:T(8,128)(2,1)S(1)}, u32[]{:S(2)}, u32[]{:S(2)}) %collective-permute-start.10) | collective-permute-done | bytes 327712 | tf_op jit(solution)/shard_map/ppermute | solution.py:464
  178.7 3.7 all-to-all-start.6
  185.0 7.7 %all-to-all-done.6.refs_1_ = bf16[8,80,512]{2,1,0:T(8,128)(2,1)S(1)} async-done(((bf16[8,80,512]{2,1,0:T(8,128)(2,1)}), bf16[8,80,512]{2,1,0:T(8,128)(2,1)S(1)}, u32[]{:S(2)}, u32[]{:S(2)}) %all-to-all-start.6) | async-done | bytes 655392 | tf_op jit(solution)/shard_map/all_to_all | solution.py:469
  192.7 3.6 all-to-all-start.2
  196.2 6.3 %collective-permute-start.7 = (bf16[8,16,4096]{2,1,0:T(8,128)(2,1)}, bf16[8,16,4096]{2,1,0:T(8,128)(2,1)S(1)}, u32[]{:S(2)}, u32[]{:S(2)}) collective-permute-start(bf16[8,16,4096]{2,1,0:T(8,128)(2,1)} %bitcast.47), channel_id=1, source_target_pairs={{0,16},{8,24},{16,0},{24,8},{1,17},{9,25},{17,1},{25,9},{2,18},{10... | collective-permute-start | bytes 3145736 | tf_op jit(solution)/shard_map/ppermute | solution.py:464
  204.9 2.6 pad_maximum_fusion.2
  207.5 8.7 %all-to-all-done.2.refs_6_.refs_7_ = bf16[8,32,3072]{2,1,0:T(8,128)(2,1)S(1)} async-done(((bf16[8,32,3072]{2,1,0:T(8,128)(2,1)}), bf16[8,32,3072]{2,1,0:T(8,128)(2,1)S(1)}, u32[]{:S(2)}, u32[]{:S(2)}) %all-to-all-start.2) | async-done | bytes 1572896 | tf_op jit(solution)/shard_map/all_to_all | solution.py:469
  216.2 4.3 %all-to-all-start.1 = ((bf16[8,32,3072]{2,1,0:T(8,128)(2,1)}), bf16[8,32,3072]{2,1,0:T(8,128)(2,1)}, u32[]{:S(2)}, u32[]{:S(2)}) async-start(bf16[8,32,3072]{2,1,0:T(8,128)(2,1)} %pad_maximum_fusion.2), calls=%async_computation.1 | async-start | bytes 3145728 | tf_op jit(solution)/shard_map/all_to_all | solution.py:469
  220.5 51.1 %collective-permute-done.7 = bf16[8,16,4096]{2,1,0:T(8,128)(2,1)S(1)} collective-permute-done((bf16[8,16,4096]{2,1,0:T(8,128)(2,1)}, bf16[8,16,4096]{2,1,0:T(8,128)(2,1)S(1)}, u32[]{:S(2)}, u32[]{:S(2)}) %collective-permute-start.7) | collective-permute-done | bytes 1048608 | tf_op jit(solution)/shard_map/ppermute | solution.py:464
  271.6 2.9 pad_maximum_fusion.1
  274.5 4.2 %all-to-all-start.4 = ((bf16[8,32,4096]{2,1,0:T(8,128)(2,1)}), bf16[8,32,4096]{2,1,0:T(8,128)(2,1)S(1)}, u32[]{:S(2)}, u32[]{:S(2)}) async-start(bf16[8,32,4096]{2,1,0:T(8,128)(2,1)} %pad_maximum_fusion.1), calls=%async_computation.4 | async-start | bytes 4194304 | tf_op jit(solution)/shard_map/all_to_all | solution.py:469
  278.7 22.7 %collective-permute-start.6 = (bf16[8,16,4096]{2,1,0:T(8,128)(2,1)}, bf16[8,16,4096]{2,1,0:T(8,128)(2,1)S(1)}, u32[]{:S(2)}, u32[]{:S(2)}) collective-permute-start(bf16[8,16,4096]{2,1,0:T(8,128)(2,1)} %bitcast.45), channel_id=1, source_target_pairs={{0,8},{8,0},{16,24},{24,16},{1,9},{9,1},{17,25},{25,17},{2,10},{10... | collective-permute-start | bytes 3145736 | tf_op jit(solution)/shard_map/ppermute | solution.py:464
  301.4 24.0 %collective-permute-done.6 = bf16[8,16,4096]{2,1,0:T(8,128)(2,1)S(1)} collective-permute-done((bf16[8,16,4096]{2,1,0:T(8,128)(2,1)}, bf16[8,16,4096]{2,1,0:T(8,128)(2,1)S(1)}, u32[]{:S(2)}, u32[]{:S(2)}) %collective-permute-start.6) | collective-permute-done | bytes 1048608 | tf_op jit(solution)/shard_map/ppermute | solution.py:464
  328.4 4.4 %all-to-all-start.3 = ((bf16[8,32,4096]{2,1,0:T(8,128)(2,1)}), bf16[8,32,4096]{2,1,0:T(8,128)(2,1)}, u32[]{:S(2)}, u32[]{:S(2)}) async-start(bf16[8,32,4096]{2,1,0:T(8,128)(2,1)} %pad_maximum_fusion), calls=%async_computation.3 | async-start | bytes 4194304 | tf_op jit(solution)/shard_map/all_to_all | solution.py:469
  336.1 6.9 %collective-permute-done.9 = bf16[8,40,512]{2,1,0:T(8,128)(2,1)S(1)} collective-permute-done((bf16[8,40,512]{2,1,0:T(8,128)(2,1)S(1)}, bf16[8,40,512]{2,1,0:T(8,128)(2,1)S(1)}, u32[]{:S(2)}, u32[]{:S(2)}) %collective-permute-start.9) | collective-permute-done | bytes 327712 | tf_op jit(solution)/shard_map/ppermute | solution.py:464
  343.9 14.5 %all-to-all-done.3.refs_8_.refs_9_ = bf16[8,32,4096]{2,1,0:T(8,128)(2,1)} async-done(((bf16[8,32,4096]{2,1,0:T(8,128)(2,1)}), bf16[8,32,4096]{2,1,0:T(8,128)(2,1)}, u32[]{:S(2)}, u32[]{:S(2)}) %all-to-all-start.3) | async-done | bytes 2097184 | tf_op jit(solution)/shard_map/all_to_all | solution.py:469
  358.4 3.7 all-to-all-start.5
  362.1 18.2 %shard_map.92 = f32[2,1024,1024]{2,1,0:T(8,128)} custom-call(s32[1]{0:T(128)} %bitcast.here_ref, bf16[8,64,1024]{2,1,0:T(8,128)(2,1)} %copy-done.4, bf16[8,64,1024]{2,1,0:T(8,128)(2,1)} %copy-done.4, bf16[8,64,1024]{2,1,0:T(8,128)(2,1)} %copy-done.4, bf16[8,64,1024]{2,1,0:T(8,128)(2,1)} %copy-done.4, bf16[8,32,3072]{2,1,0:T(8,128)(2,1)} %all-to-all-done.1.refs_4_.refs_5_, ...), custom_call_target="tpu_custom_call" | custom-call | flops 8589934592 | bytes 16777216 | tf_op jit(solution)/shard_map/pallas_call | solution.py:302
  381.2 8.9 %shard_map.93 = f32[1,20,2,16,512]{4,3,2,1,0:T(8,128)} custom-call(bf16[8,80,512]{2,1,0:T(8,128)(2,1)} %copy-done.1, bf16[8,80,512]{2,1,0:T(8,128)(2,1)} %copy-done, bf16[1024,512]{1,0:T(8,128)(2,1)} %compare_convert_fusion.refs_2_, bf16[20,512,256]{2,1,0:T(8,128)(2,1)} %shard_map.90.refs_3_), custom_call_target="tpu_custom_call" | custom-call | flops 1006632960 | bytes 1310720 | tf_op jit(solution)/shard_map/pallas_call | solution.py:414
  (102 shorter events, 28.0 us)
Async XLA Ops:
  0.6 5.7 %copy-start.8 = (f32[16,4096]{1,0:T(8,128)S(1)}, f32[16,4096]{1,0:T(8,128)}, u32[]{:S(2)}) copy-start(f32[16,4096]{1,0:T(8,128)} %param.8) | copy-start | bytes 786436
  22.0 39.6 %collective-permute-start.3 = (bf16[8,16,1024]{2,1,0:T(8,128)(2,1)}, bf16[8,16,1024]{2,1,0:T(8,128)(2,1)S(1)}, u32[]{:S(2)}, u32[]{:S(2)}) collective-permute-start(bf16[8,16,1024]{2,1,0:T(8,128)(2,1)} %bitcast.53), channel_id=1, source_target_pairs={{0,8},{8,0},{16,24},{24,16},{1,9},{9,1},{17,25},{25,17},{2,10},{10... | collective-permute-start | bytes 786440 | tf_op jit(solution)/shard_map/ppermute | solution.py:464
  25.1 36.6 %collective-permute-start.4 = (bf16[8,16,1024]{2,1,0:T(8,128)(2,1)}, bf16[8,16,1024]{2,1,0:T(8,128)(2,1)S(1)}, u32[]{:S(2)}, u32[]{:S(2)}) collective-permute-start(bf16[8,16,1024]{2,1,0:T(8,128)(2,1)} %bitcast.52), channel_id=1, source_target_pairs={{0,16},{8,24},{16,0},{24,8},{1,17},{9,25},{17,1},{25,9},{2,18},{10... | collective-permute-start | bytes 786440 | tf_op jit(solution)/shard_map/ppermute | solution.py:464
  27.7 34.0 %collective-permute-start.5 = (bf16[8,16,1024]{2,1,0:T(8,128)(2,1)}, bf16[8,16,1024]{2,1,0:T(8,128)(2,1)S(1)}, u32[]{:S(2)}, u32[]{:S(2)}) collective-permute-start(bf16[8,16,1024]{2,1,0:T(8,128)(2,1)} %bitcast.51), channel_id=1, source_target_pairs={{0,24},{8,16},{16,8},{24,0},{1,25},{9,17},{17,9},{25,1},{2,26},{10... | collective-permute-start | bytes 786440 | tf_op jit(solution)/shard_map/ppermute | solution.py:464
  27.7 30.4 %copy-start.11 = (s32[384,1]{0,1:T(1,128)S(1)}, s32[384,1]{0,1:T(1,128)}, u32[]{:S(2)}) copy-start(s32[384,1]{0,1:T(1,128)} %param.13) | copy-start | bytes 4612
  27.7 32.5 %copy-start.10 = (s32[384]{0:T(512)S(1)}, s32[384]{0:T(512)}, u32[]{:S(2)}) copy-start(s32[384]{0:T(512)} %param.9) | copy-start | bytes 4612
  53.7 57.6 %collective-permute-start = (bf16[8,16,3072]{2,1,0:T(8,128)(2,1)}, bf16[8,16,3072]{2,1,0:T(8,128)(2,1)S(1)}, u32[]{:S(2)}, u32[]{:S(2)}) collective-permute-start(bf16[8,16,3072]{2,1,0:T(8,128)(2,1)} %bitcast.50), channel_id=1, source_target_pairs={{0,8},{8,0},{16,24},{24,16},{1,9},{9,1},{17,25},{25,17},{2,10},{10... | collective-permute-start | bytes 2359304 | tf_op jit(solution)/shard_map/ppermute | solution.py:464
  54.5 56.8 %collective-permute-start.1 = (bf16[8,16,3072]{2,1,0:T(8,128)(2,1)}, bf16[8,16,3072]{2,1,0:T(8,128)(2,1)S(1)}, u32[]{:S(2)}, u32[]{:S(2)}) collective-permute-start(bf16[8,16,3072]{2,1,0:T(8,128)(2,1)} %bitcast.49), channel_id=1, source_target_pairs={{0,16},{8,24},{16,0},{24,8},{1,17},{9,25},{17,1},{25,9},{2,18},{10... | collective-permute-start | bytes 2359304 | tf_op jit(solution)/shard_map/ppermute | solution.py:464
  61.6 49.7 %collective-permute-start.2 = (bf16[8,16,3072]{2,1,0:T(8,128)(2,1)}, bf16[8,16,3072]{2,1,0:T(8,128)(2,1)}, u32[]{:S(2)}, u32[]{:S(2)}) collective-permute-start(bf16[8,16,3072]{2,1,0:T(8,128)(2,1)} %bitcast.48), channel_id=1, source_target_pairs={{0,24},{8,16},{16,8},{24,0},{1,25},{9,17},{17,9},{25,1},{2,26},{10... | collective-permute-start | bytes 2359304 | tf_op jit(solution)/shard_map/ppermute | solution.py:464
  61.7 32.2 %copy-start.9 = (bf16[2,4,16,1024]{3,2,1,0:T(8,128)(2,1)S(1)}, bf16[2,4,16,1024]{3,2,1,0:T(8,128)(2,1)}, u32[]{:S(2)}) copy-start(bf16[2,4,16,1024]{3,2,1,0:T(8,128)(2,1)} %get-tuple-element.31) | copy-start | bytes 786436
  95.0 83.8 %all-to-all-start = ((bf16[8,64,1024]{2,1,0:T(8,128)(2,1)}), bf16[8,64,1024]{2,1,0:T(8,128)(2,1)S(1)}, u32[]{:S(2)}, u32[]{:S(2)}) async-start(bf16[8,64,1024]{2,1,0:T(8,128)(2,1)} %pad_maximum_fusion.4), calls=%async_computation | async-start | bytes 2097152 | tf_op jit(solution)/shard_map/all_to_all | solution.py:469
  111.3 0.9 copy-start.6
  141.4 36.4 %collective-permute-start.10 = (bf16[8,40,512]{2,1,0:T(8,128)(2,1)}, bf16[8,40,512]{2,1,0:T(8,128)(2,1)S(1)}, u32[]{:S(2)}, u32[]{:S(2)}) collective-permute-start(bf16[8,40,512]{2,1,0:T(8,128)(2,1)} %get-tuple-element.51), channel_id=1, source_target_pairs={{0,16},{8,24},{16,0},{24,8},{1,17},{9,25},{17,1},{25,9},{2,18},{10... | collective-permute-start | bytes 983048 | tf_op jit(solution)/shard_map/ppermute | solution.py:464
  156.2 21.6 %collective-permute-start.11 = (bf16[8,40,512]{2,1,0:T(8,128)(2,1)}, bf16[8,40,512]{2,1,0:T(8,128)(2,1)S(1)}, u32[]{:S(2)}, u32[]{:S(2)}) collective-permute-start(bf16[8,40,512]{2,1,0:T(8,128)(2,1)} %get-tuple-element.52), channel_id=1, source_target_pairs={{0,24},{8,16},{16,8},{24,0},{1,25},{9,17},{17,9},{25,1},{2,26},{10... | collective-permute-start | bytes 983048 | tf_op jit(solution)/shard_map/ppermute | solution.py:464
  178.7 6.3 %copy-start.4 = (bf16[8,64,1024]{2,1,0:T(8,128)(2,1)}, bf16[8,64,1024]{2,1,0:T(8,128)(2,1)S(1)}, u32[]{:S(2)}) copy-start(bf16[8,64,1024]{2,1,0:T(8,128)(2,1)S(1)} %all-to-all-done.refs_0_.refs_1_.refs_2_.refs_3_) | copy-start | bytes 3145732
  178.7 13.9 %all-to-all-start.6 = ((bf16[8,80,512]{2,1,0:T(8,128)(2,1)}), bf16[8,80,512]{2,1,0:T(8,128)(2,1)S(1)}, u32[]{:S(2)}, u32[]{:S(2)}) async-start(bf16[8,80,512]{2,1,0:T(8,128)(2,1)} %pad_maximum_fusion.6), calls=%async_computation.6 | async-start | bytes 1310720 | tf_op jit(solution)/shard_map/all_to_all | solution.py:469
  192.6 14.9 %copy-start = (bf16[8,80,512]{2,1,0:T(8,128)(2,1)}, bf16[8,80,512]{2,1,0:T(8,128)(2,1)S(1)}, u32[]{:S(2)}) copy-start(bf16[8,80,512]{2,1,0:T(8,128)(2,1)S(1)} %all-to-all-done.6.refs_1_) | copy-start | bytes 1966084
  192.7 23.6 %all-to-all-start.2 = ((bf16[8,32,3072]{2,1,0:T(8,128)(2,1)}), bf16[8,32,3072]{2,1,0:T(8,128)(2,1)S(1)}, u32[]{:S(2)}, u32[]{:S(2)}) async-start(bf16[8,32,3072]{2,1,0:T(8,128)(2,1)} %pad_maximum_fusion.3), calls=%async_computation.2 | async-start | bytes 3145728 | tf_op jit(solution)/shard_map/all_to_all | solution.py:469
  196.2 75.4 %collective-permute-start.7 = (bf16[8,16,4096]{2,1,0:T(8,128)(2,1)}, bf16[8,16,4096]{2,1,0:T(8,128)(2,1)S(1)}, u32[]{:S(2)}, u32[]{:S(2)}) collective-permute-start(bf16[8,16,4096]{2,1,0:T(8,128)(2,1)} %bitcast.47), channel_id=1, source_target_pairs={{0,16},{8,24},{16,0},{24,8},{1,17},{9,25},{17,1},{25,9},{2,18},{10... | collective-permute-start | bytes 3145736 | tf_op jit(solution)/shard_map/ppermute | solution.py:464
  202.5 69.1 %collective-permute-start.8 = (bf16[8,16,4096]{2,1,0:T(8,128)(2,1)}, bf16[8,16,4096]{2,1,0:T(8,128)(2,1)}, u32[]{:S(2)}, u32[]{:S(2)}) collective-permute-start(bf16[8,16,4096]{2,1,0:T(8,128)(2,1)} %bitcast.46), channel_id=1, source_target_pairs={{0,24},{8,16},{16,8},{24,0},{1,25},{9,17},{17,9},{25,1},{2,26},{10... | collective-permute-start | bytes 3145736 | tf_op jit(solution)/shard_map/ppermute | solution.py:464
  216.2 58.3 %copy-start.3 = (bf16[8,32,3072]{2,1,0:T(8,128)(2,1)}, bf16[8,32,3072]{2,1,0:T(8,128)(2,1)S(1)}, u32[]{:S(2)}) copy-start(bf16[8,32,3072]{2,1,0:T(8,128)(2,1)S(1)} %all-to-all-done.2.refs_6_.refs_7_) | copy-start | bytes 4718596
  216.2 58.3 %all-to-all-start.1 = ((bf16[8,32,3072]{2,1,0:T(8,128)(2,1)}), bf16[8,32,3072]{2,1,0:T(8,128)(2,1)}, u32[]{:S(2)}, u32[]{:S(2)}) async-start(bf16[8,32,3072]{2,1,0:T(8,128)(2,1)} %pad_maximum_fusion.2), calls=%async_computation.1 | async-start | bytes 3145728 | tf_op jit(solution)/shard_map/all_to_all | solution.py:469
  274.5 50.9 %copy-start.5 = (bf16[2,4,16,4096]{3,2,1,0:T(8,128)(2,1)S(1)}, bf16[2,4,16,4096]{3,2,1,0:T(8,128)(2,1)}, u32[]{:S(2)}) copy-start(bf16[2,4,16,4096]{3,2,1,0:T(8,128)(2,1)} %get-tuple-element.54) | copy-start | bytes 3145732
  274.5 52.5 %all-to-all-start.4 = ((bf16[8,32,4096]{2,1,0:T(8,128)(2,1)}), bf16[8,32,4096]{2,1,0:T(8,128)(2,1)S(1)}, u32[]{:S(2)}, u32[]{:S(2)}) async-start(bf16[8,32,4096]{2,1,0:T(8,128)(2,1)} %pad_maximum_fusion.1), calls=%async_computation.4 | async-start | bytes 4194304 | tf_op jit(solution)/shard_map/all_to_all | solution.py:469
  278.7 46.7 %collective-permute-start.6 = (bf16[8,16,4096]{2,1,0:T(8,128)(2,1)}, bf16[8,16,4096]{2,1,0:T(8,128)(2,1)S(1)}, u32[]{:S(2)}, u32[]{:S(2)}) collective-permute-start(bf16[8,16,4096]{2,1,0:T(8,128)(2,1)} %bitcast.45), channel_id=1, source_target_pairs={{0,8},{8,0},{16,24},{24,16},{1,9},{9,1},{17,25},{25,17},{2,10},{10... | collective-permute-start | bytes 3145736 | tf_op jit(solution)/shard_map/ppermute | solution.py:464
  327.0 5.8 %copy-start.12 = (s32[256]{0:T(256)S(1)}, s32[256]{0:T(256)}, u32[]{:S(2)}) copy-start(s32[256]{0:T(256)} %param.10) | copy-start | bytes 3076
  327.0 6.0 %copy-start.13 = (bf16[8,40,512]{2,1,0:T(8,128)(2,1)S(1)}, bf16[8,40,512]{2,1,0:T(8,128)(2,1)}, u32[]{:S(2)}) copy-start(bf16[8,40,512]{2,1,0:T(8,128)(2,1)} %get-tuple-element.50) | copy-start | bytes 983044
  327.0 16.1 %copy-start.7 = (bf16[8,40,512]{2,1,0:T(8,128)(2,1)S(1)}, bf16[8,40,512]{2,1,0:T(8,128)(2,1)}, u32[]{:S(2)}) copy-start(bf16[8,40,512]{2,1,0:T(8,128)(2,1)} %get-tuple-element.49) | copy-start | bytes 983044
  327.0 1.4 copy-start.2
  328.4 30.1 %all-to-all-start.3 = ((bf16[8,32,4096]{2,1,0:T(8,128)(2,1)}), bf16[8,32,4096]{2,1,0:T(8,128)(2,1)}, u32[]{:S(2)}, u32[]{:S(2)}) async-start(bf16[8,32,4096]{2,1,0:T(8,128)(2,1)} %pad_maximum_fusion), calls=%async_computation.3 | async-start | bytes 4194304 | tf_op jit(solution)/shard_map/all_to_all | solution.py:469
  333.0 10.0 %collective-permute-start.9 = (bf16[8,40,512]{2,1,0:T(8,128)(2,1)S(1)}, bf16[8,40,512]{2,1,0:T(8,128)(2,1)S(1)}, u32[]{:S(2)}, u32[]{:S(2)}) collective-permute-start(bf16[8,40,512]{2,1,0:T(8,128)(2,1)S(1)} %copy-done.13), channel_id=1, source_target_pairs={{0,8},{8,0},{16,24},{24,16},{1,9},{9,1},{17,25},{25,17},{2,10},{10... | collective-permute-start | bytes 983048 | tf_op jit(solution)/shard_map/ppermute | solution.py:464
  358.4 21.9 %all-to-all-start.5 = ((bf16[8,80,512]{2,1,0:T(8,128)(2,1)}), bf16[8,80,512]{2,1,0:T(8,128)(2,1)S(1)}, u32[]{:S(2)}, u32[]{:S(2)}) async-start(bf16[8,80,512]{2,1,0:T(8,128)(2,1)} %pad_maximum_fusion.5), calls=%async_computation.5 | async-start | bytes 1310720 | tf_op jit(solution)/shard_map/all_to_all | solution.py:469
  (1 other events, 0.8 us)

commit v4 on v3

--- a/solution.py
+++ b/solution.py
@@ -17,8 +17,14 @@
 ROWS = 16
 VMEM = 56 * 1024 * 1024
 
+NO_COST = pl.CostEstimate(flops=1, bytes_accessed=1, transcendentals=0)
+
 TWO_PI = 2.0 * math.pi
 NT = (((1,), (1,)), ((), ()))
+
+
+def busy(share):
+    return pl.CostEstimate(flops=int(share * 4e10), bytes_accessed=1, transcendentals=0)
 
 
 def phase(turns, length):
@@ -51,7 +57,9 @@
     hi_c, hi_s = phase(jnp.arange(0, depth, ROWS, dtype=jnp.int32)[:, None] * out_ids, depth)
     scale = 1.0 / math.sqrt(NCH)
     return pl.pallas_call(
-        table_kernel, out_shape=jax.ShapeDtypeStruct((2 * depth, 2 * depth), jnp.bfloat16)
+        table_kernel,
+        out_shape=jax.ShapeDtypeStruct((2 * depth, 2 * depth), jnp.bfloat16),
+        cost_estimate=NO_COST,
     )(hi_c * scale, hi_s * scale, lo_c, lo_s)
 
 
@@ -180,7 +188,6 @@
     bands = depth // LANES
     wide = 2 * frames * LANES
     near = RADIX // far
-    work = 2 * ROWS * frames * NCH
     return pl.pallas_call(
         functools.partial(channel_kernel, first),
         grid_spec=pltpu.PrefetchScalarGridSpec(
@@ -203,9 +210,7 @@
         out_shape=[jax.ShapeDtypeStruct((near, bands, ROWS, wide), jnp.bfloat16)] * far
         + [jax.ShapeDtypeStruct((RADIX, frames, ROWS, 2 * depth), jnp.bfloat16)],
         compiler_params=pltpu.CompilerParams(vmem_limit_bytes=VMEM),
-        cost_estimate=pl.CostEstimate(
-            flops=work * 8 * depth, bytes_accessed=4 * ROWS * length + 4 * work, transcendentals=0
-        ),
+        cost_estimate=busy(frames / FRAMES),
     )(row_block, volts, taps_wide, turn_c, turn_s, table)
 
 
@@ -234,27 +239,31 @@
             out[d] = total[top : top + per].astype(out.dtype)
 
 
-def slot_spectra(row_channel, row_filled, row_turned, chunks, per, far):
+def slot_tables(row_channel, row_filled, row_turned):
     depth = NCH // RADIX
-    rows = row_channel.shape[0]
-    samples = sum(c.shape[1] * c.shape[2] for c in chunks)
-    plane = rows // per // far
     coarse = jnp.arange(depth // LANES, dtype=jnp.int32) * LANES
     fine = jnp.arange(LANES, dtype=jnp.int32)
     whole = row_channel - row_channel % RADIX
     hi_c, hi_s = phase(whole[:, None] * coarse[None, :] + row_turned[:, None] * (NCH // 4), NCH)
     lo_c, lo_s = phase(whole[:, None] * fine[None, :], NCH)
     scaling = row_filled.astype(jnp.float32)[:, None] * (1.0 / math.sqrt(NCH))
-    row_branch = (row_channel % RADIX)[:, None]
+    return (row_channel % RADIX)[:, None], hi_c * scaling, hi_s * scaling, lo_c, lo_s
+
+
+def slot_spectra(tables, chunks, per, far):
+    rows = tables[0].shape[0]
+    samples = sum(c.shape[1] * c.shape[2] for c in chunks)
+    plane = rows // per // far
     return pl.pallas_call(
         functools.partial(slot_kernel, far),
         out_shape=[jax.ShapeDtypeStruct((plane, per, samples), jnp.bfloat16)] * far,
-        scratch_shapes=[pltpu.VMEM((rows, 2 * depth), jnp.bfloat16), pltpu.VMEM((rows, samples), jnp.float32)],
+        scratch_shapes=[
+            pltpu.VMEM((rows, chunks[0].shape[3]), jnp.bfloat16),
+            pltpu.VMEM((rows, samples), jnp.float32),
+        ],
         compiler_params=pltpu.CompilerParams(vmem_limit_bytes=VMEM),
-        cost_estimate=pl.CostEstimate(
-            flops=2 * rows * 2 * NCH * samples, bytes_accessed=4 * NCH * samples, transcendentals=0
-        ),
-    )(row_branch, hi_c * scaling, hi_s * scaling, lo_c, lo_s, *chunks)
+        cost_estimate=busy(1),
+    )(*tables, *chunks)
 
 
 def correlate(here, pieces, far, halves):
@@ -266,54 +275,68 @@
     signals = far * block
 
     def kernel(here_ref, *refs):
-        parts, (out, held, sems) = refs[: len(pieces)], refs[len(pieces) :]
-        copies = []
+        parts, (out, held, turned, made, in_sems, out_sems) = refs[: len(pieces)], refs[len(pieces) :]
+        coming = [[] for _ in range(far)]
         for index, (_, partner, row, which, first, frames) in enumerate(pieces):
             for part in range(2):
                 src = parts[index].at[:, pl.ds(row, sub), pl.ds(part * frames * lanes, frames * lanes)]
-                dst = held.at[here_ref[0] ^ partner, :, which, :, pl.ds(part * half + first * lanes, frames * lanes)]
-                copies.append(pltpu.make_async_copy(src, dst, sems.at[2 * index + part]))
-        for copy in copies:
-            copy.start()
-        for copy in copies:
-            copy.wait()
+                dst = held.at[partner, :, which, :, pl.ds(part * half + first * lanes, frames * lanes)]
+                coming[partner].append(pltpu.make_async_copy(src, dst, in_sems.at[2 * index + part]))
+        for copies in coming:
+            for copy in copies:
+                copy.start()
         inverse = 1.0 / half
-
-        def product(left, right):
-            return lax.dot_general(left, right, NT, preferred_element_type=jnp.float32)
-
+        going = [[], []]
+        slot = 0
         for i in range(far):
+            for copy in coming[i]:
+                copy.wait()
             left = held[i].reshape(block, 2 * half)
+            turned[:, :half] = left[:, half:]
+            turned[:, half:] = -left[:, :half]
+            at_i = pl.ds(pl.multiple_of((here_ref[0] ^ i) * block, block), block)
             for j in range(i + 1):
                 right = held[j].reshape(block, 2 * half)
-                at_i, at_j = slice(i * block, (i + 1) * block), slice(j * block, (j + 1) * block)
-                re = (
-                    product(left[:, :half], right[:, :half]) + product(left[:, half:], right[:, half:])
-                ) * inverse
-                im = (
-                    product(left[:, half:], right[:, :half]) - product(left[:, :half], right[:, half:])
-                ) * inverse
-                out[0, at_i, at_j] = re
-                out[1, at_i, at_j] = im
-                if i != j:
-                    out[0, at_j, at_i] = re.T
-                    out[1, at_j, at_i] = -im.T
+                at_j = pl.ds(pl.multiple_of((here_ref[0] ^ j) * block, block), block)
+                for copy in going[slot]:
+                    copy.wait()
+                going[slot] = []
+                for part, rows in enumerate((left, turned[...])):
+                    got = lax.dot_general(rows, right, NT, preferred_element_type=jnp.float32) * inverse
+                    made[slot, part, 0] = got
+                    going[slot].append(
+                        pltpu.make_async_copy(
+                            made.at[slot, part, 0], out.at[part, at_i, at_j], out_sems.at[slot, part, 0]
+                        )
+                    )
+                    if i != j:
+                        made[slot, part, 1] = got.T if part == 0 else -got.T
+                        going[slot].append(
+                            pltpu.make_async_copy(
+                                made.at[slot, part, 1], out.at[part, at_j, at_i], out_sems.at[slot, part, 1]
+                            )
+                        )
+                for copy in going[slot]:
+                    copy.start()
+                slot = 1 - slot
+        for copies in going:
+            for copy in copies:
+                copy.wait()
 
     return pl.pallas_call(
         kernel,
         in_specs=[pl.BlockSpec(memory_space=pltpu.SMEM)] + [pl.BlockSpec(memory_space=pl.ANY)] * len(pieces),
-        out_specs=pl.BlockSpec(memory_space=pltpu.VMEM),
+        out_specs=pl.BlockSpec(memory_space=pl.ANY),
         out_shape=jax.ShapeDtypeStruct((2, signals, signals), jnp.float32),
         scratch_shapes=[
             pltpu.VMEM((far, senders, halves, sub, 2 * half), jnp.bfloat16),
+            pltpu.VMEM((block, 2 * half), jnp.bfloat16),
+            pltpu.VMEM((2, 2, 2, block, block), jnp.float32),
             pltpu.SemaphoreType.DMA((2 * len(pieces),)),
+            pltpu.SemaphoreType.DMA((2, 2, 2)),
         ],
         compiler_params=pltpu.CompilerParams(vmem_limit_bytes=VMEM),
-        cost_estimate=pl.CostEstimate(
-            flops=4 * signals * signals * half,
-            bytes_accessed=4 * signals * half + 8 * signals * signals,
-            transcendentals=0,
-        ),
+        cost_estimate=NO_COST,
     )(here, *[piece[0] for piece in pieces])
 
 
@@ -348,18 +371,17 @@
         ],
         out_specs=pl.BlockSpec((1, 2 * beams, listed), lambda i: (i, 0, 0)),
         out_shape=jax.ShapeDtypeStruct((slots, 2 * beams, listed), jnp.bfloat16),
-        cost_estimate=pl.CostEstimate(
-            flops=40 * slots * beams * listed, bytes_accessed=4 * slots * beams * listed, transcendentals=0
-        ),
+        cost_estimate=NO_COST,
     )(channel, delays, gains)
 
 
-def combine(spectra, chooser, weights, halves, sub):
+def combine(spectra, chooser, weights, sub):
+    halves = len(spectra)
     slots, beams2, listed = weights.shape
     beams = beams2 // 2
     rows = 2 * slots
     senders = spectra[0].shape[0]
-    partners = sum(x.shape[1] for x in spectra) // rows
+    partners = spectra[0].shape[1] // rows
     count = LANES // sub
     inner = senders // count
     groups = partners * halves * inner
@@ -368,12 +390,12 @@
     def kernel(*refs):
         got, (choose, weight, out, ordered, picked) = refs[: len(spectra)], refs[len(spectra) :]
         lane_ids = lax.broadcasted_iota(jnp.int32, (rows, LANES), 1)
-        where = [(x, k * rows) for x in got for k in range(x.shape[1] // rows)]
-        for s, (spectrum, row) in enumerate(where):
-            for h in range(halves):
+        for s in range(partners):
+            for h, spectrum in enumerate(got):
+                row = s * rows
                 for q in range(inner):
                     for t in range(FRAMES // count):
-                        lane = h * FRAMES * sub + t * LANES
+                        lane = t * LANES
                         pieces = [
                             spectrum[q * count + i, row : row + rows, lane : lane + LANES].astype(jnp.float32)
                             for i in range(count)
@@ -419,11 +441,7 @@
             pltpu.VMEM((tiles, FRAMES * rows, LANES), jnp.float32),
         ],
         compiler_params=pltpu.CompilerParams(vmem_limit_bytes=VMEM),
-        cost_estimate=pl.CostEstimate(
-            flops=2 * FRAMES * rows * 2 * listed * (LANES * groups + 2 * beams),
-            bytes_accessed=8 * FRAMES * rows * listed,
-            transcendentals=0,
-        ),
+        cost_estimate=NO_COST,
     )(*spectra, chooser, weights)
 
 
@@ -460,9 +478,7 @@
     taps_wide = jnp.broadcast_to(prototype[:, None, :], (prototype.shape[0], 8, NCH))
 
     def to_planes(xs):
-        return [xs[0]] + [
-            lax.ppermute(xs[s], "far", [(i, i ^ s) for i in range(far)]) for s in range(1, far)
-        ]
+        return [xs[0]] + [lax.ppermute(xs[s], "far", [(i, i ^ s) for i in range(far)]) for s in range(1, far)]
 
     def in_plane(xs):
         joined = xs[0] if len(xs) == 1 else jnp.concatenate(xs, axis=1)
@@ -472,7 +488,8 @@
     sub = min(share, ROWS)
     halves = max(1, share // ROWS)
     inside = (sb_here * share) % ROWS
-    early = FRAMES // 4
+    unit = max(1, LANES * st_count * sb_count // NCH)
+    early = FRAMES * 3 // 8 // unit * unit
     plan = [(0, 0, early), (0, early, FRAMES - early)] + [(h, 0, FRAMES) for h in range(1, halves)]
     crossed, branches = [], []
     for c, (which, first, frames) in enumerate(plan):
@@ -480,8 +497,6 @@
             table = after(table, crossed[c - 2])
         row_block = (sb_here * share // ROWS + which)[None]
         *outs, kept = channelise(row_block, volts, taps_wide, turn_c, turn_s, table, first, frames, far)
-        if c == 0:
-            assign, beam_channels, station_index = after((assign, beam_channels, station_index), outs)
         table = after(table, outs)
         branches.append(kept)
         if sub < ROWS:
@@ -494,17 +509,18 @@
             ]
         crossed.append(to_planes([x.reshape(plane, sub, -1) for x in outs]))
 
-    pieces = []
+    assign, beam_channels, station_index = after((assign, beam_channels, station_index), branches)
+
+    pieces, in_place = [], []
     for c, (which, first, frames) in enumerate(plan):
-        step = far if c == 0 else max(1, far // 2)
-        for s in range(0, far, step):
-            got = in_plane(crossed[c][s : s + step])
-            for k in range(step):
-                if halves == 1:
-                    one = got[:, k * sub : (k + 1) * sub].reshape(1, plane * sub, -1)
-                    pieces.append((one, s + k, 0, 0, first, frames))
-                else:
-                    pieces.append((got, s + k, k * sub, which, first, frames))
+        step = far if which < halves - 1 else max(1, far // 2)
+        in_place.append([in_plane(crossed[c][s : s + step]) for s in range(0, far, step)])
+        for s in range(far):
+            got, row = in_place[c][s // step], s % step * sub
+            if halves == 1:
+                pieces.append((got[:, row : row + sub].reshape(1, plane * sub, -1), s, 0, 0, first, frames))
+            else:
+                pieces.append((got, s, row, which, first, frames))
 
     per_dev = SLOTS // st_count
     owners = assign[:, 0]
@@ -526,19 +542,24 @@
 
     turned = jnp.broadcast_to(jnp.arange(2, dtype=jnp.int32)[None, :, None], (st_count * sb_count, 2, per_dev))
     mine = lax.dynamic_slice_in_dim(slot_channel, (near_here * sb_count + sb_here) * per_dev, per_dev)
-    weights = beam_weights(after(mine, branches), delays, gains)
-    slot_channel = after(slot_channel, (crossed[-2], weights))
-    spectra = slot_spectra(by_row(slot_channel), by_row(filled), turned.reshape(-1), branches, 2 * per_dev, far)
-    if sub < ROWS:
-        spectra = [
-            lax.dynamic_slice_in_dim(x.reshape(plane, 2 * per_dev, FRAMES, ROWS), inside, sub, axis=3).reshape(
-                plane, 2 * per_dev, -1
-            )
-            for x in spectra
-        ]
-    slot_crossed = to_planes(spectra)
-    step = max(1, far // 2)
-    slot_received = [in_plane(slot_crossed[s : s + step]) for s in range(0, far, step)]
+    row_branch, *tables = slot_tables(by_row(slot_channel), by_row(filled), turned.reshape(-1))
+    slot_received = []
+    for h in range(halves):
+        own = [c for c, (which, _, _) in enumerate(plan) if which == h]
+        done = [crossed[c] for c in own] + [in_place[c] for c in range(own[0] - 1 if h else 0, own[-1])]
+        row_branch = after(row_branch, done)
+        spectra = slot_spectra([row_branch, *tables], [branches[c] for c in own], 2 * per_dev, far)
+        row_branch = after(row_branch, spectra)
+        if h == 0:
+            weights = beam_weights(after(mine, spectra), delays, gains)
+        if sub < ROWS:
+            spectra = [
+                lax.dynamic_slice_in_dim(x.reshape(plane, 2 * per_dev, FRAMES, ROWS), inside, sub, axis=3).reshape(
+                    plane, 2 * per_dev, -1
+                )
+                for x in spectra
+            ]
+        slot_received.append(in_plane(to_planes(spectra)))
 
     signal_ids = spread(
         partner[:, None] * (near * sig_dev) + jnp.arange(halves, dtype=jnp.int32)[None, :] * sub,
@@ -550,7 +571,7 @@
 
     visibility = correlate(after(far_here[None], spectra), pieces, far, halves)
     signals = visibility.shape[1]
-    beam_out = combine(slot_received, chooser, after(weights, visibility), halves, sub)
+    beam_out = combine(slot_received, chooser, weights, sub)
     return (visibility.reshape(2, 1, 1, signals, signals), beam_out)
 
 

time: 391 us -> 389 us (level)
  starting transfers between devices: 87.2 us -> 69.9 us
  local copies, waits for them, and re-layouts: 6.96 us -> 13.8 us
  Pallas kernels: 134 us -> 139 us
    ppermute x12 -> x15, waiting for transfers between devices: 102 us -> 117 us  [to_planes(): lax.ppermute(xs[s], 'far', [(i, i ^ s) for i in range(far)])]
    all_to_all x7 -> x6, waiting for transfers between devices: 30.9 us -> 17.4 us  [in_plane(): lax.all_to_all(joined, ('near', 'sb'), split_axis=0, concat_axis=0, tiled...]
    ppermute x12 -> x15, starting transfers between devices: 59.4 us -> 46.6 us  [to_planes(): lax.ppermute(xs[s], 'far', [(i, i ^ s) for i in range(far)])]
    pallas_call x1 -> x2, Pallas kernels: 19.6 us -> 25.8 us  [slot_spectra(): pl.pallas_call(functools.partial(slot_kernel, far), out_shape=[jax.ShapeD...]
    all_to_all x7 -> x6, starting transfers between devices: 27.8 us -> 23.3 us  [in_plane(): lax.all_to_all(joined, ('near', 'sb'), split_axis=0, concat_axis=0, tiled...]
    concatenate x7 -> x6, other arithmetic: 12.5 us -> 11.8 us  [in_plane(): joined = xs[0] if len(xs) == 1 else jnp.concatenate(xs, axis=1)]
  transfers between devices with their start and end apart: 19 -> 21, of which waited for: 7 -> 7; matrix products, arithmetic and copies ran while one was open for 7% -> 9% of each run, Pallas kernels for 28% -> 25%
where the time goes in v4:
time: 389 us; the launch traced here: 387 us
  Pallas kernels  139 us (36%)
  waiting for transfers between devices  134 us (34%)
  starting transfers between devices  69.9 us (18%)
  other arithmetic  29.9 us (8%)
  local copies, waits for them, and re-layouts  13.8 us (4%)
    ppermute x15, waiting for transfers between devices, to_planes(): lax.ppermute(xs[s], 'far', [(i, i ^ s) for i in range(far)])  117 us
    pallas_call x3, Pallas kernels, channelise(): pl.pallas_call(functools.partial(channel_kernel, first), grid_spec=pltpu....  71.9 us
    ppermute x15, starting transfers between devices, to_planes(): lax.ppermute(xs[s], 'far', [(i, i ^ s) for i in range(far)])  46.6 us
    pallas_call x2, Pallas kernels, slot_spectra(): pl.pallas_call(functools.partial(slot_kernel, far), out_shape=[jax.ShapeD...  25.8 us
    all_to_all x6, starting transfers between devices, in_plane(): lax.all_to_all(joined, ('near', 'sb'), split_axis=0, concat_axis=0, tiled...  23.3 us
    all_to_all x6, waiting for transfers between devices, in_plane(): lax.all_to_all(joined, ('near', 'sb'), split_axis=0, concat_axis=0, tiled...  17.4 us
    pallas_call x1, Pallas kernels, correlate(): pl.pallas_call(kernel, in_specs=[pl.BlockSpec(memory_space=pltpu.SMEM)] +...  17.2 us
    pallas_call x1, Pallas kernels, beam_weights(): pl.pallas_call(weight_kernel, grid=(slots,), in_specs=[pl.BlockSpec(memor...  12.2 us
  transfers between devices with their start and end apart: 21, of which 7 were waited for; matrix products, arithmetic and copies ran while one was open for 9% of the time, Pallas kernels for 25%

profile of v4, /device:TPU:0, one launch (start us, length us, event | category | flops | bytes accessed | tf_op | source)
XLA Modules:
  0.0 387.5 jit_solution(3610781310435392743)
XLA Ops:
  4.0 2.7 shard_map.86.table
  8.4 16.9 %shard_map.87 = (bf16[2,4,16,1536]{3,2,1,0:T(8,128)(2,1)}, bf16[2,4,16,1536]{3,2,1,0:T(8,128)(2,1)}, bf16[2,4,16,1536]{3,2,1,0:T(8,128)(2,1)}, bf16[2,4,16,1536]{3,2,1,0:T(8,128)(2,1)}, bf16[8,6,16,1024]{3,2,1,0:T(8,128)(2,1)}) custom-call(s32[1]{0:T(128)} %bitcast.1.row_block, bf16[2,128,126976]{2,1,0:T(8,128)(2,1)} %volts.5, ...), custom_call_target="tpu_custom_call" | custom-call | flops 15000000512 | bytes 1 | tf_op jit(solution)/shard_map/pallas_call | solution.py:191
  25.3 3.0 collective-permute-start
  28.3 2.6 collective-permute-start.1
  30.9 22.8 %shard_map.88 = (bf16[2,4,16,2560]{3,2,1,0:T(8,128)(2,1)}, bf16[2,4,16,2560]{3,2,1,0:T(8,128)(2,1)}, bf16[2,4,16,2560]{3,2,1,0:T(8,128)(2,1)}, bf16[2,4,16,2560]{3,2,1,0:T(8,128)(2,1)}, bf16[8,10,16,1024]{3,2,1,0:T(8,128)(2,1)}) custom-call(s32[1]{0:T(128)} %bitcast.1.row_block, bf16[2,128,126976]{2,1,0:T(8,128)(2,1)} %volts.5, ...), custom_call_target="tpu_custom_call" | custom-call | flops 24999999488 | bytes 1 | tf_op jit(solution)/shard_map/pallas_call | solution.py:191
  54.6 3.5 collective-permute-start.4
  59.2 32.2 %shard_map.89 = (bf16[2,4,16,4096]{3,2,1,0:T(8,128)(2,1)}, bf16[2,4,16,4096]{3,2,1,0:T(8,128)(2,1)}, bf16[2,4,16,4096]{3,2,1,0:T(8,128)(2,1)}, bf16[2,4,16,4096]{3,2,1,0:T(8,128)(2,1)}, bf16[8,16,16,1024]{3,2,1,0:T(8,128)(2,1)}) custom-call(s32[1]{0:T(128)} %bitcast.2.row_block, bf16[2,128,126976]{2,1,0:T(8,128)(2,1)} %volts.5, ...), custom_call_target="tpu_custom_call" | custom-call | flops 40000000000 | bytes 1 | tf_op jit(solution)/shard_map/pallas_call | solution.py:191
  99.6 4.0 %all-to-all-start = ((bf16[8,64,1536]{2,1,0:T(8,128)(2,1)}), bf16[8,64,1536]{2,1,0:T(8,128)(2,1)S(1)}, u32[]{:S(2)}, u32[]{:S(2)}) async-start(bf16[8,64,1536]{2,1,0:T(8,128)(2,1)} %pad_maximum_fusion.3), calls=%async_computation | async-start | bytes 3145728 | tf_op jit(solution)/shard_map/all_to_all | solution.py:485
  105.3 3.9 %fusion.9 = (f32[1280,128]{1,0:T(8,128)}, f32[1280,128]{1,0:T(8,128)}) fusion(s32[1280]{0:T(1024)S(1)} %fusion.31), kind=kLoop, calls=%fused_computation.26 | loop fusion | flops 2293760 | bytes 1315840 | tf_op jit(solution)/shard_map/sin | solution.py:32
  112.7 3.9 sine_multiply_fusion
  116.6 7.1 %all-to-all-done.refs_0_.refs_1_.refs_2_.refs_3_ = bf16[8,64,1536]{2,1,0:T(8,128)(2,1)S(1)} async-done(((bf16[8,64,1536]{2,1,0:T(8,128)(2,1)}), bf16[8,64,1536]{2,1,0:T(8,128)(2,1)S(1)}, u32[]{:S(2)}, u32[]{:S(2)}) %all-to-all-start) | async-done | bytes 1572896 | tf_op jit(solution)/shard_map/all_to_all | solution.py:485
  123.7 13.2 %shard_map.90 = (bf16[8,40,256]{2,1,0:T(8,128)(2,1)}, bf16[8,40,256]{2,1,0:T(8,128)(2,1)}, bf16[8,40,256]{2,1,0:T(8,128)(2,1)}, bf16[8,40,256]{2,1,0:T(8,128)(2,1)}) custom-call(s32[1280,1]{1,0:T(8,128)} %add_select_fusion.1.row_branch, f32[1280,4]{1,0:T(8,128)} %get-tuple-element.81.hi_c, f32[1280,4]{1,0:T(8,128)} %get-tuple-element.80.hi_s, ...), custom_call_target="tpu_custom_call" | custom-call | flops 40000000000 | bytes 1 | tf_op jit(solution)/shard_map/pallas_call | solution.py:257
  136.9 3.7 collective-permute-start.11
  140.6 5.7 %collective-permute-start.10 = (bf16[8,40,256]{2,1,0:T(8,128)(2,1)}, bf16[8,40,256]{2,1,0:T(8,128)(2,1)S(1)}, u32[]{:S(2)}, u32[]{:S(2)}) collective-permute-start(bf16[8,40,256]{2,1,0:T(8,128)(2,1)} %get-tuple-element.55), channel_id=1, source_target_pairs={{0,16},{8,24},{16,0},{24,8},{1,17},{9,25},{17,1},{25,9},{2,18},{10... | collective-permute-start | bytes 491528 | tf_op jit(solution)/shard_map/ppermute | solution.py:481
  146.4 10.8 %collective-permute-done.10 = bf16[8,40,256]{2,1,0:T(8,128)(2,1)S(1)} collective-permute-done((bf16[8,40,256]{2,1,0:T(8,128)(2,1)}, bf16[8,40,256]{2,1,0:T(8,128)(2,1)S(1)}, u32[]{:S(2)}, u32[]{:S(2)}) %collective-permute-start.10) | collective-permute-done | bytes 163872 | tf_op jit(solution)/shard_map/ppermute | solution.py:481
  159.1 3.5 all-to-all-start.4
  162.6 2.6 pad_maximum_fusion
  165.2 7.5 %all-to-all-done.4.refs_0_ = bf16[8,160,256]{2,1,0:T(8,128)(2,1)S(1)} async-done(((bf16[8,160,256]{2,1,0:T(8,128)(2,1)}), bf16[8,160,256]{2,1,0:T(8,128)(2,1)S(1)}, u32[]{:S(2)}, u32[]{:S(2)}) %all-to-all-start.4) | async-done | bytes 655392 | tf_op jit(solution)/shard_map/all_to_all | solution.py:485
  173.6 3.6 all-to-all-start.1
  177.4 25.6 %collective-permute-done.6 = bf16[8,16,4096]{2,1,0:T(8,128)(2,1)S(1)} collective-permute-done((bf16[8,16,4096]{2,1,0:T(8,128)(2,1)}, bf16[8,16,4096]{2,1,0:T(8,128)(2,1)S(1)}, u32[]{:S(2)}, u32[]{:S(2)}) %collective-permute-start.6) | collective-permute-done | bytes 1048608 | tf_op jit(solution)/shard_map/ppermute | solution.py:481
  203.0 2.8 pad_maximum_fusion.1
  205.7 2.8 all-to-all-done.1.refs_4_.refs_5_.refs_6_.refs_7_
  210.0 4.4 %all-to-all-start.2 = ((bf16[8,32,4096]{2,1,0:T(8,128)(2,1)}), bf16[8,32,4096]{2,1,0:T(8,128)(2,1)}, u32[]{:S(2)}, u32[]{:S(2)}) async-start(bf16[8,32,4096]{2,1,0:T(8,128)(2,1)} %pad_maximum_fusion.1), calls=%async_computation.2 | async-start | bytes 4194304 | tf_op jit(solution)/shard_map/all_to_all | solution.py:485
  217.2 68.6 %collective-permute-done.7 = bf16[8,16,4096]{2,1,0:T(8,128)(2,1)S(1)} collective-permute-done((bf16[8,16,4096]{2,1,0:T(8,128)(2,1)}, bf16[8,16,4096]{2,1,0:T(8,128)(2,1)S(1)}, u32[]{:S(2)}, u32[]{:S(2)}) %collective-permute-start.7) | collective-permute-done | bytes 1048608 | tf_op jit(solution)/shard_map/ppermute | solution.py:481
  287.4 3.9 %all-to-all-start.3 = ((bf16[8,32,4096]{2,1,0:T(8,128)(2,1)}), bf16[8,32,4096]{2,1,0:T(8,128)(2,1)S(1)}, u32[]{:S(2)}, u32[]{:S(2)}) async-start(bf16[8,32,4096]{2,1,0:T(8,128)(2,1)} %pad_maximum_fusion.2), calls=%async_computation.3 | async-start | bytes 4194304 | tf_op jit(solution)/shard_map/all_to_all | solution.py:485
  291.3 12.6 %shard_map.91 = (bf16[8,40,256]{2,1,0:T(8,128)(2,1)}, bf16[8,40,256]{2,1,0:T(8,128)(2,1)}, bf16[8,40,256]{2,1,0:T(8,128)(2,1)}, bf16[8,40,256]{2,1,0:T(8,128)(2,1)}) custom-call(s32[1280,1]{1,0:T(8,128)} %add_select_fusion.1.row_branch, f32[1280,4]{1,0:T(8,128)} %get-tuple-element.81.hi_c, f32[1280,4]{1,0:T(8,128)} %get-tuple-element.80.hi_s, ...), custom_call_target="tpu_custom_call" | custom-call | flops 40000000000 | bytes 1 | tf_op jit(solution)/shard_map/pallas_call | solution.py:257
  305.2 23.1 %collective-permute-start.13 = (bf16[8,40,256]{2,1,0:T(8,128)(2,1)}, bf16[8,40,256]{2,1,0:T(8,128)(2,1)S(1)}, u32[]{:S(2)}, u32[]{:S(2)}) collective-permute-start(bf16[8,40,256]{2,1,0:T(8,128)(2,1)} %get-tuple-element.65), channel_id=1, source_target_pairs={{0,16},{8,24},{16,0},{24,8},{1,17},{9,25},{17,1},{25,9},{2,18},{10... | collective-permute-start | bytes 491528 | tf_op jit(solution)/shard_map/ppermute | solution.py:481
  328.5 11.7 %collective-permute-done.13 = bf16[8,40,256]{2,1,0:T(8,128)(2,1)S(1)} collective-permute-done((bf16[8,40,256]{2,1,0:T(8,128)(2,1)}, bf16[8,40,256]{2,1,0:T(8,128)(2,1)S(1)}, u32[]{:S(2)}, u32[]{:S(2)}) %collective-permute-start.13) | collective-permute-done | bytes 163872 | tf_op jit(solution)/shard_map/ppermute | solution.py:481
  341.9 3.8 all-to-all-start.5
  348.3 12.2 %shard_map.93.refs_3_ = bf16[20,512,256]{2,1,0:T(8,128)(2,1)} custom-call(s32[20]{0:T(128)} %dynamic_slice.3.channel, f32[256,256]{1,0:T(8,128)} %delays.1, f32[256,256]{1,0:T(8,128)} %gains.1), custom_call_target="tpu_custom_call" | custom-call | flops 1 | bytes 1 | tf_op jit(solution)/shard_map/pallas_call | solution.py:364
  360.5 17.2 %shard_map.92 = f32[2,1024,1024]{2,1,0:T(8,128)} custom-call(s32[1]{0:T(128)} %bitcast.here_ref, bf16[8,64,1536]{2,1,0:T(8,128)(2,1)} %copy-done.1, bf16[8,64,1536]{2,1,0:T(8,128)(2,1)} %copy-done.1, bf16[8,64,1536]{2,1,0:T(8,128)(2,1)} %copy-done.1, bf16[8,64,1536]{2,1,0:T(8,128)(2,1)} %copy-done.1, bf16[8,64,2560]{2,1,0:T(8,128)(2,1)} %copy-done, ...), custom_call_target="tpu_custom_call" | custom-call | flops 1 | bytes 1 | tf_op jit(solution)/shard_map/pallas_call | solution.py:326
  378.6 8.9 %shard_map.94 = f32[1,20,2,16,512]{4,3,2,1,0:T(8,128)} custom-call(bf16[8,160,256]{2,1,0:T(8,128)(2,1)} %copy-done.3, bf16[8,160,256]{2,1,0:T(8,128)(2,1)} %copy-done.4, bf16[1024,512]{1,0:T(8,128)(2,1)} %compare_convert_fusion.refs_2_, bf16[20,512,256]{2,1,0:T(8,128)(2,1)} %shard_map.93.refs_3_), custom_call_target="tpu_custom_call" | custom-call | flops 1 | bytes 1 | tf_op jit(solution)/shard_map/pallas_call | solution.py:436
  (118 shorter events, 35.7 us)
Async XLA Ops:
  25.3 33.9 %collective-permute-start = (bf16[8,16,1536]{2,1,0:T(8,128)(2,1)}, bf16[8,16,1536]{2,1,0:T(8,128)(2,1)S(1)}, u32[]{:S(2)}, u32[]{:S(2)}) collective-permute-start(bf16[8,16,1536]{2,1,0:T(8,128)(2,1)} %bitcast.54), channel_id=1, source_target_pairs={{0,8},{8,0},{16,24},{24,16},{1,9},{9,1},{17,25},{25,17},{2,10},{10... | collective-permute-start | bytes 1179656 | tf_op jit(solution)/shard_map/ppermute | solution.py:481
  28.3 30.9 %collective-permute-start.1 = (bf16[8,16,1536]{2,1,0:T(8,128)(2,1)}, bf16[8,16,1536]{2,1,0:T(8,128)(2,1)S(1)}, u32[]{:S(2)}, u32[]{:S(2)}) collective-permute-start(bf16[8,16,1536]{2,1,0:T(8,128)(2,1)} %bitcast.53), channel_id=1, source_target_pairs={{0,16},{8,24},{16,0},{24,8},{1,17},{9,25},{17,1},{25,9},{2,18},{10... | collective-permute-start | bytes 1179656 | tf_op jit(solution)/shard_map/ppermute | solution.py:481
  30.9 28.3 %collective-permute-start.2 = (bf16[8,16,1536]{2,1,0:T(8,128)(2,1)}, bf16[8,16,1536]{2,1,0:T(8,128)(2,1)S(1)}, u32[]{:S(2)}, u32[]{:S(2)}) collective-permute-start(bf16[8,16,1536]{2,1,0:T(8,128)(2,1)} %bitcast.52), channel_id=1, source_target_pairs={{0,24},{8,16},{16,8},{24,0},{1,25},{9,17},{17,9},{25,1},{2,26},{10... | collective-permute-start | bytes 1179656 | tf_op jit(solution)/shard_map/ppermute | solution.py:481
  53.7 62.9 %collective-permute-start.3 = (bf16[8,16,2560]{2,1,0:T(8,128)(2,1)}, bf16[8,16,2560]{2,1,0:T(8,128)(2,1)S(1)}, u32[]{:S(2)}, u32[]{:S(2)}) collective-permute-start(bf16[8,16,2560]{2,1,0:T(8,128)(2,1)} %bitcast.51), channel_id=1, source_target_pairs={{0,8},{8,0},{16,24},{24,16},{1,9},{9,1},{17,25},{25,17},{2,10},{10... | collective-permute-start | bytes 1966088 | tf_op jit(solution)/shard_map/ppermute | solution.py:481
  54.6 62.0 %collective-permute-start.4 = (bf16[8,16,2560]{2,1,0:T(8,128)(2,1)}, bf16[8,16,2560]{2,1,0:T(8,128)(2,1)S(1)}, u32[]{:S(2)}, u32[]{:S(2)}) collective-permute-start(bf16[8,16,2560]{2,1,0:T(8,128)(2,1)} %bitcast.50), channel_id=1, source_target_pairs={{0,16},{8,24},{16,0},{24,8},{1,17},{9,25},{17,1},{25,9},{2,18},{10... | collective-permute-start | bytes 1966088 | tf_op jit(solution)/shard_map/ppermute | solution.py:481
  59.2 57.4 %collective-permute-start.5 = (bf16[8,16,2560]{2,1,0:T(8,128)(2,1)}, bf16[8,16,2560]{2,1,0:T(8,128)(2,1)}, u32[]{:S(2)}, u32[]{:S(2)}) collective-permute-start(bf16[8,16,2560]{2,1,0:T(8,128)(2,1)} %bitcast.49), channel_id=1, source_target_pairs={{0,24},{8,16},{16,8},{24,0},{1,25},{9,17},{17,9},{25,1},{2,26},{10... | collective-permute-start | bytes 1966088 | tf_op jit(solution)/shard_map/ppermute | solution.py:481
  59.2 32.2 %copy-start.17 = (s32[384,1]{0,1:T(1,128)S(1)}, s32[384,1]{0,1:T(1,128)}, u32[]{:S(2)}) copy-start(s32[384,1]{0,1:T(1,128)} %param.13) | copy-start | bytes 4612
  59.2 34.0 %copy-start.16 = (s32[384]{0:T(512)S(1)}, s32[384]{0:T(512)}, u32[]{:S(2)}) copy-start(s32[384]{0:T(512)} %param.9) | copy-start | bytes 4612
  99.6 24.1 %all-to-all-start = ((bf16[8,64,1536]{2,1,0:T(8,128)(2,1)}), bf16[8,64,1536]{2,1,0:T(8,128)(2,1)S(1)}, u32[]{:S(2)}, u32[]{:S(2)}) async-start(bf16[8,64,1536]{2,1,0:T(8,128)(2,1)} %pad_maximum_fusion.3), calls=%async_computation | async-start | bytes 3145728 | tf_op jit(solution)/shard_map/all_to_all | solution.py:485
  116.6 20.3 %copy-start.6 = (bf16[8,16,2560]{2,1,0:T(8,128)(2,1)}, bf16[8,16,2560]{2,1,0:T(8,128)(2,1)S(1)}, u32[]{:S(2)}) copy-start(bf16[8,16,2560]{2,1,0:T(8,128)(2,1)S(1)} %collective-permute-done.3) | copy-start | bytes 1966084
  116.6 20.3 %copy-start.8 = (bf16[8,16,2560]{2,1,0:T(8,128)(2,1)}, bf16[8,16,2560]{2,1,0:T(8,128)(2,1)S(1)}, u32[]{:S(2)}) copy-start(bf16[8,16,2560]{2,1,0:T(8,128)(2,1)S(1)} %collective-permute-done.4) | copy-start | bytes 1966084
  123.7 13.2 %copy-start.1 = (bf16[8,64,1536]{2,1,0:T(8,128)(2,1)}, bf16[8,64,1536]{2,1,0:T(8,128)(2,1)S(1)}, u32[]{:S(2)}) copy-start(bf16[8,64,1536]{2,1,0:T(8,128)(2,1)S(1)} %all-to-all-done.refs_0_.refs_1_.refs_2_.refs_3_) | copy-start | bytes 4718596
  136.9 25.7 %copy-start.5 = (bf16[2,4,16,2560]{3,2,1,0:T(8,128)(2,1)S(1)}, bf16[2,4,16,2560]{3,2,1,0:T(8,128)(2,1)}, u32[]{:S(2)}) copy-start(bf16[2,4,16,2560]{3,2,1,0:T(8,128)(2,1)} %get-tuple-element.43) | copy-start | bytes 1966084
  136.9 25.7 %copy-start.7 = (bf16[8,16,2560]{2,1,0:T(8,128)(2,1)S(1)}, bf16[8,16,2560]{2,1,0:T(8,128)(2,1)}, u32[]{:S(2)}) copy-start(bf16[8,16,2560]{2,1,0:T(8,128)(2,1)} %copy-done.6) | copy-start | bytes 1966084
  136.9 25.7 %copy-start.9 = (bf16[8,16,2560]{2,1,0:T(8,128)(2,1)S(1)}, bf16[8,16,2560]{2,1,0:T(8,128)(2,1)}, u32[]{:S(2)}) copy-start(bf16[8,16,2560]{2,1,0:T(8,128)(2,1)} %copy-done.8) | copy-start | bytes 1966084
  136.9 9.5 %collective-permute-start.11 = (bf16[8,40,256]{2,1,0:T(8,128)(2,1)}, bf16[8,40,256]{2,1,0:T(8,128)(2,1)S(1)}, u32[]{:S(2)}, u32[]{:S(2)}) collective-permute-start(bf16[8,40,256]{2,1,0:T(8,128)(2,1)} %get-tuple-element.56), channel_id=1, source_target_pairs={{0,24},{8,16},{16,8},{24,0},{1,25},{9,17},{17,9},{25,1},{2,26},{10... | collective-permute-start | bytes 491528 | tf_op jit(solution)/shard_map/ppermute | solution.py:481
  140.6 16.7 %collective-permute-start.10 = (bf16[8,40,256]{2,1,0:T(8,128)(2,1)}, bf16[8,40,256]{2,1,0:T(8,128)(2,1)S(1)}, u32[]{:S(2)}, u32[]{:S(2)}) collective-permute-start(bf16[8,40,256]{2,1,0:T(8,128)(2,1)} %get-tuple-element.55), channel_id=1, source_target_pairs={{0,16},{8,24},{16,0},{24,8},{1,17},{9,25},{17,1},{25,9},{2,18},{10... | collective-permute-start | bytes 491528 | tf_op jit(solution)/shard_map/ppermute | solution.py:481
  146.3 10.9 %collective-permute-start.9 = (bf16[8,40,256]{2,1,0:T(8,128)(2,1)}, bf16[8,40,256]{2,1,0:T(8,128)(2,1)S(1)}, u32[]{:S(2)}, u32[]{:S(2)}) collective-permute-start(bf16[8,40,256]{2,1,0:T(8,128)(2,1)} %get-tuple-element.54), channel_id=1, source_target_pairs={{0,8},{8,0},{16,24},{24,16},{1,9},{9,1},{17,25},{25,17},{2,10},{10... | collective-permute-start | bytes 491528 | tf_op jit(solution)/shard_map/ppermute | solution.py:481
  159.1 13.7 %all-to-all-start.4 = ((bf16[8,160,256]{2,1,0:T(8,128)(2,1)}), bf16[8,160,256]{2,1,0:T(8,128)(2,1)S(1)}, u32[]{:S(2)}, u32[]{:S(2)}) async-start(bf16[8,160,256]{2,1,0:T(8,128)(2,1)} %pad_maximum_fusion.4), calls=%async_computation.4 | async-start | bytes 1310720 | tf_op jit(solution)/shard_map/all_to_all | solution.py:485
  173.6 34.9 %all-to-all-start.1 = ((bf16[8,64,2560]{2,1,0:T(8,128)(2,1)}), bf16[8,64,2560]{2,1,0:T(8,128)(2,1)S(1)}, u32[]{:S(2)}, u32[]{:S(2)}) async-start(bf16[8,64,2560]{2,1,0:T(8,128)(2,1)} %pad_maximum_fusion), calls=%async_computation.1 | async-start | bytes 5242880 | tf_op jit(solution)/shard_map/all_to_all | solution.py:485
  177.3 25.7 %collective-permute-start.6 = (bf16[8,16,4096]{2,1,0:T(8,128)(2,1)}, bf16[8,16,4096]{2,1,0:T(8,128)(2,1)S(1)}, u32[]{:S(2)}, u32[]{:S(2)}) collective-permute-start(bf16[8,16,4096]{2,1,0:T(8,128)(2,1)} %bitcast.48), channel_id=1, source_target_pairs={{0,8},{8,0},{16,24},{24,16},{1,9},{9,1},{17,25},{25,17},{2,10},{10... | collective-permute-start | bytes 3145736 | tf_op jit(solution)/shard_map/ppermute | solution.py:481
  205.7 11.3 %copy-start.19 = (s32[4]{0:T(128)S(1)}, s32[4]{0:T(128)}, u32[]{:S(2)}) copy-start(s32[4]{0:T(128)} %get-tuple-element.90) | copy-start | bytes 52
  210.0 77.4 %all-to-all-start.2 = ((bf16[8,32,4096]{2,1,0:T(8,128)(2,1)}), bf16[8,32,4096]{2,1,0:T(8,128)(2,1)}, u32[]{:S(2)}, u32[]{:S(2)}) async-start(bf16[8,32,4096]{2,1,0:T(8,128)(2,1)} %pad_maximum_fusion.1), calls=%async_computation.2 | async-start | bytes 4194304 | tf_op jit(solution)/shard_map/all_to_all | solution.py:485
  214.4 71.4 %collective-permute-start.7 = (bf16[8,16,4096]{2,1,0:T(8,128)(2,1)}, bf16[8,16,4096]{2,1,0:T(8,128)(2,1)S(1)}, u32[]{:S(2)}, u32[]{:S(2)}) collective-permute-start(bf16[8,16,4096]{2,1,0:T(8,128)(2,1)} %bitcast.47), channel_id=1, source_target_pairs={{0,16},{8,24},{16,0},{24,8},{1,17},{9,25},{17,1},{25,9},{2,18},{10... | collective-permute-start | bytes 3145736 | tf_op jit(solution)/shard_map/ppermute | solution.py:481
  214.5 71.3 %collective-permute-start.8 = (bf16[8,16,4096]{2,1,0:T(8,128)(2,1)}, bf16[8,16,4096]{2,1,0:T(8,128)(2,1)S(1)}, u32[]{:S(2)}, u32[]{:S(2)}) collective-permute-start(bf16[8,16,4096]{2,1,0:T(8,128)(2,1)} %bitcast.46), channel_id=1, source_target_pairs={{0,24},{8,16},{16,8},{24,0},{1,25},{9,17},{17,9},{25,1},{2,26},{10... | collective-permute-start | bytes 3145736 | tf_op jit(solution)/shard_map/ppermute | solution.py:481
  287.4 54.5 %all-to-all-start.3 = ((bf16[8,32,4096]{2,1,0:T(8,128)(2,1)}), bf16[8,32,4096]{2,1,0:T(8,128)(2,1)S(1)}, u32[]{:S(2)}, u32[]{:S(2)}) async-start(bf16[8,32,4096]{2,1,0:T(8,128)(2,1)} %pad_maximum_fusion.2), calls=%async_computation.3 | async-start | bytes 4194304 | tf_op jit(solution)/shard_map/all_to_all | solution.py:485
  303.9 41.9 %copy-start.18 = (s32[256]{0:T(256)S(1)}, s32[256]{0:T(256)}, u32[]{:S(2)}) copy-start(s32[256]{0:T(256)} %param.10) | copy-start | bytes 3076
  303.9 24.6 %collective-permute-start.14 = (bf16[8,40,256]{2,1,0:T(8,128)(2,1)}, bf16[8,40,256]{2,1,0:T(8,128)(2,1)S(1)}, u32[]{:S(2)}, u32[]{:S(2)}) collective-permute-start(bf16[8,40,256]{2,1,0:T(8,128)(2,1)} %get-tuple-element.66), channel_id=1, source_target_pairs={{0,24},{8,16},{16,8},{24,0},{1,25},{9,17},{17,9},{25,1},{2,26},{10... | collective-permute-start | bytes 491528 | tf_op jit(solution)/shard_map/ppermute | solution.py:481
  305.2 34.9 %collective-permute-start.13 = (bf16[8,40,256]{2,1,0:T(8,128)(2,1)}, bf16[8,40,256]{2,1,0:T(8,128)(2,1)S(1)}, u32[]{:S(2)}, u32[]{:S(2)}) collective-permute-start(bf16[8,40,256]{2,1,0:T(8,128)(2,1)} %get-tuple-element.65), channel_id=1, source_target_pairs={{0,16},{8,24},{16,0},{24,8},{1,17},{9,25},{17,1},{25,9},{2,18},{10... | collective-permute-start | bytes 491528 | tf_op jit(solution)/shard_map/ppermute | solution.py:481
  328.3 11.8 %collective-permute-start.12 = (bf16[8,40,256]{2,1,0:T(8,128)(2,1)}, bf16[8,40,256]{2,1,0:T(8,128)(2,1)S(1)}, u32[]{:S(2)}, u32[]{:S(2)}) collective-permute-start(bf16[8,40,256]{2,1,0:T(8,128)(2,1)} %get-tuple-element.64), channel_id=1, source_target_pairs={{0,8},{8,0},{16,24},{24,16},{1,9},{9,1},{17,25},{25,17},{2,10},{10... | collective-permute-start | bytes 491528 | tf_op jit(solution)/shard_map/ppermute | solution.py:481
  341.9 18.6 %copy-start.2 = (bf16[8,32,4096]{2,1,0:T(8,128)(2,1)}, bf16[8,32,4096]{2,1,0:T(8,128)(2,1)S(1)}, u32[]{:S(2)}) copy-start(bf16[8,32,4096]{2,1,0:T(8,128)(2,1)S(1)} %all-to-all-done.3.refs_10_.refs_11_) | copy-start | bytes 6291460
  341.9 35.8 %all-to-all-start.5 = ((bf16[8,160,256]{2,1,0:T(8,128)(2,1)}), bf16[8,160,256]{2,1,0:T(8,128)(2,1)S(1)}, u32[]{:S(2)}, u32[]{:S(2)}) async-start(bf16[8,160,256]{2,1,0:T(8,128)(2,1)} %pad_maximum_fusion.5), calls=%async_computation.5 | async-start | bytes 1310720 | tf_op jit(solution)/shard_map/all_to_all | solution.py:485
  (9 other events, 25.6 us)

commit v5 on v4

--- a/solution.py
+++ b/solution.py
@@ -24,7 +24,7 @@
 
 
 def busy(share):
-    return pl.CostEstimate(flops=int(share * 4e10), bytes_accessed=1, transcendentals=0)
+    return pl.CostEstimate(flops=int(share * 1e10), bytes_accessed=1, transcendentals=0)
 
 
 def phase(turns, length):
@@ -267,37 +267,46 @@
 
 
 def correlate(here, pieces, far, halves):
-    senders = pieces[0][0].shape[0]
-    sub = pieces[0][0].shape[1] if halves == 1 else ROWS
-    lanes = pieces[0][0].shape[2] // (2 * pieces[0][5])
+    senders, sub, _ = pieces[0][0].shape
+    lanes = pieces[0][0].shape[2] // (2 * pieces[0][4])
     half = FRAMES * lanes
-    block = senders * halves * sub
-    signals = far * block
+    splits = max(1, senders * halves * sub // 256)
+    each = senders // splits
+    block = each * halves * sub
+    count = far * splits
+    signals = count * block
 
     def kernel(here_ref, *refs):
         parts, (out, held, turned, made, in_sems, out_sems) = refs[: len(pieces)], refs[len(pieces) :]
-        coming = [[] for _ in range(far)]
-        for index, (_, partner, row, which, first, frames) in enumerate(pieces):
-            for part in range(2):
-                src = parts[index].at[:, pl.ds(row, sub), pl.ds(part * frames * lanes, frames * lanes)]
-                dst = held.at[partner, :, which, :, pl.ds(part * half + first * lanes, frames * lanes)]
-                coming[partner].append(pltpu.make_async_copy(src, dst, in_sems.at[2 * index + part]))
+        coming = [[] for _ in range(count)]
+        for index, (_, partner, which, first, frames) in enumerate(pieces):
+            for q in range(splits):
+                at = partner * splits + q
+                for part in range(2):
+                    src = parts[index].at[pl.ds(q * each, each), :, pl.ds(part * frames * lanes, frames * lanes)]
+                    dst = held.at[at, :, which, :, pl.ds(part * half + first * lanes, frames * lanes)]
+                    sem = in_sems.at[(index * splits + q) * 2 + part]
+                    coming[at].append(pltpu.make_async_copy(src, dst, sem))
         for copies in coming:
             for copy in copies:
                 copy.start()
+
+        def rows_of(i):
+            return pl.ds(pl.multiple_of(((here_ref[0] ^ (i // splits)) * splits + i % splits) * block, block), block)
+
         inverse = 1.0 / half
         going = [[], []]
         slot = 0
-        for i in range(far):
+        for i in range(count):
             for copy in coming[i]:
                 copy.wait()
             left = held[i].reshape(block, 2 * half)
             turned[:, :half] = left[:, half:]
             turned[:, half:] = -left[:, :half]
-            at_i = pl.ds(pl.multiple_of((here_ref[0] ^ i) * block, block), block)
+            at_i = rows_of(i)
             for j in range(i + 1):
                 right = held[j].reshape(block, 2 * half)
-                at_j = pl.ds(pl.multiple_of((here_ref[0] ^ j) * block, block), block)
+                at_j = rows_of(j)
                 for copy in going[slot]:
                     copy.wait()
                 going[slot] = []
@@ -329,10 +338,10 @@
         out_specs=pl.BlockSpec(memory_space=pl.ANY),
         out_shape=jax.ShapeDtypeStruct((2, signals, signals), jnp.float32),
         scratch_shapes=[
-            pltpu.VMEM((far, senders, halves, sub, 2 * half), jnp.bfloat16),
+            pltpu.VMEM((count, each, halves, sub, 2 * half), jnp.bfloat16),
             pltpu.VMEM((block, 2 * half), jnp.bfloat16),
             pltpu.VMEM((2, 2, 2, block, block), jnp.float32),
-            pltpu.SemaphoreType.DMA((2 * len(pieces),)),
+            pltpu.SemaphoreType.DMA((2 * splits * len(pieces),)),
             pltpu.SemaphoreType.DMA((2, 2, 2)),
         ],
         compiler_params=pltpu.CompilerParams(vmem_limit_bytes=VMEM),
@@ -376,12 +385,12 @@
 
 
 def combine(spectra, chooser, weights, sub):
-    halves = len(spectra)
     slots, beams2, listed = weights.shape
     beams = beams2 // 2
     rows = 2 * slots
     senders = spectra[0].shape[0]
-    partners = spectra[0].shape[1] // rows
+    partners = len(spectra)
+    halves = spectra[0].shape[2] // (FRAMES * sub)
     count = LANES // sub
     inner = senders // count
     groups = partners * halves * inner
@@ -390,14 +399,13 @@
     def kernel(*refs):
         got, (choose, weight, out, ordered, picked) = refs[: len(spectra)], refs[len(spectra) :]
         lane_ids = lax.broadcasted_iota(jnp.int32, (rows, LANES), 1)
-        for s in range(partners):
-            for h, spectrum in enumerate(got):
-                row = s * rows
+        for s, spectrum in enumerate(got):
+            for h in range(halves):
                 for q in range(inner):
                     for t in range(FRAMES // count):
-                        lane = t * LANES
+                        lane = h * FRAMES * sub + t * LANES
                         pieces = [
-                            spectrum[q * count + i, row : row + rows, lane : lane + LANES].astype(jnp.float32)
+                            spectrum[q * count + i, :, lane : lane + LANES].astype(jnp.float32)
                             for i in range(count)
                         ]
                         for f, piece in enumerate(swap_blocks(pieces, lane_ids)):
@@ -477,12 +485,16 @@
     )
     taps_wide = jnp.broadcast_to(prototype[:, None, :], (prototype.shape[0], 8, NCH))
 
-    def to_planes(xs):
-        return [xs[0]] + [lax.ppermute(xs[s], "far", [(i, i ^ s) for i in range(far)]) for s in range(1, far)]
-
-    def in_plane(xs):
-        joined = xs[0] if len(xs) == 1 else jnp.concatenate(xs, axis=1)
-        return lax.all_to_all(joined, ("near", "sb"), split_axis=0, concat_axis=0, tiled=True)
+    def cross(x):
+        return lax.ppermute(x, "far", [(i, i ^ 1) for i in range(far)])
+
+    latest = [None]
+
+    def in_plane(x):
+        if latest[0] is not None:
+            x = after(x, latest[0])
+        latest[0] = lax.all_to_all(x, ("near", "sb"), split_axis=0, concat_axis=0, tiled=True)
+        return latest[0]
 
     share = sig_dev // sb_count
     sub = min(share, ROWS)
@@ -491,7 +503,7 @@
     unit = max(1, LANES * st_count * sb_count // NCH)
     early = FRAMES * 3 // 8 // unit * unit
     plan = [(0, 0, early), (0, early, FRAMES - early)] + [(h, 0, FRAMES) for h in range(1, halves)]
-    crossed, branches = [], []
+    crossed, owned, branches = [], [], []
     for c, (which, first, frames) in enumerate(plan):
         if c > 1:
             table = after(table, crossed[c - 2])
@@ -507,20 +519,11 @@
                 x.reshape(near // inner, sb_count, sub, 2 * frames, RADIX, inner, fine).transpose(0, 5, 1, 2, 3, 4, 6)
                 for x in outs
             ]
-        crossed.append(to_planes([x.reshape(plane, sub, -1) for x in outs]))
+        outs = [x.reshape(plane, sub, -1) for x in outs]
+        owned.append(outs[0])
+        crossed.append(cross(outs[1]))
 
     assign, beam_channels, station_index = after((assign, beam_channels, station_index), branches)
-
-    pieces, in_place = [], []
-    for c, (which, first, frames) in enumerate(plan):
-        step = far if which < halves - 1 else max(1, far // 2)
-        in_place.append([in_plane(crossed[c][s : s + step]) for s in range(0, far, step)])
-        for s in range(far):
-            got, row = in_place[c][s // step], s % step * sub
-            if halves == 1:
-                pieces.append((got[:, row : row + sub].reshape(1, plane * sub, -1), s, 0, 0, first, frames))
-            else:
-                pieces.append((got, s, row, which, first, frames))
 
     per_dev = SLOTS // st_count
     owners = assign[:, 0]
@@ -543,23 +546,33 @@
     turned = jnp.broadcast_to(jnp.arange(2, dtype=jnp.int32)[None, :, None], (st_count * sb_count, 2, per_dev))
     mine = lax.dynamic_slice_in_dim(slot_channel, (near_here * sb_count + sb_here) * per_dev, per_dev)
     row_branch, *tables = slot_tables(by_row(slot_channel), by_row(filled), turned.reshape(-1))
-    slot_received = []
-    for h in range(halves):
-        own = [c for c, (which, _, _) in enumerate(plan) if which == h]
-        done = [crossed[c] for c in own] + [in_place[c] for c in range(own[0] - 1 if h else 0, own[-1])]
-        row_branch = after(row_branch, done)
-        spectra = slot_spectra([row_branch, *tables], [branches[c] for c in own], 2 * per_dev, far)
-        row_branch = after(row_branch, spectra)
-        if h == 0:
-            weights = beam_weights(after(mine, spectra), delays, gains)
-        if sub < ROWS:
-            spectra = [
-                lax.dynamic_slice_in_dim(x.reshape(plane, 2 * per_dev, FRAMES, ROWS), inside, sub, axis=3).reshape(
-                    plane, 2 * per_dev, -1
-                )
-                for x in spectra
-            ]
-        slot_received.append(in_plane(to_planes(spectra)))
+
+    in_place = []
+    for c in range(len(plan) - 1):
+        in_place.append([in_plane(owned[c]), in_plane(crossed[c])])
+    row_branch = after(row_branch, (crossed[-2], in_place[-1][0]))
+    spectra = slot_spectra([row_branch, *tables], branches, 2 * per_dev, far)
+    if sub < ROWS:
+        spectra = [
+            lax.dynamic_slice_in_dim(x.reshape(plane, 2 * per_dev, FRAMES, ROWS), inside, sub, axis=3).reshape(
+                plane, 2 * per_dev, -1
+            )
+            for x in spectra
+        ]
+    slot_crossed = cross(spectra[1])
+    last = in_plane(owned[-1])
+    slot_received = [in_plane(spectra[0])]
+    weights = beam_weights(after(mine, (crossed[-1], slot_received[0])), delays, gains)
+    in_place.append([last, in_plane(crossed[-1])])
+    slot_received.append(in_plane(slot_crossed))
+
+    pieces = []
+    for c, (which, first, frames) in enumerate(plan):
+        for s in range(far):
+            got = in_place[c][s]
+            if halves == 1:
+                got = got.reshape(-1, min(256, plane * sub), got.shape[2])
+            pieces.append((got, s, which, first, frames))
 
     signal_ids = spread(
         partner[:, None] * (near * sig_dev) + jnp.arange(halves, dtype=jnp.int32)[None, :] * sub,
@@ -569,7 +582,7 @@
     wanted = (station_index[None, :] * 2 + jnp.arange(2, dtype=jnp.int32)[:, None]).reshape(-1)
     chooser = (signal_ids[:, None] == wanted[None, :]).astype(jnp.bfloat16)
 
-    visibility = correlate(after(far_here[None], spectra), pieces, far, halves)
+    visibility = correlate(after(far_here[None], weights), pieces, far, halves)
     signals = visibility.shape[1]
     beam_out = combine(slot_received, chooser, weights, sub)
     return (visibility.reshape(2, 1, 1, signals, signals), beam_out)
@@ -577,7 +590,7 @@
 
 def solution(mesh):
     st_count, sb_count = mesh.shape["st"], mesh.shape["sb"]
-    far = math.gcd(4, st_count)
+    far = 2
     planes = Mesh(mesh.devices.reshape(far, st_count // far, sb_count), ("far", "near", "sb"))
     st = ("far", "near")
     in_specs = (P(None, st, None), P(), P(), P(), P(), P(), P())

time: 389 us -> 400 us (1.028)
  waiting for transfers between devices: 134 us -> 191 us
  starting transfers between devices: 69.9 us -> 52.6 us
  other arithmetic: 29.9 us -> 15.3 us
  local copies, waits for them, and re-layouts: 13.8 us -> 6.66 us
  Pallas kernels: 139 us -> 133 us
    ppermute x15 -> x4, waiting for transfers between devices: 117 us -> 169 us  [cross(): return lax.ppermute(x, 'far', [(i, i ^ 1) for i in range(far)])]
    ppermute x15 -> x4, starting transfers between devices: 46.6 us -> 12.7 us  [cross(): return lax.ppermute(x, 'far', [(i, i ^ 1) for i in range(far)])]
    all_to_all x6 -> x8, starting transfers between devices: 23.3 us -> 39.9 us  [in_plane(): lax.all_to_all(x, ('near', 'sb'), split_axis=0, concat_axis=0, tiled=True)]
    concatenate x6 -> x0, other arithmetic: 11.8 us -> none  [in_plane(): joined = xs[0] if len(xs) == 1 else jnp.concatenate(xs, axis=1)]
    pallas_call x2 -> x1, Pallas kernels: 25.8 us -> 19.6 us  [slot_spectra(): pl.pallas_call(functools.partial(slot_kernel, far), out_shape=[jax.ShapeD...]
    all_to_all x6 -> x8, waiting for transfers between devices: 17.4 us -> 21.5 us  [in_plane(): lax.all_to_all(x, ('near', 'sb'), split_axis=0, concat_axis=0, tiled=True)]
  transfers between devices with their start and end apart: 21 -> 12, of which waited for: 7 -> 6; matrix products, arithmetic and copies ran while one was open for 9% -> 4% of each run, Pallas kernels for 25% -> 26%
where the time goes in v5:
time: 400 us; the launch traced here: 399 us
  waiting for transfers between devices  191 us (48%)
  Pallas kernels  133 us (33%)
  starting transfers between devices  52.6 us (13%)
  other arithmetic  15.3 us (4%)
  local copies, waits for them, and re-layouts  6.66 us (2%)
    ppermute x4, waiting for transfers between devices, cross(): return lax.ppermute(x, 'far', [(i, i ^ 1) for i in range(far)])  169 us
    pallas_call x3, Pallas kernels, channelise(): pl.pallas_call(functools.partial(channel_kernel, first), grid_spec=pltpu....  71.8 us
    all_to_all x8, starting transfers between devices, in_plane(): lax.all_to_all(x, ('near', 'sb'), split_axis=0, concat_axis=0, tiled=True)  39.9 us
    all_to_all x8, waiting for transfers between devices, in_plane(): lax.all_to_all(x, ('near', 'sb'), split_axis=0, concat_axis=0, tiled=True)  21.5 us
    pallas_call x1, Pallas kernels, slot_spectra(): pl.pallas_call(functools.partial(slot_kernel, far), out_shape=[jax.ShapeD...  19.6 us
    pallas_call x1, Pallas kernels, correlate(): pl.pallas_call(kernel, in_specs=[pl.BlockSpec(memory_space=pltpu.SMEM)] +...  17.2 us
    ppermute x4, starting transfers between devices, cross(): return lax.ppermute(x, 'far', [(i, i ^ 1) for i in range(far)])  12.7 us
    pallas_call x1, Pallas kernels, beam_weights(): pl.pallas_call(weight_kernel, grid=(slots,), in_specs=[pl.BlockSpec(memor...  12.3 us
  transfers between devices with their start and end apart: 12, of which 6 were waited for; matrix products, arithmetic and copies ran while one was open for 4% of the time, Pallas kernels for 26%

profile of v5, /device:TPU:0, one launch (start us, length us, event | category | flops | bytes accessed | tf_op | source)
XLA Modules:
  0.0 398.8 jit_solution(6378893735649702875)
XLA Ops:
  3.6 2.8 shard_map.86.table
  6.4 1.5 broadcast_in_dim.18.taps_wide
  7.9 16.8 %shard_map.87 = (bf16[4,4,16,1536]{3,2,1,0:T(8,128)(2,1)}, bf16[4,4,16,1536]{3,2,1,0:T(8,128)(2,1)}, bf16[8,6,16,1024]{3,2,1,0:T(8,128)(2,1)}) custom-call(s32[1]{0:T(128)} %bitcast.1.row_block, bf16[2,128,126976]{2,1,0:T(8,128)(2,1)} %volts.5, f32[16,8,4096]{2,1,0:T(8,128)} %broadcast_in_dim.18.taps_wide, f32[8,512]{1,0:T(8,128)} %get-tuple-element.79.turn_c, ...), custom_call_target="tpu_custom_call" | custom-call | flops 3750000128 | bytes 1 | tf_op jit(solution)/shard_map/pallas_call | solution.py:191
  24.7 6.3 %all-to-all-start = ((bf16[16,16,1536]{2,1,0:T(8,128)(2,1)}), bf16[16,16,1536]{2,1,0:T(8,128)(2,1)S(1)}, u32[]{:S(2)}, u32[]{:S(2)}) async-start(bf16[16,16,1536]{2,1,0:T(8,128)(2,1)} %bitcast.36), calls=%async_computation | async-start | bytes 1572864 | tf_op jit(solution)/shard_map/all_to_all | solution.py:496
  31.0 2.7 collective-permute-start
  33.7 35.3 %collective-permute-done = bf16[16,16,1536]{2,1,0:T(8,128)(2,1)} collective-permute-done((bf16[16,16,1536]{2,1,0:T(8,128)(2,1)}, bf16[16,16,1536]{2,1,0:T(8,128)(2,1)}, u32[]{:S(2)}, u32[]{:S(2)}) %collective-permute-start) | collective-permute-done | bytes 786464 | tf_op jit(solution)/shard_map/ppermute | solution.py:489
  69.0 4.1 %all-to-all-start.1 = ((bf16[16,16,1536]{2,1,0:T(8,128)(2,1)}), bf16[16,16,1536]{2,1,0:T(8,128)(2,1)S(1)}, u32[]{:S(2)}, u32[]{:S(2)}) async-start(bf16[16,16,1536]{2,1,0:T(8,128)(2,1)} %collective-permute-done), calls=%async_computation.1 | async-start | bytes 1572864 | tf_op jit(solution)/shard_map/all_to_all | solution.py:496
  73.1 22.8 %shard_map.88 = (bf16[4,4,16,2560]{3,2,1,0:T(8,128)(2,1)}, bf16[4,4,16,2560]{3,2,1,0:T(8,128)(2,1)}, bf16[8,10,16,1024]{3,2,1,0:T(8,128)(2,1)}) custom-call(s32[1]{0:T(128)} %bitcast.1.row_block, bf16[2,128,126976]{2,1,0:T(8,128)(2,1)} %volts.5, f32[16,8,4096]{2,1,0:T(8,128)} %broadcast_in_dim.18.taps_wide, f32[8,512]{1,0:T(8,128)} %get-tuple-element.79.turn_c, ...), custom_call_target="tpu_custom_call" | custom-call | flops 6249999872 | bytes 1 | tf_op jit(solution)/shard_map/pallas_call | solution.py:191
  95.9 5.1 %all-to-all-start.2 = ((bf16[16,16,2560]{2,1,0:T(8,128)(2,1)}), bf16[16,16,2560]{2,1,0:T(8,128)(2,1)S(1)}, u32[]{:S(2)}, u32[]{:S(2)}) async-start(bf16[16,16,2560]{2,1,0:T(8,128)(2,1)} %bitcast.35), calls=%async_computation.2 | async-start | bytes 2621440 | tf_op jit(solution)/shard_map/all_to_all | solution.py:496
  101.0 3.4 collective-permute-start.2
  104.5 57.7 %collective-permute-done.2 = bf16[16,16,2560]{2,1,0:T(8,128)(2,1)} collective-permute-done((bf16[16,16,2560]{2,1,0:T(8,128)(2,1)}, bf16[16,16,2560]{2,1,0:T(8,128)(2,1)}, u32[]{:S(2)}, u32[]{:S(2)}) %collective-permute-start.2) | collective-permute-done | bytes 1310752 | tf_op jit(solution)/shard_map/ppermute | solution.py:489
  162.2 4.1 %all-to-all-start.3 = ((bf16[16,16,2560]{2,1,0:T(8,128)(2,1)}), bf16[16,16,2560]{2,1,0:T(8,128)(2,1)S(1)}, u32[]{:S(2)}, u32[]{:S(2)}) async-start(bf16[16,16,2560]{2,1,0:T(8,128)(2,1)} %collective-permute-done.2), calls=%async_computation.3 | async-start | bytes 2621440 | tf_op jit(solution)/shard_map/all_to_all | solution.py:496
  166.8 32.1 %shard_map.89 = (bf16[4,4,16,4096]{3,2,1,0:T(8,128)(2,1)}, bf16[4,4,16,4096]{3,2,1,0:T(8,128)(2,1)}, bf16[8,16,16,1024]{3,2,1,0:T(8,128)(2,1)}) custom-call(s32[1]{0:T(128)} %bitcast.2.row_block, bf16[2,128,126976]{2,1,0:T(8,128)(2,1)} %volts.5, f32[16,8,4096]{2,1,0:T(8,128)} %broadcast_in_dim.18.taps_wide, f32[8,512]{1,0:T(8,128)} %get-tuple-element.79.turn_c, ...), custom_call_target="tpu_custom_call" | custom-call | flops 10000000000 | bytes 1 | tf_op jit(solution)/shard_map/pallas_call | solution.py:191
  198.9 1.2 reduce-window.6
  201.7 5.2 %all-to-all-start.4 = ((bf16[16,16,4096]{2,1,0:T(8,128)(2,1)}), bf16[16,16,4096]{2,1,0:T(8,128)(2,1)S(1)}, u32[]{:S(2)}, u32[]{:S(2)}) async-start(bf16[16,16,4096]{2,1,0:T(8,128)(2,1)} %bitcast.34), calls=%async_computation.4 | async-start | bytes 4194304 | tf_op jit(solution)/shard_map/all_to_all | solution.py:496
  208.6 3.5 collective-permute-start.1
  212.0 1.1 add_select_fusion.1.row_branch
  213.1 3.9 fusion.9
  217.1 3.8 sine_multiply_fusion
  220.9 19.6 %shard_map.90 = (bf16[16,40,512]{2,1,0:T(8,128)(2,1)}, bf16[16,40,512]{2,1,0:T(8,128)(2,1)}) custom-call(s32[1280,1]{1,0:T(8,128)} %add_select_fusion.1.row_branch, f32[1280,4]{1,0:T(8,128)} %get-tuple-element.67.hi_c, f32[1280,4]{1,0:T(8,128)} %get-tuple-element.66.hi_s, f32[1280,128]{1,0:T(8,128)} %get-tuple-element.69.lo_c, ...), custom_call_target="tpu_custom_call" | custom-call | flops 10000000000 | bytes 1 | tf_op jit(solution)/shard_map/pallas_call | solution.py:257
  240.5 18.1 %all-to-all-done.4.refs_4_ = bf16[16,16,4096]{2,1,0:T(8,128)(2,1)S(1)} async-done(((bf16[16,16,4096]{2,1,0:T(8,128)(2,1)}), bf16[16,16,4096]{2,1,0:T(8,128)(2,1)S(1)}, u32[]{:S(2)}, u32[]{:S(2)}) %all-to-all-start.4) | async-done | bytes 2097184 | tf_op jit(solution)/shard_map/all_to_all | solution.py:496
  258.6 3.6 all-to-all-start.5
  262.2 41.4 %collective-permute-done.1 = bf16[16,16,4096]{2,1,0:T(8,128)(2,1)} collective-permute-done((bf16[16,16,4096]{2,1,0:T(8,128)(2,1)}, bf16[16,16,4096]{2,1,0:T(8,128)(2,1)}, u32[]{:S(2)}, u32[]{:S(2)}) %collective-permute-start.1) | collective-permute-done | bytes 2097184 | tf_op jit(solution)/shard_map/ppermute | solution.py:489
  304.4 4.4 %all-to-all-start.6 = ((bf16[16,16,4096]{2,1,0:T(8,128)(2,1)}), bf16[16,16,4096]{2,1,0:T(8,128)(2,1)}, u32[]{:S(2)}, u32[]{:S(2)}) async-start(bf16[16,16,4096]{2,1,0:T(8,128)(2,1)} %collective-permute-done.1), calls=%async_computation.6 | async-start | bytes 4194304 | tf_op jit(solution)/shard_map/all_to_all | solution.py:496
  308.8 3.2 collective-permute-start.3
  312.1 34.8 %collective-permute-done.3 = bf16[16,40,512]{2,1,0:T(8,128)(2,1)} collective-permute-done((bf16[16,40,512]{2,1,0:T(8,128)(2,1)S(1)}, bf16[16,40,512]{2,1,0:T(8,128)(2,1)}, u32[]{:S(2)}, u32[]{:S(2)}) %collective-permute-start.3) | collective-permute-done | bytes 655392 | tf_op jit(solution)/shard_map/ppermute | solution.py:489
  346.9 3.4 all-to-all-done.6.refs_5_
  350.3 7.1 %all-to-all-start.7 = ((bf16[16,40,512]{2,1,0:T(8,128)(2,1)}), bf16[16,40,512]{2,1,0:T(8,128)(2,1)S(1)}, u32[]{:S(2)}, u32[]{:S(2)}) async-start(bf16[16,40,512]{2,1,0:T(8,128)(2,1)} %collective-permute-done.3), calls=%async_computation.7 | async-start | bytes 1310720 | tf_op jit(solution)/shard_map/all_to_all | solution.py:496
  358.2 1.2 compare_convert_fusion.refs_2_
  359.5 12.3 %shard_map.91.refs_3_ = bf16[20,512,256]{2,1,0:T(8,128)(2,1)} custom-call(s32[20]{0:T(128)} %dynamic_slice.3.channel, f32[256,256]{1,0:T(8,128)} %delays.1, f32[256,256]{1,0:T(8,128)} %gains.1), custom_call_target="tpu_custom_call" | custom-call | flops 1 | bytes 1 | tf_op jit(solution)/shard_map/pallas_call | solution.py:373
  371.8 17.2 %shard_map.92 = f32[2,1024,1024]{2,1,0:T(8,128)} custom-call(s32[1]{0:T(128)} %bitcast.here_ref, bf16[16,16,1536]{2,1,0:T(8,128)(2,1)} %copy-done.3, bf16[16,16,1536]{2,1,0:T(8,128)(2,1)} %copy-done.4, bf16[16,16,2560]{2,1,0:T(8,128)(2,1)} %copy-done.1, bf16[16,16,2560]{2,1,0:T(8,128)(2,1)} %copy-done.2, bf16[16,16,4096]{2,1,0:T(8,128)(2,1)} %copy-done, ...), custom_call_target="tpu_custom_call" | custom-call | flops 1 | bytes 1 | tf_op jit(solution)/shard_map/pallas_call | solution.py:335
  389.9 8.9 %shard_map.93 = f32[1,20,2,16,512]{4,3,2,1,0:T(8,128)} custom-call(bf16[16,40,512]{2,1,0:T(8,128)(2,1)} %copy-done.5, bf16[16,40,512]{2,1,0:T(8,128)(2,1)} %copy-done.6, bf16[1024,512]{1,0:T(8,128)(2,1)} %compare_convert_fusion.refs_2_, bf16[20,512,256]{2,1,0:T(8,128)(2,1)} %shard_map.91.refs_3_), custom_call_target="tpu_custom_call" | custom-call | flops 1 | bytes 1 | tf_op jit(solution)/shard_map/pallas_call | solution.py:444
  (77 shorter events, 9.1 us)
Async XLA Ops:
  0.6 5.8 %copy-start.7 = (f32[16,4096]{1,0:T(8,128)S(1)}, f32[16,4096]{1,0:T(8,128)}, u32[]{:S(2)}) copy-start(f32[16,4096]{1,0:T(8,128)} %param.8) | copy-start | bytes 786436
  24.7 44.3 %all-to-all-start = ((bf16[16,16,1536]{2,1,0:T(8,128)(2,1)}), bf16[16,16,1536]{2,1,0:T(8,128)(2,1)S(1)}, u32[]{:S(2)}, u32[]{:S(2)}) async-start(bf16[16,16,1536]{2,1,0:T(8,128)(2,1)} %bitcast.36), calls=%async_computation | async-start | bytes 1572864 | tf_op jit(solution)/shard_map/all_to_all | solution.py:496
  31.0 38.0 %collective-permute-start = (bf16[16,16,1536]{2,1,0:T(8,128)(2,1)}, bf16[16,16,1536]{2,1,0:T(8,128)(2,1)}, u32[]{:S(2)}, u32[]{:S(2)}) collective-permute-start(bf16[16,16,1536]{2,1,0:T(8,128)(2,1)} %bitcast.42), channel_id=1, source_target_pairs={{0,16},{16,0},{1,17},{17,1},{2,18},{18,2},{3,19},{19,3},{4,20},{20... | collective-permute-start | bytes 2359304 | tf_op jit(solution)/shard_map/ppermute | solution.py:489
  69.0 26.9 %copy-start.3 = (bf16[16,16,1536]{2,1,0:T(8,128)(2,1)}, bf16[16,16,1536]{2,1,0:T(8,128)(2,1)S(1)}, u32[]{:S(2)}) copy-start(bf16[16,16,1536]{2,1,0:T(8,128)(2,1)S(1)} %all-to-all-done.refs_0_) | copy-start | bytes 2359300
  69.0 26.9 %all-to-all-start.1 = ((bf16[16,16,1536]{2,1,0:T(8,128)(2,1)}), bf16[16,16,1536]{2,1,0:T(8,128)(2,1)S(1)}, u32[]{:S(2)}, u32[]{:S(2)}) async-start(bf16[16,16,1536]{2,1,0:T(8,128)(2,1)} %collective-permute-done), calls=%async_computation.1 | async-start | bytes 1572864 | tf_op jit(solution)/shard_map/all_to_all | solution.py:496
  95.9 66.3 %copy-start.4 = (bf16[16,16,1536]{2,1,0:T(8,128)(2,1)}, bf16[16,16,1536]{2,1,0:T(8,128)(2,1)S(1)}, u32[]{:S(2)}) copy-start(bf16[16,16,1536]{2,1,0:T(8,128)(2,1)S(1)} %all-to-all-done.1.refs_1_) | copy-start | bytes 2359300
  95.9 66.3 %all-to-all-start.2 = ((bf16[16,16,2560]{2,1,0:T(8,128)(2,1)}), bf16[16,16,2560]{2,1,0:T(8,128)(2,1)S(1)}, u32[]{:S(2)}, u32[]{:S(2)}) async-start(bf16[16,16,2560]{2,1,0:T(8,128)(2,1)} %bitcast.35), calls=%async_computation.2 | async-start | bytes 2621440 | tf_op jit(solution)/shard_map/all_to_all | solution.py:496
  101.0 61.2 %collective-permute-start.2 = (bf16[16,16,2560]{2,1,0:T(8,128)(2,1)}, bf16[16,16,2560]{2,1,0:T(8,128)(2,1)}, u32[]{:S(2)}, u32[]{:S(2)}) collective-permute-start(bf16[16,16,2560]{2,1,0:T(8,128)(2,1)} %bitcast.41), channel_id=1, source_target_pairs={{0,16},{16,0},{1,17},{17,1},{2,18},{18,2},{3,19},{19,3},{4,20},{20... | collective-permute-start | bytes 3932168 | tf_op jit(solution)/shard_map/ppermute | solution.py:489
  162.2 36.7 %copy-start.1 = (bf16[16,16,2560]{2,1,0:T(8,128)(2,1)}, bf16[16,16,2560]{2,1,0:T(8,128)(2,1)S(1)}, u32[]{:S(2)}) copy-start(bf16[16,16,2560]{2,1,0:T(8,128)(2,1)S(1)} %all-to-all-done.2.refs_2_) | copy-start | bytes 3932164
  162.2 38.3 %all-to-all-start.3 = ((bf16[16,16,2560]{2,1,0:T(8,128)(2,1)}), bf16[16,16,2560]{2,1,0:T(8,128)(2,1)S(1)}, u32[]{:S(2)}, u32[]{:S(2)}) async-start(bf16[16,16,2560]{2,1,0:T(8,128)(2,1)} %collective-permute-done.2), calls=%async_computation.3 | async-start | bytes 2621440 | tf_op jit(solution)/shard_map/all_to_all | solution.py:496
  166.8 32.1 %copy-start.9 = (s32[384,1]{0,1:T(1,128)S(1)}, s32[384,1]{0,1:T(1,128)}, u32[]{:S(2)}) copy-start(s32[384,1]{0,1:T(1,128)} %param.13) | copy-start | bytes 4612
  200.6 1.1 copy-start.2
  200.6 6.4 %copy-start.8 = (s32[384]{0:T(512)S(1)}, s32[384]{0:T(512)}, u32[]{:S(2)}) copy-start(s32[384]{0:T(512)} %param.9) | copy-start | bytes 4612
  201.7 56.9 %all-to-all-start.4 = ((bf16[16,16,4096]{2,1,0:T(8,128)(2,1)}), bf16[16,16,4096]{2,1,0:T(8,128)(2,1)S(1)}, u32[]{:S(2)}, u32[]{:S(2)}) async-start(bf16[16,16,4096]{2,1,0:T(8,128)(2,1)} %bitcast.34), calls=%async_computation.4 | async-start | bytes 4194304 | tf_op jit(solution)/shard_map/all_to_all | solution.py:496
  208.6 95.0 %collective-permute-start.1 = (bf16[16,16,4096]{2,1,0:T(8,128)(2,1)}, bf16[16,16,4096]{2,1,0:T(8,128)(2,1)}, u32[]{:S(2)}, u32[]{:S(2)}) collective-permute-start(bf16[16,16,4096]{2,1,0:T(8,128)(2,1)} %bitcast.40), channel_id=1, source_target_pairs={{0,16},{16,0},{1,17},{17,1},{2,18},{18,2},{3,19},{19,3},{4,20},{20... | collective-permute-start | bytes 6291464 | tf_op jit(solution)/shard_map/ppermute | solution.py:489
  258.6 45.0 %copy-start = (bf16[16,16,4096]{2,1,0:T(8,128)(2,1)}, bf16[16,16,4096]{2,1,0:T(8,128)(2,1)S(1)}, u32[]{:S(2)}) copy-start(bf16[16,16,4096]{2,1,0:T(8,128)(2,1)S(1)} %all-to-all-done.4.refs_4_) | copy-start | bytes 6291460
  258.6 45.0 %all-to-all-start.5 = ((bf16[16,40,512]{2,1,0:T(8,128)(2,1)}), bf16[16,40,512]{2,1,0:T(8,128)(2,1)S(1)}, u32[]{:S(2)}, u32[]{:S(2)}) async-start(bf16[16,40,512]{2,1,0:T(8,128)(2,1)} %get-tuple-element.49), calls=%async_computation.5 | async-start | bytes 1310720 | tf_op jit(solution)/shard_map/all_to_all | solution.py:496
  262.2 46.7 %copy-start.11 = (bf16[16,40,512]{2,1,0:T(8,128)(2,1)S(1)}, bf16[16,40,512]{2,1,0:T(8,128)(2,1)}, u32[]{:S(2)}) copy-start(bf16[16,40,512]{2,1,0:T(8,128)(2,1)} %get-tuple-element.53) | copy-start | bytes 1966084
  262.2 96.1 %copy-start.10 = (s32[256]{0:T(256)S(1)}, s32[256]{0:T(256)}, u32[]{:S(2)}) copy-start(s32[256]{0:T(256)} %param.10) | copy-start | bytes 3076
  303.5 0.8 copy-start.5
  304.4 45.9 %all-to-all-start.6 = ((bf16[16,16,4096]{2,1,0:T(8,128)(2,1)}), bf16[16,16,4096]{2,1,0:T(8,128)(2,1)}, u32[]{:S(2)}, u32[]{:S(2)}) async-start(bf16[16,16,4096]{2,1,0:T(8,128)(2,1)} %collective-permute-done.1), calls=%async_computation.6 | async-start | bytes 4194304 | tf_op jit(solution)/shard_map/all_to_all | solution.py:496
  308.8 38.0 %collective-permute-start.3 = (bf16[16,40,512]{2,1,0:T(8,128)(2,1)S(1)}, bf16[16,40,512]{2,1,0:T(8,128)(2,1)}, u32[]{:S(2)}, u32[]{:S(2)}) collective-permute-start(bf16[16,40,512]{2,1,0:T(8,128)(2,1)S(1)} %copy-done.11), channel_id=1, source_target_pairs={{0,16},{16,0},{1,17},{17,1},{2,18},{18,2},{3,19},{19,3},{4,20},{20... | collective-permute-start | bytes 1966088 | tf_op jit(solution)/shard_map/ppermute | solution.py:489
  350.3 38.7 %all-to-all-start.7 = ((bf16[16,40,512]{2,1,0:T(8,128)(2,1)}), bf16[16,40,512]{2,1,0:T(8,128)(2,1)S(1)}, u32[]{:S(2)}, u32[]{:S(2)}) async-start(bf16[16,40,512]{2,1,0:T(8,128)(2,1)} %collective-permute-done.3), calls=%async_computation.7 | async-start | bytes 1310720 | tf_op jit(solution)/shard_map/all_to_all | solution.py:496
  389.0 0.9 copy-start.6

commit v6 on v5

--- a/solution.py
+++ b/solution.py
@@ -266,9 +266,8 @@
     )(*tables, *chunks)
 
 
-def correlate(here, pieces, far, halves):
+def correlate(here, pieces, far, halves, lanes):
     senders, sub, _ = pieces[0][0].shape
-    lanes = pieces[0][0].shape[2] // (2 * pieces[0][4])
     half = FRAMES * lanes
     splits = max(1, senders * halves * sub // 256)
     each = senders // splits
@@ -279,11 +278,13 @@
     def kernel(here_ref, *refs):
         parts, (out, held, turned, made, in_sems, out_sems) = refs[: len(pieces)], refs[len(pieces) :]
         coming = [[] for _ in range(count)]
-        for index, (_, partner, which, first, frames) in enumerate(pieces):
+        for index, (_, lane, partner, which, first, frames) in enumerate(pieces):
             for q in range(splits):
-                at = partner * splits + q
+                at = partner * splits + (q ^ partner)
                 for part in range(2):
-                    src = parts[index].at[pl.ds(q * each, each), :, pl.ds(part * frames * lanes, frames * lanes)]
+                    src = parts[index].at[
+                        pl.ds(q * each, each), :, pl.ds(lane + part * frames * lanes, frames * lanes)
+                    ]
                     dst = held.at[at, :, which, :, pl.ds(part * half + first * lanes, frames * lanes)]
                     sem = in_sems.at[(index * splits + q) * 2 + part]
                     coming[at].append(pltpu.make_async_copy(src, dst, sem))
@@ -388,24 +389,23 @@
     slots, beams2, listed = weights.shape
     beams = beams2 // 2
     rows = 2 * slots
-    senders = spectra[0].shape[0]
-    partners = len(spectra)
-    halves = spectra[0].shape[2] // (FRAMES * sub)
+    senders = spectra.shape[0]
+    partners = spectra.shape[1] // rows
+    halves = spectra.shape[2] // (FRAMES * sub)
     count = LANES // sub
     inner = senders // count
     groups = partners * halves * inner
     tiles = 2 * listed // LANES
 
-    def kernel(*refs):
-        got, (choose, weight, out, ordered, picked) = refs[: len(spectra)], refs[len(spectra) :]
+    def kernel(spectrum, choose, weight, out, ordered, picked):
         lane_ids = lax.broadcasted_iota(jnp.int32, (rows, LANES), 1)
-        for s, spectrum in enumerate(got):
+        for s in range(partners):
             for h in range(halves):
                 for q in range(inner):
                     for t in range(FRAMES // count):
                         lane = h * FRAMES * sub + t * LANES
                         pieces = [
-                            spectrum[q * count + i, :, lane : lane + LANES].astype(jnp.float32)
+                            spectrum[q * count + i, s * rows : (s + 1) * rows, lane : lane + LANES].astype(jnp.float32)
                             for i in range(count)
                         ]
                         for f, piece in enumerate(swap_blocks(pieces, lane_ids)):
@@ -450,11 +450,7 @@
         ],
         compiler_params=pltpu.CompilerParams(vmem_limit_bytes=VMEM),
         cost_estimate=NO_COST,
-    )(*spectra, chooser, weights)
-
-
-def after(value, other):
-    return lax.optimization_barrier((value, other))[0]
+    )(spectra, chooser, weights)
 
 
 def body(volts, prototype, beam_channels, station_index, delays, gains, assign):
@@ -486,15 +482,12 @@
     taps_wide = jnp.broadcast_to(prototype[:, None, :], (prototype.shape[0], 8, NCH))
 
     def cross(x):
-        return lax.ppermute(x, "far", [(i, i ^ 1) for i in range(far)])
-
-    latest = [None]
-
-    def in_plane(x):
-        if latest[0] is not None:
-            x = after(x, latest[0])
-        latest[0] = lax.all_to_all(x, ("near", "sb"), split_axis=0, concat_axis=0, tiled=True)
-        return latest[0]
+        pairs = [(i, i ^ (near + near // 2)) for i in range(st_count)]
+        return lax.ppermute(x, ("far", "near"), pairs)
+
+    def in_plane(xs, axis):
+        joined = xs[0] if len(xs) == 1 else jnp.concatenate(xs, axis=axis)
+        return lax.all_to_all(joined, ("near", "sb"), split_axis=0, concat_axis=0, tiled=True)
 
     share = sig_dev // sb_count
     sub = min(share, ROWS)
@@ -503,14 +496,12 @@
     unit = max(1, LANES * st_count * sb_count // NCH)
     early = FRAMES * 3 // 8 // unit * unit
     plan = [(0, 0, early), (0, early, FRAMES - early)] + [(h, 0, FRAMES) for h in range(1, halves)]
-    crossed, owned, branches = [], [], []
-    for c, (which, first, frames) in enumerate(plan):
-        if c > 1:
-            table = after(table, crossed[c - 2])
+    group = NCH // (st_count * sb_count)
+
+    def channels_of(c, table):
+        which, first, frames = plan[c]
         row_block = (sb_here * share // ROWS + which)[None]
         *outs, kept = channelise(row_block, volts, taps_wide, turn_c, turn_s, table, first, frames, far)
-        table = after(table, outs)
-        branches.append(kept)
         if sub < ROWS:
             outs = [lax.dynamic_slice_in_dim(x, inside, sub, axis=2) for x in outs]
         inner = st_count // RADIX
@@ -519,11 +510,25 @@
                 x.reshape(near // inner, sb_count, sub, 2 * frames, RADIX, inner, fine).transpose(0, 5, 1, 2, 3, 4, 6)
                 for x in outs
             ]
-        outs = [x.reshape(plane, sub, -1) for x in outs]
-        owned.append(outs[0])
-        crossed.append(cross(outs[1]))
-
-    assign, beam_channels, station_index = after((assign, beam_channels, station_index), branches)
+        return [x.reshape(plane, sub, -1) for x in outs], kept
+
+    barrier = lax.optimization_barrier
+    lists = (assign, beam_channels, station_index)
+    outs, kept = channels_of(0, table)
+    branches, arrived, waiting, pieces = [kept], [], [], []
+    for c in range(len(plan)):
+        outs, waiting, table, lists, arrived[-1:] = barrier((outs, waiting, table, lists, arrived[-1:]))
+        lane = 0
+        for s, k in [(1, c - 1)][: len(waiting)] + [(0, c)]:
+            pieces.append((c, lane, s, *plan[k]))
+            lane += 2 * plan[k][2] * group
+        arrived.append(in_plane(waiting + [outs[0]], 2))
+        waiting = [cross(outs[1])]
+        if c + 1 < len(plan):
+            outs, kept = channels_of(c + 1, table)
+            branches.append(kept)
+    pieces.append((len(plan), 0, 1, *plan[-1]))
+    assign, beam_channels, station_index = lists
 
     per_dev = SLOTS // st_count
     owners = assign[:, 0]
@@ -545,13 +550,8 @@
 
     turned = jnp.broadcast_to(jnp.arange(2, dtype=jnp.int32)[None, :, None], (st_count * sb_count, 2, per_dev))
     mine = lax.dynamic_slice_in_dim(slot_channel, (near_here * sb_count + sb_here) * per_dev, per_dev)
-    row_branch, *tables = slot_tables(by_row(slot_channel), by_row(filled), turned.reshape(-1))
-
-    in_place = []
-    for c in range(len(plan) - 1):
-        in_place.append([in_plane(owned[c]), in_plane(crossed[c])])
-    row_branch = after(row_branch, (crossed[-2], in_place[-1][0]))
-    spectra = slot_spectra([row_branch, *tables], branches, 2 * per_dev, far)
+    tables = slot_tables(by_row(slot_channel), by_row(filled), turned.reshape(-1))
+    spectra = slot_spectra(tables, branches, 2 * per_dev, far)
     if sub < ROWS:
         spectra = [
             lax.dynamic_slice_in_dim(x.reshape(plane, 2 * per_dev, FRAMES, ROWS), inside, sub, axis=3).reshape(
@@ -559,30 +559,26 @@
             )
             for x in spectra
         ]
+    spectra, waiting, mine, arrived[-1:] = barrier((spectra, waiting, mine, arrived[-1:]))
+    arrived.append(in_plane(waiting, 2))
     slot_crossed = cross(spectra[1])
-    last = in_plane(owned[-1])
-    slot_received = [in_plane(spectra[0])]
-    weights = beam_weights(after(mine, (crossed[-1], slot_received[0])), delays, gains)
-    in_place.append([last, in_plane(crossed[-1])])
-    slot_received.append(in_plane(slot_crossed))
-
-    pieces = []
-    for c, (which, first, frames) in enumerate(plan):
-        for s in range(far):
-            got = in_place[c][s]
-            if halves == 1:
-                got = got.reshape(-1, min(256, plane * sub), got.shape[2])
-            pieces.append((got, s, which, first, frames))
-
-    signal_ids = spread(
-        partner[:, None] * (near * sig_dev) + jnp.arange(halves, dtype=jnp.int32)[None, :] * sub,
-        jnp.arange(plane, dtype=jnp.int32) * share,
-        jnp.arange(sub, dtype=jnp.int32),
-    )
+    weights = beam_weights(mine, delays, gains)
+    spectra, slot_crossed, weights, arrived[-1:] = barrier((spectra, slot_crossed, weights, arrived[-1:]))
+    slot_received = in_plane([spectra[0], slot_crossed], 1)
+    if halves == 1:
+        arrived = [x.reshape(-1, min(256, plane * sub), x.shape[2]) for x in arrived]
+    visibility = correlate(far_here[None], [(arrived[p[0]], *p[1:]) for p in pieces], far, halves, group)
+
+    by_way = jnp.arange(near, dtype=jnp.int32)[None, :] ^ (jnp.arange(far, dtype=jnp.int32)[:, None] * (near // 2))
+    signal_ids = (
+        (partner[:, None] * near + by_way)[:, None, :, None, None] * sig_dev
+        + jnp.arange(halves, dtype=jnp.int32)[:, None, None, None] * sub
+        + jnp.arange(sb_count, dtype=jnp.int32)[:, None] * share
+        + jnp.arange(sub, dtype=jnp.int32)
+    ).reshape(-1)
     wanted = (station_index[None, :] * 2 + jnp.arange(2, dtype=jnp.int32)[:, None]).reshape(-1)
     chooser = (signal_ids[:, None] == wanted[None, :]).astype(jnp.bfloat16)
 
-    visibility = correlate(after(far_here[None], weights), pieces, far, halves)
     signals = visibility.shape[1]
     beam_out = combine(slot_received, chooser, weights, sub)
     return (visibility.reshape(2, 1, 1, signals, signals), beam_out)

time: 400 us -> 327 us (0.82)
  waiting for transfers between devices: 191 us -> 106 us
  other arithmetic: 15.3 us -> 26.4 us
    ppermute x4, waiting for transfers between devices: 169 us -> 106 us  [cross(): return lax.ppermute(x, ('far', 'near'), pairs)]
    all_to_all x8 -> x5, waiting for transfers between devices: 21.5 us -> 0.61 us  [in_plane(): lax.all_to_all(joined, ('near', 'sb'), split_axis=0, concat_axis=0, tiled...]
    concatenate x0 -> x3, other arithmetic: none -> 8.74 us  [in_plane(): joined = xs[0] if len(xs) == 1 else jnp.concatenate(xs, axis=axis)]
    all_to_all x8 -> x5, starting transfers between devices: 39.9 us -> 40.9 us  [in_plane(): lax.all_to_all(joined, ('near', 'sb'), split_axis=0, concat_axis=0, tiled...]
  transfers between devices with their start and end apart: 12 -> 9, of which waited for: 6 -> 5; matrix products, arithmetic and copies ran while one was open for 4% -> 6% of each run, Pallas kernels for 26% -> 32%
where the time goes in v6:
time: 327 us
  Pallas kernels  132 us (40%)
  waiting for transfers between devices  106 us (32%)
  starting transfers between devices  52.2 us (16%)
  other arithmetic  26.4 us (8%)
  local copies, waits for them, and re-layouts  8.64 us (3%)
    ppermute x4, waiting for transfers between devices, cross(): return lax.ppermute(x, ('far', 'near'), pairs)  106 us
    pallas_call x3, Pallas kernels, channelise(): pl.pallas_call(functools.partial(channel_kernel, first), grid_spec=pltpu....  71.7 us
    all_to_all x5, starting transfers between devices, in_plane(): lax.all_to_all(joined, ('near', 'sb'), split_axis=0, concat_axis=0, tiled...  40.9 us
    pallas_call x1, Pallas kernels, slot_spectra(): pl.pallas_call(functools.partial(slot_kernel, far), out_shape=[jax.ShapeD...  19.6 us
    pallas_call x1, Pallas kernels, correlate(): pl.pallas_call(kernel, in_specs=[pl.BlockSpec(memory_space=pltpu.SMEM)] +...  17.2 us
    pallas_call x1, Pallas kernels, beam_weights(): pl.pallas_call(weight_kernel, grid=(slots,), in_specs=[pl.BlockSpec(memor...  12.3 us
    ppermute x4, starting transfers between devices, cross(): return lax.ppermute(x, ('far', 'near'), pairs)  11.4 us
    pallas_call x1, Pallas kernels, combine(): pl.pallas_call(kernel, out_shape=jax.ShapeDtypeStruct((1, slots, 2, FRAME...  8.89 us
  transfers between devices with their start and end apart: 9, of which 5 were waited for; matrix products, arithmetic and copies ran while one was open for 6% of the time, Pallas kernels for 32%

profile of v6, /device:TPU:0, one launch (start us, length us, event | category | flops | bytes accessed | tf_op | source)
XLA Modules:
  0.0 326.7 jit_solution(9266887557266457248)
XLA Ops:
  3.5 2.7 shard_map.86.table
  6.2 1.6 broadcast_in_dim.18.taps_wide
  7.9 16.8 %shard_map.87 = (bf16[4,4,16,1536]{3,2,1,0:T(8,128)(2,1)}, bf16[4,4,16,1536]{3,2,1,0:T(8,128)(2,1)}, bf16[8,6,16,1024]{3,2,1,0:T(8,128)(2,1)}) custom-call(s32[1]{0:T(128)} %bitcast.1.row_block, bf16[2,128,126976]{2,1,0:T(8,128)(2,1)} %volts.5, f32[16,8,4096]{2,1,0:T(8,128)} %broadcast_in_dim.18.taps_wide, f32[8,512]{1,0:T(8,128)} %get-tuple-element.108.turn_c, ...), custom_call_target="tpu_custom_call" | custom-call | flops 3750000128 | bytes 1 | tf_op jit(solution)/shard_map/pallas_call | solution.py:191
  24.7 6.3 %all-to-all-start = ((bf16[16,16,1536]{2,1,0:T(8,128)(2,1)}), bf16[16,16,1536]{2,1,0:T(8,128)(2,1)S(1)}, u32[]{:S(2)}, u32[]{:S(2)}) async-start(bf16[16,16,1536]{2,1,0:T(8,128)(2,1)} %bitcast.34), calls=%async_computation | async-start | bytes 1572864 | tf_op jit(solution)/shard_map/all_to_all | solution.py:490
  31.0 4.0 %collective-permute-start = (bf16[16,16,1536]{2,1,0:T(8,128)(2,1)}, bf16[16,16,1536]{2,1,0:T(8,128)(2,1)S(1)}, u32[]{:S(2)}, u32[]{:S(2)}) collective-permute-start(bf16[16,16,1536]{2,1,0:T(8,128)(2,1)} %bitcast.40), channel_id=1, source_target_pairs={{0,24},{4,28},{8,16},{12,20},{16,8},{20,12},{24,0},{28,4},{1,25},{... | collective-permute-start | bytes 2359304 | tf_op jit(solution)/shard_map/ppermute | solution.py:486
  34.9 22.8 %shard_map.88 = (bf16[4,4,16,2560]{3,2,1,0:T(8,128)(2,1)}, bf16[4,4,16,2560]{3,2,1,0:T(8,128)(2,1)}, bf16[8,10,16,1024]{3,2,1,0:T(8,128)(2,1)}) custom-call(s32[1]{0:T(128)} %bitcast.1.row_block, bf16[2,128,126976]{2,1,0:T(8,128)(2,1)} %volts.5, f32[16,8,4096]{2,1,0:T(8,128)} %broadcast_in_dim.18.taps_wide, f32[8,512]{1,0:T(8,128)} %get-tuple-element.108.turn_c, ...), custom_call_target="tpu_custom_call" | custom-call | flops 6249999872 | bytes 1 | tf_op jit(solution)/shard_map/pallas_call | solution.py:191
  57.7 3.8 %collective-permute-done = bf16[16,16,1536]{2,1,0:T(8,128)(2,1)S(1)} collective-permute-done((bf16[16,16,1536]{2,1,0:T(8,128)(2,1)}, bf16[16,16,1536]{2,1,0:T(8,128)(2,1)S(1)}, u32[]{:S(2)}, u32[]{:S(2)}) %collective-permute-start) | collective-permute-done | bytes 786464 | tf_op jit(solution)/shard_map/ppermute | solution.py:486
  61.6 3.2 pad_maximum_fusion.1
  64.7 11.2 %all-to-all-start.1 = ((bf16[16,16,4096]{2,1,0:T(8,128)(2,1)}), bf16[16,16,4096]{2,1,0:T(8,128)(2,1)S(1)}, u32[]{:S(2)}, u32[]{:S(2)}) async-start(bf16[16,16,4096]{2,1,0:T(8,128)(2,1)} %pad_maximum_fusion.1), calls=%async_computation.1 | async-start | bytes 4194304 | tf_op jit(solution)/shard_map/all_to_all | solution.py:490
  75.9 3.1 collective-permute-start.1
  79.0 32.1 %shard_map.89 = (bf16[4,4,16,4096]{3,2,1,0:T(8,128)(2,1)}, bf16[4,4,16,4096]{3,2,1,0:T(8,128)(2,1)}, bf16[8,16,16,1024]{3,2,1,0:T(8,128)(2,1)}) custom-call(s32[1]{0:T(128)} %bitcast.6.row_block, bf16[2,128,126976]{2,1,0:T(8,128)(2,1)} %volts.5, f32[16,8,4096]{2,1,0:T(8,128)} %broadcast_in_dim.18.taps_wide, f32[8,512]{1,0:T(8,128)} %get-tuple-element.108.turn_c, ...), custom_call_target="tpu_custom_call" | custom-call | flops 10000000000 | bytes 1 | tf_op jit(solution)/shard_map/pallas_call | solution.py:191
  111.1 20.6 %collective-permute-done.1 = bf16[16,16,2560]{2,1,0:T(8,128)(2,1)S(1)} collective-permute-done((bf16[16,16,2560]{2,1,0:T(8,128)(2,1)}, bf16[16,16,2560]{2,1,0:T(8,128)(2,1)S(1)}, u32[]{:S(2)}, u32[]{:S(2)}) %collective-permute-start.1) | collective-permute-done | bytes 1310752 | tf_op jit(solution)/shard_map/ppermute | solution.py:486
  131.7 4.4 %pad_maximum_fusion = bf16[16,16,6656]{2,1,0:T(8,128)(2,1)} fusion(bf16[16,16,4096]{2,1,0:T(8,128)(2,1)} %bitcast.32, bf16[16,16,2560]{2,1,0:T(8,128)(2,1)S(1)} %collective-permute-done.1), kind=kLoop, calls=%fused_computation | loop fusion | flops 6815744 | bytes 6815744 | tf_op jit(solution)/shard_map/concatenate | solution.py:489
  136.1 8.6 %all-to-all-start.2 = ((bf16[16,16,6656]{2,1,0:T(8,128)(2,1)}), bf16[16,16,6656]{2,1,0:T(8,128)(2,1)S(1)}, u32[]{:S(2)}, u32[]{:S(2)}) async-start(bf16[16,16,6656]{2,1,0:T(8,128)(2,1)} %pad_maximum_fusion), calls=%async_computation.2 | async-start | bytes 6815744 | tf_op jit(solution)/shard_map/all_to_all | solution.py:490
  145.2 1.2 reduce-window.6
  147.6 1.1 reshape.386
  150.0 2.1 collective-permute-start.2
  152.1 2.2 add_select_fusion.1.row_branch
  155.2 3.9 %fusion.9 = (f32[1280,128]{1,0:T(8,128)}, f32[1280,128]{1,0:T(8,128)}) fusion(s32[1280]{0:T(1024)S(1)} %fusion.31), kind=kLoop, calls=%fused_computation.23 | loop fusion | flops 2293760 | bytes 1315840 | tf_op jit(solution)/shard_map/sin | solution.py:32
  159.1 5.1 %sine_multiply_fusion = (f32[1280,4]{1,0:T(8,128)}, f32[1280,4]{1,0:T(8,128)}) fusion(f32[1280,4]{1,0:T(8,128)} %copy.21, f32[1280]{0:T(1024)S(1)} %mul.364), kind=kLoop, calls=%fused_computation.20 | loop fusion | flops 15360 | bytes 66560 | tf_op jit(solution)/shard_map/mul | solution.py:250
  164.3 19.6 %shard_map.90 = (bf16[16,40,512]{2,1,0:T(8,128)(2,1)}, bf16[16,40,512]{2,1,0:T(8,128)(2,1)}) custom-call(s32[1280,1]{1,0:T(8,128)} %add_select_fusion.1.row_branch, f32[1280,4]{1,0:T(8,128)} %get-tuple-element.95.hi_c, f32[1280,4]{1,0:T(8,128)} %get-tuple-element.94.hi_s, f32[1280,128]{1,0:T(8,128)} %get-tuple-element.97.lo_c, ...), custom_call_target="tpu_custom_call" | custom-call | flops 10000000000 | bytes 1 | tf_op jit(solution)/shard_map/pallas_call | solution.py:257
  183.9 55.0 %collective-permute-done.2 = bf16[16,16,4096]{2,1,0:T(8,128)(2,1)} collective-permute-done((bf16[16,16,4096]{2,1,0:T(8,128)(2,1)}, bf16[16,16,4096]{2,1,0:T(8,128)(2,1)}, u32[]{:S(2)}, u32[]{:S(2)}) %collective-permute-start.2) | collective-permute-done | bytes 2097184 | tf_op jit(solution)/shard_map/ppermute | solution.py:486
  238.9 1.8 copy-done
  240.7 9.2 %all-to-all-start.3 = ((bf16[16,16,4096]{2,1,0:T(8,128)(2,1)}), bf16[16,16,4096]{2,1,0:T(8,128)(2,1)}, u32[]{:S(2)}, u32[]{:S(2)}) async-start(bf16[16,16,4096]{2,1,0:T(8,128)(2,1)} %collective-permute-done.2), calls=%async_computation.3 | async-start | bytes 4194304 | tf_op jit(solution)/shard_map/all_to_all | solution.py:490
  249.9 2.2 collective-permute-start.3
  252.1 12.3 %shard_map.91.weight = bf16[20,512,256]{2,1,0:T(8,128)(2,1)} custom-call(s32[20]{0:T(128)} %dynamic_slice.3.channel, f32[256,256]{1,0:T(8,128)} %delays.1, f32[256,256]{1,0:T(8,128)} %gains.1), custom_call_target="tpu_custom_call" | custom-call | flops 1 | bytes 1 | tf_op jit(solution)/shard_map/pallas_call | solution.py:374
  264.5 26.1 %collective-permute-done.3 = bf16[16,40,512]{2,1,0:T(8,128)(2,1)S(1)} collective-permute-done((bf16[16,40,512]{2,1,0:T(8,128)(2,1)}, bf16[16,40,512]{2,1,0:T(8,128)(2,1)S(1)}, u32[]{:S(2)}, u32[]{:S(2)}) %collective-permute-start.3) | collective-permute-done | bytes 655392 | tf_op jit(solution)/shard_map/ppermute | solution.py:486
  290.6 1.2 pad_maximum_fusion.2
  291.8 5.6 %all-to-all-start.4 = ((bf16[16,80,512]{2,1,0:T(8,128)(2,1)}), bf16[16,80,512]{2,1,0:T(8,128)(2,1)S(1)}, u32[]{:S(2)}, u32[]{:S(2)}) async-start(bf16[16,80,512]{2,1,0:T(8,128)(2,1)} %pad_maximum_fusion.2), calls=%async_computation.4 | async-start | bytes 2621440 | tf_op jit(solution)/shard_map/all_to_all | solution.py:490
  297.7 1.2 compare_convert_fusion.choose
  298.9 17.2 %shard_map.92 = f32[2,1024,1024]{2,1,0:T(8,128)} custom-call(s32[1]{0:T(128)} %bitcast.here_ref, bf16[16,16,1536]{2,1,0:T(8,128)(2,1)} %copy-done.3, bf16[16,16,4096]{2,1,0:T(8,128)(2,1)} %copy-done.1, bf16[16,16,4096]{2,1,0:T(8,128)(2,1)} %copy-done.1, bf16[16,16,6656]{2,1,0:T(8,128)(2,1)} %copy-done, bf16[16,16,6656]{2,1,0:T(8,128)(2,1)} %copy-done, ...), custom_call_target="tpu_custom_call" | custom-call | flops 1 | bytes 1 | tf_op jit(solution)/shard_map/pallas_call | solution.py:336
  317.8 8.9 %shard_map.93 = f32[1,20,2,16,512]{4,3,2,1,0:T(8,128)} custom-call(bf16[16,80,512]{2,1,0:T(8,128)(2,1)} %copy-done.2, bf16[1024,512]{1,0:T(8,128)(2,1)} %compare_convert_fusion.choose, bf16[20,512,256]{2,1,0:T(8,128)(2,1)} %shard_map.91.weight), custom_call_target="tpu_custom_call" | custom-call | flops 1 | bytes 1 | tf_op jit(solution)/shard_map/pallas_call | solution.py:444
  (68 shorter events, 8.6 us)
Async XLA Ops:
  0.6 5.6 %copy-start.5 = (f32[16,4096]{1,0:T(8,128)S(1)}, f32[16,4096]{1,0:T(8,128)}, u32[]{:S(2)}) copy-start(f32[16,4096]{1,0:T(8,128)} %param.8) | copy-start | bytes 786436
  24.7 36.9 %all-to-all-start = ((bf16[16,16,1536]{2,1,0:T(8,128)(2,1)}), bf16[16,16,1536]{2,1,0:T(8,128)(2,1)S(1)}, u32[]{:S(2)}, u32[]{:S(2)}) async-start(bf16[16,16,1536]{2,1,0:T(8,128)(2,1)} %bitcast.34), calls=%async_computation | async-start | bytes 1572864 | tf_op jit(solution)/shard_map/all_to_all | solution.py:490
  31.0 30.6 %collective-permute-start = (bf16[16,16,1536]{2,1,0:T(8,128)(2,1)}, bf16[16,16,1536]{2,1,0:T(8,128)(2,1)S(1)}, u32[]{:S(2)}, u32[]{:S(2)}) collective-permute-start(bf16[16,16,1536]{2,1,0:T(8,128)(2,1)} %bitcast.40), channel_id=1, source_target_pairs={{0,24},{4,28},{8,16},{12,20},{16,8},{20,12},{24,0},{28,4},{1,25},{... | collective-permute-start | bytes 2359304 | tf_op jit(solution)/shard_map/ppermute | solution.py:486
  61.6 3.2 copy-start.3
  64.7 67.0 %all-to-all-start.1 = ((bf16[16,16,4096]{2,1,0:T(8,128)(2,1)}), bf16[16,16,4096]{2,1,0:T(8,128)(2,1)S(1)}, u32[]{:S(2)}, u32[]{:S(2)}) async-start(bf16[16,16,4096]{2,1,0:T(8,128)(2,1)} %pad_maximum_fusion.1), calls=%async_computation.1 | async-start | bytes 4194304 | tf_op jit(solution)/shard_map/all_to_all | solution.py:490
  75.9 55.8 %collective-permute-start.1 = (bf16[16,16,2560]{2,1,0:T(8,128)(2,1)}, bf16[16,16,2560]{2,1,0:T(8,128)(2,1)S(1)}, u32[]{:S(2)}, u32[]{:S(2)}) collective-permute-start(bf16[16,16,2560]{2,1,0:T(8,128)(2,1)} %bitcast.39), channel_id=1, source_target_pairs={{0,24},{4,28},{8,16},{12,20},{16,8},{20,12},{24,0},{28,4},{1,25},{... | collective-permute-start | bytes 3932168 | tf_op jit(solution)/shard_map/ppermute | solution.py:486
  131.7 4.4 %copy-start.1 = (bf16[16,16,4096]{2,1,0:T(8,128)(2,1)}, bf16[16,16,4096]{2,1,0:T(8,128)(2,1)S(1)}, u32[]{:S(2)}) copy-start(bf16[16,16,4096]{2,1,0:T(8,128)(2,1)S(1)} %all-to-all-done.1.refs_1_.refs_2_) | copy-start | bytes 6291460
  136.1 9.1 %copy-start.7 = (s32[384,1]{0,1:T(1,128)S(1)}, s32[384,1]{0,1:T(1,128)}, u32[]{:S(2)}) copy-start(s32[384,1]{0,1:T(1,128)} %param.13) | copy-start | bytes 4612
  136.1 10.9 %copy-start.6 = (s32[384]{0:T(512)S(1)}, s32[384]{0:T(512)}, u32[]{:S(2)}) copy-start(s32[384]{0:T(512)} %param.9) | copy-start | bytes 4612
  136.1 102.7 %all-to-all-start.2 = ((bf16[16,16,6656]{2,1,0:T(8,128)(2,1)}), bf16[16,16,6656]{2,1,0:T(8,128)(2,1)S(1)}, u32[]{:S(2)}, u32[]{:S(2)}) async-start(bf16[16,16,6656]{2,1,0:T(8,128)(2,1)} %pad_maximum_fusion), calls=%async_computation.2 | async-start | bytes 6815744 | tf_op jit(solution)/shard_map/all_to_all | solution.py:490
  150.0 88.9 %collective-permute-start.2 = (bf16[16,16,4096]{2,1,0:T(8,128)(2,1)}, bf16[16,16,4096]{2,1,0:T(8,128)(2,1)}, u32[]{:S(2)}, u32[]{:S(2)}) collective-permute-start(bf16[16,16,4096]{2,1,0:T(8,128)(2,1)} %bitcast.38), channel_id=1, source_target_pairs={{0,24},{4,28},{8,16},{12,20},{16,8},{20,12},{24,0},{28,4},{1,25},{... | collective-permute-start | bytes 6291464 | tf_op jit(solution)/shard_map/ppermute | solution.py:486
  238.9 1.8 copy-start
  240.7 49.9 %all-to-all-start.3 = ((bf16[16,16,4096]{2,1,0:T(8,128)(2,1)}), bf16[16,16,4096]{2,1,0:T(8,128)(2,1)}, u32[]{:S(2)}, u32[]{:S(2)}) async-start(bf16[16,16,4096]{2,1,0:T(8,128)(2,1)} %collective-permute-done.2), calls=%async_computation.3 | async-start | bytes 4194304 | tf_op jit(solution)/shard_map/all_to_all | solution.py:490
  249.9 40.7 %copy-start.4 = (bf16[16,40,512]{2,1,0:T(8,128)(2,1)S(1)}, bf16[16,40,512]{2,1,0:T(8,128)(2,1)}, u32[]{:S(2)}) copy-start(bf16[16,40,512]{2,1,0:T(8,128)(2,1)} %get-tuple-element.80) | copy-start | bytes 1966084
  249.9 40.6 %collective-permute-start.3 = (bf16[16,40,512]{2,1,0:T(8,128)(2,1)}, bf16[16,40,512]{2,1,0:T(8,128)(2,1)S(1)}, u32[]{:S(2)}, u32[]{:S(2)}) collective-permute-start(bf16[16,40,512]{2,1,0:T(8,128)(2,1)} %get-tuple-element.76), channel_id=1, source_target_pairs={{0,24},{4,28},{8,16},{12,20},{16,8},{20,12},{24,0},{28,4},{1,25},{... | collective-permute-start | bytes 1966088 | tf_op jit(solution)/shard_map/ppermute | solution.py:486
  264.5 33.2 %copy-start.8 = (s32[256]{0:T(256)S(1)}, s32[256]{0:T(256)}, u32[]{:S(2)}) copy-start(s32[256]{0:T(256)} %param.10) | copy-start | bytes 3076
  291.8 24.9 %all-to-all-start.4 = ((bf16[16,80,512]{2,1,0:T(8,128)(2,1)}), bf16[16,80,512]{2,1,0:T(8,128)(2,1)S(1)}, u32[]{:S(2)}, u32[]{:S(2)}) async-start(bf16[16,80,512]{2,1,0:T(8,128)(2,1)} %pad_maximum_fusion.2), calls=%async_computation.4 | async-start | bytes 2621440 | tf_op jit(solution)/shard_map/all_to_all | solution.py:490
  316.7 1.1 copy-start.2

commit v7 on v6

v7 whole, which is shorter than its diff:
```python
import functools
import math

import jax
import jax.numpy as jnp
import numpy as np
from jax import lax
from jax.experimental import pallas as pl
from jax.experimental.pallas import tpu as pltpu
from jax.sharding import PartitionSpec as P

NCH = 4096
FRAMES = 16
SLOTS = 160
RADIX = 8
LANES = 128
ROWS = 16
EARLY = 4
VMEM = 56 * 1024 * 1024

NO_COST = pl.CostEstimate(flops=1, bytes_accessed=1, transcendentals=0)

TWO_PI = 2.0 * math.pi
NT = (((1,), (1,)), ((), ()))


def busy(share):
    return pl.CostEstimate(flops=int(share * 1e10), bytes_accessed=1, transcendentals=0)


def phase(turns, length):
    angles = (turns % length).astype(jnp.float32) * (TWO_PI / length)
    return jnp.cos(angles), jnp.sin(angles)


def transform_tables():
    depth = NCH // RADIX
    ids = np.arange(depth)
    angles = 2 * np.pi / depth * (ids[:, None] * ids[None, :] % depth)
    turns = 2 * np.pi / NCH * (np.arange(RADIX)[:, None] * ids[None, :])
    scale = 1.0 / math.sqrt(NCH)
    both = (np.cos(angles) * scale, np.sin(angles) * scale, np.cos(turns), np.sin(turns))
    return [jnp.asarray(x.astype(np.float32)) for x in both]


def radix8(re, im):
    half = math.sqrt(0.5)

    def four(xr, xi):
        ar, ai, br, bi = xr[0] + xr[2], xi[0] + xi[2], xr[0] - xr[2], xi[0] - xi[2]
        cr, ci, dr, di = xr[1] + xr[3], xi[1] + xi[3], xr[1] - xr[3], xi[1] - xi[3]
        return [ar + cr, br + di, ar - cr, br - di], [ai + ci, bi - dr, ai - ci, bi + dr]

    er, ei = four(re[0::2], im[0::2])
    odd_r, odd_i = four(re[1::2], im[1::2])
    tr = [odd_r[0], (odd_r[1] + odd_i[1]) * half, odd_i[2], (odd_i[3] - odd_r[3]) * half]
    ti = [odd_i[0], (odd_i[1] - odd_r[1]) * half, -odd_r[2], (odd_r[3] + odd_i[3]) * -half]
    return (
        [e + t for e, t in zip(er, tr)] + [e - t for e, t in zip(er, tr)],
        [e + t for e, t in zip(ei, ti)] + [e - t for e, t in zip(ei, ti)],
    )


def swap_blocks(parts, lane_ids):
    count = len(parts)
    width = LANES // count
    parts = list(parts)
    step = 1
    while step < count:
        keep = (lane_ids // width) % (2 * step) < step
        for b in range(count):
            if b & step == 0:
                low, high = parts[b], parts[b + step]
                parts[b] = jnp.where(keep, low, pltpu.roll(high, step * width, 1))
                parts[b + step] = jnp.where(keep, pltpu.roll(low, LANES - step * width, 1), high)
        step *= 2
    return parts


def gather_blocks(parts, lane_ids):
    count = len(parts)
    width = LANES // count
    turned = [parts[0]] + [pltpu.roll(parts[b], b * width, 1) for b in range(1, count)]
    turned = [turned[-b % count] for b in range(count)]
    step = 1
    while step < count:
        moved = (lane_ids // width) & step != 0
        turned = [jnp.where(moved, turned[(g - step) % count], turned[g]) for g in range(count)]
        step *= 2
    return [turned[0]] + [pltpu.roll(turned[g], LANES - g * width, 1) for g in range(1, count)]


def channel_kernel(first, row_block, volts, prototype, cosines, sines, turn_c, turn_s, out, branches, *scratch):
    taps_wide, table, filtered, product = scratch
    taps = taps_wide.shape[0]
    length = taps_wide.shape[2]
    frames = filtered.shape[2]
    depth = length // RADIX
    bands = depth // LANES
    for t in range(taps):
        taps_wide[t] = jnp.broadcast_to(prototype[t : t + 1, :], taps_wide.shape[1:])
    cos_t, sin_t = cosines[...].astype(table.dtype), sines[...].astype(table.dtype)
    table[:depth, :depth] = cos_t
    table[:depth, depth:] = -sin_t
    table[depth:, :depth] = sin_t
    table[depth:, depth:] = cos_t

    def column(j, carry):
        lane = pl.multiple_of(j * LANES, LANES)

        def strip(n1, inner):
            base = pl.multiple_of(n1 * depth + j * LANES, LANES)
            for part in range(2):
                sums = [None] * frames
                for seg in range(frames + taps - 1):
                    start = pl.multiple_of((first + seg) * length + base, LANES)
                    value = volts[part, :, pl.ds(start, LANES)].astype(jnp.float32)
                    for f in range(max(0, seg - taps + 1), min(frames, seg + 1)):
                        coef = taps_wide[seg - f, :, pl.ds(base, LANES)]
                        term = value * jnp.concatenate([coef, coef], axis=0)
                        sums[f] = term if sums[f] is None else sums[f] + term
                    if seg >= taps - 1:
                        filtered[part, n1, seg - taps + 1] = sums[seg - taps + 1]
            return inner

        lax.fori_loop(0, RADIX, strip, 0)

        def butterfly(f, inner):
            re, im = radix8(
                [filtered[0, n1, f] for n1 in range(RADIX)],
                [filtered[1, n1, f] for n1 in range(RADIX)],
            )
            for b in range(RADIX):
                turned_r, turned_i = re[b], im[b]
                if b > 0:
                    cos_t, sin_t = turn_c[b : b + 1, pl.ds(lane, LANES)], turn_s[b : b + 1, pl.ds(lane, LANES)]
                    turned_r, turned_i = re[b] * cos_t + im[b] * sin_t, im[b] * cos_t - re[b] * sin_t
                branches[b, f, :, pl.ds(lane, LANES)] = turned_r.astype(branches.dtype)
                branches[b, f, :, pl.ds(pl.multiple_of(depth + lane, LANES), LANES)] = turned_i.astype(branches.dtype)
            return inner

        lax.fori_loop(0, frames, butterfly, 0)
        return carry

    lax.fori_loop(0, bands, column, 0)

    def multiply(b, carry):
        rows = branches[b].reshape(frames * ROWS, 2 * depth)
        product[b] = jnp.dot(rows, table[...], preferred_element_type=jnp.float32)
        return carry

    lax.fori_loop(0, RADIX, multiply, 0)
    lane_ids = lax.broadcasted_iota(jnp.int32, (ROWS, LANES), 1)

    def regroup(f, carry):
        top = pl.multiple_of(f * ROWS, ROWS)
        for part in range(2):
            for band in range(bands):
                lane = part * depth + band * LANES
                pieces = [product[b, pl.ds(top, ROWS), lane : lane + LANES] for b in range(RADIX)]
                for g, piece in enumerate(gather_blocks(pieces, lane_ids)):
                    at = pl.multiple_of((part * frames + f) * LANES, LANES)
                    out[g, band, :, pl.ds(at, LANES)] = piece.astype(out.dtype)
        return carry

    lax.fori_loop(0, frames, regroup, 0)


def channelise(row_block, volts, prototype, tables, first, frames):
    taps = prototype.shape[0]
    length = volts.shape[2] if first > 0 else (frames + taps - 1) * NCH
    depth = NCH // RADIX
    bands = depth // LANES
    wide = 2 * frames * LANES
    return pl.pallas_call(
        functools.partial(channel_kernel, first),
        grid_spec=pltpu.PrefetchScalarGridSpec(
            num_scalar_prefetch=1,
            grid=(1,),
            in_specs=[
                pl.BlockSpec((2, ROWS, length), lambda i, row: (0, row[0], 0)),
            ]
            + [pl.BlockSpec(x.shape, lambda i, row: (0, 0)) for x in (prototype, *tables)],
            out_specs=[
                pl.BlockSpec((RADIX, bands, ROWS, wide), lambda i, row: (0, 0, 0, 0)),
                pl.BlockSpec((RADIX, frames, ROWS, 2 * depth), lambda i, row: (0, 0, 0, 0)),
            ],
            scratch_shapes=[
                pltpu.VMEM((taps, 8, NCH), jnp.float32),
                pltpu.VMEM((2 * depth, 2 * depth), jnp.bfloat16),
                pltpu.VMEM((2, RADIX, frames, ROWS, LANES), jnp.float32),
                pltpu.VMEM((RADIX, frames * ROWS, 2 * depth), jnp.float32),
            ],
        ),
        out_shape=[
            jax.ShapeDtypeStruct((RADIX, bands, ROWS, wide), jnp.bfloat16),
            jax.ShapeDtypeStruct((RADIX, frames, ROWS, 2 * depth), jnp.bfloat16),
        ],
        compiler_params=pltpu.CompilerParams(vmem_limit_bytes=VMEM),
        cost_estimate=busy(frames / FRAMES),
    )(row_block, volts, prototype, *tables)


def slot_kernel(row_branch, hi_c, hi_s, lo_c, lo_s, *rest):
    chunks, (out, table, total) = rest[:-3], rest[-3:]
    depth = chunks[0].shape[3] // 2
    for a in range(hi_c.shape[1]):
        high_c, high_s = hi_c[:, a : a + 1], hi_s[:, a : a + 1]
        table[:, a * LANES : (a + 1) * LANES] = (high_c * lo_c[...] - high_s * lo_s[...]).astype(table.dtype)
        table[:, depth + a * LANES : depth + (a + 1) * LANES] = (
            high_s * lo_c[...] + high_c * lo_s[...]
        ).astype(table.dtype)
    total[...] = jnp.zeros_like(total)

    def branch(b, carry):
        rows = jnp.concatenate([c[b].reshape(c.shape[1] * c.shape[2], c.shape[3]) for c in chunks], axis=0)
        got = lax.dot_general(table[...], rows, NT, preferred_element_type=jnp.float32)
        total[...] = jnp.where(row_branch[...] == b, got, total[...])
        return carry

    lax.fori_loop(0, RADIX, branch, 0)
    per = out.shape[1]
    for d in range(out.shape[0]):
        out[d] = total[d * per : (d + 1) * per].astype(out.dtype)


def slot_tables(row_channel, row_filled, row_turned):
    depth = NCH // RADIX
    coarse = jnp.arange(depth // LANES, dtype=jnp.int32) * LANES
    fine = jnp.arange(LANES, dtype=jnp.int32)
    whole = row_channel - row_channel % RADIX
    hi_c, hi_s = phase(whole[:, None] * coarse[None, :] + row_turned[:, None] * (NCH // 4), NCH)
    lo_c, lo_s = phase(whole[:, None] * fine[None, :], NCH)
    scaling = row_filled.astype(jnp.float32)[:, None] * (1.0 / math.sqrt(NCH))
    return (row_channel % RADIX)[:, None], hi_c * scaling, hi_s * scaling, lo_c, lo_s


def slot_spectra(tables, chunks, per):
    rows = tables[0].shape[0]
    samples = sum(c.shape[1] * c.shape[2] for c in chunks)
    return pl.pallas_call(
        slot_kernel,
        out_shape=jax.ShapeDtypeStruct((rows // per, per, samples), jnp.bfloat16),
        scratch_shapes=[
            pltpu.VMEM((rows, chunks[0].shape[3]), jnp.bfloat16),
            pltpu.VMEM((rows, samples), jnp.float32),
        ],
        compiler_params=pltpu.CompilerParams(vmem_limit_bytes=VMEM),
        cost_estimate=busy(1),
    )(*tables, *chunks)


def correlate(pieces, halves, lanes):
    senders, sub, _ = pieces[0][0].shape
    half = FRAMES * lanes
    signals = senders * halves * sub
    count = max(1, signals // 256)
    each = senders // count
    block = each * halves * sub

    def kernel(*refs):
        parts, (out, held, turned, made, in_sems, out_sems) = refs[: len(pieces)], refs[len(pieces) :]
        coming = [[] for _ in range(count)]
        for index, (_, which, first, frames) in enumerate(pieces):
            for q in range(count):
                for part in range(2):
                    src = parts[index].at[pl.ds(q * each, each), :, pl.ds(part * frames * lanes, frames * lanes)]
                    dst = held.at[q, :, which, :, pl.ds(part * half + first * lanes, frames * lanes)]
                    sem = in_sems.at[(index * count + q) * 2 + part]
                    coming[q].append(pltpu.make_async_copy(src, dst, sem))
        for copies in coming:
            for copy in copies:
                copy.start()

        def rows_of(i):
            return pl.ds(i * block, block)

        inverse = 1.0 / half
        going = [[], []]
        slot = 0
        for i in range(count):
            for copy in coming[i]:
                copy.wait()
            left = held[i].reshape(block, 2 * half)
            turned[:, :half] = left[:, half:]
            turned[:, half:] = -left[:, :half]
            at_i = rows_of(i)
            for j in range(i + 1):
                right = held[j].reshape(block, 2 * half)
                at_j = rows_of(j)
                for copy in going[slot]:
                    copy.wait()
                going[slot] = []
                for part, rows in enumerate((left, turned[...])):
                    got = lax.dot_general(rows, right, NT, preferred_element_type=jnp.float32) * inverse
                    made[slot, part, 0] = got
                    going[slot].append(
                        pltpu.make_async_copy(
                            made.at[slot, part, 0], out.at[part, at_i, at_j], out_sems.at[slot, part, 0]
                        )
                    )
                    if i != j:
                        made[slot, part, 1] = got.T if part == 0 else -got.T
                        going[slot].append(
                            pltpu.make_async_copy(
                                made.at[slot, part, 1], out.at[part, at_j, at_i], out_sems.at[slot, part, 1]
                            )
                        )
                for copy in going[slot]:
                    copy.start()
                slot = 1 - slot
        for copies in going:
            for copy in copies:
                copy.wait()

    return pl.pallas_call(
        kernel,
        in_specs=[pl.BlockSpec(memory_space=pl.ANY)] * len(pieces),
        out_specs=pl.BlockSpec(memory_space=pl.ANY),
        out_shape=jax.ShapeDtypeStruct((2, signals, signals), jnp.float32),
        scratch_shapes=[
            pltpu.VMEM((count, each, halves, sub, 2 * half), jnp.bfloat16),
            pltpu.VMEM((block, 2 * half), jnp.bfloat16),
            pltpu.VMEM((2, 2, 2, block, block), jnp.float32),
            pltpu.SemaphoreType.DMA((2 * count * len(pieces),)),
            pltpu.SemaphoreType.DMA((2, 2, 2)),
        ],
        compiler_params=pltpu.CompilerParams(vmem_limit_bytes=VMEM),
        cost_estimate=NO_COST,
    )(*[piece[0] for piece in pieces])


def weight_kernel(channel, delays, gains, out):
    beams = delays.shape[0]
    turns = delays[...] * (channel[pl.program_id(0)].astype(jnp.float32) * (1.0 / NCH))
    part = turns - jnp.floor(turns + 0.5)
    square = part * part
    cos_t = jnp.full_like(part, TWO_PI**16 / math.factorial(16))
    sin_t = jnp.full_like(part, -(TWO_PI**15) / math.factorial(15))
    for power in range(14, -1, -2):
        sign = -1.0 if power % 4 == 2 else 1.0
        cos_t = cos_t * square + sign * TWO_PI**power / math.factorial(power)
        if power > 0:
            sign = -1.0 if (power - 1) % 4 == 3 else 1.0
            sin_t = sin_t * square + sign * TWO_PI ** (power - 1) / math.factorial(power - 1)
    scaled = gains[...] * (1.0 / math.sqrt(gains.shape[1]))
    out[0, :beams] = (scaled * cos_t).astype(out.dtype)
    out[0, beams:] = (-scaled * sin_t * part).astype(out.dtype)


def beam_weights(channel, delays, gains):
    beams, listed = delays.shape
    slots = channel.shape[0]
    return pl.pallas_call(
        weight_kernel,
        grid=(slots,),
        in_specs=[
            pl.BlockSpec(memory_space=pltpu.SMEM),
            pl.BlockSpec(delays.shape, lambda i: (0, 0)),
            pl.BlockSpec(gains.shape, lambda i: (0, 0)),
        ],
        out_specs=pl.BlockSpec((1, 2 * beams, listed), lambda i: (i, 0, 0)),
        out_shape=jax.ShapeDtypeStruct((slots, 2 * beams, listed), jnp.bfloat16),
        cost_estimate=NO_COST,
    )(channel, delays, gains)


def combine(spectra, chooser, weights, sub):
    slots, beams2, listed = weights.shape
    beams = beams2 // 2
    rows = 2 * slots
    senders = spectra.shape[0]
    halves = spectra.shape[2] // (FRAMES * sub)
    count = LANES // sub
    inner = senders // count
    groups = halves * inner
    tiles = 2 * listed // LANES

    def kernel(spectrum, choose, weight, out, ordered, picked):
        lane_ids = lax.broadcasted_iota(jnp.int32, (rows, LANES), 1)
        for h in range(halves):
            for q in range(inner):
                for t in range(FRAMES // count):
                    lane = h * FRAMES * sub + t * LANES
                    pieces = [
                        spectrum[q * count + i, :, lane : lane + LANES].astype(jnp.float32) for i in range(count)
                    ]
                    for f, piece in enumerate(swap_blocks(pieces, lane_ids)):
                        top = (t * count + f) * rows
                        ordered[h * inner + q, top : top + rows, :] = piece
        acc = None
        for q in range(groups):
            term = jnp.dot(
                ordered[q].astype(jnp.bfloat16),
                choose[q * LANES : (q + 1) * LANES, :],
                preferred_element_type=jnp.float32,
            )
            acc = term if acc is None else acc + term
        for lane in range(tiles):
            picked[lane] = acc[:, lane * LANES : (lane + 1) * LANES]
        for i in range(slots):
            chosen = [
                jnp.concatenate(
                    [
                        picked[p * tiles // 2 + lane, pl.ds(part * slots + i, FRAMES, rows), :]
                        for lane in range(tiles // 2)
                    ],
                    axis=1,
                )
                for p in range(2)
                for part in range(2)
            ]
            stacked = jnp.concatenate(chosen, axis=0).astype(jnp.bfloat16)
            mixed = lax.dot_general(stacked, weight[i], NT, preferred_element_type=jnp.float32)
            for p in range(2):
                at = 2 * FRAMES * p
                of_re, of_im = mixed[at : at + FRAMES], mixed[at + FRAMES : at + 2 * FRAMES]
                out[0, i, 0, :, p * beams : (p + 1) * beams] = of_re[:, :beams] - of_im[:, beams:]
                out[0, i, 1, :, p * beams : (p + 1) * beams] = of_im[:, :beams] + of_re[:, beams:]

    return pl.pallas_call(
        kernel,
        out_shape=jax.ShapeDtypeStruct((1, slots, 2, FRAMES, 2 * beams), jnp.float32),
        scratch_shapes=[
            pltpu.VMEM((groups, FRAMES * rows, LANES), jnp.float32),
            pltpu.VMEM((tiles, FRAMES * rows, LANES), jnp.float32),
        ],
        compiler_params=pltpu.CompilerParams(vmem_limit_bytes=VMEM),
        cost_estimate=NO_COST,
    )(spectra, chooser, weights)


def body(volts, prototype, beam_channels, station_index, delays, gains, assign):
    sig_dev = volts.shape[1]
    st_count, sb_count = lax.axis_size("st"), lax.axis_size("sb")
    st_here, sb_here = lax.axis_index("st").astype(jnp.int32), lax.axis_index("sb").astype(jnp.int32)
    devices = st_count * sb_count
    group = NCH // devices
    fine = group // RADIX
    constants = transform_tables()
    barrier = lax.optimization_barrier

    def exchange(x):
        return lax.all_to_all(x, ("st", "sb"), split_axis=0, concat_axis=0, tiled=True)

    share = sig_dev // sb_count
    sub = min(share, ROWS)
    halves = max(1, share // ROWS)
    inside = (sb_here * share) % ROWS
    unit = max(1, LANES // group)
    early = max(unit, EARLY // unit * unit)
    plan = [(0, 0, early), (0, early, FRAMES - early)] + [(h, 0, FRAMES) for h in range(1, halves)]

    def channels_of(c, here):
        which, first, frames = plan[c]
        row_block = (here * share // ROWS + which)[None]
        out, kept = channelise(row_block, volts, prototype, constants, first, frames)
        if sub < ROWS:
            out = lax.dynamic_slice_in_dim(out, inside, sub, axis=2)
        inner = st_count // RADIX
        if inner > 1:
            out = out.reshape(RADIX, sb_count, sub, 2 * frames, RADIX, inner, fine).transpose(0, 5, 1, 2, 3, 4, 6)
        return out.reshape(devices, sub, -1), kept

    lists = (assign, beam_channels, station_index)
    here = sb_here
    out, kept = channels_of(0, here)
    branches, arrived = [kept], []
    for c in range(1, len(plan)):
        out, here, lists, arrived[-1:] = barrier((out, here, lists, arrived[-1:]))
        arrived.append(exchange(out))
        out, kept = channels_of(c, here)
        branches.append(kept)

    assign, beam_channels, station_index = barrier((lists, kept))[0]
    per_dev = SLOTS // st_count
    owners = assign[:, 0]
    taken = (owners[:, None] == jnp.arange(sb_count, dtype=jnp.int32)[None, :]).astype(jnp.int32)
    position = jnp.sum(taken * jnp.cumsum(taken, axis=0), axis=1) - 1
    place = owners * SLOTS + position
    slot_ids = (
        jnp.arange(st_count, dtype=jnp.int32)[:, None, None] * per_dev
        + jnp.arange(sb_count, dtype=jnp.int32)[:, None] * SLOTS
        + jnp.arange(per_dev, dtype=jnp.int32)
    ).reshape(-1)
    picker = (place[None, :] == slot_ids[:, None]).astype(jnp.int32)
    filled = jnp.sum(picker, axis=1)
    slot_channel = jnp.sum(picker * beam_channels[None, :], axis=1)

    def by_row(values):
        return jnp.broadcast_to(values.reshape(devices, 1, per_dev), (devices, 2, per_dev)).reshape(-1)

    turned = jnp.broadcast_to(jnp.arange(2, dtype=jnp.int32)[None, :, None], (devices, 2, per_dev)).reshape(-1)
    mine = lax.dynamic_slice_in_dim(slot_channel, (st_here * sb_count + sb_here) * per_dev, per_dev)
    tables = slot_tables(by_row(slot_channel), by_row(filled), turned)
    spectra = slot_spectra(tables, branches, 2 * per_dev)
    if sub < ROWS:
        spectra = spectra.reshape(devices, 2 * per_dev, FRAMES, ROWS)
        spectra = lax.dynamic_slice_in_dim(spectra, inside, sub, axis=3).reshape(devices, 2 * per_dev, -1)

    out, spectra, mine, arrived[-1:] = barrier((out, spectra, mine, arrived[-1:]))
    arrived.append(exchange(out))
    weights = beam_weights(mine, delays, gains)
    signal_ids = (
        jnp.arange(halves, dtype=jnp.int32)[:, None, None] * sub
        + jnp.arange(devices, dtype=jnp.int32)[:, None] * share
        + jnp.arange(sub, dtype=jnp.int32)
    ).reshape(-1)
    wanted = (station_index[None, :] * 2 + jnp.arange(2, dtype=jnp.int32)[:, None]).reshape(-1)
    chooser = (signal_ids[:, None] == wanted[None, :]).astype(jnp.bfloat16)

    spectra, weights, chooser, arrived[-1:] = barrier((spectra, weights, chooser, arrived[-1:]))
    slot_received = exchange(spectra)
    if halves == 1:
        arrived = [x.reshape(-1, min(256, devices * sub), x.shape[2]) for x in arrived]
    visibility = correlate([(x, *part) for x, part in zip(arrived, plan)], halves, group)
    signals = visibility.shape[1]
    beam_out = combine(slot_received, chooser, weights, sub)
    return (visibility.reshape(2, 1, 1, signals, signals), beam_out)


def solution(mesh):
    in_specs = (P(None, "st", None), P(), P(), P(), P(), P(), P())
    out_specs = (P(None, "sb", "st", None, None), P("sb", "st", None, None, None))
    return jax.shard_map(body, mesh=mesh, in_specs=in_specs, out_specs=out_specs, check_vma=False)
```

time: 327 us -> 274 us (0.84)
  starting transfers between devices: 52.2 us -> 22.3 us
  other arithmetic: 26.4 us -> 14.9 us
  waiting for transfers between devices: 106 us -> 99 us
    ppermute x4 -> x0, waiting for transfers between devices: 106 us -> none  [cross(): return lax.ppermute(x, ('far', 'near'), pairs)]
    all_to_all x5 -> x4, waiting for transfers between devices: 0.61 us -> 99 us  [exchange(): lax.all_to_all(x, ('st', 'sb'), split_axis=0, concat_axis=0, tiled=True)]
    all_to_all x5 -> x4, starting transfers between devices: 40.9 us -> 22.3 us  [exchange(): lax.all_to_all(x, ('st', 'sb'), split_axis=0, concat_axis=0, tiled=True)]
    ppermute x4 -> x0, starting transfers between devices: 11.4 us -> none  [cross(): return lax.ppermute(x, ('far', 'near'), pairs)]
    concatenate x3 -> x0, other arithmetic: 8.74 us -> none  [in_plane(): joined = xs[0] if len(xs) == 1 else jnp.concatenate(xs, axis=axis)]
    pallas_call x3 -> x2, Pallas kernels: 39.5 us -> 36.8 us  [the longest x1 19.7 us: slot_spectra(): pl.pallas_call(slot_kernel, out_shape=jax.ShapeDtypeStruct((rows // per,...]
  transfers between devices with their start and end apart: 9 -> 4, of which waited for: 5 -> 4; matrix products, arithmetic and copies ran while one was open for 6% -> 7% of each run, Pallas kernels for 32% -> 39%
where the time goes in v7:
time: 274 us; the launch traced here: 273 us
  Pallas kernels  129 us (47%)
  waiting for transfers between devices  99 us (36%)
  starting transfers between devices  22.3 us (8%)
  other arithmetic  14.9 us (5%)
  local copies, waits for them, and re-layouts  7.74 us (3%)
    all_to_all x4, waiting for transfers between devices, exchange(): lax.all_to_all(x, ('st', 'sb'), split_axis=0, concat_axis=0, tiled=True)  99 us
    pallas_call x3, Pallas kernels, channelise(): pl.pallas_call(functools.partial(channel_kernel, first), grid_spec=pltpu....  70.5 us
    all_to_all x4, starting transfers between devices, exchange(): lax.all_to_all(x, ('st', 'sb'), split_axis=0, concat_axis=0, tiled=True)  22.3 us
    pallas_call x1, Pallas kernels, slot_spectra(): pl.pallas_call(slot_kernel, out_shape=jax.ShapeDtypeStruct((rows // per,...  19.7 us
    pallas_call x1, Pallas kernels, correlate(): pl.pallas_call(kernel, in_specs=[pl.BlockSpec(memory_space=pl.ANY)] * len...  17.2 us
    pallas_call x1, Pallas kernels, beam_weights(): pl.pallas_call(weight_kernel, grid=(slots,), in_specs=[pl.BlockSpec(memor...  12.4 us
    pallas_call x1, Pallas kernels, combine(): pl.pallas_call(kernel, out_shape=jax.ShapeDtypeStruct((1, slots, 2, FRAME...  8.89 us
  transfers between devices with their start and end apart: 4, of which 4 were waited for; matrix products, arithmetic and copies ran while one was open for 7% of the time, Pallas kernels for 39%

profile of v7, /device:TPU:0, one launch (start us, length us, event | category | flops | bytes accessed | tf_op | source)
XLA Modules:
  0.0 273.4 jit_solution(9637766446969355649)
XLA Ops:
  0.6 13.6 %shard_map.122 = (bf16[8,4,16,1024]{3,2,1,0:T(8,128)(2,1)}, bf16[8,4,16,1024]{3,2,1,0:T(8,128)(2,1)}) custom-call(s32[1]{0:T(128)} %bitcast.row_block, bf16[2,128,126976]{2,1,0:T(8,128)(2,1)} %volts.5, f32[16,4096]{1,0:T(8,128)} %prototype.5, f32[512,512]{1,0:T(8,128)} %constant.120.clone.cosines, f32[512,512]{1,0:T(8,128)} %constant.121.clone.sines, ...), custom_call_target="tpu_custom_call" | custom-call | flops 2500000000 | bytes 1 | tf_op jit(solution)/shard_map/pallas_call | solution.py:175
  14.2 7.3 %all-to-all-start = ((bf16[32,16,1024]{2,1,0:T(8,128)(2,1)}), bf16[32,16,1024]{2,1,0:T(8,128)(2,1)S(1)}, u32[]{:S(2)}, u32[]{:S(2)}) async-start(bf16[32,16,1024]{2,1,0:T(8,128)(2,1)} %bitcast.31), calls=%async_computation | async-start | bytes 2097152 | tf_op jit(solution)/shard_map/all_to_all | solution.py:444
  21.6 25.3 %shard_map.123 = (bf16[8,4,16,3072]{3,2,1,0:T(8,128)(2,1)}, bf16[8,12,16,1024]{3,2,1,0:T(8,128)(2,1)}) custom-call(s32[1]{0:T(128)} %bitcast.2.row_block, bf16[2,128,126976]{2,1,0:T(8,128)(2,1)} %volts.5, f32[16,4096]{1,0:T(8,128)} %prototype.5, f32[512,512]{1,0:T(8,128)} %constant.120.clone.cosines, f32[512,512]{1,0:T(8,128)} %constant.121.clone.sines, ...), custom_call_target="tpu_custom_call" | custom-call | flops 7500000256 | bytes 1 | tf_op jit(solution)/shard_map/pallas_call | solution.py:175
  46.9 0.9 all-to-all-done.refs_0_
  47.8 1.0 copy-done.2
  48.8 4.9 %all-to-all-start.1 = ((bf16[32,16,3072]{2,1,0:T(8,128)(2,1)}), bf16[32,16,3072]{2,1,0:T(8,128)(2,1)S(1)}, u32[]{:S(2)}, u32[]{:S(2)}) async-start(bf16[32,16,3072]{2,1,0:T(8,128)(2,1)} %bitcast.30), calls=%async_computation.1 | async-start | bytes 6291456 | tf_op jit(solution)/shard_map/all_to_all | solution.py:444
  53.9 0.1 add.168
  54.0 0.1 mul.187
  54.2 31.6 %shard_map.124 = (bf16[8,4,16,4096]{3,2,1,0:T(8,128)(2,1)}, bf16[8,16,16,1024]{3,2,1,0:T(8,128)(2,1)}) custom-call(s32[1]{0:T(128)} %bitcast.4.row_block, bf16[2,128,126976]{2,1,0:T(8,128)(2,1)} %volts.5, f32[16,4096]{1,0:T(8,128)} %prototype.5, f32[512,512]{1,0:T(8,128)} %constant.120.clone.cosines, f32[512,512]{1,0:T(8,128)} %constant.121.clone.sines, ...), custom_call_target="tpu_custom_call" | custom-call | flops 10000000000 | bytes 1 | tf_op jit(solution)/shard_map/pallas_call | solution.py:175
  85.8 1.2 reduce-window.6
  87.0 0.2 slice_reduce_fusion
  87.2 0.2 reduce-window.9
  87.5 0.4 fusion.1
  88.1 0.1 reshape.276
  88.2 1.1 reshape.278
  89.4 1.1 copy.25
  90.8 0.7 dynamic_slice.3.channel
  91.5 2.2 add_select_fusion.1.row_branch
  93.6 3.9 %fusion.9 = (f32[1280,128]{1,0:T(8,128)}, f32[1280,128]{1,0:T(8,128)}) fusion(s32[1280]{0:T(1024)S(1)} %fusion.14), kind=kLoop, calls=%fused_computation.20 | loop fusion | flops 2293760 | bytes 1315840 | tf_op jit(solution)/shard_map/sin | solution.py:33
  97.5 5.2 %sine_multiply_fusion = (f32[1280,4]{1,0:T(8,128)}, f32[1280,4]{1,0:T(8,128)}) fusion(f32[1280,4]{1,0:T(8,128)} %copy.25, f32[1280]{0:T(1024)S(1)} %mul.193), kind=kLoop, calls=%fused_computation.17 | loop fusion | flops 15360 | bytes 66560 | tf_op jit(solution)/shard_map/mul | solution.py:235
  102.7 19.7 %shard_map.125 = bf16[32,40,512]{2,1,0:T(8,128)(2,1)} custom-call(s32[1280,1]{1,0:T(8,128)} %add_select_fusion.1.row_branch, f32[1280,4]{1,0:T(8,128)} %get-tuple-element.69.hi_c, f32[1280,4]{1,0:T(8,128)} %get-tuple-element.68.hi_s, f32[1280,128]{1,0:T(8,128)} %get-tuple-element.71.lo_c, f32[1280,128]{1,0:T(8,128)} %get-tuple-element.70.lo_s, ...), custom_call_target="tpu_custom_call" | custom-call | flops 10000000000 | bytes 1 | tf_op jit(solution)/shard_map/pallas_call | solution.py:241
  122.4 3.1 %all-to-all-done.1.refs_1_ = bf16[32,16,3072]{2,1,0:T(8,128)(2,1)S(1)} async-done(((bf16[32,16,3072]{2,1,0:T(8,128)(2,1)}), bf16[32,16,3072]{2,1,0:T(8,128)(2,1)S(1)}, u32[]{:S(2)}, u32[]{:S(2)}) %all-to-all-start.1) | async-done | bytes 3145760 | tf_op jit(solution)/shard_map/all_to_all | solution.py:444
  125.5 1.7 copy-done
  127.2 4.6 %all-to-all-start.2 = ((bf16[32,16,4096]{2,1,0:T(8,128)(2,1)}), bf16[32,16,4096]{2,1,0:T(8,128)(2,1)}, u32[]{:S(2)}, u32[]{:S(2)}) async-start(bf16[32,16,4096]{2,1,0:T(8,128)(2,1)} %bitcast.29), calls=%async_computation.2 | async-start | bytes 8388608 | tf_op jit(solution)/shard_map/all_to_all | solution.py:444
  132.1 1.2 compare_convert_fusion.choose
  133.4 12.4 %shard_map.126.weight = bf16[20,512,256]{2,1,0:T(8,128)(2,1)} custom-call(s32[20]{0:T(128)} %dynamic_slice.3.channel, f32[256,256]{1,0:T(8,128)} %delays.1, f32[256,256]{1,0:T(8,128)} %gains.1), custom_call_target="tpu_custom_call" | custom-call | flops 1 | bytes 1 | tf_op jit(solution)/shard_map/pallas_call | solution.py:354
  145.7 80.5 %all-to-all-done.2.refs_2_ = bf16[32,16,4096]{2,1,0:T(8,128)(2,1)} async-done(((bf16[32,16,4096]{2,1,0:T(8,128)(2,1)}), bf16[32,16,4096]{2,1,0:T(8,128)(2,1)}, u32[]{:S(2)}, u32[]{:S(2)}) %all-to-all-start.2) | async-done | bytes 4194336 | tf_op jit(solution)/shard_map/all_to_all | solution.py:444
  226.2 5.5 %all-to-all-start.3 = ((bf16[32,40,512]{2,1,0:T(8,128)(2,1)}), bf16[32,40,512]{2,1,0:T(8,128)(2,1)S(1)}, u32[]{:S(2)}, u32[]{:S(2)}) async-start(bf16[32,40,512]{2,1,0:T(8,128)(2,1)} %shard_map.125), calls=%async_computation.3 | async-start | bytes 2621440 | tf_op jit(solution)/shard_map/all_to_all | solution.py:444
  231.7 17.2 %shard_map.127 = f32[2,1024,1024]{2,1,0:T(8,128)} custom-call(bf16[32,16,1024]{2,1,0:T(8,128)(2,1)} %copy-done.2, bf16[32,16,3072]{2,1,0:T(8,128)(2,1)} %copy-done, bf16[32,16,4096]{2,1,0:T(8,128)(2,1)} %all-to-all-done.2.refs_2_), custom_call_target="tpu_custom_call" | custom-call | flops 1 | bytes 1 | tf_op jit(solution)/shard_map/pallas_call | solution.py:316
  248.8 14.6 %all-to-all-done.3.spectrum = bf16[32,40,512]{2,1,0:T(8,128)(2,1)S(1)} async-done(((bf16[32,40,512]{2,1,0:T(8,128)(2,1)}), bf16[32,40,512]{2,1,0:T(8,128)(2,1)S(1)}, u32[]{:S(2)}, u32[]{:S(2)}) %all-to-all-start.3) | async-done | bytes 1310752 | tf_op jit(solution)/shard_map/all_to_all | solution.py:444
  263.4 1.1 copy-done.1
  264.5 8.9 %shard_map.128 = f32[1,20,2,16,512]{4,3,2,1,0:T(8,128)} custom-call(bf16[32,40,512]{2,1,0:T(8,128)(2,1)} %copy-done.1, bf16[1024,512]{1,0:T(8,128)(2,1)} %compare_convert_fusion.choose, bf16[20,512,256]{2,1,0:T(8,128)(2,1)} %shard_map.126.weight), custom_call_target="tpu_custom_call" | custom-call | flops 1 | bytes 1 | tf_op jit(solution)/shard_map/pallas_call | solution.py:421
  (36 shorter events, 1.0 us)
Async XLA Ops:
  14.2 33.5 %all-to-all-start = ((bf16[32,16,1024]{2,1,0:T(8,128)(2,1)}), bf16[32,16,1024]{2,1,0:T(8,128)(2,1)S(1)}, u32[]{:S(2)}, u32[]{:S(2)}) async-start(bf16[32,16,1024]{2,1,0:T(8,128)(2,1)} %bitcast.31), calls=%async_computation | async-start | bytes 2097152 | tf_op jit(solution)/shard_map/all_to_all | solution.py:444
  47.8 1.0 copy-start.2
  48.8 76.7 %all-to-all-start.1 = ((bf16[32,16,3072]{2,1,0:T(8,128)(2,1)}), bf16[32,16,3072]{2,1,0:T(8,128)(2,1)S(1)}, u32[]{:S(2)}, u32[]{:S(2)}) async-start(bf16[32,16,3072]{2,1,0:T(8,128)(2,1)} %bitcast.30), calls=%async_computation.1 | async-start | bytes 6291456 | tf_op jit(solution)/shard_map/all_to_all | solution.py:444
  54.2 31.6 %copy-start.4 = (s32[384,1]{0,1:T(1,128)S(1)}, s32[384,1]{0,1:T(1,128)}, u32[]{:S(2)}) copy-start(s32[384,1]{0,1:T(1,128)} %param.17) | copy-start | bytes 4612
  54.2 33.3 %copy-start.3 = (s32[384]{0:T(512)S(1)}, s32[384]{0:T(512)}, u32[]{:S(2)}) copy-start(s32[384]{0:T(512)} %param.13) | copy-start | bytes 4612
  125.5 1.7 copy-start
  125.5 6.6 %copy-start.5 = (s32[256]{0:T(256)S(1)}, s32[256]{0:T(256)}, u32[]{:S(2)}) copy-start(s32[256]{0:T(256)} %param.14) | copy-start | bytes 3076
  127.2 99.0 %all-to-all-start.2 = ((bf16[32,16,4096]{2,1,0:T(8,128)(2,1)}), bf16[32,16,4096]{2,1,0:T(8,128)(2,1)}, u32[]{:S(2)}, u32[]{:S(2)}) async-start(bf16[32,16,4096]{2,1,0:T(8,128)(2,1)} %bitcast.29), calls=%async_computation.2 | async-start | bytes 8388608 | tf_op jit(solution)/shard_map/all_to_all | solution.py:444
  226.2 37.2 %all-to-all-start.3 = ((bf16[32,40,512]{2,1,0:T(8,128)(2,1)}), bf16[32,40,512]{2,1,0:T(8,128)(2,1)S(1)}, u32[]{:S(2)}, u32[]{:S(2)}) async-start(bf16[32,40,512]{2,1,0:T(8,128)(2,1)} %shard_map.125), calls=%async_computation.3 | async-start | bytes 2621440 | tf_op jit(solution)/shard_map/all_to_all | solution.py:444
  263.4 1.1 copy-start.1

commit v8 on v7

--- a/solution.py
+++ b/solution.py
@@ -144,12 +144,20 @@
 
     lax.fori_loop(0, bands, column, 0)
 
-    def multiply(b, carry):
-        rows = branches[b].reshape(frames * ROWS, 2 * depth)
-        product[b] = jnp.dot(rows, table[...], preferred_element_type=jnp.float32)
+    rows = frames * ROWS
+    joined = RADIX
+    while joined * rows > 1024:
+        joined //= 2
+
+    def multiply(step, carry):
+        some = pl.ds(step // bands * joined, joined)
+        lanes = pl.ds(pl.multiple_of(step % bands * 2 * LANES, 2 * LANES), 2 * LANES)
+        left = branches[some].reshape(joined * rows, 2 * depth)
+        got = jnp.dot(left, table[:, lanes], preferred_element_type=jnp.float32)
+        product[some, :, lanes] = got.reshape(joined, rows, 2 * LANES)
         return carry
 
-    lax.fori_loop(0, RADIX, multiply, 0)
+    lax.fori_loop(0, RADIX // joined * bands, multiply, 0)
     lane_ids = lax.broadcasted_iota(jnp.int32, (ROWS, LANES), 1)
 
     def regroup(f, carry):
@@ -376,7 +384,9 @@
     groups = halves * inner
     tiles = 2 * listed // LANES
 
-    def kernel(spectrum, choose, weight, out, ordered, picked):
+    def kernel(spectrum, choose, weight_hbm, out, ordered, picked, weight, sem):
+        coming = pltpu.make_async_copy(weight_hbm, weight, sem)
+        coming.start()
         lane_ids = lax.broadcasted_iota(jnp.int32, (rows, LANES), 1)
         for h in range(halves):
             for q in range(inner):
@@ -387,17 +397,12 @@
                     ]
                     for f, piece in enumerate(swap_blocks(pieces, lane_ids)):
                         top = (t * count + f) * rows
-                        ordered[h * inner + q, top : top + rows, :] = piece
-        acc = None
-        for q in range(groups):
-            term = jnp.dot(
-                ordered[q].astype(jnp.bfloat16),
-                choose[q * LANES : (q + 1) * LANES, :],
-                preferred_element_type=jnp.float32,
-            )
-            acc = term if acc is None else acc + term
+                        group = (h * inner + q) * LANES
+                        ordered[top : top + rows, group : group + LANES] = piece
+        acc = jnp.dot(ordered[...].astype(jnp.bfloat16), choose[...], preferred_element_type=jnp.float32)
         for lane in range(tiles):
             picked[lane] = acc[:, lane * LANES : (lane + 1) * LANES]
+        coming.wait()
         for i in range(slots):
             chosen = [
                 jnp.concatenate(
@@ -420,10 +425,13 @@
 
     return pl.pallas_call(
         kernel,
+        in_specs=[pl.BlockSpec(memory_space=pltpu.VMEM)] * 2 + [pl.BlockSpec(memory_space=pl.ANY)],
         out_shape=jax.ShapeDtypeStruct((1, slots, 2, FRAMES, 2 * beams), jnp.float32),
         scratch_shapes=[
-            pltpu.VMEM((groups, FRAMES * rows, LANES), jnp.float32),
+            pltpu.VMEM((FRAMES * rows, groups * LANES), jnp.float32),
             pltpu.VMEM((tiles, FRAMES * rows, LANES), jnp.float32),
+            pltpu.VMEM(weights.shape, weights.dtype),
+            pltpu.SemaphoreType.DMA,
         ],
         compiler_params=pltpu.CompilerParams(vmem_limit_bytes=VMEM),
         cost_estimate=NO_COST,

time: 274 us -> 271 us (0.989)
  Pallas kernels: 129 us -> 125 us
where the time goes in v8:
time: 271 us; the launch traced here: 270 us
  Pallas kernels  125 us (46%)
  waiting for transfers between devices  98.9 us (36%)
  starting transfers between devices  22.3 us (8%)
  other arithmetic  14.9 us (5%)
  local copies, waits for them, and re-layouts  7.74 us (3%)
    all_to_all x4, waiting for transfers between devices, exchange(): lax.all_to_all(x, ('st', 'sb'), split_axis=0, concat_axis=0, tiled=True)  98.9 us
    pallas_call x3, Pallas kernels, channelise(): pl.pallas_call(functools.partial(channel_kernel, first), grid_spec=pltpu....  68.6 us
    all_to_all x4, starting transfers between devices, exchange(): lax.all_to_all(x, ('st', 'sb'), split_axis=0, concat_axis=0, tiled=True)  22.3 us
    pallas_call x1, Pallas kernels, slot_spectra(): pl.pallas_call(slot_kernel, out_shape=jax.ShapeDtypeStruct((rows // per,...  19.7 us
    pallas_call x1, Pallas kernels, correlate(): pl.pallas_call(kernel, in_specs=[pl.BlockSpec(memory_space=pl.ANY)] * len...  17.2 us
    pallas_call x1, Pallas kernels, beam_weights(): pl.pallas_call(weight_kernel, grid=(slots,), in_specs=[pl.BlockSpec(memor...  12.4 us
    pallas_call x1, Pallas kernels, combine(): pl.pallas_call(kernel, in_specs=[pl.BlockSpec(memory_space=pltpu.VMEM)] *...  7.33 us
  transfers between devices with their start and end apart: 4, of which 4 were waited for; matrix products, arithmetic and copies ran while one was open for 7% of the time, Pallas kernels for 39%

profile of v8, /device:TPU:0, one launch (start us, length us, event | category | flops | bytes accessed | tf_op | source)
XLA Modules:
  0.0 270.0 jit_solution(6909293995174538122)
XLA Ops:
  0.6 11.5 %shard_map.122 = (bf16[8,4,16,1024]{3,2,1,0:T(8,128)(2,1)}, bf16[8,4,16,1024]{3,2,1,0:T(8,128)(2,1)}) custom-call(s32[1]{0:T(128)} %bitcast.row_block, bf16[2,128,126976]{2,1,0:T(8,128)(2,1)} %volts.5, f32[16,4096]{1,0:T(8,128)} %prototype.5, f32[512,512]{1,0:T(8,128)} %constant.120.clone.cosines, f32[512,512]{1,0:T(8,128)} %constant.121.clone.sines, ...), custom_call_target="tpu_custom_call" | custom-call | flops 2500000000 | bytes 1 | tf_op jit(solution)/shard_map/pallas_call | solution.py:183
  12.2 7.3 %all-to-all-start = ((bf16[32,16,1024]{2,1,0:T(8,128)(2,1)}), bf16[32,16,1024]{2,1,0:T(8,128)(2,1)S(1)}, u32[]{:S(2)}, u32[]{:S(2)}) async-start(bf16[32,16,1024]{2,1,0:T(8,128)(2,1)} %bitcast.31), calls=%async_computation | async-start | bytes 2097152 | tf_op jit(solution)/shard_map/all_to_all | solution.py:452
  19.5 25.3 %shard_map.123 = (bf16[8,4,16,3072]{3,2,1,0:T(8,128)(2,1)}, bf16[8,12,16,1024]{3,2,1,0:T(8,128)(2,1)}) custom-call(s32[1]{0:T(128)} %bitcast.2.row_block, bf16[2,128,126976]{2,1,0:T(8,128)(2,1)} %volts.5, f32[16,4096]{1,0:T(8,128)} %prototype.5, f32[512,512]{1,0:T(8,128)} %constant.120.clone.cosines, f32[512,512]{1,0:T(8,128)} %constant.121.clone.sines, ...), custom_call_target="tpu_custom_call" | custom-call | flops 7500000256 | bytes 1 | tf_op jit(solution)/shard_map/pallas_call | solution.py:183
  44.9 0.9 all-to-all-done.refs_0_
  45.7 1.0 copy-done.2
  46.7 5.0 %all-to-all-start.1 = ((bf16[32,16,3072]{2,1,0:T(8,128)(2,1)}), bf16[32,16,3072]{2,1,0:T(8,128)(2,1)S(1)}, u32[]{:S(2)}, u32[]{:S(2)}) async-start(bf16[32,16,3072]{2,1,0:T(8,128)(2,1)} %bitcast.30), calls=%async_computation.1 | async-start | bytes 6291456 | tf_op jit(solution)/shard_map/all_to_all | solution.py:452
  51.9 0.1 add.168
  52.0 0.1 mul.187
  52.2 31.7 %shard_map.124 = (bf16[8,4,16,4096]{3,2,1,0:T(8,128)(2,1)}, bf16[8,16,16,1024]{3,2,1,0:T(8,128)(2,1)}) custom-call(s32[1]{0:T(128)} %bitcast.4.row_block, bf16[2,128,126976]{2,1,0:T(8,128)(2,1)} %volts.5, f32[16,4096]{1,0:T(8,128)} %prototype.5, f32[512,512]{1,0:T(8,128)} %constant.120.clone.cosines, f32[512,512]{1,0:T(8,128)} %constant.121.clone.sines, ...), custom_call_target="tpu_custom_call" | custom-call | flops 10000000000 | bytes 1 | tf_op jit(solution)/shard_map/pallas_call | solution.py:183
  83.9 1.2 reduce-window.6
  85.1 0.2 slice_reduce_fusion
  85.3 0.2 reduce-window.9
  85.6 0.4 fusion.1
  86.3 1.1 reshape.278
  87.5 1.1 copy.25
  88.8 0.1 mul.193
  88.9 0.7 dynamic_slice.3.channel
  89.5 2.2 add_select_fusion.1.row_branch
  91.7 3.9 %fusion.9 = (f32[1280,128]{1,0:T(8,128)}, f32[1280,128]{1,0:T(8,128)}) fusion(s32[1280]{0:T(1024)S(1)} %fusion.14), kind=kLoop, calls=%fused_computation.20 | loop fusion | flops 2293760 | bytes 1315840 | tf_op jit(solution)/shard_map/sin | solution.py:33
  95.6 5.2 %sine_multiply_fusion = (f32[1280,4]{1,0:T(8,128)}, f32[1280,4]{1,0:T(8,128)}) fusion(f32[1280,4]{1,0:T(8,128)} %copy.25, f32[1280]{0:T(1024)S(1)} %mul.193), kind=kLoop, calls=%fused_computation.17 | loop fusion | flops 15360 | bytes 66560 | tf_op jit(solution)/shard_map/mul | solution.py:243
  100.8 19.7 %shard_map.125 = bf16[32,40,512]{2,1,0:T(8,128)(2,1)} custom-call(s32[1280,1]{1,0:T(8,128)} %add_select_fusion.1.row_branch, f32[1280,4]{1,0:T(8,128)} %get-tuple-element.69.hi_c, f32[1280,4]{1,0:T(8,128)} %get-tuple-element.68.hi_s, f32[1280,128]{1,0:T(8,128)} %get-tuple-element.71.lo_c, f32[1280,128]{1,0:T(8,128)} %get-tuple-element.70.lo_s, ...), custom_call_target="tpu_custom_call" | custom-call | flops 10000000000 | bytes 1 | tf_op jit(solution)/shard_map/pallas_call | solution.py:249
  120.4 3.0 %all-to-all-done.1.refs_1_ = bf16[32,16,3072]{2,1,0:T(8,128)(2,1)S(1)} async-done(((bf16[32,16,3072]{2,1,0:T(8,128)(2,1)}), bf16[32,16,3072]{2,1,0:T(8,128)(2,1)S(1)}, u32[]{:S(2)}, u32[]{:S(2)}) %all-to-all-start.1) | async-done | bytes 3145760 | tf_op jit(solution)/shard_map/all_to_all | solution.py:452
  123.4 1.7 copy-done
  125.2 4.6 %all-to-all-start.2 = ((bf16[32,16,4096]{2,1,0:T(8,128)(2,1)}), bf16[32,16,4096]{2,1,0:T(8,128)(2,1)}, u32[]{:S(2)}, u32[]{:S(2)}) async-start(bf16[32,16,4096]{2,1,0:T(8,128)(2,1)} %bitcast.29), calls=%async_computation.2 | async-start | bytes 8388608 | tf_op jit(solution)/shard_map/all_to_all | solution.py:452
  130.1 1.2 compare_convert_fusion.choose
  131.3 12.4 %shard_map.126.weight_hbm = bf16[20,512,256]{2,1,0:T(8,128)(2,1)} custom-call(s32[20]{0:T(128)} %dynamic_slice.3.channel, f32[256,256]{1,0:T(8,128)} %delays.1, f32[256,256]{1,0:T(8,128)} %gains.1), custom_call_target="tpu_custom_call" | custom-call | flops 1 | bytes 1 | tf_op jit(solution)/shard_map/pallas_call | solution.py:362
  143.7 80.5 %all-to-all-done.2.refs_2_ = bf16[32,16,4096]{2,1,0:T(8,128)(2,1)} async-done(((bf16[32,16,4096]{2,1,0:T(8,128)(2,1)}), bf16[32,16,4096]{2,1,0:T(8,128)(2,1)}, u32[]{:S(2)}, u32[]{:S(2)}) %all-to-all-start.2) | async-done | bytes 4194336 | tf_op jit(solution)/shard_map/all_to_all | solution.py:452
  224.2 5.5 %all-to-all-start.3 = ((bf16[32,40,512]{2,1,0:T(8,128)(2,1)}), bf16[32,40,512]{2,1,0:T(8,128)(2,1)S(1)}, u32[]{:S(2)}, u32[]{:S(2)}) async-start(bf16[32,40,512]{2,1,0:T(8,128)(2,1)} %shard_map.125), calls=%async_computation.3 | async-start | bytes 2621440 | tf_op jit(solution)/shard_map/all_to_all | solution.py:452
  229.6 17.2 %shard_map.127 = f32[2,1024,1024]{2,1,0:T(8,128)} custom-call(bf16[32,16,1024]{2,1,0:T(8,128)(2,1)} %copy-done.2, bf16[32,16,3072]{2,1,0:T(8,128)(2,1)} %copy-done, bf16[32,16,4096]{2,1,0:T(8,128)(2,1)} %all-to-all-done.2.refs_2_), custom_call_target="tpu_custom_call" | custom-call | flops 1 | bytes 1 | tf_op jit(solution)/shard_map/pallas_call | solution.py:324
  246.8 14.5 %all-to-all-done.3.spectrum = bf16[32,40,512]{2,1,0:T(8,128)(2,1)S(1)} async-done(((bf16[32,40,512]{2,1,0:T(8,128)(2,1)}), bf16[32,40,512]{2,1,0:T(8,128)(2,1)S(1)}, u32[]{:S(2)}, u32[]{:S(2)}) %all-to-all-start.3) | async-done | bytes 1310752 | tf_op jit(solution)/shard_map/all_to_all | solution.py:452
  261.4 1.1 copy-done.1
  262.5 7.3 %shard_map.128 = f32[1,20,2,16,512]{4,3,2,1,0:T(8,128)} custom-call(bf16[32,40,512]{2,1,0:T(8,128)(2,1)} %copy-done.1, bf16[1024,512]{1,0:T(8,128)(2,1)} %compare_convert_fusion.choose, bf16[20,512,256]{2,1,0:T(8,128)(2,1)} %shard_map.126.weight_hbm), custom_call_target="tpu_custom_call" | custom-call | flops 1 | bytes 1 | tf_op jit(solution)/shard_map/pallas_call | solution.py:426
  (36 shorter events, 1.0 us)
Async XLA Ops:
  12.2 33.5 %all-to-all-start = ((bf16[32,16,1024]{2,1,0:T(8,128)(2,1)}), bf16[32,16,1024]{2,1,0:T(8,128)(2,1)S(1)}, u32[]{:S(2)}, u32[]{:S(2)}) async-start(bf16[32,16,1024]{2,1,0:T(8,128)(2,1)} %bitcast.31), calls=%async_computation | async-start | bytes 2097152 | tf_op jit(solution)/shard_map/all_to_all | solution.py:452
  45.7 1.0 copy-start.2
  46.7 76.7 %all-to-all-start.1 = ((bf16[32,16,3072]{2,1,0:T(8,128)(2,1)}), bf16[32,16,3072]{2,1,0:T(8,128)(2,1)S(1)}, u32[]{:S(2)}, u32[]{:S(2)}) async-start(bf16[32,16,3072]{2,1,0:T(8,128)(2,1)} %bitcast.30), calls=%async_computation.1 | async-start | bytes 6291456 | tf_op jit(solution)/shard_map/all_to_all | solution.py:452
  52.1 31.7 %copy-start.4 = (s32[384,1]{0,1:T(1,128)S(1)}, s32[384,1]{0,1:T(1,128)}, u32[]{:S(2)}) copy-start(s32[384,1]{0,1:T(1,128)} %param.17) | copy-start | bytes 4612
  52.1 33.4 %copy-start.3 = (s32[384]{0:T(512)S(1)}, s32[384]{0:T(512)}, u32[]{:S(2)}) copy-start(s32[384]{0:T(512)} %param.13) | copy-start | bytes 4612
  123.4 1.7 copy-start
  123.4 6.6 %copy-start.5 = (s32[256]{0:T(256)S(1)}, s32[256]{0:T(256)}, u32[]{:S(2)}) copy-start(s32[256]{0:T(256)} %param.14) | copy-start | bytes 3076
  125.2 99.0 %all-to-all-start.2 = ((bf16[32,16,4096]{2,1,0:T(8,128)(2,1)}), bf16[32,16,4096]{2,1,0:T(8,128)(2,1)}, u32[]{:S(2)}, u32[]{:S(2)}) async-start(bf16[32,16,4096]{2,1,0:T(8,128)(2,1)} %bitcast.29), calls=%async_computation.2 | async-start | bytes 8388608 | tf_op jit(solution)/shard_map/all_to_all | solution.py:452
  224.2 37.2 %all-to-all-start.3 = ((bf16[32,40,512]{2,1,0:T(8,128)(2,1)}), bf16[32,40,512]{2,1,0:T(8,128)(2,1)S(1)}, u32[]{:S(2)}, u32[]{:S(2)}) async-start(bf16[32,40,512]{2,1,0:T(8,128)(2,1)} %shard_map.125), calls=%async_computation.3 | async-start | bytes 2621440 | tf_op jit(solution)/shard_map/all_to_all | solution.py:452
  261.3 1.1 copy-start.1

commit v9 on v8

--- a/solution.py
+++ b/solution.py
@@ -7,6 +7,7 @@
 from jax import lax
 from jax.experimental import pallas as pl
 from jax.experimental.pallas import tpu as pltpu
+from jax.sharding import Mesh
 from jax.sharding import PartitionSpec as P
 
 NCH = 4096
@@ -16,6 +17,7 @@
 LANES = 128
 ROWS = 16
 EARLY = 4
+LATE = 6
 VMEM = 56 * 1024 * 1024
 
 NO_COST = pl.CostEstimate(flops=1, bytes_accessed=1, transcendentals=0)
@@ -90,8 +92,21 @@
     return [turned[0]] + [pltpu.roll(turned[g], LANES - g * width, 1) for g in range(1, count)]
 
 
-def channel_kernel(first, row_block, volts, prototype, cosines, sines, turn_c, turn_s, out, branches, *scratch):
-    taps_wide, table, filtered, product = scratch
+def by_partner(x, here, far):
+    width = LANES // far
+    lane_ids = lax.broadcasted_iota(jnp.int32, x.shape, 1)
+    step = 1
+    while step < far:
+        upper = (lane_ids // width) & step != 0
+        other = jnp.where(upper, pltpu.roll(x, step * width, 1), pltpu.roll(x, LANES - step * width, 1))
+        x = jnp.where(here & step != 0, other, x)
+        step *= 2
+    return x
+
+
+def channel_kernel(first, place, volts, prototype, cosines, sines, turn_c, turn_s, *rest):
+    outs, (branches, taps_wide, table, filtered, product) = rest[:-5], rest[-5:]
+    near = RADIX // len(outs)
     taps = taps_wide.shape[0]
     length = taps_wide.shape[2]
     frames = filtered.shape[2]
@@ -99,7 +114,12 @@
     bands = depth // LANES
     for t in range(taps):
         taps_wide[t] = jnp.broadcast_to(prototype[t : t + 1, :], taps_wide.shape[1:])
-    cos_t, sin_t = cosines[...].astype(table.dtype), sines[...].astype(table.dtype)
+    cos_t, sin_t = [
+        jnp.concatenate(
+            [by_partner(x[:, lane : lane + LANES], place[1], len(outs)) for lane in range(0, depth, LANES)], axis=1
+        ).astype(table.dtype)
+        for x in (cosines, sines)
+    ]
     table[:depth, :depth] = cos_t
     table[:depth, depth:] = -sin_t
     table[depth:, :depth] = sin_t
@@ -168,13 +188,15 @@
                 pieces = [product[b, pl.ds(top, ROWS), lane : lane + LANES] for b in range(RADIX)]
                 for g, piece in enumerate(gather_blocks(pieces, lane_ids)):
                     at = pl.multiple_of((part * frames + f) * LANES, LANES)
-                    out[g, band, :, pl.ds(at, LANES)] = piece.astype(out.dtype)
+                    out = outs[g // near]
+                    out[g % near, band, :, pl.ds(at, LANES)] = piece.astype(out.dtype)
         return carry
 
     lax.fori_loop(0, frames, regroup, 0)
 
 
-def channelise(row_block, volts, prototype, tables, first, frames):
+def channelise(place, volts, prototype, tables, first, frames, far):
+    near = RADIX // far
     taps = prototype.shape[0]
     length = volts.shape[2] if first > 0 else (frames + taps - 1) * NCH
     depth = NCH // RADIX
@@ -190,7 +212,7 @@
             ]
             + [pl.BlockSpec(x.shape, lambda i, row: (0, 0)) for x in (prototype, *tables)],
             out_specs=[
-                pl.BlockSpec((RADIX, bands, ROWS, wide), lambda i, row: (0, 0, 0, 0)),
+                *[pl.BlockSpec((near, bands, ROWS, wide), lambda i, row: (0, 0, 0, 0))] * far,
                 pl.BlockSpec((RADIX, frames, ROWS, 2 * depth), lambda i, row: (0, 0, 0, 0)),
             ],
             scratch_shapes=[
@@ -201,16 +223,16 @@
             ],
         ),
         out_shape=[
-            jax.ShapeDtypeStruct((RADIX, bands, ROWS, wide), jnp.bfloat16),
+            *[jax.ShapeDtypeStruct((near, bands, ROWS, wide), jnp.bfloat16)] * far,
             jax.ShapeDtypeStruct((RADIX, frames, ROWS, 2 * depth), jnp.bfloat16),
         ],
         compiler_params=pltpu.CompilerParams(vmem_limit_bytes=VMEM),
         cost_estimate=busy(frames / FRAMES),
-    )(row_block, volts, prototype, *tables)
-
-
-def slot_kernel(row_branch, hi_c, hi_s, lo_c, lo_s, *rest):
-    chunks, (out, table, total) = rest[:-3], rest[-3:]
+    )(place, volts, prototype, *tables)
+
+
+def slot_kernel(far, row_branch, hi_c, hi_s, lo_c, lo_s, *rest):
+    chunks, outs, (table, total) = rest[: -2 - far], rest[-2 - far : -2], rest[-2:]
     depth = chunks[0].shape[3] // 2
     for a in range(hi_c.shape[1]):
         high_c, high_s = hi_c[:, a : a + 1], hi_s[:, a : a + 1]
@@ -227,9 +249,11 @@
         return carry
 
     lax.fori_loop(0, RADIX, branch, 0)
-    per = out.shape[1]
-    for d in range(out.shape[0]):
-        out[d] = total[d * per : (d + 1) * per].astype(out.dtype)
+    plane, per = outs[0].shape[:2]
+    for s, out in enumerate(outs):
+        for d in range(plane):
+            top = (s * plane + d) * per
+            out[d] = total[top : top + per].astype(out.dtype)
 
 
 def slot_tables(row_channel, row_filled, row_turned):
@@ -243,12 +267,12 @@
     return (row_channel % RADIX)[:, None], hi_c * scaling, hi_s * scaling, lo_c, lo_s
 
 
-def slot_spectra(tables, chunks, per):
+def slot_spectra(tables, chunks, per, far):
     rows = tables[0].shape[0]
     samples = sum(c.shape[1] * c.shape[2] for c in chunks)
     return pl.pallas_call(
-        slot_kernel,
-        out_shape=jax.ShapeDtypeStruct((rows // per, per, samples), jnp.bfloat16),
+        functools.partial(slot_kernel, far),
+        out_shape=[jax.ShapeDtypeStruct((rows // per // far, per, samples), jnp.bfloat16)] * far,
         scratch_shapes=[
             pltpu.VMEM((rows, chunks[0].shape[3]), jnp.bfloat16),
             pltpu.VMEM((rows, samples), jnp.float32),
@@ -258,35 +282,32 @@
     )(*tables, *chunks)
 
 
-def correlate(pieces, halves, lanes):
-    senders, sub, _ = pieces[0][0].shape
+def correlate(here, pieces, far, halves, lanes):
+    senders = pieces[0][0].shape[0]
+    sub = pieces[0][0].shape[1] if halves == 1 else ROWS
     half = FRAMES * lanes
-    signals = senders * halves * sub
-    count = max(1, signals // 256)
-    each = senders // count
-    block = each * halves * sub
-
-    def kernel(*refs):
+    block = senders * halves * sub
+    signals = far * block
+
+    def kernel(here_ref, *refs):
         parts, (out, held, turned, made, in_sems, out_sems) = refs[: len(pieces)], refs[len(pieces) :]
-        coming = [[] for _ in range(count)]
-        for index, (_, which, first, frames) in enumerate(pieces):
-            for q in range(count):
-                for part in range(2):
-                    src = parts[index].at[pl.ds(q * each, each), :, pl.ds(part * frames * lanes, frames * lanes)]
-                    dst = held.at[q, :, which, :, pl.ds(part * half + first * lanes, frames * lanes)]
-                    sem = in_sems.at[(index * count + q) * 2 + part]
-                    coming[q].append(pltpu.make_async_copy(src, dst, sem))
+        coming = [[] for _ in range(far)]
+        for index, (_, partner, row, which, first, frames) in enumerate(pieces):
+            for part in range(2):
+                src = parts[index].at[:, pl.ds(row, sub), pl.ds(part * frames * lanes, frames * lanes)]
+                dst = held.at[partner, :, which, :, pl.ds(part * half + first * lanes, frames * lanes)]
+                coming[partner].append(pltpu.make_async_copy(src, dst, in_sems.at[2 * index + part]))
         for copies in coming:
             for copy in copies:
                 copy.start()
 
         def rows_of(i):
-            return pl.ds(i * block, block)
+            return pl.ds(pl.multiple_of((here_ref[0] ^ i) * block, block), block)
 
         inverse = 1.0 / half
         going = [[], []]
         slot = 0
-        for i in range(count):
+        for i in range(far):
             for copy in coming[i]:
                 copy.wait()
             left = held[i].reshape(block, 2 * half)
@@ -323,19 +344,19 @@
 
     return pl.pallas_call(
         kernel,
-        in_specs=[pl.BlockSpec(memory_space=pl.ANY)] * len(pieces),
+        in_specs=[pl.BlockSpec(memory_space=pltpu.SMEM)] + [pl.BlockSpec(memory_space=pl.ANY)] * len(pieces),
         out_specs=pl.BlockSpec(memory_space=pl.ANY),
         out_shape=jax.ShapeDtypeStruct((2, signals, signals), jnp.float32),
         scratch_shapes=[
-            pltpu.VMEM((count, each, halves, sub, 2 * half), jnp.bfloat16),
+            pltpu.VMEM((far, senders, halves, sub, 2 * half), jnp.bfloat16),
             pltpu.VMEM((block, 2 * half), jnp.bfloat16),
             pltpu.VMEM((2, 2, 2, block, block), jnp.float32),
-            pltpu.SemaphoreType.DMA((2 * count * len(pieces),)),
+            pltpu.SemaphoreType.DMA((2 * len(pieces),)),
             pltpu.SemaphoreType.DMA((2, 2, 2)),
         ],
-        compiler_params=pltpu.CompilerParams(vmem_limit_bytes=VMEM),
+        compiler_params=pltpu.CompilerParams(vmem_limit_bytes=VMEM // 2),
         cost_estimate=NO_COST,
-    )(*[piece[0] for piece in pieces])
+    )(here, *[piece[0] for piece in pieces])
 
 
 def weight_kernel(channel, delays, gains, out):
@@ -381,24 +402,27 @@
     halves = spectra.shape[2] // (FRAMES * sub)
     count = LANES // sub
     inner = senders // count
-    groups = halves * inner
+    partners = spectra.shape[1] // rows
+    groups = partners * halves * inner
     tiles = 2 * listed // LANES
 
     def kernel(spectrum, choose, weight_hbm, out, ordered, picked, weight, sem):
         coming = pltpu.make_async_copy(weight_hbm, weight, sem)
         coming.start()
         lane_ids = lax.broadcasted_iota(jnp.int32, (rows, LANES), 1)
-        for h in range(halves):
-            for q in range(inner):
-                for t in range(FRAMES // count):
-                    lane = h * FRAMES * sub + t * LANES
-                    pieces = [
-                        spectrum[q * count + i, :, lane : lane + LANES].astype(jnp.float32) for i in range(count)
-                    ]
-                    for f, piece in enumerate(swap_blocks(pieces, lane_ids)):
-                        top = (t * count + f) * rows
-                        group = (h * inner + q) * LANES
-                        ordered[top : top + rows, group : group + LANES] = piece
+        for s in range(partners):
+            for h in range(halves):
+                for q in range(inner):
+                    for t in range(FRAMES // count):
+                        lane = h * FRAMES * sub + t * LANES
+                        pieces = [
+                            spectrum[q * count + i, s * rows : (s + 1) * rows, lane : lane + LANES].astype(jnp.float32)
+                            for i in range(count)
+                        ]
+                        for f, piece in enumerate(swap_blocks(pieces, lane_ids)):
+                            top = (t * count + f) * rows
+                            group = ((s * halves + h) * inner + q) * LANES
+                            ordered[top : top + rows, group : group + LANES] = piece
         acc = jnp.dot(ordered[...].astype(jnp.bfloat16), choose[...], preferred_element_type=jnp.float32)
         for lane in range(tiles):
             picked[lane] = acc[:, lane * LANES : (lane + 1) * LANES]
@@ -433,61 +457,78 @@
             pltpu.VMEM(weights.shape, weights.dtype),
             pltpu.SemaphoreType.DMA,
         ],
-        compiler_params=pltpu.CompilerParams(vmem_limit_bytes=VMEM),
+        compiler_params=pltpu.CompilerParams(vmem_limit_bytes=VMEM // 2),
         cost_estimate=NO_COST,
     )(spectra, chooser, weights)
 
 
 def body(volts, prototype, beam_channels, station_index, delays, gains, assign):
     sig_dev = volts.shape[1]
-    st_count, sb_count = lax.axis_size("st"), lax.axis_size("sb")
-    st_here, sb_here = lax.axis_index("st").astype(jnp.int32), lax.axis_index("sb").astype(jnp.int32)
+    far, near, sb_count = lax.axis_size("far"), lax.axis_size("near"), lax.axis_size("sb")
+    far_here, near_here, sb_here = [lax.axis_index(name).astype(jnp.int32) for name in ("far", "near", "sb")]
+    st_count = far * near
     devices = st_count * sb_count
+    plane = near * sb_count
     group = NCH // devices
     fine = group // RADIX
+    partner = far_here ^ jnp.arange(far, dtype=jnp.int32)
     constants = transform_tables()
     barrier = lax.optimization_barrier
 
-    def exchange(x):
-        return lax.all_to_all(x, ("st", "sb"), split_axis=0, concat_axis=0, tiled=True)
+    def to_planes(xs):
+        return [xs[0]] + [lax.ppermute(xs[s], "far", [(i, i ^ s) for i in range(far)]) for s in range(far - 1, 0, -1)][::-1]
+
+    def in_plane(xs):
+        joined = jnp.concatenate(xs, axis=1)
+        return lax.all_to_all(joined, ("near", "sb"), split_axis=0, concat_axis=0, tiled=True)
 
     share = sig_dev // sb_count
     sub = min(share, ROWS)
     halves = max(1, share // ROWS)
     inside = (sb_here * share) % ROWS
     unit = max(1, LANES // group)
-    early = max(unit, EARLY // unit * unit)
-    plan = [(0, 0, early), (0, early, FRAMES - early)] + [(h, 0, FRAMES) for h in range(1, halves)]
+    early, late = [max(unit, x // unit * unit) for x in (EARLY, LATE)]
+    plan = [(0, 0, early), (0, early, FRAMES - early)]
+    for h in range(1, halves):
+        plan += [(h, 0, FRAMES - late), (h, FRAMES - late, late)]
 
     def channels_of(c, here):
         which, first, frames = plan[c]
-        row_block = (here * share // ROWS + which)[None]
-        out, kept = channelise(row_block, volts, prototype, constants, first, frames)
+        place = jnp.stack([here * share // ROWS + which, far_here])
+        *outs, kept = channelise(place, volts, prototype, constants, first, frames, far)
         if sub < ROWS:
-            out = lax.dynamic_slice_in_dim(out, inside, sub, axis=2)
+            outs = [lax.dynamic_slice_in_dim(x, inside, sub, axis=2) for x in outs]
         inner = st_count // RADIX
         if inner > 1:
-            out = out.reshape(RADIX, sb_count, sub, 2 * frames, RADIX, inner, fine).transpose(0, 5, 1, 2, 3, 4, 6)
-        return out.reshape(devices, sub, -1), kept
+            outs = [
+                x.reshape(near // inner, sb_count, sub, 2 * frames, RADIX, inner, fine).transpose(0, 5, 1, 2, 3, 4, 6)
+                for x in outs
+            ]
+        return [x.reshape(plane, sub, -1) for x in outs], kept
 
     lists = (assign, beam_channels, station_index)
     here = sb_here
-    out, kept = channels_of(0, here)
-    branches, arrived = [kept], []
+    outs, kept = channels_of(0, here)
+    branches, arrived, crossed = [kept], [], None
     for c in range(1, len(plan)):
-        out, here, lists, arrived[-1:] = barrier((out, here, lists, arrived[-1:]))
-        arrived.append(exchange(out))
-        out, kept = channels_of(c, here)
+        outs, crossed, here, lists, arrived[-1:] = barrier((outs, crossed, here, lists, arrived[-1:]))
+        if crossed is not None:
+            arrived.append(in_plane(crossed))
+        crossed = to_planes(outs)
+        outs, kept = channels_of(c, here)
         branches.append(kept)
 
-    assign, beam_channels, station_index = barrier((lists, kept))[0]
+    outs, crossed, lists, branches, arrived[-1:] = barrier((outs, crossed, lists, branches, arrived[-1:]))
+    arrived.append(in_plane(crossed))
+    crossed = to_planes(outs)
+    assign, beam_channels, station_index = lists
     per_dev = SLOTS // st_count
     owners = assign[:, 0]
     taken = (owners[:, None] == jnp.arange(sb_count, dtype=jnp.int32)[None, :]).astype(jnp.int32)
     position = jnp.sum(taken * jnp.cumsum(taken, axis=0), axis=1) - 1
     place = owners * SLOTS + position
     slot_ids = (
-        jnp.arange(st_count, dtype=jnp.int32)[:, None, None] * per_dev
+        (partner[:, None] * near + jnp.arange(near, dtype=jnp.int32)).reshape(-1)[:, None, None] * per_dev
         + jnp.arange(sb_count, dtype=jnp.int32)[:, None] * SLOTS
         + jnp.arange(per_dev, dtype=jnp.int32)
     ).reshape(-1)
@@ -499,35 +540,49 @@
         return jnp.broadcast_to(values.reshape(devices, 1, per_dev), (devices, 2, per_dev)).reshape(-1)
 
     turned = jnp.broadcast_to(jnp.arange(2, dtype=jnp.int32)[None, :, None], (devices, 2, per_dev)).reshape(-1)
-    mine = lax.dynamic_slice_in_dim(slot_channel, (st_here * sb_count + sb_here) * per_dev, per_dev)
+    mine = lax.dynamic_slice_in_dim(slot_channel, (near_here * sb_count + sb_here) * per_dev, per_dev)
     tables = slot_tables(by_row(slot_channel), by_row(filled), turned)
-    spectra = slot_spectra(tables, branches, 2 * per_dev)
+    spectra = slot_spectra(tables, branches, 2 * per_dev, far)
     if sub < ROWS:
-        spectra = spectra.reshape(devices, 2 * per_dev, FRAMES, ROWS)
-        spectra = lax.dynamic_slice_in_dim(spectra, inside, sub, axis=3).reshape(devices, 2 * per_dev, -1)
-
-    out, spectra, mine, arrived[-1:] = barrier((out, spectra, mine, arrived[-1:]))
-    arrived.append(exchange(out))
+        spectra = [
+            lax.dynamic_slice_in_dim(x.reshape(plane, 2 * per_dev, FRAMES, ROWS), inside, sub, axis=3).reshape(
+                plane, 2 * per_dev, -1
+            )
+            for x in spectra
+        ]
+
+    crossed, spectra, mine, arrived[-1:] = barrier((crossed, spectra, mine, arrived[-1:]))
+    arrived.append(in_plane(crossed))
+    slot_crossed = to_planes(spectra)
     weights = beam_weights(mine, delays, gains)
     signal_ids = (
-        jnp.arange(halves, dtype=jnp.int32)[:, None, None] * sub
-        + jnp.arange(devices, dtype=jnp.int32)[:, None] * share
+        (partner[:, None] * (near * sig_dev) + jnp.arange(halves, dtype=jnp.int32) * sub)[:, :, None, None]
+        + jnp.arange(plane, dtype=jnp.int32)[:, None] * share
         + jnp.arange(sub, dtype=jnp.int32)
     ).reshape(-1)
     wanted = (station_index[None, :] * 2 + jnp.arange(2, dtype=jnp.int32)[:, None]).reshape(-1)
     chooser = (signal_ids[:, None] == wanted[None, :]).astype(jnp.bfloat16)
 
-    spectra, weights, chooser, arrived[-1:] = barrier((spectra, weights, chooser, arrived[-1:]))
-    slot_received = exchange(spectra)
-    if halves == 1:
-        arrived = [x.reshape(-1, min(256, devices * sub), x.shape[2]) for x in arrived]
-    visibility = correlate([(x, *part) for x, part in zip(arrived, plan)], halves, group)
+    slot_crossed, weights, chooser, arrived[-1:] = barrier((slot_crossed, weights, chooser, arrived[-1:]))
+    slot_received = in_plane(slot_crossed)
+    pieces = []
+    for x, part in zip(arrived, plan):
+        for s in range(far):
+            if halves == 1:
+                pieces.append((x[:, s * sub : (s + 1) * sub].reshape(1, plane * sub, -1), s, 0, *part))
+            else:
+                pieces.append((x, s, s * sub, *part))
+    visibility = correlate(far_here[None], pieces, far, halves, group)
     signals = visibility.shape[1]
     beam_out = combine(slot_received, chooser, weights, sub)
     return (visibility.reshape(2, 1, 1, signals, signals), beam_out)
 
 
 def solution(mesh):
-    in_specs = (P(None, "st", None), P(), P(), P(), P(), P(), P())
-    out_specs = (P(None, "sb", "st", None, None), P("sb", "st", None, None, None))
-    return jax.shard_map(body, mesh=mesh, in_specs=in_specs, out_specs=out_specs, check_vma=False)
+    st_count, sb_count = mesh.shape["st"], mesh.shape["sb"]
+    far = math.gcd(4, st_count)
+    planes = Mesh(mesh.devices.reshape(far, st_count // far, sb_count), ("far", "near", "sb"))
+    st = ("far", "near")
+    in_specs = (P(None, st, None), P(), P(), P(), P(), P(), P())
+    out_specs = (P(None, "sb", st, None, None), P("sb", st, None, None, None))
+    return jax.shard_map(body, mesh=planes, in_specs=in_specs, out_specs=out_specs, check_vma=False)

time: 271 us -> 320 us (1.18); the launches traced: 270 us -> 315 us
  starting transfers between devices: 22.3 us -> 73.6 us
  waiting for transfers between devices: 98.9 us -> 63.3 us
  Pallas kernels: 125 us -> 140 us
  other arithmetic: 14.9 us -> 28.8 us
    all_to_all x4 -> x5, waiting for transfers between devices: 98.9 us -> 0.01 us  [in_plane(): lax.all_to_all(joined, ('near', 'sb'), split_axis=0, concat_axis=0, tiled...]
    ppermute x0 -> x15, waiting for transfers between devices: none -> 63.3 us  [to_planes(): lax.ppermute(xs[s], 'far', [(i, i ^ s) for i in range(far)])]
    ppermute x0 -> x15, starting transfers between devices: none -> 52.2 us  [to_planes(): lax.ppermute(xs[s], 'far', [(i, i ^ s) for i in range(far)])]
    pallas_call x3 -> x4, Pallas kernels: 68.6 us -> 83.1 us  [channelise(): pl.pallas_call(functools.partial(channel_kernel, first), grid_spec=pltpu....]
    concatenate x0 -> x5, other arithmetic: none -> 12.7 us  [in_plane(): joined = jnp.concatenate(xs, axis=1)]
    all_to_all x4 -> x5, starting transfers between devices: 22.3 us -> 21.3 us  [in_plane(): lax.all_to_all(joined, ('near', 'sb'), split_axis=0, concat_axis=0, tiled...]
  transfers between devices with their start and end apart: 4 -> 20, of which waited for: 4 -> 5; matrix products, arithmetic and copies ran while one was open for 7% -> 5% of each run, Pallas kernels for 39% -> 38%
where the time goes in v9:
time: 320 us; the launch traced here: 315 us
  Pallas kernels  140 us (44%)
  starting transfers between devices  73.6 us (23%)
  waiting for transfers between devices  63.3 us (20%)
  other arithmetic  28.8 us (9%)
  local copies, waits for them, and re-layouts  8.84 us (3%)
    pallas_call x4, Pallas kernels, channelise(): pl.pallas_call(functools.partial(channel_kernel, first), grid_spec=pltpu....  83.1 us
    ppermute x15, waiting for transfers between devices, to_planes(): lax.ppermute(xs[s], 'far', [(i, i ^ s) for i in range(far)])  63.3 us
    ppermute x15, starting transfers between devices, to_planes(): lax.ppermute(xs[s], 'far', [(i, i ^ s) for i in range(far)])  52.2 us
    all_to_all x5, starting transfers between devices, in_plane(): lax.all_to_all(joined, ('near', 'sb'), split_axis=0, concat_axis=0, tiled...  21.3 us
    pallas_call x1, Pallas kernels, slot_spectra(): pl.pallas_call(functools.partial(slot_kernel, far), out_shape=[jax.ShapeD...  19.6 us
    pallas_call x1, Pallas kernels, correlate(): pl.pallas_call(kernel, in_specs=[pl.BlockSpec(memory_space=pltpu.SMEM)] +...  16.9 us
    concatenate x5, other arithmetic, in_plane(): joined = jnp.concatenate(xs, axis=1)  12.7 us
    pallas_call x1, Pallas kernels, beam_weights(): pl.pallas_call(weight_kernel, grid=(slots,), in_specs=[pl.BlockSpec(memor...  12.4 us
  transfers between devices with their start and end apart: 20, of which 5 were waited for; matrix products, arithmetic and copies ran while one was open for 5% of the time, Pallas kernels for 38%

profile of v9, /device:TPU:0, one launch (start us, length us, event | category | flops | bytes accessed | tf_op | source)
XLA Modules:
  0.0 315.4 jit_solution(8463858236898106598)
XLA Ops:
  1.2 13.6 %shard_map.122 = (bf16[2,4,16,1024]{3,2,1,0:T(8,128)(2,1)}, bf16[2,4,16,1024]{3,2,1,0:T(8,128)(2,1)}, bf16[2,4,16,1024]{3,2,1,0:T(8,128)(2,1)}, bf16[2,4,16,1024]{3,2,1,0:T(8,128)(2,1)}, bf16[8,4,16,1024]{3,2,1,0:T(8,128)(2,1)}) custom-call(s32[2]{0:T(128)} %pad_add_fusion.place, bf16[2,128,126976]{2,1,0:T(8,128)(2,1)} %volts.7, f32[16,4096]{1,0:T(8,128)} %prototype.7, ...), custom_call_target="tpu_custom_call" | custom-call | flops 2500000000 | bytes 1 | tf_op jit(solution)/shard_map/pallas_call | solution.py:205
  14.8 3.0 collective-permute-start
  17.8 2.6 collective-permute-start.1
  21.1 27.6 %shard_map.123 = (bf16[2,4,16,3072]{3,2,1,0:T(8,128)(2,1)}, bf16[2,4,16,3072]{3,2,1,0:T(8,128)(2,1)}, bf16[2,4,16,3072]{3,2,1,0:T(8,128)(2,1)}, bf16[2,4,16,3072...) custom-call(s32[2]{0:T(128)} %pad_add_fusion.1.place, bf16[2,128,126976]{2,1,0:T(8,128)(2,1)} %volts.7, f32[16,4096]{1,0:T(8,128)} %prototype.7, ...), custom_call_target="tpu_custom_call" | custom-call | flops 7500000256 | bytes 1 | tf_op jit(solution)/shard_map/pallas_call | solution.py:205
  49.8 3.9 %all-to-all-start = ((bf16[8,64,1024]{2,1,0:T(8,128)(2,1)}), bf16[8,64,1024]{2,1,0:T(8,128)(2,1)S(1)}, u32[]{:S(2)}, u32[]{:S(2)}) async-start(bf16[8,64,1024]{2,1,0:T(8,128)(2,1)} %pad_maximum_fusion.4), calls=%async_computation | async-start | bytes 2097152 | tf_op jit(solution)/shard_map/all_to_all | solution.py:483
  54.4 3.5 %collective-permute-start.4 = (bf16[8,16,3072]{2,1,0:T(8,128)(2,1)}, bf16[8,16,3072]{2,1,0:T(8,128)(2,1)}, u32[]{:S(2)}, u32[]{:S(2)}) collective-permute-start(bf16[8,16,3072]{2,1,0:T(8,128)(2,1)} %bitcast.9), channel_id=1, source_target_pairs={{0,16},{8,24},{16,0},{24,8},{1,17},{9,25},{17,1},{25,9},{2,18},{10... | collective-permute-start | bytes 2359304 | tf_op jit(solution)/shard_map/ppermute | solution.py:479
  58.7 24.0 %shard_map.124 = (bf16[2,4,16,2560]{3,2,1,0:T(8,128)(2,1)}, bf16[2,4,16,2560]{3,2,1,0:T(8,128)(2,1)}, bf16[2,4,16,2560]{3,2,1,0:T(8,128)(2,1)}, bf16[2,4,16,2560...) custom-call(s32[2]{0:T(128)} %pad_add_fusion.2.place, bf16[2,128,126976]{2,1,0:T(8,128)(2,1)} %volts.7, f32[16,4096]{1,0:T(8,128)} %prototype.7, ...), custom_call_target="tpu_custom_call" | custom-call | flops 6249999872 | bytes 1 | tf_op jit(solution)/shard_map/pallas_call | solution.py:205
  82.7 7.7 %collective-permute-done.3 = bf16[8,16,3072]{2,1,0:T(8,128)(2,1)S(1)} collective-permute-done((bf16[8,16,3072]{2,1,0:T(8,128)(2,1)}, bf16[8,16,3072]{2,1,0:T(8,128)(2,1)S(1)}, u32[]{:S(2)}, u32[]{:S(2)}) %collective-permute-start.3) | collective-permute-done | bytes 786464 | tf_op jit(solution)/shard_map/ppermute | solution.py:479
  90.4 19.8 %collective-permute-done.4 = bf16[8,16,3072]{2,1,0:T(8,128)(2,1)} collective-permute-done((bf16[8,16,3072]{2,1,0:T(8,128)(2,1)}, bf16[8,16,3072]{2,1,0:T(8,128)(2,1)}, u32[]{:S(2)}, u32[]{:S(2)}) %collective-permute-start.4) | collective-permute-done | bytes 786464 | tf_op jit(solution)/shard_map/ppermute | solution.py:479
  110.3 3.9 %pad_maximum_fusion = bf16[8,64,3072]{2,1,0:T(8,128)(2,1)} fusion(bf16[8,16,3072]{2,1,0:T(8,128)(2,1)} %collective-permute-done.5, bf16[8,16,3072]{2,1,0:T(8,128)(2,1)} %collective-permute-done.4, bf16[8,16,3072]{2,1,0:T(8,128)(2,1)S(1)} %collective-permute-done.3, bf16[8,16,3072]{2,1,0:T(8,128)(2,1)S(1)} %bitcast.46), kind=kLoop, calls=%fused_computation | loop fusion | flops 12582912 | bytes 6291456 | tf_op jit(solution)/shard_map/concatenate | solution.py:482
  114.2 4.2 %all-to-all-start.1 = ((bf16[8,64,3072]{2,1,0:T(8,128)(2,1)}), bf16[8,64,3072]{2,1,0:T(8,128)(2,1)S(1)}, u32[]{:S(2)}, u32[]{:S(2)}) async-start(bf16[8,64,3072]{2,1,0:T(8,128)(2,1)} %pad_maximum_fusion), calls=%async_computation.1 | async-start | bytes 6291456 | tf_op jit(solution)/shard_map/all_to_all | solution.py:483
  119.1 16.7 %collective-permute-start.6 = (bf16[8,16,2560]{2,1,0:T(8,128)(2,1)}, bf16[8,16,2560]{2,1,0:T(8,128)(2,1)}, u32[]{:S(2)}, u32[]{:S(2)}) collective-permute-start(bf16[8,16,2560]{2,1,0:T(8,128)(2,1)} %bitcast.55), channel_id=1, source_target_pairs={{0,8},{8,0},{16,24},{24,16},{1,9},{9,1},{17,25},{25,17},{2,10},{10... | collective-permute-start | bytes 1966088 | tf_op jit(solution)/shard_map/ppermute | solution.py:479
  138.9 17.9 %shard_map.125 = (bf16[2,4,16,1536]{3,2,1,0:T(8,128)(2,1)}, bf16[2,4,16,1536]{3,2,1,0:T(8,128)(2,1)}, bf16[2,4,16,1536]{3,2,1,0:T(8,128)(2,1)}, bf16[2,4,16,1536]{3,2,1,0:T(8,128)(2,1)}, bf16[8,6,16,1024]{3,2,1,0:T(8,128)(2,1)}) custom-call(s32[2]{0:T(128)} %pad_add_fusion.3.place, bf16[2,128,126976]{2,1,0:T(8,128)(2,1)} %volts.7, f32[16,4096]{1,0:T(8,128)} %prototype.7, ...), custom_call_target="tpu_custom_call" | custom-call | flops 3750000128 | bytes 1 | tf_op jit(solution)/shard_map/pallas_call | solution.py:205
  156.8 8.3 %collective-permute-done.6 = bf16[8,16,2560]{2,1,0:T(8,128)(2,1)} collective-permute-done((bf16[8,16,2560]{2,1,0:T(8,128)(2,1)}, bf16[8,16,2560]{2,1,0:T(8,128)(2,1)}, u32[]{:S(2)}, u32[]{:S(2)}) %collective-permute-start.6) | collective-permute-done | bytes 655392 | tf_op jit(solution)/shard_map/ppermute | solution.py:479
  165.1 17.6 %collective-permute-done.7 = bf16[8,16,2560]{2,1,0:T(8,128)(2,1)} collective-permute-done((bf16[8,16,2560]{2,1,0:T(8,128)(2,1)}, bf16[8,16,2560]{2,1,0:T(8,128)(2,1)}, u32[]{:S(2)}, u32[]{:S(2)}) %collective-permute-start.7) | collective-permute-done | bytes 655392 | tf_op jit(solution)/shard_map/ppermute | solution.py:479
  186.3 2.8 pad_maximum_fusion.1
  189.1 4.4 %all-to-all-start.2 = ((bf16[8,64,2560]{2,1,0:T(8,128)(2,1)}), bf16[8,64,2560]{2,1,0:T(8,128)(2,1)}, u32[]{:S(2)}, u32[]{:S(2)}) async-start(bf16[8,64,2560]{2,1,0:T(8,128)(2,1)} %pad_maximum_fusion.1), calls=%async_computation.2 | async-start | bytes 5242880 | tf_op jit(solution)/shard_map/all_to_all | solution.py:483
  194.9 14.9 %collective-permute-start.10 = (bf16[8,16,1536]{2,1,0:T(8,128)(2,1)}, bf16[8,16,1536]{2,1,0:T(8,128)(2,1)}, u32[]{:S(2)}, u32[]{:S(2)}) collective-permute-start(bf16[8,16,1536]{2,1,0:T(8,128)(2,1)} %bitcast.58), channel_id=1, source_target_pairs={{0,16},{8,24},{16,0},{24,8},{1,17},{9,25},{17,1},{25,9},{2,18},{10... | collective-permute-start | bytes 1179656 | tf_op jit(solution)/shard_map/ppermute | solution.py:479
  213.5 3.9 %fusion.9 = (f32[1280,128]{1,0:T(8,128)}, f32[1280,128]{1,0:T(8,128)}) fusion(s32[1280]{0:T(1024)S(1)} %fusion.14), kind=kLoop, calls=%fused_computation.25 | loop fusion | flops 2293760 | bytes 1315840 | tf_op jit(solution)/shard_map/sin | solution.py:35
  217.4 3.8 %sine_multiply_fusion = (f32[1280,4]{1,0:T(8,128)}, f32[1280,4]{1,0:T(8,128)}) fusion(f32[1280,4]{1,0:T(8,128)S(1)} %copy-done.4, f32[1280]{0:T(1024)S(1)} %mul.214), kind=kLoop, calls=%fused_computation.22 | loop fusion | flops 15360 | bytes 66560 | tf_op jit(solution)/shard_map/mul | solution.py:267
  221.2 19.6 %shard_map.126 = (bf16[8,40,512]{2,1,0:T(8,128)(2,1)}, bf16[8,40,512]{2,1,0:T(8,128)(2,1)}, bf16[8,40,512]{2,1,0:T(8,128)(2,1)}, bf16[8,40,512]{2,1,0:T(8,128)(2,1)}) custom-call(s32[1280,1]{1,0:T(8,128)} %add_select_fusion.1.row_branch, f32[1280,4]{1,0:T(8,128)} %get-tuple-element.193.hi_c, f32[1280,4]{1,0:T(8,128)} %get-tuple-element.192.hi_s, ...), custom_call_target="tpu_custom_call" | custom-call | flops 10000000000 | bytes 1 | tf_op jit(solution)/shard_map/pallas_call | solution.py:273
  241.4 2.5 pad_maximum_fusion.2
  243.9 4.3 %all-to-all-start.3 = ((bf16[8,64,1536]{2,1,0:T(8,128)(2,1)}), bf16[8,64,1536]{2,1,0:T(8,128)(2,1)}, u32[]{:S(2)}, u32[]{:S(2)}) async-start(bf16[8,64,1536]{2,1,0:T(8,128)(2,1)} %pad_maximum_fusion.2), calls=%async_computation.3 | async-start | bytes 3145728 | tf_op jit(solution)/shard_map/all_to_all | solution.py:483
  248.5 4.3 %collective-permute-start.12 = (bf16[8,40,512]{2,1,0:T(8,128)(2,1)}, bf16[8,40,512]{2,1,0:T(8,128)(2,1)}, u32[]{:S(2)}, u32[]{:S(2)}) collective-permute-start(bf16[8,40,512]{2,1,0:T(8,128)(2,1)} %get-tuple-element.166), channel_id=1, source_target_pairs={{0,8},{8,0},{16,24},{24,16},{1,9},{9,1},{17,25},{25,17},{2,10},{10... | collective-permute-start | bytes 983048 | tf_op jit(solution)/shard_map/ppermute | solution.py:479
  253.0 2.4 collective-permute-start.14
  256.6 12.4 %shard_map.127.weight_hbm = bf16[20,512,256]{2,1,0:T(8,128)(2,1)} custom-call(s32[20]{0:T(128)} %dynamic_slice.3.channel, f32[256,256]{1,0:T(8,128)} %delays.1, f32[256,256]{1,0:T(8,128)} %gains.1), custom_call_target="tpu_custom_call" | custom-call | flops 1 | bytes 1 | tf_op jit(solution)/shard_map/pallas_call | solution.py:383
  269.0 9.8 %collective-permute-done.13 = bf16[8,40,512]{2,1,0:T(8,128)(2,1)} collective-permute-done((bf16[8,40,512]{2,1,0:T(8,128)(2,1)}, bf16[8,40,512]{2,1,0:T(8,128)(2,1)}, u32[]{:S(2)}, u32[]{:S(2)}) %collective-permute-start.13) | collective-permute-done | bytes 327712 | tf_op jit(solution)/shard_map/ppermute | solution.py:479
  278.8 2.4 pad_maximum_fusion.3
  281.1 4.5 %all-to-all-start.4 = ((bf16[8,160,512]{2,1,0:T(8,128)(2,1)}), bf16[8,160,512]{2,1,0:T(8,128)(2,1)}, u32[]{:S(2)}, u32[]{:S(2)}) async-start(bf16[8,160,512]{2,1,0:T(8,128)(2,1)} %pad_maximum_fusion.3), calls=%async_computation.4 | async-start | bytes 2621440 | tf_op jit(solution)/shard_map/all_to_all | solution.py:483
  286.9 16.9 %shard_map.128 = f32[2,1024,1024]{2,1,0:T(8,128)} custom-call(s32[1]{0:T(128)} %bitcast.here_ref, bf16[8,64,1024]{2,1,0:T(8,128)(2,1)S(1)} %copy-done.1, bf16[8,64,1024]{2,1,0:T(8,128)(2,1)S(1)} %copy-done.1, bf16[8,64,1024]{2,1,0:T(8,128)(2,1)S(1)} %copy-done.1, bf16[8,64,1024]{2,1,0:T(8,128)(2,1)S(1)} %copy-done.1, ...), custom_call_target="tpu_custom_call" | custom-call | flops 1 | bytes 1 | tf_op jit(solution)/shard_map/pallas_call | solution.py:345
  303.8 2.5 copy-done.2
  307.5 7.6 %shard_map.129 = f32[1,20,2,16,512]{4,3,2,1,0:T(8,128)} custom-call(bf16[8,160,512]{2,1,0:T(8,128)(2,1)} %all-to-all-done.4.spectrum, bf16[1024,512]{1,0:T(8,128)(2,1)S(1)} %copy-done.3, bf16[20,512,256]{2,1,0:T(8,128)(2,1)S(1)} %copy-done.2), custom_call_target="tpu_custom_call" | custom-call | flops 1 | bytes 1 | tf_op jit(solution)/shard_map/pallas_call | solution.py:450
  (93 shorter events, 20.8 us)
Async XLA Ops:
  14.8 33.9 %collective-permute-start = (bf16[8,16,1024]{2,1,0:T(8,128)(2,1)}, bf16[8,16,1024]{2,1,0:T(8,128)(2,1)S(1)}, u32[]{:S(2)}, u32[]{:S(2)}) collective-permute-start(bf16[8,16,1024]{2,1,0:T(8,128)(2,1)} %bitcast.61), channel_id=1, source_target_pairs={{0,8},{8,0},{16,24},{24,16},{1,9},{9,1},{17,25},{25,17},{2,10},{10... | collective-permute-start | bytes 786440 | tf_op jit(solution)/shard_map/ppermute | solution.py:479
  17.8 30.9 %collective-permute-start.1 = (bf16[8,16,1024]{2,1,0:T(8,128)(2,1)}, bf16[8,16,1024]{2,1,0:T(8,128)(2,1)S(1)}, u32[]{:S(2)}, u32[]{:S(2)}) collective-permute-start(bf16[8,16,1024]{2,1,0:T(8,128)(2,1)} %bitcast.60), channel_id=1, source_target_pairs={{0,16},{8,24},{16,0},{24,8},{1,17},{9,25},{17,1},{25,9},{2,18},{10... | collective-permute-start | bytes 786440 | tf_op jit(solution)/shard_map/ppermute | solution.py:479
  20.4 28.3 %collective-permute-start.2 = (bf16[8,16,1024]{2,1,0:T(8,128)(2,1)}, bf16[8,16,1024]{2,1,0:T(8,128)(2,1)S(1)}, u32[]{:S(2)}, u32[]{:S(2)}) collective-permute-start(bf16[8,16,1024]{2,1,0:T(8,128)(2,1)} %bitcast.59), channel_id=1, source_target_pairs={{0,24},{8,16},{16,8},{24,0},{1,25},{9,17},{17,9},{25,1},{2,26},{10... | collective-permute-start | bytes 786440 | tf_op jit(solution)/shard_map/ppermute | solution.py:479
  21.1 27.7 %copy-start.8 = (bf16[2,4,16,1024]{3,2,1,0:T(8,128)(2,1)S(1)}, bf16[2,4,16,1024]{3,2,1,0:T(8,128)(2,1)}, u32[]{:S(2)}) copy-start(bf16[2,4,16,1024]{3,2,1,0:T(8,128)(2,1)} %get-tuple-element.92) | copy-start | bytes 786436
  49.8 60.5 %all-to-all-start = ((bf16[8,64,1024]{2,1,0:T(8,128)(2,1)}), bf16[8,64,1024]{2,1,0:T(8,128)(2,1)S(1)}, u32[]{:S(2)}, u32[]{:S(2)}) async-start(bf16[8,64,1024]{2,1,0:T(8,128)(2,1)} %pad_maximum_fusion.4), calls=%async_computation | async-start | bytes 2097152 | tf_op jit(solution)/shard_map/all_to_all | solution.py:483
  53.7 36.7 %collective-permute-start.3 = (bf16[8,16,3072]{2,1,0:T(8,128)(2,1)}, bf16[8,16,3072]{2,1,0:T(8,128)(2,1)S(1)}, u32[]{:S(2)}, u32[]{:S(2)}) collective-permute-start(bf16[8,16,3072]{2,1,0:T(8,128)(2,1)} %bitcast.8), channel_id=1, source_target_pairs={{0,8},{8,0},{16,24},{24,16},{1,9},{9,1},{17,25},{25,17},{2,10},{10... | collective-permute-start | bytes 2359304 | tf_op jit(solution)/shard_map/ppermute | solution.py:479
  54.4 55.9 %collective-permute-start.4 = (bf16[8,16,3072]{2,1,0:T(8,128)(2,1)}, bf16[8,16,3072]{2,1,0:T(8,128)(2,1)}, u32[]{:S(2)}, u32[]{:S(2)}) collective-permute-start(bf16[8,16,3072]{2,1,0:T(8,128)(2,1)} %bitcast.9), channel_id=1, source_target_pairs={{0,16},{8,24},{16,0},{24,8},{1,17},{9,25},{17,1},{25,9},{2,18},{10... | collective-permute-start | bytes 2359304 | tf_op jit(solution)/shard_map/ppermute | solution.py:479
  57.9 52.4 %collective-permute-start.5 = (bf16[8,16,3072]{2,1,0:T(8,128)(2,1)}, bf16[8,16,3072]{2,1,0:T(8,128)(2,1)}, u32[]{:S(2)}, u32[]{:S(2)}) collective-permute-start(bf16[8,16,3072]{2,1,0:T(8,128)(2,1)} %bitcast.10), channel_id=1, source_target_pairs={{0,24},{8,16},{16,8},{24,0},{1,25},{9,17},{17,9},{25,1},{2,26},{10... | collective-permute-start | bytes 2359304 | tf_op jit(solution)/shard_map/ppermute | solution.py:479
  58.7 51.6 %copy-start.5 = (bf16[2,4,16,3072]{3,2,1,0:T(8,128)(2,1)S(1)}, bf16[2,4,16,3072]{3,2,1,0:T(8,128)(2,1)}, u32[]{:S(2)}) copy-start(bf16[2,4,16,3072]{3,2,1,0:T(8,128)(2,1)} %get-tuple-element.97) | copy-start | bytes 2359300
  110.3 3.9 %copy-start = (bf16[8,64,1024]{2,1,0:T(8,128)(2,1)}, bf16[8,64,1024]{2,1,0:T(8,128)(2,1)S(1)}, u32[]{:S(2)}) copy-start(bf16[8,64,1024]{2,1,0:T(8,128)(2,1)S(1)} %all-to-all-done.refs_0_.refs_1_.refs_2_.refs_3_) | copy-start | bytes 3145732
  114.2 68.4 %all-to-all-start.1 = ((bf16[8,64,3072]{2,1,0:T(8,128)(2,1)}), bf16[8,64,3072]{2,1,0:T(8,128)(2,1)S(1)}, u32[]{:S(2)}, u32[]{:S(2)}) async-start(bf16[8,64,3072]{2,1,0:T(8,128)(2,1)} %pad_maximum_fusion), calls=%async_computation.1 | async-start | bytes 6291456 | tf_op jit(solution)/shard_map/all_to_all | solution.py:483
  119.1 46.0 %collective-permute-start.6 = (bf16[8,16,2560]{2,1,0:T(8,128)(2,1)}, bf16[8,16,2560]{2,1,0:T(8,128)(2,1)}, u32[]{:S(2)}, u32[]{:S(2)}) collective-permute-start(bf16[8,16,2560]{2,1,0:T(8,128)(2,1)} %bitcast.55), channel_id=1, source_target_pairs={{0,8},{8,0},{16,24},{24,16},{1,9},{9,1},{17,25},{25,17},{2,10},{10... | collective-permute-start | bytes 1966088 | tf_op jit(solution)/shard_map/ppermute | solution.py:479
  135.8 46.9 %collective-permute-start.7 = (bf16[8,16,2560]{2,1,0:T(8,128)(2,1)}, bf16[8,16,2560]{2,1,0:T(8,128)(2,1)}, u32[]{:S(2)}, u32[]{:S(2)}) collective-permute-start(bf16[8,16,2560]{2,1,0:T(8,128)(2,1)} %bitcast.54), channel_id=1, source_target_pairs={{0,16},{8,24},{16,0},{24,8},{1,17},{9,25},{17,1},{25,9},{2,18},{10... | collective-permute-start | bytes 1966088 | tf_op jit(solution)/shard_map/ppermute | solution.py:479
  136.7 45.9 %collective-permute-start.8 = (bf16[8,16,2560]{2,1,0:T(8,128)(2,1)}, bf16[8,16,2560]{2,1,0:T(8,128)(2,1)}, u32[]{:S(2)}, u32[]{:S(2)}) collective-permute-start(bf16[8,16,2560]{2,1,0:T(8,128)(2,1)} %bitcast.53), channel_id=1, source_target_pairs={{0,24},{8,16},{16,8},{24,0},{1,25},{9,17},{17,9},{25,1},{2,26},{10... | collective-permute-start | bytes 1966088 | tf_op jit(solution)/shard_map/ppermute | solution.py:479
  138.9 43.8 %copy-start.10 = (s32[384,1]{0,1:T(1,128)S(1)}, s32[384,1]{0,1:T(1,128)}, u32[]{:S(2)}) copy-start(s32[384,1]{0,1:T(1,128)} %param.17) | copy-start | bytes 4612
  138.9 45.6 %copy-start.9 = (s32[384]{0:T(512)S(1)}, s32[384]{0:T(512)}, u32[]{:S(2)}) copy-start(s32[384]{0:T(512)} %param.13) | copy-start | bytes 4612
  189.1 52.3 %all-to-all-start.2 = ((bf16[8,64,2560]{2,1,0:T(8,128)(2,1)}), bf16[8,64,2560]{2,1,0:T(8,128)(2,1)}, u32[]{:S(2)}, u32[]{:S(2)}) async-start(bf16[8,64,2560]{2,1,0:T(8,128)(2,1)} %pad_maximum_fusion.1), calls=%async_computation.2 | async-start | bytes 5242880 | tf_op jit(solution)/shard_map/all_to_all | solution.py:483
  194.9 22.4 %copy-start.4 = (f32[1280,4]{1,0:T(8,128)S(1)}, f32[1280,4]{1,0:T(8,128)}, u32[]{:S(2)}) copy-start(f32[1280,4]{1,0:T(8,128)} %copy.25) | copy-start | bytes 61444
  194.9 46.4 %collective-permute-start.10 = (bf16[8,16,1536]{2,1,0:T(8,128)(2,1)}, bf16[8,16,1536]{2,1,0:T(8,128)(2,1)}, u32[]{:S(2)}, u32[]{:S(2)}) collective-permute-start(bf16[8,16,1536]{2,1,0:T(8,128)(2,1)} %bitcast.58), channel_id=1, source_target_pairs={{0,16},{8,24},{16,0},{24,8},{1,17},{9,25},{17,1},{25,9},{2,18},{10... | collective-permute-start | bytes 1179656 | tf_op jit(solution)/shard_map/ppermute | solution.py:479
  209.8 31.6 %collective-permute-start.11 = (bf16[8,16,1536]{2,1,0:T(8,128)(2,1)}, bf16[8,16,1536]{2,1,0:T(8,128)(2,1)}, u32[]{:S(2)}, u32[]{:S(2)}) collective-permute-start(bf16[8,16,1536]{2,1,0:T(8,128)(2,1)} %bitcast.57), channel_id=1, source_target_pairs={{0,24},{8,16},{16,8},{24,0},{1,25},{9,17},{17,9},{25,1},{2,26},{10... | collective-permute-start | bytes 1179656 | tf_op jit(solution)/shard_map/ppermute | solution.py:479
  211.3 30.1 %collective-permute-start.9 = (bf16[8,16,1536]{2,1,0:T(8,128)(2,1)}, bf16[8,16,1536]{2,1,0:T(8,128)(2,1)}, u32[]{:S(2)}, u32[]{:S(2)}) collective-permute-start(bf16[8,16,1536]{2,1,0:T(8,128)(2,1)} %bitcast.56), channel_id=1, source_target_pairs={{0,8},{8,0},{16,24},{24,16},{1,9},{9,1},{17,25},{25,17},{2,10},{10... | collective-permute-start | bytes 1179656 | tf_op jit(solution)/shard_map/ppermute | solution.py:479
  221.2 20.2 %copy-start.6 = (bf16[2,4,16,1536]{3,2,1,0:T(8,128)(2,1)S(1)}, bf16[2,4,16,1536]{3,2,1,0:T(8,128)(2,1)}, u32[]{:S(2)}) copy-start(bf16[2,4,16,1536]{3,2,1,0:T(8,128)(2,1)} %get-tuple-element.126) | copy-start | bytes 1179652
  241.4 7.1 %copy-start.11 = (s32[256]{0:T(256)S(1)}, s32[256]{0:T(256)}, u32[]{:S(2)}) copy-start(s32[256]{0:T(256)} %param.14) | copy-start | bytes 3076
  243.9 34.8 %all-to-all-start.3 = ((bf16[8,64,1536]{2,1,0:T(8,128)(2,1)}), bf16[8,64,1536]{2,1,0:T(8,128)(2,1)}, u32[]{:S(2)}, u32[]{:S(2)}) async-start(bf16[8,64,1536]{2,1,0:T(8,128)(2,1)} %pad_maximum_fusion.2), calls=%async_computation.3 | async-start | bytes 3145728 | tf_op jit(solution)/shard_map/all_to_all | solution.py:483
  248.5 20.4 %collective-permute-start.12 = (bf16[8,40,512]{2,1,0:T(8,128)(2,1)}, bf16[8,40,512]{2,1,0:T(8,128)(2,1)}, u32[]{:S(2)}, u32[]{:S(2)}) collective-permute-start(bf16[8,40,512]{2,1,0:T(8,128)(2,1)} %get-tuple-element.166), channel_id=1, source_target_pairs={{0,8},{8,0},{16,24},{24,16},{1,9},{9,1},{17,25},{25,17},{2,10},{10... | collective-permute-start | bytes 983048 | tf_op jit(solution)/shard_map/ppermute | solution.py:479
  252.9 25.9 %collective-permute-start.13 = (bf16[8,40,512]{2,1,0:T(8,128)(2,1)}, bf16[8,40,512]{2,1,0:T(8,128)(2,1)}, u32[]{:S(2)}, u32[]{:S(2)}) collective-permute-start(bf16[8,40,512]{2,1,0:T(8,128)(2,1)} %get-tuple-element.167), channel_id=1, source_target_pairs={{0,16},{8,24},{16,0},{24,8},{1,17},{9,25},{17,1},{25,9},{2,18},{10... | collective-permute-start | bytes 983048 | tf_op jit(solution)/shard_map/ppermute | solution.py:479
  253.0 25.8 %collective-permute-start.14 = (bf16[8,40,512]{2,1,0:T(8,128)(2,1)}, bf16[8,40,512]{2,1,0:T(8,128)(2,1)}, u32[]{:S(2)}, u32[]{:S(2)}) collective-permute-start(bf16[8,40,512]{2,1,0:T(8,128)(2,1)} %get-tuple-element.168), channel_id=1, source_target_pairs={{0,24},{8,16},{16,8},{24,0},{1,25},{9,17},{17,9},{25,1},{2,26},{10... | collective-permute-start | bytes 983048 | tf_op jit(solution)/shard_map/ppermute | solution.py:479
  256.6 22.2 %copy-start.7 = (bf16[8,40,512]{2,1,0:T(8,128)(2,1)S(1)}, bf16[8,40,512]{2,1,0:T(8,128)(2,1)}, u32[]{:S(2)}) copy-start(bf16[8,40,512]{2,1,0:T(8,128)(2,1)} %get-tuple-element.176) | copy-start | bytes 983044
  281.1 22.7 %all-to-all-start.4 = ((bf16[8,160,512]{2,1,0:T(8,128)(2,1)}), bf16[8,160,512]{2,1,0:T(8,128)(2,1)}, u32[]{:S(2)}, u32[]{:S(2)}) async-start(bf16[8,160,512]{2,1,0:T(8,128)(2,1)} %pad_maximum_fusion.3), calls=%async_computation.4 | async-start | bytes 2621440 | tf_op jit(solution)/shard_map/all_to_all | solution.py:483
  285.6 1.2 copy-start.1
  303.8 2.5 copy-start.2
  306.3 1.2 copy-start.3

commit v10 on v8

--- a/solution.py
+++ b/solution.py
@@ -7,6 +7,7 @@
 from jax import lax
 from jax.experimental import pallas as pl
 from jax.experimental.pallas import tpu as pltpu
+from jax.sharding import Mesh
 from jax.sharding import PartitionSpec as P
 
 NCH = 4096
@@ -92,6 +93,7 @@
 
 def channel_kernel(first, row_block, volts, prototype, cosines, sines, turn_c, turn_s, out, branches, *scratch):
     taps_wide, table, filtered, product = scratch
+    near = out.shape[1]
     taps = taps_wide.shape[0]
     length = taps_wide.shape[2]
     frames = filtered.shape[2]
@@ -168,13 +170,14 @@
                 pieces = [product[b, pl.ds(top, ROWS), lane : lane + LANES] for b in range(RADIX)]
                 for g, piece in enumerate(gather_blocks(pieces, lane_ids)):
                     at = pl.multiple_of((part * frames + f) * LANES, LANES)
-                    out[g, band, :, pl.ds(at, LANES)] = piece.astype(out.dtype)
+                    out[band, g % near, g // near, :, pl.ds(at, LANES)] = piece.astype(out.dtype)
         return carry
 
     lax.fori_loop(0, frames, regroup, 0)
 
 
-def channelise(row_block, volts, prototype, tables, first, frames):
+def channelise(row_block, volts, prototype, tables, first, frames, far):
+    near = RADIX // far
     taps = prototype.shape[0]
     length = volts.shape[2] if first > 0 else (frames + taps - 1) * NCH
     depth = NCH // RADIX
@@ -190,7 +193,7 @@
             ]
             + [pl.BlockSpec(x.shape, lambda i, row: (0, 0)) for x in (prototype, *tables)],
             out_specs=[
-                pl.BlockSpec((RADIX, bands, ROWS, wide), lambda i, row: (0, 0, 0, 0)),
+                pl.BlockSpec((bands, near, far, ROWS, wide), lambda i, row: (0, 0, 0, 0, 0)),
                 pl.BlockSpec((RADIX, frames, ROWS, 2 * depth), lambda i, row: (0, 0, 0, 0)),
             ],
             scratch_shapes=[
@@ -201,7 +204,7 @@
             ],
         ),
         out_shape=[
-            jax.ShapeDtypeStruct((RADIX, bands, ROWS, wide), jnp.bfloat16),
+            jax.ShapeDtypeStruct((bands, near, far, ROWS, wide), jnp.bfloat16),
             jax.ShapeDtypeStruct((RADIX, frames, ROWS, 2 * depth), jnp.bfloat16),
         ],
         compiler_params=pltpu.CompilerParams(vmem_limit_bytes=VMEM),
@@ -259,23 +262,24 @@
 
 
 def correlate(pieces, halves, lanes):
-    senders, sub, _ = pieces[0][0].shape
+    sb_count, near, far, sub, _ = pieces[0][0].shape
     half = FRAMES * lanes
-    signals = senders * halves * sub
-    count = max(1, signals // 256)
-    each = senders // count
+    each = near * sb_count
     block = each * halves * sub
+    signals = far * block
 
     def kernel(*refs):
         parts, (out, held, turned, made, in_sems, out_sems) = refs[: len(pieces)], refs[len(pieces) :]
-        coming = [[] for _ in range(count)]
+        coming = [[] for _ in range(far)]
         for index, (_, which, first, frames) in enumerate(pieces):
-            for q in range(count):
-                for part in range(2):
-                    src = parts[index].at[pl.ds(q * each, each), :, pl.ds(part * frames * lanes, frames * lanes)]
-                    dst = held.at[q, :, which, :, pl.ds(part * half + first * lanes, frames * lanes)]
-                    sem = in_sems.at[(index * count + q) * 2 + part]
-                    coming[q].append(pltpu.make_async_copy(src, dst, sem))
+            for q in range(far):
+                for x in range(near):
+                    for part in range(2):
+                        src = parts[index].at[:, x, q, :, pl.ds(part * frames * lanes, frames * lanes)]
+                        at = pl.ds(part * half + first * lanes, frames * lanes)
+                        dst = held.at[q, pl.ds(x * sb_count, sb_count), which, :, at]
+                        sem = in_sems.at[((index * far + q) * near + x) * 2 + part]
+                        coming[q].append(pltpu.make_async_copy(src, dst, sem))
         for copies in coming:
             for copy in copies:
                 copy.start()
@@ -286,7 +290,7 @@
         inverse = 1.0 / half
         going = [[], []]
         slot = 0
-        for i in range(count):
+        for i in range(far):
             for copy in coming[i]:
                 copy.wait()
             left = held[i].reshape(block, 2 * half)
@@ -327,13 +331,13 @@
         out_specs=pl.BlockSpec(memory_space=pl.ANY),
         out_shape=jax.ShapeDtypeStruct((2, signals, signals), jnp.float32),
         scratch_shapes=[
-            pltpu.VMEM((count, each, halves, sub, 2 * half), jnp.bfloat16),
+            pltpu.VMEM((far, each, halves, sub, 2 * half), jnp.bfloat16),
             pltpu.VMEM((block, 2 * half), jnp.bfloat16),
             pltpu.VMEM((2, 2, 2, block, block), jnp.float32),
-            pltpu.SemaphoreType.DMA((2 * count * len(pieces),)),
+            pltpu.SemaphoreType.DMA((2 * far * near * len(pieces),)),
             pltpu.SemaphoreType.DMA((2, 2, 2)),
         ],
-        compiler_params=pltpu.CompilerParams(vmem_limit_bytes=VMEM),
+        compiler_params=pltpu.CompilerParams(vmem_limit_bytes=VMEM // 2),
         cost_estimate=NO_COST,
     )(*[piece[0] for piece in pieces])
 
@@ -433,15 +437,16 @@
             pltpu.VMEM(weights.shape, weights.dtype),
             pltpu.SemaphoreType.DMA,
         ],
-        compiler_params=pltpu.CompilerParams(vmem_limit_bytes=VMEM),
+        compiler_params=pltpu.CompilerParams(vmem_limit_bytes=VMEM // 2),
         cost_estimate=NO_COST,
     )(spectra, chooser, weights)
 
 
 def body(volts, prototype, beam_channels, station_index, delays, gains, assign):
     sig_dev = volts.shape[1]
-    st_count, sb_count = lax.axis_size("st"), lax.axis_size("sb")
-    st_here, sb_here = lax.axis_index("st").astype(jnp.int32), lax.axis_index("sb").astype(jnp.int32)
+    far, near, sb_count = lax.axis_size("far"), lax.axis_size("near"), lax.axis_size("sb")
+    far_here, near_here, sb_here = [lax.axis_index(name).astype(jnp.int32) for name in ("far", "near", "sb")]
+    st_count = far * near
     devices = st_count * sb_count
     group = NCH // devices
     fine = group // RADIX
@@ -449,7 +454,7 @@
     barrier = lax.optimization_barrier
 
     def exchange(x):
-        return lax.all_to_all(x, ("st", "sb"), split_axis=0, concat_axis=0, tiled=True)
+        return lax.all_to_all(x, ("sb", "near", "far"), split_axis=0, concat_axis=0, tiled=True)
 
     share = sig_dev // sb_count
     sub = min(share, ROWS)
@@ -462,12 +467,13 @@
     def channels_of(c, here):
         which, first, frames = plan[c]
         row_block = (here * share // ROWS + which)[None]
-        out, kept = channelise(row_block, volts, prototype, constants, first, frames)
+        out, kept = channelise(row_block, volts, prototype, constants, first, frames, far)
         if sub < ROWS:
-            out = lax.dynamic_slice_in_dim(out, inside, sub, axis=2)
+            out = lax.dynamic_slice_in_dim(out, inside, sub, axis=3)
         inner = st_count // RADIX
         if inner > 1:
-            out = out.reshape(RADIX, sb_count, sub, 2 * frames, RADIX, inner, fine).transpose(0, 5, 1, 2, 3, 4, 6)
+            out = out.reshape(sb_count, near // inner, far, sub, 2 * frames, RADIX, inner, fine)
+            out = out.transpose(0, 1, 6, 2, 3, 4, 5, 7)
         return out.reshape(devices, sub, -1), kept
 
     lists = (assign, beam_channels, station_index)
@@ -487,8 +493,9 @@
     position = jnp.sum(taken * jnp.cumsum(taken, axis=0), axis=1) - 1
     place = owners * SLOTS + position
     slot_ids = (
-        jnp.arange(st_count, dtype=jnp.int32)[:, None, None] * per_dev
-        + jnp.arange(sb_count, dtype=jnp.int32)[:, None] * SLOTS
+        jnp.arange(sb_count, dtype=jnp.int32)[:, None, None, None] * SLOTS
+        + jnp.arange(near, dtype=jnp.int32)[:, None, None] * per_dev
+        + jnp.arange(far, dtype=jnp.int32)[:, None] * (near * per_dev)
         + jnp.arange(per_dev, dtype=jnp.int32)
     ).reshape(-1)
     picker = (place[None, :] == slot_ids[:, None]).astype(jnp.int32)
@@ -499,7 +506,8 @@
         return jnp.broadcast_to(values.reshape(devices, 1, per_dev), (devices, 2, per_dev)).reshape(-1)
 
     turned = jnp.broadcast_to(jnp.arange(2, dtype=jnp.int32)[None, :, None], (devices, 2, per_dev)).reshape(-1)
-    mine = lax.dynamic_slice_in_dim(slot_channel, (st_here * sb_count + sb_here) * per_dev, per_dev)
+    own = ((sb_here * near + near_here) * far + far_here) * per_dev
+    mine = lax.dynamic_slice_in_dim(slot_channel, own, per_dev)
     tables = slot_tables(by_row(slot_channel), by_row(filled), turned)
     spectra = slot_spectra(tables, branches, 2 * per_dev)
     if sub < ROWS:
@@ -510,8 +518,10 @@
     arrived.append(exchange(out))
     weights = beam_weights(mine, delays, gains)
     signal_ids = (
-        jnp.arange(halves, dtype=jnp.int32)[:, None, None] * sub
-        + jnp.arange(devices, dtype=jnp.int32)[:, None] * share
+        jnp.arange(halves, dtype=jnp.int32)[:, None, None, None, None] * sub
+        + jnp.arange(sb_count, dtype=jnp.int32)[:, None, None, None] * share
+        + jnp.arange(near, dtype=jnp.int32)[:, None, None] * sig_dev
+        + jnp.arange(far, dtype=jnp.int32)[:, None] * (near * sig_dev)
         + jnp.arange(sub, dtype=jnp.int32)
     ).reshape(-1)
     wanted = (station_index[None, :] * 2 + jnp.arange(2, dtype=jnp.int32)[:, None]).reshape(-1)
@@ -519,8 +529,9 @@
 
     spectra, weights, chooser, arrived[-1:] = barrier((spectra, weights, chooser, arrived[-1:]))
     slot_received = exchange(spectra)
+    arrived = [x.reshape(sb_count, near, far, sub, -1) for x in arrived]
     if halves == 1:
-        arrived = [x.reshape(-1, min(256, devices * sub), x.shape[2]) for x in arrived]
+        arrived = [x.transpose(2, 1, 0, 3, 4).reshape(1, 1, far, near * sb_count * sub, -1) for x in arrived]
     visibility = correlate([(x, *part) for x, part in zip(arrived, plan)], halves, group)
     signals = visibility.shape[1]
     beam_out = combine(slot_received, chooser, weights, sub)
@@ -528,6 +539,10 @@
 
 
 def solution(mesh):
-    in_specs = (P(None, "st", None), P(), P(), P(), P(), P(), P())
-    out_specs = (P(None, "sb", "st", None, None), P("sb", "st", None, None, None))
-    return jax.shard_map(body, mesh=mesh, in_specs=in_specs, out_specs=out_specs, check_vma=False)
+    st_count, sb_count = mesh.shape["st"], mesh.shape["sb"]
+    far = math.gcd(4, st_count)
+    planes = Mesh(mesh.devices.reshape(far, st_count // far, sb_count), ("far", "near", "sb"))
+    st = ("far", "near")
+    in_specs = (P(None, st, None), P(), P(), P(), P(), P(), P())
+    out_specs = (P(None, "sb", st, None, None), P("sb", st, None, None, None))
+    return jax.shard_map(body, mesh=planes, in_specs=in_specs, out_specs=out_specs, check_vma=False)

time: 271 us -> 271 us (level)
  waiting for transfers between devices: 98.9 us -> 95.6 us
    all_to_all x4, waiting for transfers between devices: 98.9 us -> 95.6 us  [exchange(): lax.all_to_all(x, ('sb', 'near', 'far'), split_axis=0, concat_axis=0, til...]
    unnamed x13 -> x15, local copies, waits for them, and re-layouts: 3.87 us -> 5.93 us
where the time goes in v10:
time: 271 us; the launch traced here: 270 us
  Pallas kernels  125 us (46%)
  waiting for transfers between devices  95.6 us (35%)
  starting transfers between devices  23 us (8%)
  other arithmetic  15.1 us (6%)
  local copies, waits for them, and re-layouts  9.77 us (4%)
    all_to_all x4, waiting for transfers between devices, exchange(): lax.all_to_all(x, ('sb', 'near', 'far'), split_axis=0, concat_axis=0, til...  95.6 us
    pallas_call x3, Pallas kernels, channelise(): pl.pallas_call(functools.partial(channel_kernel, first), grid_spec=pltpu....  68.5 us
    all_to_all x4, starting transfers between devices, exchange(): lax.all_to_all(x, ('sb', 'near', 'far'), split_axis=0, concat_axis=0, til...  23 us
    pallas_call x1, Pallas kernels, slot_spectra(): pl.pallas_call(slot_kernel, out_shape=jax.ShapeDtypeStruct((rows // per,...  19.7 us
    pallas_call x1, Pallas kernels, correlate(): pl.pallas_call(kernel, in_specs=[pl.BlockSpec(memory_space=pl.ANY)] * len...  17.2 us
    pallas_call x1, Pallas kernels, beam_weights(): pl.pallas_call(weight_kernel, grid=(slots,), in_specs=[pl.BlockSpec(memor...  12.4 us
    pallas_call x1, Pallas kernels, combine(): pl.pallas_call(kernel, in_specs=[pl.BlockSpec(memory_space=pltpu.VMEM)] *...  7.6 us
    unnamed x15, local copies, waits for them, and re-layouts  5.93 us
  transfers between devices with their start and end apart: 4, of which 4 were waited for; matrix products, arithmetic and copies ran while one was open for 7% of the time, Pallas kernels for 39%

profile of v10, /device:TPU:0, one launch (start us, length us, event | category | flops | bytes accessed | tf_op | source)
XLA Modules:
  0.0 270.0 jit_solution(16919386722479127282)
XLA Ops:
  0.6 11.5 %shard_map.122 = (bf16[4,2,4,16,1024]{4,3,2,1,0:T(8,128)(2,1)}, bf16[8,4,16,1024]{3,2,1,0:T(8,128)(2,1)}) custom-call(s32[1]{0:T(128)} %bitcast.row_block, bf16[2,128,126976]{2,1,0:T(8,128)(2,1)} %volts.5, f32[16,4096]{1,0:T(8,128)} %prototype.5, f32[512,512]{1,0:T(8,128)} %constant.129.clone.cosines, f32[512,512]{1,0:T(8,128)} %constant.130.clone.sines, ...), custom_call_target="tpu_custom_call" | custom-call | flops 2500000000 | bytes 1 | tf_op jit(solution)/shard_map/pallas_call | solution.py:186
  12.2 7.3 %all-to-all-start = ((bf16[32,16,1024]{2,1,0:T(8,128)(2,1)}), bf16[32,16,1024]{2,1,0:T(8,128)(2,1)S(1)}, u32[]{:S(2)}, u32[]{:S(2)}) async-start(bf16[32,16,1024]{2,1,0:T(8,128)(2,1)} %bitcast.36), calls=%async_computation | async-start | bytes 2097152 | tf_op jit(solution)/shard_map/all_to_all | solution.py:457
  19.6 25.3 %shard_map.123 = (bf16[4,2,4,16,3072]{4,3,2,1,0:T(8,128)(2,1)}, bf16[8,12,16,1024]{3,2,1,0:T(8,128)(2,1)}) custom-call(s32[1]{0:T(128)} %bitcast.2.row_block, bf16[2,128,126976]{2,1,0:T(8,128)(2,1)} %volts.5, f32[16,4096]{1,0:T(8,128)} %prototype.5, f32[512,512]{1,0:T(8,128)} %constant.129.clone.cosines, f32[512,512]{1,0:T(8,128)} %constant.130.clone.sines, ...), custom_call_target="tpu_custom_call" | custom-call | flops 7500000256 | bytes 1 | tf_op jit(solution)/shard_map/pallas_call | solution.py:186
  44.9 1.4 all-to-all-done
  46.3 1.0 copy-done.1
  47.3 4.5 %all-to-all-start.1 = ((bf16[32,16,3072]{2,1,0:T(8,128)(2,1)}), bf16[32,16,3072]{2,1,0:T(8,128)(2,1)S(1)}, u32[]{:S(2)}, u32[]{:S(2)}) async-start(bf16[32,16,3072]{2,1,0:T(8,128)(2,1)} %bitcast.35), calls=%async_computation.1 | async-start | bytes 6291456 | tf_op jit(solution)/shard_map/all_to_all | solution.py:457
  51.9 0.1 add.228
  52.1 0.1 mul.215
  52.2 31.7 %shard_map.124 = (bf16[4,2,4,16,4096]{4,3,2,1,0:T(8,128)(2,1)}, bf16[8,16,16,1024]{3,2,1,0:T(8,128)(2,1)}) custom-call(s32[1]{0:T(128)} %bitcast.5.row_block, bf16[2,128,126976]{2,1,0:T(8,128)(2,1)} %volts.5, f32[16,4096]{1,0:T(8,128)} %prototype.5, f32[512,512]{1,0:T(8,128)} %constant.129.clone.cosines, f32[512,512]{1,0:T(8,128)} %constant.130.clone.sines, ...), custom_call_target="tpu_custom_call" | custom-call | flops 10000000000 | bytes 1 | tf_op jit(solution)/shard_map/pallas_call | solution.py:186
  84.0 1.2 reduce-window.6
  85.2 0.2 slice_reduce_fusion
  85.4 0.2 reduce-window.9
  85.7 0.4 fusion.1
  86.3 1.1 reshape.326
  87.6 1.1 copy.25
  89.0 0.6 dynamic_slice.3.channel
  89.6 2.2 add_select_fusion.1.row_branch
  91.7 3.9 %fusion.9 = (f32[1280,128]{1,0:T(8,128)}, f32[1280,128]{1,0:T(8,128)}) fusion(s32[1280]{0:T(1024)S(1)} %fusion.14), kind=kLoop, calls=%fused_computation.20 | loop fusion | flops 2293760 | bytes 1315840 | tf_op jit(solution)/shard_map/sin | solution.py:34
  95.7 5.1 %sine_multiply_fusion = (f32[1280,4]{1,0:T(8,128)}, f32[1280,4]{1,0:T(8,128)}) fusion(f32[1280,4]{1,0:T(8,128)} %copy.25, f32[1280]{0:T(1024)S(1)} %mul.221), kind=kLoop, calls=%fused_computation.17 | loop fusion | flops 15360 | bytes 66560 | tf_op jit(solution)/shard_map/mul | solution.py:246
  100.8 19.7 %shard_map.125 = bf16[32,40,512]{2,1,0:T(8,128)(2,1)} custom-call(s32[1280,1]{1,0:T(8,128)} %add_select_fusion.1.row_branch, f32[1280,4]{1,0:T(8,128)} %get-tuple-element.69.hi_c, f32[1280,4]{1,0:T(8,128)} %get-tuple-element.68.hi_s, f32[1280,128]{1,0:T(8,128)} %get-tuple-element.71.lo_c, f32[1280,128]{1,0:T(8,128)} %get-tuple-element.70.lo_s, ...), custom_call_target="tpu_custom_call" | custom-call | flops 10000000000 | bytes 1 | tf_op jit(solution)/shard_map/pallas_call | solution.py:252
  120.5 2.1 all-to-all-done.1
  122.5 4.8 %all-to-all-start.2 = ((bf16[32,16,4096]{2,1,0:T(8,128)(2,1)}), bf16[32,16,4096]{2,1,0:T(8,128)(2,1)}, u32[]{:S(2)}, u32[]{:S(2)}) async-start(bf16[32,16,4096]{2,1,0:T(8,128)(2,1)} %bitcast.34), calls=%async_computation.2 | async-start | bytes 8388608 | tf_op jit(solution)/shard_map/all_to_all | solution.py:457
  127.8 1.3 compare_convert_fusion.choose
  129.1 12.4 %shard_map.126.weight_hbm = bf16[20,512,256]{2,1,0:T(8,128)(2,1)} custom-call(s32[20]{0:T(128)} %dynamic_slice.3.channel, f32[256,256]{1,0:T(8,128)} %delays.1, f32[256,256]{1,0:T(8,128)} %gains.1), custom_call_target="tpu_custom_call" | custom-call | flops 1 | bytes 1 | tf_op jit(solution)/shard_map/pallas_call | solution.py:366
  141.4 78.4 %all-to-all-done.2 = bf16[32,16,4096]{2,1,0:T(8,128)(2,1)} async-done(((bf16[32,16,4096]{2,1,0:T(8,128)(2,1)}), bf16[32,16,4096]{2,1,0:T(8,128)(2,1)}, u32[]{:S(2)}, u32[]{:S(2)}) %all-to-all-start.2) | async-done | bytes 4194336 | tf_op jit(solution)/shard_map/all_to_all | solution.py:457
  219.9 6.4 %all-to-all-start.3 = ((bf16[32,40,512]{2,1,0:T(8,128)(2,1)}), bf16[32,40,512]{2,1,0:T(8,128)(2,1)}, u32[]{:S(2)}, u32[]{:S(2)}) async-start(bf16[32,40,512]{2,1,0:T(8,128)(2,1)} %shard_map.125), calls=%async_computation.3 | async-start | bytes 2621440 | tf_op jit(solution)/shard_map/all_to_all | solution.py:457
  226.3 1.2 copy-done.2
  227.6 17.2 %shard_map.127 = f32[2,1024,1024]{2,1,0:T(8,128)} custom-call(bf16[4,2,4,16,1024]{4,3,2,1,0:T(8,128)(2,1)S(1)} %bitcast.32, bf16[4,2,4,16,3072]{4,3,2,1,0:T(8,128)(2,1)S(1)} %bitcast.31, bf16[4,2,4,16,4096]{4,3,2,1,0:T(8,128)(2,1)} %bitcast.9.refs_2_), custom_call_target="tpu_custom_call" | custom-call | flops 1 | bytes 1 | tf_op jit(solution)/shard_map/pallas_call | solution.py:328
  244.7 13.7 %all-to-all-done.3.spectrum = bf16[32,40,512]{2,1,0:T(8,128)(2,1)} async-done(((bf16[32,40,512]{2,1,0:T(8,128)(2,1)}), bf16[32,40,512]{2,1,0:T(8,128)(2,1)}, u32[]{:S(2)}, u32[]{:S(2)}) %all-to-all-start.3) | async-done | bytes 1310752 | tf_op jit(solution)/shard_map/all_to_all | solution.py:457
  258.5 2.5 copy-done
  261.0 1.2 copy-done.3
  262.2 7.6 %shard_map.128 = f32[1,20,2,16,512]{4,3,2,1,0:T(8,128)} custom-call(bf16[32,40,512]{2,1,0:T(8,128)(2,1)} %all-to-all-done.3.spectrum, bf16[1024,512]{1,0:T(8,128)(2,1)S(1)} %copy-done.3, bf16[20,512,256]{2,1,0:T(8,128)(2,1)S(1)} %copy-done), custom_call_target="tpu_custom_call" | custom-call | flops 1 | bytes 1 | tf_op jit(solution)/shard_map/pallas_call | solution.py:430
  (44 shorter events, 1.4 us)
Async XLA Ops:
  12.2 34.1 %all-to-all-start = ((bf16[32,16,1024]{2,1,0:T(8,128)(2,1)}), bf16[32,16,1024]{2,1,0:T(8,128)(2,1)S(1)}, u32[]{:S(2)}, u32[]{:S(2)}) async-start(bf16[32,16,1024]{2,1,0:T(8,128)(2,1)} %bitcast.36), calls=%async_computation | async-start | bytes 2097152 | tf_op jit(solution)/shard_map/all_to_all | solution.py:457
  46.3 1.0 copy-start.1
  47.3 75.2 %all-to-all-start.1 = ((bf16[32,16,3072]{2,1,0:T(8,128)(2,1)}), bf16[32,16,3072]{2,1,0:T(8,128)(2,1)S(1)}, u32[]{:S(2)}, u32[]{:S(2)}) async-start(bf16[32,16,3072]{2,1,0:T(8,128)(2,1)} %bitcast.35), calls=%async_computation.1 | async-start | bytes 6291456 | tf_op jit(solution)/shard_map/all_to_all | solution.py:457
  52.2 31.7 %copy-start.5 = (s32[384,1]{0,1:T(1,128)S(1)}, s32[384,1]{0,1:T(1,128)}, u32[]{:S(2)}) copy-start(s32[384,1]{0,1:T(1,128)} %param.17) | copy-start | bytes 4612
  52.2 33.5 %copy-start.4 = (s32[384]{0:T(512)S(1)}, s32[384]{0:T(512)}, u32[]{:S(2)}) copy-start(s32[384]{0:T(512)} %param.13) | copy-start | bytes 4612
  122.5 5.3 %copy-start.6 = (s32[256]{0:T(256)S(1)}, s32[256]{0:T(256)}, u32[]{:S(2)}) copy-start(s32[256]{0:T(256)} %param.14) | copy-start | bytes 3076
  122.5 97.4 %all-to-all-start.2 = ((bf16[32,16,4096]{2,1,0:T(8,128)(2,1)}), bf16[32,16,4096]{2,1,0:T(8,128)(2,1)}, u32[]{:S(2)}, u32[]{:S(2)}) async-start(bf16[32,16,4096]{2,1,0:T(8,128)(2,1)} %bitcast.34), calls=%async_computation.2 | async-start | bytes 8388608 | tf_op jit(solution)/shard_map/all_to_all | solution.py:457
  219.9 38.6 %all-to-all-start.3 = ((bf16[32,40,512]{2,1,0:T(8,128)(2,1)}), bf16[32,40,512]{2,1,0:T(8,128)(2,1)}, u32[]{:S(2)}, u32[]{:S(2)}) async-start(bf16[32,40,512]{2,1,0:T(8,128)(2,1)} %shard_map.125), calls=%async_computation.3 | async-start | bytes 2621440 | tf_op jit(solution)/shard_map/all_to_all | solution.py:457
  226.3 1.2 copy-start.2
  258.5 2.5 copy-start
  261.0 1.2 copy-start.3

commit v11 on v10

--- a/solution.py
+++ b/solution.py
@@ -91,46 +91,53 @@
     return [turned[0]] + [pltpu.roll(turned[g], LANES - g * width, 1) for g in range(1, count)]
 
 
-def channel_kernel(first, row_block, volts, prototype, cosines, sines, turn_c, turn_s, out, branches, *scratch):
-    taps_wide, table, filtered, product = scratch
+def channel_kernel(first, row_block, volts_hbm, prototype, cosines, sines, turn_c, turn_s, out, branches, *scratch):
+    volts, waves, taps_wide, table, filtered, product, sems = scratch
     near = out.shape[1]
     taps = taps_wide.shape[0]
     length = taps_wide.shape[2]
-    frames = filtered.shape[2]
+    frames = filtered.shape[3]
     depth = length // RADIX
     bands = depth // LANES
+    top = pl.multiple_of(row_block[0] * ROWS, ROWS)
+    reach = pl.ds(first * length, volts.shape[2])
+    coming = [
+        pltpu.make_async_copy(volts_hbm.at[part, pl.ds(top, ROWS), reach], volts.at[part], sems.at[part])
+        for part in range(2)
+    ]
+    coming += [pltpu.make_async_copy(x, waves.at[i], sems.at[2 + i]) for i, x in enumerate((cosines, sines))]
+    for copy in coming:
+        copy.start()
     for t in range(taps):
         taps_wide[t] = jnp.broadcast_to(prototype[t : t + 1, :], taps_wide.shape[1:])
-    cos_t, sin_t = cosines[...].astype(table.dtype), sines[...].astype(table.dtype)
-    table[:depth, :depth] = cos_t
-    table[:depth, depth:] = -sin_t
-    table[depth:, :depth] = sin_t
-    table[depth:, depth:] = cos_t
+
+    for part in range(2):
+        coming[part].wait()
+
+        def strip(step, carry, part=part):
+            j, n1 = step // RADIX, step % RADIX
+            base = pl.multiple_of(n1 * depth + j * LANES, LANES)
+            sums = [None] * frames
+            for seg in range(frames + taps - 1):
+                start = pl.multiple_of(seg * length + base, LANES)
+                value = volts[part, :, pl.ds(start, LANES)].astype(jnp.float32)
+                for f in range(max(0, seg - taps + 1), min(frames, seg + 1)):
+                    coef = taps_wide[seg - f, :, pl.ds(base, LANES)]
+                    term = value * jnp.concatenate([coef, coef], axis=0)
+                    sums[f] = term if sums[f] is None else sums[f] + term
+                if seg >= taps - 1:
+                    filtered[j, part, n1, seg - taps + 1] = sums[seg - taps + 1]
+            return carry
+
+        lax.fori_loop(0, bands * RADIX, strip, 0)
 
     def column(j, carry):
         lane = pl.multiple_of(j * LANES, LANES)
 
-        def strip(n1, inner):
-            base = pl.multiple_of(n1 * depth + j * LANES, LANES)
-            for part in range(2):
-                sums = [None] * frames
-                for seg in range(frames + taps - 1):
-                    start = pl.multiple_of((first + seg) * length + base, LANES)
-                    value = volts[part, :, pl.ds(start, LANES)].astype(jnp.float32)
-                    for f in range(max(0, seg - taps + 1), min(frames, seg + 1)):
-                        coef = taps_wide[seg - f, :, pl.ds(base, LANES)]
-                        term = value * jnp.concatenate([coef, coef], axis=0)
-                        sums[f] = term if sums[f] is None else sums[f] + term
-                    if seg >= taps - 1:
-                        filtered[part, n1, seg - taps + 1] = sums[seg - taps + 1]
-            return inner
-
-        lax.fori_loop(0, RADIX, strip, 0)
-
         def butterfly(f, inner):
             re, im = radix8(
-                [filtered[0, n1, f] for n1 in range(RADIX)],
-                [filtered[1, n1, f] for n1 in range(RADIX)],
+                [filtered[j, 0, n1, f] for n1 in range(RADIX)],
+                [filtered[j, 1, n1, f] for n1 in range(RADIX)],
             )
             for b in range(RADIX):
                 turned_r, turned_i = re[b], im[b]
@@ -146,6 +153,13 @@
 
     lax.fori_loop(0, bands, column, 0)
 
+    for copy in coming[2:]:
+        copy.wait()
+    cos_t, sin_t = waves[0].astype(table.dtype), waves[1].astype(table.dtype)
+    table[:depth, :depth] = cos_t
+    table[:depth, depth:] = -sin_t
+    table[depth:, :depth] = sin_t
+    table[depth:, depth:] = cos_t
     rows = frames * ROWS
     joined = RADIX
     while joined * rows > 1024:
@@ -179,7 +193,7 @@
 def channelise(row_block, volts, prototype, tables, first, frames, far):
     near = RADIX // far
     taps = prototype.shape[0]
-    length = volts.shape[2] if first > 0 else (frames + taps - 1) * NCH
+    length = (frames + taps - 1) * NCH
     depth = NCH // RADIX
     bands = depth // LANES
     wide = 2 * frames * LANES
@@ -189,18 +203,25 @@
             num_scalar_prefetch=1,
             grid=(1,),
             in_specs=[
-                pl.BlockSpec((2, ROWS, length), lambda i, row: (0, row[0], 0)),
-            ]
-            + [pl.BlockSpec(x.shape, lambda i, row: (0, 0)) for x in (prototype, *tables)],
+                pl.BlockSpec(memory_space=pl.ANY),
+                pl.BlockSpec(prototype.shape, lambda i, row: (0, 0)),
+                pl.BlockSpec(memory_space=pl.ANY),
+                pl.BlockSpec(memory_space=pl.ANY),
+                pl.BlockSpec(tables[2].shape, lambda i, row: (0, 0)),
+                pl.BlockSpec(tables[3].shape, lambda i, row: (0, 0)),
+            ],
             out_specs=[
                 pl.BlockSpec((bands, near, far, ROWS, wide), lambda i, row: (0, 0, 0, 0, 0)),
                 pl.BlockSpec((RADIX, frames, ROWS, 2 * depth), lambda i, row: (0, 0, 0, 0)),
             ],
             scratch_shapes=[
+                pltpu.VMEM((2, ROWS, length), jnp.bfloat16),
+                pltpu.VMEM((2, depth, depth), jnp.float32),
                 pltpu.VMEM((taps, 8, NCH), jnp.float32),
                 pltpu.VMEM((2 * depth, 2 * depth), jnp.bfloat16),
-                pltpu.VMEM((2, RADIX, frames, ROWS, LANES), jnp.float32),
+                pltpu.VMEM((bands, 2, RADIX, frames, ROWS, LANES), jnp.float32),
                 pltpu.VMEM((RADIX, frames * ROWS, 2 * depth), jnp.float32),
+                pltpu.SemaphoreType.DMA((4,)),
             ],
         ),
         out_shape=[
@@ -437,7 +458,7 @@
             pltpu.VMEM(weights.shape, weights.dtype),
             pltpu.SemaphoreType.DMA,
         ],
-        compiler_params=pltpu.CompilerParams(vmem_limit_bytes=VMEM // 2),
+        compiler_params=pltpu.CompilerParams(vmem_limit_bytes=VMEM),
         cost_estimate=NO_COST,
     )(spectra, chooser, weights)
 

time: 271 us -> 267 us (0.985)
  local copies, waits for them, and re-layouts: 9.77 us -> 6.04 us
    unnamed x15 -> x11, local copies, waits for them, and re-layouts: 5.93 us -> 2.23 us
  transfers between devices with their start and end apart: 4 -> 4, of which waited for: 4 -> 4; matrix products, arithmetic and copies ran while one was open for 7% -> 7% of each run, Pallas kernels for 39% -> 40%
where the time goes in v11:
time: 267 us; the launch traced here: 266 us
  Pallas kernels  125 us (47%)
  waiting for transfers between devices  96.2 us (36%)
  starting transfers between devices  22.7 us (9%)
  other arithmetic  15.1 us (6%)
  local copies, waits for them, and re-layouts  6.04 us (2%)
    all_to_all x4, waiting for transfers between devices, exchange(): lax.all_to_all(x, ('sb', 'near', 'far'), split_axis=0, concat_axis=0, til...  96.2 us
    pallas_call x3, Pallas kernels, channelise(): pl.pallas_call(functools.partial(channel_kernel, first), grid_spec=pltpu....  68.4 us
    all_to_all x4, starting transfers between devices, exchange(): lax.all_to_all(x, ('sb', 'near', 'far'), split_axis=0, concat_axis=0, til...  22.7 us
    pallas_call x1, Pallas kernels, slot_spectra(): pl.pallas_call(slot_kernel, out_shape=jax.ShapeDtypeStruct((rows // per,...  19.7 us
    pallas_call x1, Pallas kernels, correlate(): pl.pallas_call(kernel, in_specs=[pl.BlockSpec(memory_space=pl.ANY)] * len...  17.2 us
    pallas_call x1, Pallas kernels, beam_weights(): pl.pallas_call(weight_kernel, grid=(slots,), in_specs=[pl.BlockSpec(memor...  12.4 us
    pallas_call x1, Pallas kernels, combine(): pl.pallas_call(kernel, in_specs=[pl.BlockSpec(memory_space=pltpu.VMEM)] *...  7.33 us
  transfers between devices with their start and end apart: 4, of which 4 were waited for; matrix products, arithmetic and copies ran while one was open for 7% of the time, Pallas kernels for 40%

profile of v11, /device:TPU:0, one launch (start us, length us, event | category | flops | bytes accessed | tf_op | source)
XLA Modules:
  0.0 266.1 jit_solution(15574192497393600917)
XLA Ops:
  0.6 11.9 %shard_map.122 = (bf16[4,2,4,16,1024]{4,3,2,1,0:T(8,128)(2,1)}, bf16[8,4,16,1024]{3,2,1,0:T(8,128)(2,1)}) custom-call(s32[1]{0:T(128)} %bitcast.row_block, bf16[2,128,126976]{2,1,0:T(8,128)(2,1)} %volts_hbm.5, f32[16,4096]{1,0:T(8,128)} %prototype.5, f32[512,512]{1,0:T(8,128)} %constant.129.clone.cosines, f32[512,512]{1,0:T(8,128)} %constant.130.clone.sines, ...), custom_call_target="tpu_custom_call" | custom-call | flops 2500000000 | bytes 1 | tf_op jit(solution)/shard_map/pallas_call | solution.py:200
  12.5 7.3 %all-to-all-start = ((bf16[32,16,1024]{2,1,0:T(8,128)(2,1)}), bf16[32,16,1024]{2,1,0:T(8,128)(2,1)S(1)}, u32[]{:S(2)}, u32[]{:S(2)}) async-start(bf16[32,16,1024]{2,1,0:T(8,128)(2,1)} %bitcast.36), calls=%async_computation | async-start | bytes 2097152 | tf_op jit(solution)/shard_map/all_to_all | solution.py:478
  20.0 25.1 %shard_map.123 = (bf16[4,2,4,16,3072]{4,3,2,1,0:T(8,128)(2,1)}, bf16[8,12,16,1024]{3,2,1,0:T(8,128)(2,1)}) custom-call(s32[1]{0:T(128)} %bitcast.2.row_block, bf16[2,128,126976]{2,1,0:T(8,128)(2,1)} %volts_hbm.5, f32[16,4096]{1,0:T(8,128)} %prototype.5, f32[512,512]{1,0:T(8,128)} %constant.129.clone.cosines, f32[512,512]{1,0:T(8,128)} %constant.130.clone.sines, ...), custom_call_target="tpu_custom_call" | custom-call | flops 7500000256 | bytes 1 | tf_op jit(solution)/shard_map/pallas_call | solution.py:200
  45.1 1.6 all-to-all-done
  46.7 1.0 copy-done
  47.6 4.3 %all-to-all-start.1 = ((bf16[32,16,3072]{2,1,0:T(8,128)(2,1)}), bf16[32,16,3072]{2,1,0:T(8,128)(2,1)S(1)}, u32[]{:S(2)}, u32[]{:S(2)}) async-start(bf16[32,16,3072]{2,1,0:T(8,128)(2,1)} %bitcast.35), calls=%async_computation.1 | async-start | bytes 6291456 | tf_op jit(solution)/shard_map/all_to_all | solution.py:478
  52.1 0.1 add.228
  52.2 0.1 mul.215
  52.4 31.4 %shard_map.124 = (bf16[4,2,4,16,4096]{4,3,2,1,0:T(8,128)(2,1)}, bf16[8,16,16,1024]{3,2,1,0:T(8,128)(2,1)}) custom-call(s32[1]{0:T(128)} %bitcast.5.row_block, bf16[2,128,126976]{2,1,0:T(8,128)(2,1)} %volts_hbm.5, f32[16,4096]{1,0:T(8,128)} %prototype.5, f32[512,512]{1,0:T(8,128)} %constant.129.clone.cosines, f32[512,512]{1,0:T(8,128)} %constant.130.clone.sines, ...), custom_call_target="tpu_custom_call" | custom-call | flops 10000000000 | bytes 1 | tf_op jit(solution)/shard_map/pallas_call | solution.py:200
  83.8 1.2 reduce-window.6
  85.0 0.2 slice_reduce_fusion
  85.3 0.2 reduce-window.9
  85.6 0.4 fusion.1
  86.1 0.1 reshape.322
  86.2 1.1 reshape.326
  87.5 1.1 copy.25
  88.7 0.1 mul.221
  88.8 0.6 dynamic_slice.3.channel
  89.4 2.2 add_select_fusion.1.row_branch
  91.6 3.9 %fusion.9 = (f32[1280,128]{1,0:T(8,128)}, f32[1280,128]{1,0:T(8,128)}) fusion(s32[1280]{0:T(1024)S(1)} %fusion.14), kind=kLoop, calls=%fused_computation.20 | loop fusion | flops 2293760 | bytes 1315840 | tf_op jit(solution)/shard_map/sin | solution.py:34
  95.5 5.2 %sine_multiply_fusion = (f32[1280,4]{1,0:T(8,128)}, f32[1280,4]{1,0:T(8,128)}) fusion(f32[1280,4]{1,0:T(8,128)} %copy.25, f32[1280]{0:T(1024)S(1)} %mul.221), kind=kLoop, calls=%fused_computation.17 | loop fusion | flops 15360 | bytes 66560 | tf_op jit(solution)/shard_map/mul | solution.py:267
  100.7 19.7 %shard_map.125 = bf16[32,40,512]{2,1,0:T(8,128)(2,1)} custom-call(s32[1280,1]{1,0:T(8,128)} %add_select_fusion.1.row_branch, f32[1280,4]{1,0:T(8,128)} %get-tuple-element.69.hi_c, f32[1280,4]{1,0:T(8,128)} %get-tuple-element.68.hi_s, f32[1280,128]{1,0:T(8,128)} %get-tuple-element.71.lo_c, f32[1280,128]{1,0:T(8,128)} %get-tuple-element.70.lo_s, ...), custom_call_target="tpu_custom_call" | custom-call | flops 10000000000 | bytes 1 | tf_op jit(solution)/shard_map/pallas_call | solution.py:273
  120.3 2.4 all-to-all-done.1
  122.7 4.8 %all-to-all-start.2 = ((bf16[32,16,4096]{2,1,0:T(8,128)(2,1)}), bf16[32,16,4096]{2,1,0:T(8,128)(2,1)}, u32[]{:S(2)}, u32[]{:S(2)}) async-start(bf16[32,16,4096]{2,1,0:T(8,128)(2,1)} %bitcast.34), calls=%async_computation.2 | async-start | bytes 8388608 | tf_op jit(solution)/shard_map/all_to_all | solution.py:478
  128.0 1.3 compare_convert_fusion.choose
  129.3 12.4 %shard_map.126.weight_hbm = bf16[20,512,256]{2,1,0:T(8,128)(2,1)} custom-call(s32[20]{0:T(128)} %dynamic_slice.3.channel, f32[256,256]{1,0:T(8,128)} %delays.1, f32[256,256]{1,0:T(8,128)} %gains.1), custom_call_target="tpu_custom_call" | custom-call | flops 1 | bytes 1 | tf_op jit(solution)/shard_map/pallas_call | solution.py:387
  141.6 78.4 %all-to-all-done.2 = bf16[32,16,4096]{2,1,0:T(8,128)(2,1)} async-done(((bf16[32,16,4096]{2,1,0:T(8,128)(2,1)}), bf16[32,16,4096]{2,1,0:T(8,128)(2,1)}, u32[]{:S(2)}, u32[]{:S(2)}) %all-to-all-start.2) | async-done | bytes 4194336 | tf_op jit(solution)/shard_map/all_to_all | solution.py:478
  220.1 6.3 %all-to-all-start.3 = ((bf16[32,40,512]{2,1,0:T(8,128)(2,1)}), bf16[32,40,512]{2,1,0:T(8,128)(2,1)}, u32[]{:S(2)}, u32[]{:S(2)}) async-start(bf16[32,40,512]{2,1,0:T(8,128)(2,1)} %shard_map.125), calls=%async_computation.3 | async-start | bytes 2621440 | tf_op jit(solution)/shard_map/all_to_all | solution.py:478
  226.3 1.2 copy-done.1
  227.5 17.2 %shard_map.127 = f32[2,1024,1024]{2,1,0:T(8,128)} custom-call(bf16[4,2,4,16,1024]{4,3,2,1,0:T(8,128)(2,1)S(1)} %bitcast.32, bf16[4,2,4,16,3072]{4,3,2,1,0:T(8,128)(2,1)S(1)} %bitcast.31, bf16[4,2,4,16,4096]{4,3,2,1,0:T(8,128)(2,1)} %bitcast.9.refs_2_), custom_call_target="tpu_custom_call" | custom-call | flops 1 | bytes 1 | tf_op jit(solution)/shard_map/pallas_call | solution.py:349
  244.7 13.9 %all-to-all-done.3.spectrum = bf16[32,40,512]{2,1,0:T(8,128)(2,1)} async-done(((bf16[32,40,512]{2,1,0:T(8,128)(2,1)}), bf16[32,40,512]{2,1,0:T(8,128)(2,1)}, u32[]{:S(2)}, u32[]{:S(2)}) %all-to-all-start.3) | async-done | bytes 1310752 | tf_op jit(solution)/shard_map/all_to_all | solution.py:478
  258.6 7.3 %shard_map.128 = f32[1,20,2,16,512]{4,3,2,1,0:T(8,128)} custom-call(bf16[32,40,512]{2,1,0:T(8,128)(2,1)} %all-to-all-done.3.spectrum, bf16[1024,512]{1,0:T(8,128)(2,1)} %compare_convert_fusion.choose, bf16[20,512,256]{2,1,0:T(8,128)(2,1)} %shard_map.126.weight_hbm), custom_call_target="tpu_custom_call" | custom-call | flops 1 | bytes 1 | tf_op jit(solution)/shard_map/pallas_call | solution.py:451
  (40 shorter events, 1.1 us)
Async XLA Ops:
  12.5 34.1 %all-to-all-start = ((bf16[32,16,1024]{2,1,0:T(8,128)(2,1)}), bf16[32,16,1024]{2,1,0:T(8,128)(2,1)S(1)}, u32[]{:S(2)}, u32[]{:S(2)}) async-start(bf16[32,16,1024]{2,1,0:T(8,128)(2,1)} %bitcast.36), calls=%async_computation | async-start | bytes 2097152 | tf_op jit(solution)/shard_map/all_to_all | solution.py:478
  46.7 1.0 copy-start
  47.6 75.0 %all-to-all-start.1 = ((bf16[32,16,3072]{2,1,0:T(8,128)(2,1)}), bf16[32,16,3072]{2,1,0:T(8,128)(2,1)S(1)}, u32[]{:S(2)}, u32[]{:S(2)}) async-start(bf16[32,16,3072]{2,1,0:T(8,128)(2,1)} %bitcast.35), calls=%async_computation.1 | async-start | bytes 6291456 | tf_op jit(solution)/shard_map/all_to_all | solution.py:478
  52.4 31.4 %copy-start.3 = (s32[384,1]{0,1:T(1,128)S(1)}, s32[384,1]{0,1:T(1,128)}, u32[]{:S(2)}) copy-start(s32[384,1]{0,1:T(1,128)} %param.17) | copy-start | bytes 4612
  52.4 33.2 %copy-start.2 = (s32[384]{0:T(512)S(1)}, s32[384]{0:T(512)}, u32[]{:S(2)}) copy-start(s32[384]{0:T(512)} %param.13) | copy-start | bytes 4612
  122.7 5.3 %copy-start.4 = (s32[256]{0:T(256)S(1)}, s32[256]{0:T(256)}, u32[]{:S(2)}) copy-start(s32[256]{0:T(256)} %param.14) | copy-start | bytes 3076
  122.7 97.4 %all-to-all-start.2 = ((bf16[32,16,4096]{2,1,0:T(8,128)(2,1)}), bf16[32,16,4096]{2,1,0:T(8,128)(2,1)}, u32[]{:S(2)}, u32[]{:S(2)}) async-start(bf16[32,16,4096]{2,1,0:T(8,128)(2,1)} %bitcast.34), calls=%async_computation.2 | async-start | bytes 8388608 | tf_op jit(solution)/shard_map/all_to_all | solution.py:478
  220.1 38.6 %all-to-all-start.3 = ((bf16[32,40,512]{2,1,0:T(8,128)(2,1)}), bf16[32,40,512]{2,1,0:T(8,128)(2,1)}, u32[]{:S(2)}, u32[]{:S(2)}) async-start(bf16[32,40,512]{2,1,0:T(8,128)(2,1)} %shard_map.125), calls=%async_computation.3 | async-start | bytes 2621440 | tf_op jit(solution)/shard_map/all_to_all | solution.py:478
  226.3 1.2 copy-start.1

commit v12 on v11

--- a/solution.py
+++ b/solution.py
@@ -111,30 +111,36 @@
     for t in range(taps):
         taps_wide[t] = jnp.broadcast_to(prototype[t : t + 1, :], taps_wide.shape[1:])
 
+    def strip(part, step):
+        j, n1 = step // RADIX, step % RADIX
+        base = pl.multiple_of(n1 * depth + j * LANES, LANES)
+        sums = [None] * frames
+        for seg in range(frames + taps - 1):
+            start = pl.multiple_of(seg * length + base, LANES)
+            value = volts[part, :, pl.ds(start, LANES)].astype(jnp.float32)
+            for f in range(max(0, seg - taps + 1), min(frames, seg + 1)):
+                coef = taps_wide[seg - f, :, pl.ds(base, LANES)]
+                term = value * jnp.concatenate([coef, coef], axis=0)
+                sums[f] = term if sums[f] is None else sums[f] + term
+            if seg >= taps - 1:
+                filtered[j, part, n1, seg - taps + 1] = sums[seg - taps + 1]
+
+    together = 4 if frames <= 4 else 1
+
     for part in range(2):
         coming[part].wait()
 
-        def strip(step, carry, part=part):
-            j, n1 = step // RADIX, step % RADIX
-            base = pl.multiple_of(n1 * depth + j * LANES, LANES)
-            sums = [None] * frames
-            for seg in range(frames + taps - 1):
-                start = pl.multiple_of(seg * length + base, LANES)
-                value = volts[part, :, pl.ds(start, LANES)].astype(jnp.float32)
-                for f in range(max(0, seg - taps + 1), min(frames, seg + 1)):
-                    coef = taps_wide[seg - f, :, pl.ds(base, LANES)]
-                    term = value * jnp.concatenate([coef, coef], axis=0)
-                    sums[f] = term if sums[f] is None else sums[f] + term
-                if seg >= taps - 1:
-                    filtered[j, part, n1, seg - taps + 1] = sums[seg - taps + 1]
+        def strips(step, carry, part=part):
+            for k in range(together):
+                strip(part, step * together + k)
             return carry
 
-        lax.fori_loop(0, bands * RADIX, strip, 0)
+        lax.fori_loop(0, bands * RADIX // together, strips, 0)
 
     def column(j, carry):
         lane = pl.multiple_of(j * LANES, LANES)
 
-        def butterfly(f, inner):
+        def butterfly(f):
             re, im = radix8(
                 [filtered[j, 0, n1, f] for n1 in range(RADIX)],
                 [filtered[j, 1, n1, f] for n1 in range(RADIX)],
@@ -146,9 +152,13 @@
                     turned_r, turned_i = re[b] * cos_t + im[b] * sin_t, im[b] * cos_t - re[b] * sin_t
                 branches[b, f, :, pl.ds(lane, LANES)] = turned_r.astype(branches.dtype)
                 branches[b, f, :, pl.ds(pl.multiple_of(depth + lane, LANES), LANES)] = turned_i.astype(branches.dtype)
+
+        def pair(step, inner):
+            butterfly(2 * step)
+            butterfly(2 * step + 1)
             return inner
 
-        lax.fori_loop(0, frames, butterfly, 0)
+        lax.fori_loop(0, frames // 2, pair, 0)
         return carry
 
     lax.fori_loop(0, bands, column, 0)

time: 267 us -> 266 us (level)
  no operation moved by 1% of the time
where the time goes in v12:
time: 266 us; the launch traced here: 265 us
  Pallas kernels  124 us (47%)
  waiting for transfers between devices  96.5 us (36%)
  starting transfers between devices  22.5 us (8%)
  other arithmetic  15.1 us (6%)
  local copies, waits for them, and re-layouts  6.04 us (2%)
    all_to_all x4, waiting for transfers between devices, exchange(): lax.all_to_all(x, ('sb', 'near', 'far'), split_axis=0, concat_axis=0, til...  96.5 us
    pallas_call x3, Pallas kernels, channelise(): pl.pallas_call(functools.partial(channel_kernel, first), grid_spec=pltpu....  67.2 us
    all_to_all x4, starting transfers between devices, exchange(): lax.all_to_all(x, ('sb', 'near', 'far'), split_axis=0, concat_axis=0, til...  22.5 us
    pallas_call x1, Pallas kernels, slot_spectra(): pl.pallas_call(slot_kernel, out_shape=jax.ShapeDtypeStruct((rows // per,...  19.7 us
    pallas_call x1, Pallas kernels, correlate(): pl.pallas_call(kernel, in_specs=[pl.BlockSpec(memory_space=pl.ANY)] * len...  17.2 us
    pallas_call x1, Pallas kernels, beam_weights(): pl.pallas_call(weight_kernel, grid=(slots,), in_specs=[pl.BlockSpec(memor...  12.4 us
    pallas_call x1, Pallas kernels, combine(): pl.pallas_call(kernel, in_specs=[pl.BlockSpec(memory_space=pltpu.VMEM)] *...  7.33 us
  transfers between devices with their start and end apart: 4, of which 4 were waited for; matrix products, arithmetic and copies ran while one was open for 7% of the time, Pallas kernels for 40%

profile of v12, /device:TPU:0, one launch (start us, length us, event | category | flops | bytes accessed | tf_op | source)
XLA Modules:
  0.0 265.1 jit_solution(2255428171133241517)
XLA Ops:
  0.6 11.0 %shard_map.122 = (bf16[4,2,4,16,1024]{4,3,2,1,0:T(8,128)(2,1)}, bf16[8,4,16,1024]{3,2,1,0:T(8,128)(2,1)}) custom-call(s32[1]{0:T(128)} %bitcast.row_block, bf16[2,128,126976]{2,1,0:T(8,128)(2,1)} %volts_hbm.5, f32[16,4096]{1,0:T(8,128)} %prototype.5, f32[512,512]{1,0:T(8,128)} %constant.129.clone.cosines, f32[512,512]{1,0:T(8,128)} %constant.130.clone.sines, ...), custom_call_target="tpu_custom_call" | custom-call | flops 2500000000 | bytes 1 | tf_op jit(solution)/shard_map/pallas_call | solution.py:210
  11.7 7.3 %all-to-all-start = ((bf16[32,16,1024]{2,1,0:T(8,128)(2,1)}), bf16[32,16,1024]{2,1,0:T(8,128)(2,1)S(1)}, u32[]{:S(2)}, u32[]{:S(2)}) async-start(bf16[32,16,1024]{2,1,0:T(8,128)(2,1)} %bitcast.36), calls=%async_computation | async-start | bytes 2097152 | tf_op jit(solution)/shard_map/all_to_all | solution.py:488
  19.1 25.0 %shard_map.123 = (bf16[4,2,4,16,3072]{4,3,2,1,0:T(8,128)(2,1)}, bf16[8,12,16,1024]{3,2,1,0:T(8,128)(2,1)}) custom-call(s32[1]{0:T(128)} %bitcast.2.row_block, bf16[2,128,126976]{2,1,0:T(8,128)(2,1)} %volts_hbm.5, f32[16,4096]{1,0:T(8,128)} %prototype.5, f32[512,512]{1,0:T(8,128)} %constant.129.clone.cosines, f32[512,512]{1,0:T(8,128)} %constant.130.clone.sines, ...), custom_call_target="tpu_custom_call" | custom-call | flops 7500000256 | bytes 1 | tf_op jit(solution)/shard_map/pallas_call | solution.py:210
  44.1 1.7 all-to-all-done
  45.8 1.0 copy-done
  46.8 4.2 %all-to-all-start.1 = ((bf16[32,16,3072]{2,1,0:T(8,128)(2,1)}), bf16[32,16,3072]{2,1,0:T(8,128)(2,1)S(1)}, u32[]{:S(2)}, u32[]{:S(2)}) async-start(bf16[32,16,3072]{2,1,0:T(8,128)(2,1)} %bitcast.35), calls=%async_computation.1 | async-start | bytes 6291456 | tf_op jit(solution)/shard_map/all_to_all | solution.py:488
  51.1 0.1 add.228
  51.2 0.1 mul.215
  51.4 31.2 %shard_map.124 = (bf16[4,2,4,16,4096]{4,3,2,1,0:T(8,128)(2,1)}, bf16[8,16,16,1024]{3,2,1,0:T(8,128)(2,1)}) custom-call(s32[1]{0:T(128)} %bitcast.5.row_block, bf16[2,128,126976]{2,1,0:T(8,128)(2,1)} %volts_hbm.5, f32[16,4096]{1,0:T(8,128)} %prototype.5, f32[512,512]{1,0:T(8,128)} %constant.129.clone.cosines, f32[512,512]{1,0:T(8,128)} %constant.130.clone.sines, ...), custom_call_target="tpu_custom_call" | custom-call | flops 10000000000 | bytes 1 | tf_op jit(solution)/shard_map/pallas_call | solution.py:210
  82.7 1.2 reduce-window.6
  83.9 0.2 slice_reduce_fusion
  84.1 0.2 reduce-window.9
  84.4 0.4 fusion.1
  85.0 0.1 reshape.322
  85.1 1.1 reshape.326
  86.3 1.1 copy.25
  87.6 0.1 mul.221
  87.7 0.6 dynamic_slice.3.channel
  88.3 2.2 add_select_fusion.1.row_branch
  90.5 3.9 %fusion.9 = (f32[1280,128]{1,0:T(8,128)}, f32[1280,128]{1,0:T(8,128)}) fusion(s32[1280]{0:T(1024)S(1)} %fusion.14), kind=kLoop, calls=%fused_computation.20 | loop fusion | flops 2293760 | bytes 1315840 | tf_op jit(solution)/shard_map/sin | solution.py:34
  94.4 5.2 %sine_multiply_fusion = (f32[1280,4]{1,0:T(8,128)}, f32[1280,4]{1,0:T(8,128)}) fusion(f32[1280,4]{1,0:T(8,128)} %copy.25, f32[1280]{0:T(1024)S(1)} %mul.221), kind=kLoop, calls=%fused_computation.17 | loop fusion | flops 15360 | bytes 66560 | tf_op jit(solution)/shard_map/mul | solution.py:277
  99.5 19.7 %shard_map.125 = bf16[32,40,512]{2,1,0:T(8,128)(2,1)} custom-call(s32[1280,1]{1,0:T(8,128)} %add_select_fusion.1.row_branch, f32[1280,4]{1,0:T(8,128)} %get-tuple-element.69.hi_c, f32[1280,4]{1,0:T(8,128)} %get-tuple-element.68.hi_s, f32[1280,128]{1,0:T(8,128)} %get-tuple-element.71.lo_c, f32[1280,128]{1,0:T(8,128)} %get-tuple-element.70.lo_s, ...), custom_call_target="tpu_custom_call" | custom-call | flops 10000000000 | bytes 1 | tf_op jit(solution)/shard_map/pallas_call | solution.py:283
  119.2 2.5 all-to-all-done.1
  121.7 4.8 %all-to-all-start.2 = ((bf16[32,16,4096]{2,1,0:T(8,128)(2,1)}), bf16[32,16,4096]{2,1,0:T(8,128)(2,1)}, u32[]{:S(2)}, u32[]{:S(2)}) async-start(bf16[32,16,4096]{2,1,0:T(8,128)(2,1)} %bitcast.34), calls=%async_computation.2 | async-start | bytes 8388608 | tf_op jit(solution)/shard_map/all_to_all | solution.py:488
  127.0 1.3 compare_convert_fusion.choose
  128.3 12.4 %shard_map.126.weight_hbm = bf16[20,512,256]{2,1,0:T(8,128)(2,1)} custom-call(s32[20]{0:T(128)} %dynamic_slice.3.channel, f32[256,256]{1,0:T(8,128)} %delays.1, f32[256,256]{1,0:T(8,128)} %gains.1), custom_call_target="tpu_custom_call" | custom-call | flops 1 | bytes 1 | tf_op jit(solution)/shard_map/pallas_call | solution.py:397
  140.7 78.4 %all-to-all-done.2 = bf16[32,16,4096]{2,1,0:T(8,128)(2,1)} async-done(((bf16[32,16,4096]{2,1,0:T(8,128)(2,1)}), bf16[32,16,4096]{2,1,0:T(8,128)(2,1)}, u32[]{:S(2)}, u32[]{:S(2)}) %all-to-all-start.2) | async-done | bytes 4194336 | tf_op jit(solution)/shard_map/all_to_all | solution.py:488
  219.1 6.3 %all-to-all-start.3 = ((bf16[32,40,512]{2,1,0:T(8,128)(2,1)}), bf16[32,40,512]{2,1,0:T(8,128)(2,1)}, u32[]{:S(2)}, u32[]{:S(2)}) async-start(bf16[32,40,512]{2,1,0:T(8,128)(2,1)} %shard_map.125), calls=%async_computation.3 | async-start | bytes 2621440 | tf_op jit(solution)/shard_map/all_to_all | solution.py:488
  225.3 1.2 copy-done.1
  226.6 17.2 %shard_map.127 = f32[2,1024,1024]{2,1,0:T(8,128)} custom-call(bf16[4,2,4,16,1024]{4,3,2,1,0:T(8,128)(2,1)S(1)} %bitcast.32, bf16[4,2,4,16,3072]{4,3,2,1,0:T(8,128)(2,1)S(1)} %bitcast.31, bf16[4,2,4,16,4096]{4,3,2,1,0:T(8,128)(2,1)} %bitcast.9.refs_2_), custom_call_target="tpu_custom_call" | custom-call | flops 1 | bytes 1 | tf_op jit(solution)/shard_map/pallas_call | solution.py:359
  243.7 13.9 %all-to-all-done.3.spectrum = bf16[32,40,512]{2,1,0:T(8,128)(2,1)} async-done(((bf16[32,40,512]{2,1,0:T(8,128)(2,1)}), bf16[32,40,512]{2,1,0:T(8,128)(2,1)}, u32[]{:S(2)}, u32[]{:S(2)}) %all-to-all-start.3) | async-done | bytes 1310752 | tf_op jit(solution)/shard_map/all_to_all | solution.py:488
  257.6 7.3 %shard_map.128 = f32[1,20,2,16,512]{4,3,2,1,0:T(8,128)} custom-call(bf16[32,40,512]{2,1,0:T(8,128)(2,1)} %all-to-all-done.3.spectrum, bf16[1024,512]{1,0:T(8,128)(2,1)} %compare_convert_fusion.choose, bf16[20,512,256]{2,1,0:T(8,128)(2,1)} %shard_map.126.weight_hbm), custom_call_target="tpu_custom_call" | custom-call | flops 1 | bytes 1 | tf_op jit(solution)/shard_map/pallas_call | solution.py:461
  (40 shorter events, 1.1 us)
Async XLA Ops:
  11.7 34.1 %all-to-all-start = ((bf16[32,16,1024]{2,1,0:T(8,128)(2,1)}), bf16[32,16,1024]{2,1,0:T(8,128)(2,1)S(1)}, u32[]{:S(2)}, u32[]{:S(2)}) async-start(bf16[32,16,1024]{2,1,0:T(8,128)(2,1)} %bitcast.36), calls=%async_computation | async-start | bytes 2097152 | tf_op jit(solution)/shard_map/all_to_all | solution.py:488
  45.8 1.0 copy-start
  46.8 74.9 %all-to-all-start.1 = ((bf16[32,16,3072]{2,1,0:T(8,128)(2,1)}), bf16[32,16,3072]{2,1,0:T(8,128)(2,1)S(1)}, u32[]{:S(2)}, u32[]{:S(2)}) async-start(bf16[32,16,3072]{2,1,0:T(8,128)(2,1)} %bitcast.35), calls=%async_computation.1 | async-start | bytes 6291456 | tf_op jit(solution)/shard_map/all_to_all | solution.py:488
  51.4 31.3 %copy-start.3 = (s32[384,1]{0,1:T(1,128)S(1)}, s32[384,1]{0,1:T(1,128)}, u32[]{:S(2)}) copy-start(s32[384,1]{0,1:T(1,128)} %param.17) | copy-start | bytes 4612
  51.4 33.0 %copy-start.2 = (s32[384]{0:T(512)S(1)}, s32[384]{0:T(512)}, u32[]{:S(2)}) copy-start(s32[384]{0:T(512)} %param.13) | copy-start | bytes 4612
  121.7 5.3 %copy-start.4 = (s32[256]{0:T(256)S(1)}, s32[256]{0:T(256)}, u32[]{:S(2)}) copy-start(s32[256]{0:T(256)} %param.14) | copy-start | bytes 3076
  121.7 97.4 %all-to-all-start.2 = ((bf16[32,16,4096]{2,1,0:T(8,128)(2,1)}), bf16[32,16,4096]{2,1,0:T(8,128)(2,1)}, u32[]{:S(2)}, u32[]{:S(2)}) async-start(bf16[32,16,4096]{2,1,0:T(8,128)(2,1)} %bitcast.34), calls=%async_computation.2 | async-start | bytes 8388608 | tf_op jit(solution)/shard_map/all_to_all | solution.py:488
  219.1 38.6 %all-to-all-start.3 = ((bf16[32,40,512]{2,1,0:T(8,128)(2,1)}), bf16[32,40,512]{2,1,0:T(8,128)(2,1)}, u32[]{:S(2)}, u32[]{:S(2)}) async-start(bf16[32,40,512]{2,1,0:T(8,128)(2,1)} %shard_map.125), calls=%async_computation.3 | async-start | bytes 2621440 | tf_op jit(solution)/shard_map/all_to_all | solution.py:488
  225.3 1.2 copy-start.1
